TPU v7x, 32 devices: a whole 2x2x4 slice. The times are simulated.
32 devices in a mesh: grp: 2 (over x), chol: 16 (over z, y, core).
Axes of the slice: x: 2, y: 2, z: 4, core: 2. Of those that a mesh axis runs over, the one named last changes fastest.
Arguments:
- theta: bfloat16 [32, 64, 1280], P(('grp', 'chol')), parts along dimension 0
- chol_tiles: bfloat16 [16, 4, 32, 64, 128], P('chol')
- screen: int32 [16, 4], P('chol'), may hold values 0 or 1
- tile_list: int32 [16, 4], replicated, may hold values from 0 to 9, as said below
Outputs:
- force_bias: float32 [32, 512], P(('grp', 'chol')), parts along dimension 0
- energy: float32 [32], P(('grp', 'chol')), parts along dimension 0
There are 2 independent parts, one for each index of `grp`. A program takes and returns all parts, laid end to end along the dimension named above; an argument that names none is the same for every part. Nothing has to cross between parts.
Inputs may be any that keep to these rules, and one draw needn't show every extreme that they name: `tile_list`: each row holds 4 different tiles.
All inputs are finite; a program needn't handle non-finite values. No bound on the sum of `screen` on one device may be relied on, other than what follows from the above.
Results may differ from a plain program's by a relative error of at most 0.0003.
Values may be sent and summed in bfloat16 or wider, within the bound.
No kernel may reach another device: no remote copies, remote signals or barrier semaphores. Data moves between devices by JAX's collectives and lax.ppermute only.
A program may use at most 128 MiB of HBM per device.

v0:
```python
import jax
import jax.numpy as jnp
from jax import lax
from jax.sharding import PartitionSpec as P


def block_terms(chol_tiles, screen, selected):
    masked = chol_tiles * screen[:, :, None, None, None].astype(jnp.bfloat16)
    inner_mat = jnp.einsum(
        "bmkaq,ncmq->nbkac", masked, selected, preferred_element_type=jnp.float32
    )
    bias_rows = jnp.trace(inner_mat, axis1=3, axis2=4)
    cross_sum = jnp.sum(inner_mat * jnp.swapaxes(inner_mat, 3, 4), axis=(3, 4))
    return (bias_rows, cross_sum)


def walker_terms(chol_tiles, screen, selected):
    walker_count = selected.shape[0]
    if walker_count % 16 == 0 and walker_count > 16:
        grouped = selected.reshape((walker_count // 16, 16) + selected.shape[1:])

        def one_block(walker_block):
            return block_terms(chol_tiles, screen, walker_block)

        bias_rows, cross_sum = lax.map(one_block, grouped)
        bias_rows = bias_rows.reshape((walker_count,) + bias_rows.shape[2:])
        cross_sum = cross_sum.reshape((walker_count,) + cross_sum.shape[2:])
    else:
        bias_rows, cross_sum = block_terms(chol_tiles, screen, selected)
    part_sums = jnp.sum(bias_rows * bias_rows - cross_sum, axis=(1, 2))
    return (bias_rows.reshape(walker_count, -1), part_sums)


def body(theta, chol_tiles, screen, tile_list):
    groups = lax.axis_size("chol")
    local_count, occupied, orbitals = theta.shape
    tile_width = chol_tiles.shape[-1]
    tile_count = orbitals // tile_width
    own_list = lax.dynamic_slice_in_dim(tile_list, lax.axis_index("chol"), 1, 0)[0]
    walkers = groups * local_count
    vector_count = chol_tiles.shape[0] * chol_tiles.shape[2]
    starting = (jnp.zeros((walkers, vector_count), jnp.float32), jnp.zeros((walkers,), jnp.float32))
    walker_piece = lax.all_gather(theta, "chol", axis=0, tiled=True)
    first_row = jnp.int32(0)
    piece_tiles = walker_piece.reshape(walker_piece.shape[0], occupied, tile_count, tile_width)
    selected = jnp.take(piece_tiles, own_list, axis=2)
    bias_flat, part_sums = walker_terms(chol_tiles, screen, selected)
    bias_all = lax.dynamic_update_slice_in_dim(starting[0], bias_flat, first_row, 0)
    part_all = lax.dynamic_update_slice_in_dim(starting[1], part_sums, first_row, 0)
    force_bias = lax.all_to_all(bias_all, "chol", split_axis=0, concat_axis=1, tiled=True)
    energy_sum = lax.psum_scatter(part_all, "chol", scatter_dimension=0, tiled=True)
    energy = energy_sum / (2.0 * occupied * occupied)
    return (force_bias, energy)


def solution(mesh):
    in_specs = (
        P(("grp", "chol"), None, None),
        P("chol", None, None, None, None),
        P("chol", None),
        P(),
    )
    out_specs = (P(("grp", "chol"), None), P(("grp", "chol")))
    return jax.shard_map(body, mesh=mesh, in_specs=in_specs, out_specs=out_specs, check_vma=False)
```

profile of v0, /device:TPU:0, one launch (start us, length us, event | category | flops | bytes accessed | tf_op | source)
XLA Modules:
  0.0 153.5 jit_solution(17158756118303717928)
XLA Ops:
  7.2 0.0 copy-start
  7.2 0.0 all-gather.2.cloned.1.call-start
  7.2 0.7 all-gather.2.cloned.1.call-update
  7.9 0.0 copy-done
  7.9 0.2 dynamic-slice_reduce_fusion
  8.2 0.7 convert_bitcast_fusion
  8.8 47.4 %all-gather.2.cloned.1.call-done = bf16[16,64,1280]{2,1,0:T(8,128)(2,1)} async-done(((bf16[1,64,1280]{2,1,0:T(8,128)(2,1)}), bf16[16,64,1280]{2,1,0:T(8,128)(2,1)}) %all-gather.2.cloned.1.call-update) | async-done | bytes 2621456 | tf_op jit(solution)/shard_map/all_gather | solution.py:43
  56.2 2.5 %copy_bitcast_fusion = bf16[16,64,10,128]{3,1,2,0:T(8,128)(2,1)S(1)} fusion(bf16[16,64,1280]{2,1,0:T(8,128)(2,1)} %all-gather.2.cloned.1.call-done), kind=kLoop, calls=%fused_computation.5 | loop fusion | bytes 5242880 | tf_op jit(solution)/shard_map/reshape | solution.py:45
  58.7 1.7 %gather_fusion = bf16[4,16,64,128]{3,2,1,0:T(8,128)(2,1)} fusion(bf16[16,64,10,128]{3,1,2,0:T(8,128)(2,1)S(1)} %copy_bitcast_fusion, s32[1024]{0:T(1024)S(1)} %pad_clamp_fusion), kind=kCustom, calls=%fused_computation | custom fusion | bytes 2097168 | tf_op jit(solution)/shard_map/jit(_take)/gather | solution.py:46
  60.4 9.7 %fusion.2 = f32[16,64,32,64,1]{3,1,4,2,0:T(8,128)} fusion(bf16[1,4,32,64,128]{4,3,2,1,0:T(8,128)(2,1)} %param.5, bf16[4]{0:T(256)(128)(2,1)S(1)} %convert_bitcast_fusion, bf16[4,16,64,128]{3,2,1,0:T(8,128)(2,1)} %gather_fusion, pred[4]{0:T(512)(128)(4,1)S(1)} %compare_and_fusion), kind=kOutput, calls=%fused_computation.6 | convolution fusion | flops 2149056512 | bytes 11534348 | tf_op jit(solution)/shard_map/bmkaq,ncmq->nbkac/dot_general | solution.py:9
  70.1 17.5 %copy.15 = f32[16,64,1,32,64]{1,4,3,0,2:T(8,128)} copy(f32[16,64,1,32,64]{4,1,3,0,2:T(8,128)} %bitcast.39) | data formatting | bytes 16777216 | tf_op jit(solution)/shard_map/bmkaq,ncmq->nbkac/dot_general | solution.py:9
  87.5 0.0 copy-start.1
  87.6 15.5 %fusion = (f32[16,32]{1,0:T(8,128)S(1)}, f32[16,32]{1,0:T(8,128)}) fusion(f32[16,64,32,64,1]{3,1,4,2,0:T(8,128)} %fusion.2, f32[16,64,1,32,64]{1,4,3,0,2:T(8,128)} %copy.15, pred[64,64]{1,0:T(8,128)(4,1)S(1)} %iota_compare_fusion), kind=kLoop, calls=%fused_computation.2 | loop fusion | flops 8387584 | bytes 16785408 | tf_op jit(solution)/shard_map/reduce_sum | solution.py:13
  103.0 3.5 %all-to-all-start = ((f32[16,1,32]{2,1,0:T(1,128)}), f32[16,1,32]{2,1,0:T(1,128)S(1)}, u32[]{:S(2)}, u32[]{:S(2)}) async-start(f32[16,1,32]{2,1,0:T(1,128)} %bitcast.10), calls=%async_computation | async-start | bytes 16384 | tf_op jit(solution)/shard_map/all_to_all | solution.py:50
  106.5 0.8 subtract_reduce_fusion
  107.4 0.0 copy-done.1
  107.4 0.6 dynamic-slice
  108.0 33.8 %all-reduce = f32[16]{0:T(128)S(1)} all-reduce(f32[16]{0:T(128)S(1)} %subtract_reduce_fusion), channel_id=2, replica_groups=mesh['grp'=2,'chol'=16] {'chol'}, use_global_device_ids=true, to_apply=%region_3.4.clone | all-reduce | flops 16 | bytes 128
  141.8 1.2 dynamic-slice.1
  143.6 0.0 all-to-all-done
  143.7 0.5 broadcast.47
  144.2 0.7 reduce.9
  144.8 0.7 all_to_all.14
  (4 shorter events, 0.0 us)
Async XLA Ops:
  7.2 0.8 copy-start
  7.2 49.1 %all-gather.2.cloned.1.call-start = ((), (), s32[]{:S(2)}) async-start(), calls=%async_computation.1 | async-start | bytes 2785280 | tf_op jit(solution)/shard_map/all_gather | solution.py:43
  87.5 19.8 %copy-start.1 = (u32[32]{0:T(128)S(1)}, u32[32]{0:T(128)}, u32[]{:S(2)}) copy-start(u32[32]{0:T(128)} %constant.37) | copy-start | bytes 388
  103.0 40.6 %all-to-all-start = ((f32[16,1,32]{2,1,0:T(1,128)}), f32[16,1,32]{2,1,0:T(1,128)S(1)}, u32[]{:S(2)}, u32[]{:S(2)}) async-start(f32[16,1,32]{2,1,0:T(1,128)} %bitcast.10), calls=%async_computation | async-start | bytes 16384 | tf_op jit(solution)/shard_map/all_to_all | solution.py:50
Sparse Core Ops, SparseCore 0:
  10.3 45.8 all-gather.1
where the time goes:
time: 154 us; the launch traced here: 153 us
  waiting for transfers between devices  48.1 us (31%)
  blocking collectives  33.8 us (22%)
  local copies, waits for them, and re-layouts  24.8 us (16%)
  other arithmetic  17.7 us (11%)
  between operations  15.9 us (10%)
  matrix products  9.69 us (6%)
  starting transfers between devices  3.51 us (2%)
    all_gather x1, waiting for transfers between devices, body(): walker_piece = lax.all_gather(theta, 'chol', axis=0, tiled=True)  47.4 us
    unnamed x1, blocking collectives  33.8 us
    dot_general x1, local copies, waits for them, and re-layouts, block_terms(): jnp.einsum('bmkaq,ncmq->nbkac', masked, selected, preferred_element_type=...  17.5 us
    reduce_sum x1, other arithmetic, block_terms(): cross_sum = jnp.sum(inner_mat * jnp.swapaxes(inner_mat, 3, 4), axis=(3, 4))  15.5 us
    dot_general x1, matrix products, block_terms(): jnp.einsum('bmkaq,ncmq->nbkac', masked, selected, preferred_element_type=...  9.69 us
    all_to_all x1, starting transfers between devices, body(): lax.all_to_all(bias_all, 'chol', split_axis=0, concat_axis=1, tiled=True)  3.48 us
  transfers between devices with their start and end apart: 2, of which 1 were waited for; matrix products, arithmetic and copies ran while one was open for 2% of the time, Pallas kernels for 0%

commit v1 on v0

v1 whole, which is shorter than its diff:
```python
import functools

import jax
import jax.numpy as jnp
from jax import lax
from jax.experimental import pallas as pl
from jax.experimental.pallas import tpu as pltpu
from jax.sharding import PartitionSpec as P

LANES = 128
VMEM_LIMIT = 48 * 1024 * 1024


def pick_kernel(list_ref, theta_ref, out_ref):
    group = pl.program_id(0)
    listed = list_ref.shape[1]
    width = out_ref.shape[2] // listed
    for m in range(listed):
        start = pl.multiple_of(list_ref[group, m] * width, width)
        out_ref[0, :, m * width:(m + 1) * width] = theta_ref[0, :, pl.ds(start, width)]


def pick_tiles(theta, tile_list, width):
    _, occupied, orbitals = theta.shape
    groups, listed = tile_list.shape
    return pl.pallas_call(
        pick_kernel,
        grid=(groups,),
        in_specs=[
            pl.BlockSpec(memory_space=pltpu.SMEM),
            pl.BlockSpec((1, occupied, orbitals), lambda g: (0, 0, 0)),
        ],
        out_specs=pl.BlockSpec((1, occupied, listed * width), lambda g: (g, 0, 0)),
        out_shape=jax.ShapeDtypeStruct((groups, occupied, listed * width), theta.dtype),
        compiler_params=pltpu.CompilerParams(vmem_limit_bytes=VMEM_LIMIT),
        name="pick_tiles",
    )(tile_list, theta)


def terms_kernel(screen_ref, chol_ref, theta_ref, out_ref, *, k_step):
    _, listed, vectors, occupied, width = chol_ref.shape
    walkers = theta_ref.shape[0]
    columns = walkers * occupied
    depth = listed * width
    tiles = columns // LANES
    per_tile = LANES // occupied

    lane = lax.broadcasted_iota(jnp.int32, (1, depth), 1)
    mask = jnp.zeros((1, depth), jnp.float32)
    for m in range(listed):
        keep = screen_ref[0, m].astype(jnp.float32)
        mask = jnp.where((lane >= m * width) & (lane < (m + 1) * width), keep, mask)
    theta = theta_ref[...].reshape(columns, depth) * mask.astype(theta_ref.dtype)

    row = lax.broadcasted_iota(jnp.int32, (occupied, LANES), 0)
    col = lax.broadcasted_iota(jnp.int32, (occupied, LANES), 1)
    on_diag = (col % occupied) == row
    low = col < occupied

    def one_chunk(chunk_index, cross):
        k0 = chunk_index * k_step
        left = jnp.concatenate(
            [chol_ref[0, m, pl.ds(k0, k_step)].reshape(k_step * occupied, width) for m in range(listed)],
            axis=1,
        )
        inner = lax.dot_general(
            left, theta, (((1,), (1,)), ((), ())), preferred_element_type=jnp.float32
        )
        cross = list(cross)
        diag_rows = []
        for pair in range(k_step // 2):
            parts = []
            for t in range(tiles):
                tile = inner[pair * 2 * occupied:(pair + 1) * 2 * occupied, t * LANES:(t + 1) * LANES]
                flipped = tile.T
                top, bottom = tile[:occupied], tile[occupied:]
                f_top, f_bottom = flipped[:occupied], flipped[occupied:]
                swapped = pltpu.roll(jnp.where(low, f_bottom, f_top), occupied, 1)
                g_top = jnp.where(low, f_top, swapped)
                g_bottom = jnp.where(low, swapped, f_bottom)
                product = top * g_top + bottom * g_bottom
                cross[t] = cross[t] + jnp.sum(product.reshape(occupied // 8, 8, LANES), axis=0)
                d_top = jnp.where(on_diag, top, 0.0)
                d_bottom = jnp.where(on_diag, bottom, 0.0)
                parts.append((jnp.sum(d_top, axis=0, keepdims=True), jnp.sum(d_bottom, axis=0, keepdims=True)))
            diag_rows.append(jnp.concatenate([p[0] for p in parts], axis=1))
            diag_rows.append(jnp.concatenate([p[1] for p in parts], axis=1))
        return tuple(cross), jnp.concatenate(diag_rows, axis=0)

    cross = tuple(jnp.zeros((8, LANES), jnp.float32) for _ in range(tiles))
    diags = []
    for chunk in range(vectors // k_step):
        cross, rows = one_chunk(chunk, cross)
        diags.append(rows)
    cross_row = jnp.concatenate([jnp.sum(c, axis=0, keepdims=True) for c in cross], axis=1)
    rows = jnp.concatenate(diags + [jnp.broadcast_to(cross_row, (8, columns))], axis=0)
    seg_row = lax.broadcasted_iota(jnp.int32, (8, columns), 0)
    seg_col = lax.broadcasted_iota(jnp.int32, (8, columns), 1)
    segment = jnp.where(seg_col // occupied == seg_row, 1.0, 0.0).astype(jnp.float32)
    sums = lax.dot_general(
        segment, rows, (((1,), (1,)), ((), ())),
        precision=lax.Precision.HIGHEST, preferred_element_type=jnp.float32,
    )[:walkers]
    bias = sums[:, :vectors]
    energy = jnp.sum(bias * bias, axis=1, keepdims=True) - sums[:, vectors:vectors + 1]
    out_ref[:, 0, :] = jnp.zeros((walkers, out_ref.shape[2]), jnp.float32)
    out_ref[:, 0, :vectors] = bias
    out_ref[:, 0, vectors:vectors + 1] = energy


def block_terms(screen, chol_tiles, selected, out_width):
    walkers, occupied, depth = selected.shape
    per_step = 4
    _, listed, vectors, _, width = chol_tiles.shape
    return pl.pallas_call(
        functools.partial(terms_kernel, k_step=4),
        grid=(walkers // per_step,),
        in_specs=[
            pl.BlockSpec(memory_space=pltpu.SMEM),
            pl.BlockSpec(chol_tiles.shape, lambda i: (0, 0, 0, 0, 0)),
            pl.BlockSpec((per_step, occupied, depth), lambda i: (i, 0, 0)),
        ],
        out_specs=pl.BlockSpec((per_step, 1, out_width), lambda i: (i, 0, 0)),
        out_shape=jax.ShapeDtypeStruct((walkers, 1, out_width), jnp.float32),
        compiler_params=pltpu.CompilerParams(vmem_limit_bytes=VMEM_LIMIT),
        cost_estimate=pl.CostEstimate(
            flops=2 * walkers * vectors * occupied * occupied * depth,
            bytes_accessed=2 * (chol_tiles.size + selected.size),
            transcendentals=0,
        ),
        name="block_terms",
    )(screen, chol_tiles, selected)


def body(theta, chol_tiles, screen, tile_list):
    groups = lax.axis_size("chol")
    _, occupied, _ = theta.shape
    width = chol_tiles.shape[-1]
    vectors = chol_tiles.shape[2]
    out_width = LANES * ((vectors + 1 + LANES - 1) // LANES)
    outgoing = pick_tiles(theta, tile_list, width)
    selected = lax.all_to_all(outgoing, "chol", split_axis=0, concat_axis=0, tiled=True)
    rows = block_terms(screen, chol_tiles, selected, out_width)
    back = lax.all_to_all(rows, "chol", split_axis=0, concat_axis=0, tiled=True)
    force_bias = back[:, 0, :vectors].reshape(1, groups * vectors)
    energy = jnp.sum(back[:, 0, vectors]).reshape(1) / (2.0 * occupied * occupied)
    return (force_bias, energy)


def solution(mesh):
    in_specs = (
        P(("grp", "chol"), None, None),
        P("chol", None, None, None, None),
        P("chol", None),
        P(),
    )
    out_specs = (P(("grp", "chol"), None), P(("grp", "chol")))
    return jax.shard_map(body, mesh=mesh, in_specs=in_specs, out_specs=out_specs, check_vma=False)
```

time: 154 us -> 56.5 us (0.37)
  waiting for transfers between devices: 48.1 us -> 0 us
  local copies, waits for them, and re-layouts: 24.8 us -> 2.37 us
  other arithmetic: 17.7 us -> 0.69 us
  between operations: 15.9 us -> 2.43 us
  matrix products: 9.69 us -> 0 us
  blocking collectives: 33.8 us -> 43.2 us
  Pallas kernels: 0 us -> 7.55 us
  starting transfers between devices: 3.51 us -> 0 us
    all_gather x1 -> x0, waiting for transfers between devices: 47.4 us -> none  [body(): walker_piece = lax.all_gather(theta, 'chol', axis=0, tiled=True)]
    all_to_all x0 -> x2, blocking collectives: none -> 43.2 us  [the longest x1 32 us: body(): lax.all_to_all(outgoing, 'chol', split_axis=0, concat_axis=0, tiled=True)]
    unnamed x1 -> x0, blocking collectives: 33.8 us -> none
    dot_general x1 -> x0, local copies, waits for them, and re-layouts: 17.5 us -> none  [block_terms(): jnp.einsum('bmkaq,ncmq->nbkac', masked, selected, preferred_element_type=...]
    reduce_sum x2 -> x1, other arithmetic: 16.3 us -> 0.69 us  [body(): jnp.sum(back[:, 0, vectors]).reshape(1) / (2.0 * occupied * occupied)]
    dot_general x1 -> x0, matrix products: 9.69 us -> none  [block_terms(): jnp.einsum('bmkaq,ncmq->nbkac', masked, selected, preferred_element_type=...]
    pallas_call x0 -> x2, Pallas kernels: none -> 7.55 us  [the longest x1 6.3 us: block_terms(): pl.pallas_call(functools.partial(terms_kernel, k_step=4), grid=(walkers /...]
    all_to_all x1 -> x0, starting transfers between devices: 3.48 us -> none  [body(): lax.all_to_all(bias_all, 'chol', split_axis=0, concat_axis=1, tiled=True)]
  transfers between devices with their start and end apart: 2 -> 0, of which waited for: 1 -> 0; matrix products, arithmetic and copies ran while one was open for 2% -> 0% of each run, Pallas kernels for 0% -> 0%
where the time goes in v1:
time: 56.5 us; the launch traced here: 56.3 us
  blocking collectives  43.2 us (76%)
  Pallas kernels  7.55 us (13%)
  between operations  2.43 us (4%)
  local copies, waits for them, and re-layouts  2.37 us (4%)
  other arithmetic  0.69 us (1%)
    all_to_all x1, blocking collectives, body(): lax.all_to_all(outgoing, 'chol', split_axis=0, concat_axis=0, tiled=True)  32 us
    all_to_all x1, blocking collectives, body(): back = lax.all_to_all(rows, 'chol', split_axis=0, concat_axis=0, tiled=True)  11.2 us
    pallas_call x1, Pallas kernels, block_terms(): pl.pallas_call(functools.partial(terms_kernel, k_step=4), grid=(walkers /...  6.3 us
    unnamed x7, local copies, waits for them, and re-layouts  1.69 us
    pallas_call x1, Pallas kernels, pick_tiles(): pl.pallas_call(pick_kernel, grid=(groups,), in_specs=[pl.BlockSpec(memory...  1.25 us

profile of v1, /device:TPU:0, one launch (start us, length us, event | category | flops | bytes accessed | tf_op | source)
XLA Modules:
  0.0 56.3 jit_solution(11777743844397833048)
XLA Ops:
  0.6 0.0 copy-start.2
  0.6 0.8 %copy.6.list_ref = s32[16,4]{1,0:T(8,128)S(1)} copy(s32[16,4]{0,1:T(4,128)} %param.7) | data formatting | bytes 512 | tf_op args[3]
  1.4 0.0 copy-start
  1.4 0.9 %copy-done = bf16[1,64,1280]{2,1,0:T(8,128)(2,1)S(1)} copy-done((bf16[1,64,1280]{2,1,0:T(8,128)(2,1)S(1)}, bf16[1,64,1280]{2,1,0:T(8,128)(2,1)}, u32[]{:S(2)}) %copy-start) | copy-done | bytes 163864
  2.3 0.0 copy-start.1
  2.3 1.3 %pick_tiles.1 = bf16[16,64,512]{2,1,0:T(8,128)(2,1)S(1)} custom-call(s32[16,4]{1,0:T(8,128)S(1)} %copy.6.list_ref, bf16[1,64,1280]{2,1,0:T(8,128)(2,1)S(1)} %copy-done), custom_call_target="tpu_custom_call" | custom-call | tf_op jit(solution)/shard_map/pick_tiles/pallas_call | solution.py:26
  3.6 32.0 %all_to_all.10.theta_ref = bf16[16,64,512]{2,1,0:T(8,128)(2,1)S(1)} all-to-all(bf16[16,64,512]{2,1,0:T(8,128)(2,1)S(1)} %pick_tiles.1), channel_id=1, replica_groups=mesh['grp'=2,'chol'=16] {'chol'}, dimensions={0} | all-to-all | bytes 2097152 | tf_op jit(solution)/shard_map/all_to_all | solution.py:142
  35.6 0.0 copy-done.2
  35.6 0.0 copy-done.1
  35.6 6.3 %block_terms.1 = f32[16,1,128]{2,1,0:T(1,128)S(1)} custom-call(s32[1,4]{1,0:T(1,128)S(1)} %copy-done.2, bf16[1,4,32,64,128]{4,3,2,1,0:T(8,128)(2,1)S(1)} %copy-done.1, bf16[16,64,512]{2,1,0:T(8,128)(2,1)S(1)} %all_to_all.10.theta_ref), custom_call_target="tpu_custom_call" | custom-call | flops 2147483648 | bytes 3145728 | tf_op jit(solution)/shard_map/block_terms/pallas_call | solution.py:115
  41.9 11.2 %all_to_all.11 = f32[16,1,128]{2,1,0:T(1,128)S(1)} all-to-all(f32[16,1,128]{2,1,0:T(1,128)S(1)} %block_terms.1), channel_id=1, replica_groups=mesh['grp'=2,'chol'=16] {'chol'}, dimensions={0} | all-to-all | bytes 16384 | tf_op jit(solution)/shard_map/all_to_all | solution.py:144
  53.2 0.7 %reshape_squeeze.3 = f32[1,512]{1,0:T(1,128)} reshape(f32[16,32]{1,0:T(8,128)S(1)} %slice_reduce_fusion.1) | data formatting | bytes 4096 | tf_op jit(solution)/shard_map/reshape;squeeze | solution.py:145
  53.8 0.7 %slice_reduce_fusion = f32[]{:T(128)} fusion(f32[16,1,128]{2,1,0:T(1,128)S(1)} %all_to_all.11), kind=kLoop, calls=%fused_computation | loop fusion | flops 15 | bytes 68 | tf_op jit(solution)/shard_map/reduce_sum | solution.py:146
  (1 shorter events, 0.0 us)
Async XLA Ops:
  0.6 35.0 %copy-start.2 = (s32[1,4]{1,0:T(1,128)S(1)}, s32[1,4]{1,0:T(1,128)}, u32[]{:S(2)}) copy-start(s32[1,4]{1,0:T(1,128)} %screen_ref.1) | copy-start | bytes 52
  1.4 0.9 %copy-start = (bf16[1,64,1280]{2,1,0:T(8,128)(2,1)S(1)}, bf16[1,64,1280]{2,1,0:T(8,128)(2,1)}, u32[]{:S(2)}) copy-start(bf16[1,64,1280]{2,1,0:T(8,128)(2,1)} %theta_ref.1) | copy-start | bytes 491524
  2.3 33.3 %copy-start.1 = (bf16[1,4,32,64,128]{4,3,2,1,0:T(8,128)(2,1)S(1)}, bf16[1,4,32,64,128]{4,3,2,1,0:T(8,128)(2,1)}, u32[]{:S(2)}) copy-start(bf16[1,4,32,64,128]{4,3,2,1,0:T(8,128)(2,1)} %chol_ref.1) | copy-start | bytes 6291460

commit v2 on v1

v2 whole, which is shorter than its diff:
```python
import functools

import jax
import jax.numpy as jnp
from jax import lax
from jax.experimental import pallas as pl
from jax.experimental.pallas import tpu as pltpu
from jax.sharding import PartitionSpec as P

LANES = 128
VMEM_LIMIT = 48 * 1024 * 1024
BATCH = 4


def split_axis(groups):
    outer = 1
    while outer * outer * 4 <= groups:
        outer *= 2
    return outer, groups // outer


def pick_kernel(list_ref, theta_ref, *out_refs):
    listed, groups = list_ref.shape
    inner = len(out_refs)
    width = out_refs[0].shape[2] // listed
    me = lax.axis_index("chol")
    first = (me // inner) * inner
    for t, out_ref in enumerate(out_refs):
        group = first + lax.rem(me - first + t, inner)
        for m in range(listed):
            start = pl.multiple_of(list_ref[m, group] * width, width)
            out_ref[0, :, m * width:(m + 1) * width] = theta_ref[0, :, pl.ds(start, width)]


def pick_tiles(theta, listing, width, inner):
    _, occupied, _ = theta.shape
    listed = listing.shape[0]
    piece = jax.ShapeDtypeStruct((1, occupied, listed * width), theta.dtype)
    return pl.pallas_call(
        pick_kernel,
        in_specs=[pl.BlockSpec(memory_space=pltpu.SMEM), pl.BlockSpec(memory_space=pltpu.VMEM)],
        out_specs=[pl.BlockSpec(memory_space=pltpu.VMEM)] * inner,
        out_shape=[piece] * inner,
        compiler_params=pltpu.CompilerParams(vmem_limit_bytes=VMEM_LIMIT),
        cost_estimate=pl.CostEstimate(
            flops=0, bytes_accessed=4 * inner * occupied * listed * width, transcendentals=0
        ),
        name="pick_tiles",
    )(listing, theta)


def batch_terms(chol_ref, theta, k_step):
    _, listed, vectors, occupied, width = chol_ref.shape
    columns = theta.shape[0]
    walkers = columns // occupied
    tiles = columns // LANES

    row = lax.broadcasted_iota(jnp.int32, (occupied, LANES), 0)
    col = lax.broadcasted_iota(jnp.int32, (occupied, LANES), 1)
    on_diag = (col % occupied) == row
    low = col < occupied

    cross = [jnp.zeros((8, LANES), jnp.float32) for _ in range(tiles)]
    diag_rows = []
    for k0 in range(0, vectors, k_step):
        left = jnp.concatenate(
            [chol_ref[0, m, k0:k0 + k_step].reshape(k_step * occupied, width) for m in range(listed)],
            axis=1,
        )
        inner_mat = lax.dot_general(
            left, theta, (((1,), (1,)), ((), ())), preferred_element_type=jnp.float32
        )
        for pair in range(k_step // 2):
            tops, bottoms = [], []
            for t in range(tiles):
                tile = inner_mat[pair * 2 * occupied:(pair + 1) * 2 * occupied, t * LANES:(t + 1) * LANES]
                flipped = tile.T
                top, bottom = tile[:occupied], tile[occupied:]
                f_top, f_bottom = flipped[:occupied], flipped[occupied:]
                swapped = pltpu.roll(jnp.where(low, f_bottom, f_top), occupied, 1)
                product = top * jnp.where(low, f_top, swapped) + bottom * jnp.where(low, swapped, f_bottom)
                cross[t] = cross[t] + jnp.sum(product.reshape(occupied // 8, 8, LANES), axis=0)
                tops.append(jnp.sum(jnp.where(on_diag, top, 0.0), axis=0, keepdims=True))
                bottoms.append(jnp.sum(jnp.where(on_diag, bottom, 0.0), axis=0, keepdims=True))
            diag_rows.append(jnp.concatenate(tops, axis=1))
            diag_rows.append(jnp.concatenate(bottoms, axis=1))
    cross_row = jnp.concatenate([jnp.sum(c, axis=0, keepdims=True) for c in cross], axis=1)
    rows = jnp.concatenate(diag_rows + [jnp.broadcast_to(cross_row, (8, columns))], axis=0)
    seg_row = lax.broadcasted_iota(jnp.int32, (8, columns), 0)
    seg_col = lax.broadcasted_iota(jnp.int32, (8, columns), 1)
    segment = jnp.where(seg_col // occupied == seg_row, 1.0, 0.0).astype(jnp.float32)
    sums = lax.dot_general(
        segment, rows, (((1,), (1,)), ((), ())),
        precision=lax.Precision.HIGHEST, preferred_element_type=jnp.float32,
    )[:walkers]
    bias = sums[:, :vectors]
    energy = jnp.sum(bias * bias, axis=1, keepdims=True) - sums[:, vectors:vectors + 1]
    return bias, energy


def terms_kernel(screen_ref, chol_ref, *refs, shift, inner, carried):
    piece_refs, rest = refs[:inner], refs[inner:]
    out_ref = rest[-1]
    _, listed, vectors, occupied, width = chol_ref.shape
    depth = listed * width
    groups = out_ref.shape[0]
    outer = groups // inner
    me = lax.axis_index("chol")
    zone, spot = me // inner, lax.rem(me, inner)
    owner_zone = lax.rem(zone - shift + outer, outer)

    lane = lax.broadcasted_iota(jnp.int32, (1, depth), 1)
    mask = jnp.zeros((1, depth), jnp.float32)
    for m in range(listed):
        keep = screen_ref[0, m].astype(jnp.float32)
        mask = jnp.where((lane >= m * width) & (lane < (m + 1) * width), keep, mask)
    mask = mask.astype(piece_refs[0].dtype)

    if carried:
        out_ref[...] = rest[0][...]
    else:
        out_ref[...] = jnp.zeros(out_ref.shape, out_ref.dtype)
    for first in range(0, inner, BATCH):
        theta = jnp.concatenate([ref[0] for ref in piece_refs[first:first + BATCH]], axis=0) * mask
        bias, energy = batch_terms(chol_ref, theta, 4)
        for offset in range(BATCH):
            owner = owner_zone * inner + lax.rem(spot - (first + offset) + inner, inner)
            out_ref[pl.ds(owner, 1), 0, :vectors] = bias[offset:offset + 1]
            out_ref[pl.ds(owner, 1), 0, vectors:vectors + 1] = energy[offset:offset + 1]


def block_terms(screen, chol_tiles, pieces, carried, shift, groups, out_width):
    inner = len(pieces)
    _, occupied, depth = pieces[0].shape
    vectors = chol_tiles.shape[2]
    operands = [screen, chol_tiles, *pieces] + ([] if carried is None else [carried])
    return pl.pallas_call(
        functools.partial(terms_kernel, shift=shift, inner=inner, carried=carried is not None),
        in_specs=[pl.BlockSpec(memory_space=pltpu.SMEM)]
        + [pl.BlockSpec(memory_space=pltpu.VMEM)] * (len(operands) - 1),
        out_specs=pl.BlockSpec(memory_space=pltpu.VMEM),
        out_shape=jax.ShapeDtypeStruct((groups, 1, out_width), jnp.float32),
        compiler_params=pltpu.CompilerParams(vmem_limit_bytes=VMEM_LIMIT),
        cost_estimate=pl.CostEstimate(
            flops=2 * inner * vectors * occupied * occupied * depth,
            bytes_accessed=2 * chol_tiles.size,
            transcendentals=0,
        ),
        name="block_terms",
    )(*operands)


def body(theta, chol_tiles, screen, tile_list):
    groups = lax.axis_size("chol")
    outer, inner = split_axis(groups)
    _, occupied, _ = theta.shape
    width = chol_tiles.shape[-1]
    vectors = chol_tiles.shape[2]
    out_width = LANES * ((vectors + 1 + LANES - 1) // LANES)
    listing = tile_list.T

    def moved(zone_step, spot_step):
        return [
            (i, ((i // inner + zone_step) % outer) * inner + (i + spot_step) % inner) for i in range(groups)
        ]

    held = [theta] + [lax.ppermute(theta, "chol", moved(s, 0)) for s in range(1, outer)]
    rows = None
    for s in range(outer):
        picked = pick_tiles(held[s], listing, width, inner)
        pieces = [picked[0]] + [lax.ppermute(picked[t], "chol", moved(0, t)) for t in range(1, inner)]
        rows = block_terms(screen, chol_tiles, pieces, rows, s, groups, out_width)
    back = lax.all_to_all(rows, "chol", split_axis=0, concat_axis=0, tiled=True)
    force_bias = back[:, 0, :vectors].reshape(1, groups * vectors)
    energy = jnp.sum(back[:, 0, vectors]).reshape(1) / (2.0 * occupied * occupied)
    return (force_bias, energy)


def solution(mesh):
    in_specs = (
        P(("grp", "chol"), None, None),
        P("chol", None, None, None, None),
        P("chol", None),
        P(),
    )
    out_specs = (P(("grp", "chol"), None), P(("grp", "chol")))
    return jax.shard_map(body, mesh=mesh, in_specs=in_specs, out_specs=out_specs, check_vma=False)
```

time: 56.5 us -> 52 us (0.920)
  blocking collectives: 43.2 us -> 12.6 us
  starting transfers between devices: 0 us -> 17.1 us
  waiting for transfers between devices: 0 us -> 3.67 us
  Pallas kernels: 7.55 us -> 10.5 us
  local copies, waits for them, and re-layouts: 2.37 us -> 4.57 us
    all_to_all x1 -> x0, blocking collectives: 32 us -> none  [body(): lax.all_to_all(outgoing, 'chol', split_axis=0, concat_axis=0, tiled=True)]
    ppermute x0 -> x15, starting transfers between devices: none -> 17.1 us  [the longest x12 10.1 us: body(): lax.ppermute(picked[t], 'chol', moved(0, t))]
    ppermute x0 -> x15, waiting for transfers between devices: none -> 3.67 us  [the longest x3 3.62 us: body(): lax.ppermute(theta, 'chol', moved(s, 0))]
    pallas_call x2 -> x8, Pallas kernels: 7.55 us -> 10.5 us  [the longest x4 7.86 us: block_terms(): pl.pallas_call(functools.partial(terms_kernel, shift=shift, inner=inner,...]
    unnamed x7 -> x12, local copies, waits for them, and re-layouts: 1.69 us -> 3.89 us
    all_to_all x1, blocking collectives: 11.2 us -> 12.6 us  [body(): back = lax.all_to_all(rows, 'chol', split_axis=0, concat_axis=0, tiled=True)]
  transfers between devices with their start and end apart: 0 -> 15, of which waited for: 0 -> 1; matrix products, arithmetic and copies ran while one was open for 0% -> 0% of each run, Pallas kernels for 0% -> 17%
where the time goes in v2:
time: 52 us; the launch traced here: 51.7 us
  starting transfers between devices  17.1 us (33%)
  blocking collectives  12.6 us (24%)
  Pallas kernels  10.5 us (20%)
  local copies, waits for them, and re-layouts  4.57 us (9%)
  waiting for transfers between devices  3.67 us (7%)
  between operations  2.55 us (5%)
  other arithmetic  0.69 us (1%)
    all_to_all x1, blocking collectives, body(): back = lax.all_to_all(rows, 'chol', split_axis=0, concat_axis=0, tiled=True)  12.6 us
    ppermute x12, starting transfers between devices, body(): lax.ppermute(picked[t], 'chol', moved(0, t))  10.1 us
    pallas_call x4, Pallas kernels, block_terms(): pl.pallas_call(functools.partial(terms_kernel, shift=shift, inner=inner,...  7.86 us
    ppermute x3, starting transfers between devices, body(): lax.ppermute(theta, 'chol', moved(s, 0))  7.01 us
    unnamed x12, local copies, waits for them, and re-layouts  3.89 us
    ppermute x3, waiting for transfers between devices, body(): lax.ppermute(theta, 'chol', moved(s, 0))  3.62 us
    pallas_call x4, Pallas kernels, pick_tiles(): pl.pallas_call(pick_kernel, in_specs=[pl.BlockSpec(memory_space=pltpu.SME...  2.64 us
  transfers between devices with their start and end apart: 15, of which 1 were waited for; matrix products, arithmetic and copies ran while one was open for 0% of the time, Pallas kernels for 17%

profile of v2, /device:TPU:0, one launch (start us, length us, event | category | flops | bytes accessed | tf_op | source)
XLA Modules:
  0.0 51.7 jit_solution(6080655468297282729)
XLA Ops:
  0.6 3.1 %collective-permute-start.8 = (bf16[1,64,1280]{2,1,0:T(8,128)(2,1)}, bf16[1,64,1280]{2,1,0:T(8,128)(2,1)S(1)}, u32[]{:S(2)}, u32[]{:S(2)}) collective-permute-start(bf16[1,64,1280]{2,1,0:T(8,128)(2,1)} %theta_ref.1), channel_id=1, source_target_pairs={{0,4},{1,5},{2,6},{3,7},{4,8},{5,9},{6,10},{7,11},{8,12},{9,13},{1... | collective-permute-start | bytes 491528 | tf_op jit(solution)/shard_map/ppermute | solution.py:167
  3.7 2.6 %collective-permute-start.4 = (bf16[1,64,1280]{2,1,0:T(8,128)(2,1)}, bf16[1,64,1280]{2,1,0:T(8,128)(2,1)S(1)}, u32[]{:S(2)}, u32[]{:S(2)}) collective-permute-start(bf16[1,64,1280]{2,1,0:T(8,128)(2,1)} %theta_ref.1), channel_id=1, source_target_pairs={{0,8},{1,9},{2,10},{3,11},{4,12},{5,13},{6,14},{7,15},{8,0},{9,1},... | collective-permute-start | bytes 491528 | tf_op jit(solution)/shard_map/ppermute | solution.py:167
  6.3 1.3 %collective-permute-start = (bf16[1,64,1280]{2,1,0:T(8,128)(2,1)}, bf16[1,64,1280]{2,1,0:T(8,128)(2,1)S(1)}, u32[]{:S(2)}, u32[]{:S(2)}) collective-permute-start(bf16[1,64,1280]{2,1,0:T(8,128)(2,1)} %theta_ref.1), channel_id=1, source_target_pairs={{0,12},{1,13},{2,14},{3,15},{4,0},{5,1},{6,2},{7,3},{8,4},{9,5},{1... | collective-permute-start | bytes 491528 | tf_op jit(solution)/shard_map/ppermute | solution.py:167
  7.7 0.9 %copy-done.2 = bf16[1,64,1280]{2,1,0:T(8,128)(2,1)S(1)} copy-done((bf16[1,64,1280]{2,1,0:T(8,128)(2,1)S(1)}, bf16[1,64,1280]{2,1,0:T(8,128)(2,1)}, u32[]{:S(2)}) %copy-start.2) | copy-done | bytes 163864
  8.6 0.7 %copy-done.3 = s32[16,4]{0,1:T(4,128)S(1)} copy-done((s32[16,4]{0,1:T(4,128)S(1)}, s32[16,4]{0,1:T(4,128)}, u32[]{:S(2)}) %copy-start.3) | copy-done | bytes 280
  9.3 0.7 %pick_tiles.7 = (bf16[1,64,512]{2,1,0:T(8,128)(2,1)S(1)}, bf16[1,64,512]{2,1,0:T(8,128)(2,1)S(1)}, bf16[1,64,512]{2,1,0:T(8,128)(2,1)S(1)}, bf16[1,64,512]{2,1,0:T(8,128)(2,1)S(1)}) custom-call(s32[4,16]{1,0:T(4,128)S(1)} %bitcast.2, bf16[1,64,1280]{2,1,0:T(8,128)(2,1)S(1)} %copy-done.2), custom_call_target="tpu_custom_call" | custom-call | bytes 524288 | tf_op jit(solution)/shard_map/pick_tiles/pallas_call | solution.py:39
  10.0 0.1 collective-permute-start.12
  10.0 1.6 %collective-permute-start.13 = (bf16[1,64,512]{2,1,0:T(8,128)(2,1)S(1)}, bf16[1,64,512]{2,1,0:T(8,128)(2,1)S(1)}, u32[]{:S(2)}, u32[]{:S(2)}) collective-permute-start(bf16[1,64,512]{2,1,0:T(8,128)(2,1)S(1)} %get-tuple-element.32), channel_id=1, source_target_pairs={{0,2},{1,3},{2,0},{3,1},{4,6},{5,7},{6,4},{7,5},{8,10},{9,11},{10,... | collective-permute-start | bytes 196616 | tf_op jit(solution)/shard_map/ppermute | solution.py:171
  11.6 1.4 %collective-permute-start.14 = (bf16[1,64,512]{2,1,0:T(8,128)(2,1)S(1)}, bf16[1,64,512]{2,1,0:T(8,128)(2,1)S(1)}, u32[]{:S(2)}, u32[]{:S(2)}) collective-permute-start(bf16[1,64,512]{2,1,0:T(8,128)(2,1)S(1)} %get-tuple-element.33), channel_id=1, source_target_pairs={{0,3},{1,0},{2,1},{3,2},{4,7},{5,4},{6,5},{7,6},{8,11},{9,8},{10,9... | collective-permute-start | bytes 196616 | tf_op jit(solution)/shard_map/ppermute | solution.py:171
  13.0 0.7 %pick_tiles.6 = (bf16[1,64,512]{2,1,0:T(8,128)(2,1)S(1)}, bf16[1,64,512]{2,1,0:T(8,128)(2,1)S(1)}, bf16[1,64,512]{2,1,0:T(8,128)(2,1)S(1)}, bf16[1,64,512]{2,1,0:T(8,128)(2,1)S(1)}) custom-call(s32[4,16]{1,0:T(4,128)S(1)} %bitcast.3, bf16[1,64,1280]{2,1,0:T(8,128)(2,1)S(1)} %collective-permute-done.8.theta_ref), custom_call_target="tpu_custom_call" | custom-call | bytes 524288 | tf_op jit(solution)/shard_map/pick_tiles/pallas_call | solution.py:39
  13.7 3.6 %collective-permute-done.4.theta_ref = bf16[1,64,1280]{2,1,0:T(8,128)(2,1)S(1)} collective-permute-done((bf16[1,64,1280]{2,1,0:T(8,128)(2,1)}, bf16[1,64,1280]{2,1,0:T(8,128)(2,1)S(1)}, u32[]{:S(2)}, u32[]{:S(2)}) %collective-permute-start.4) | collective-permute-done | bytes 163872 | tf_op jit(solution)/shard_map/ppermute | solution.py:167
  17.3 1.5 %collective-permute-start.10 = (bf16[1,64,512]{2,1,0:T(8,128)(2,1)S(1)}, bf16[1,64,512]{2,1,0:T(8,128)(2,1)S(1)}, u32[]{:S(2)}, u32[]{:S(2)}) collective-permute-start(bf16[1,64,512]{2,1,0:T(8,128)(2,1)S(1)} %get-tuple-element.28), channel_id=1, source_target_pairs={{0,2},{1,3},{2,0},{3,1},{4,6},{5,7},{6,4},{7,5},{8,10},{9,11},{10,... | collective-permute-start | bytes 196616 | tf_op jit(solution)/shard_map/ppermute | solution.py:171
  18.8 0.7 %pick_tiles.5 = (bf16[1,64,512]{2,1,0:T(8,128)(2,1)S(1)}, bf16[1,64,512]{2,1,0:T(8,128)(2,1)S(1)}, bf16[1,64,512]{2,1,0:T(8,128)(2,1)S(1)}, bf16[1,64,512]{2,1,0:T(8,128)(2,1)S(1)}) custom-call(s32[4,16]{1,0:T(4,128)S(1)} %bitcast.4, bf16[1,64,1280]{2,1,0:T(8,128)(2,1)S(1)} %collective-permute-done.4.theta_ref), custom_call_target="tpu_custom_call" | custom-call | bytes 524288 | tf_op jit(solution)/shard_map/pick_tiles/pallas_call | solution.py:39
  19.5 0.1 collective-permute-start.11
  19.5 0.5 collective-permute-start.9
  20.0 0.9 %collective-permute-start.5 = (bf16[1,64,512]{2,1,0:T(8,128)(2,1)S(1)}, bf16[1,64,512]{2,1,0:T(8,128)(2,1)S(1)}, u32[]{:S(2)}, u32[]{:S(2)}) collective-permute-start(bf16[1,64,512]{2,1,0:T(8,128)(2,1)S(1)} %get-tuple-element.23), channel_id=1, source_target_pairs={{0,1},{1,2},{2,3},{3,0},{4,5},{5,6},{6,7},{7,4},{8,9},{9,10},{10,1... | collective-permute-start | bytes 196616 | tf_op jit(solution)/shard_map/ppermute | solution.py:171
  20.9 0.8 %collective-permute-start.6 = (bf16[1,64,512]{2,1,0:T(8,128)(2,1)S(1)}, bf16[1,64,512]{2,1,0:T(8,128)(2,1)S(1)}, u32[]{:S(2)}, u32[]{:S(2)}) collective-permute-start(bf16[1,64,512]{2,1,0:T(8,128)(2,1)S(1)} %get-tuple-element.24), channel_id=1, source_target_pairs={{0,2},{1,3},{2,0},{3,1},{4,6},{5,7},{6,4},{7,5},{8,10},{9,11},{10,... | collective-permute-start | bytes 196616 | tf_op jit(solution)/shard_map/ppermute | solution.py:171
  21.7 0.6 %collective-permute-start.7 = (bf16[1,64,512]{2,1,0:T(8,128)(2,1)S(1)}, bf16[1,64,512]{2,1,0:T(8,128)(2,1)S(1)}, u32[]{:S(2)}, u32[]{:S(2)}) collective-permute-start(bf16[1,64,512]{2,1,0:T(8,128)(2,1)S(1)} %get-tuple-element.25), channel_id=1, source_target_pairs={{0,3},{1,0},{2,1},{3,2},{4,7},{5,4},{6,5},{7,6},{8,11},{9,8},{10,9... | collective-permute-start | bytes 196616 | tf_op jit(solution)/shard_map/ppermute | solution.py:171
  22.3 1.6 %copy-done = bf16[1,4,32,64,128]{4,3,2,1,0:T(8,128)(2,1)S(1)} copy-done((bf16[1,4,32,64,128]{4,3,2,1,0:T(8,128)(2,1)S(1)}, bf16[1,4,32,64,128]{4,3,2,1,0:T(8,128)(2,1)}, u32[]{:S(2)}) %copy-start) | copy-done | bytes 2097176
  23.9 0.7 %copy-done.4 = s32[1,4]{1,0:T(1,128)S(1)} copy-done((s32[1,4]{1,0:T(1,128)S(1)}, s32[1,4]{1,0:T(1,128)}, u32[]{:S(2)}) %copy-start.4) | copy-done | bytes 40
  24.6 2.0 %block_terms.4.refs_4_ = f32[16,1,128]{2,1,0:T(1,128)S(1)} custom-call(s32[1,4]{1,0:T(1,128)S(1)} %copy-done.4, bf16[1,4,32,64,128]{4,3,2,1,0:T(8,128)(2,1)S(1)} %copy-done, bf16[1,64,512]{2,1,0:T(8,128)(2,1)S(1)} %get-tuple-element.30.refs_0_, bf16[1,64,512]{2,1,0:T(8,128)(2,1)S(1)} %collective-permute-done.12.refs_1_, ...), custom_call_target="tpu_custom_call" | custom-call | flops 536870912 | bytes 2097152 | tf_op jit(solution)/shard_map/block_terms/pallas_call | solution.py:137
  26.5 0.7 %pick_tiles.4 = (bf16[1,64,512]{2,1,0:T(8,128)(2,1)S(1)}, bf16[1,64,512]{2,1,0:T(8,128)(2,1)S(1)}, bf16[1,64,512]{2,1,0:T(8,128)(2,1)S(1)}, bf16[1,64,512]{2,1,0:T(8,128)(2,1)S(1)}) custom-call(s32[4,16]{1,0:T(4,128)S(1)} %bitcast.5, bf16[1,64,1280]{2,1,0:T(8,128)(2,1)S(1)} %collective-permute-done.theta_ref), custom_call_target="tpu_custom_call" | custom-call | bytes 524288 | tf_op jit(solution)/shard_map/pick_tiles/pallas_call | solution.py:39
  27.2 0.1 collective-permute-start.1
  27.3 1.3 %collective-permute-start.2 = (bf16[1,64,512]{2,1,0:T(8,128)(2,1)S(1)}, bf16[1,64,512]{2,1,0:T(8,128)(2,1)S(1)}, u32[]{:S(2)}, u32[]{:S(2)}) collective-permute-start(bf16[1,64,512]{2,1,0:T(8,128)(2,1)S(1)} %get-tuple-element.20), channel_id=1, source_target_pairs={{0,2},{1,3},{2,0},{3,1},{4,6},{5,7},{6,4},{7,5},{8,10},{9,11},{10,... | collective-permute-start | bytes 196616 | tf_op jit(solution)/shard_map/ppermute | solution.py:171
  28.6 1.4 %collective-permute-start.3 = (bf16[1,64,512]{2,1,0:T(8,128)(2,1)S(1)}, bf16[1,64,512]{2,1,0:T(8,128)(2,1)S(1)}, u32[]{:S(2)}, u32[]{:S(2)}) collective-permute-start(bf16[1,64,512]{2,1,0:T(8,128)(2,1)S(1)} %get-tuple-element.21), channel_id=1, source_target_pairs={{0,3},{1,0},{2,1},{3,2},{4,7},{5,4},{6,5},{7,6},{8,11},{9,8},{10,9... | collective-permute-start | bytes 196616 | tf_op jit(solution)/shard_map/ppermute | solution.py:171
  30.0 2.0 %block_terms.5.refs_4_ = f32[16,1,128]{2,1,0:T(1,128)S(1)} custom-call(s32[1,4]{1,0:T(1,128)S(1)} %copy-done.5, bf16[1,4,32,64,128]{4,3,2,1,0:T(8,128)(2,1)S(1)} %copy-done.1, bf16[1,64,512]{2,1,0:T(8,128)(2,1)S(1)} %get-tuple-element.26.refs_0_, bf16[1,64,512]{2,1,0:T(8,128)(2,1)S(1)} %collective-permute-done.9.refs_1_, ...), custom_call_target="tpu_custom_call" | custom-call | flops 536870912 | bytes 2097152 | tf_op jit(solution)/shard_map/block_terms/pallas_call | solution.py:137
  32.0 2.0 %block_terms.6.refs_4_ = f32[16,1,128]{2,1,0:T(1,128)S(1)} custom-call(s32[1,4]{1,0:T(1,128)S(1)} %copy-done.5, bf16[1,4,32,64,128]{4,3,2,1,0:T(8,128)(2,1)S(1)} %copy-done.1, bf16[1,64,512]{2,1,0:T(8,128)(2,1)S(1)} %get-tuple-element.22.refs_0_, bf16[1,64,512]{2,1,0:T(8,128)(2,1)S(1)} %collective-permute-done.5.refs_1_, ...), custom_call_target="tpu_custom_call" | custom-call | flops 536870912 | bytes 2097152 | tf_op jit(solution)/shard_map/block_terms/pallas_call | solution.py:137
  33.9 0.0 collective-permute-done.2.refs_2_
  34.0 2.0 %block_terms.7 = f32[16,1,128]{2,1,0:T(1,128)S(1)} custom-call(s32[1,4]{1,0:T(1,128)S(1)} %copy-done.5, bf16[1,4,32,64,128]{4,3,2,1,0:T(8,128)(2,1)S(1)} %copy-done.1, bf16[1,64,512]{2,1,0:T(8,128)(2,1)S(1)} %get-tuple-element.18.refs_0_, bf16[1,64,512]{2,1,0:T(8,128)(2,1)S(1)} %collective-permute-done.1.refs_1_, ...), custom_call_target="tpu_custom_call" | custom-call | flops 536870912 | bytes 2097152 | tf_op jit(solution)/shard_map/block_terms/pallas_call | solution.py:137
  35.9 12.6 %all_to_all.5 = f32[16,1,128]{2,1,0:T(1,128)S(1)} all-to-all(f32[16,1,128]{2,1,0:T(1,128)S(1)} %block_terms.7), channel_id=1, replica_groups=mesh['grp'=2,'chol'=16] {'chol'}, dimensions={0} | all-to-all | bytes 16384 | tf_op jit(solution)/shard_map/all_to_all | solution.py:173
  48.6 0.7 %reshape_squeeze.3 = f32[1,512]{1,0:T(1,128)} reshape(f32[16,32]{1,0:T(8,128)S(1)} %slice_reduce_fusion.1) | data formatting | bytes 4096 | tf_op jit(solution)/shard_map/reshape;squeeze | solution.py:174
  49.3 0.7 %slice_reduce_fusion = f32[]{:T(128)} fusion(f32[16,1,128]{2,1,0:T(1,128)S(1)} %all_to_all.5), kind=kLoop, calls=%fused_computation | loop fusion | flops 15 | bytes 68 | tf_op jit(solution)/shard_map/reduce_sum | solution.py:175
  (22 shorter events, 0.1 us)
Async XLA Ops:
  0.6 29.3 %copy-start.5 = (s32[1,4]{1,0:T(1,128)S(1)}, s32[1,4]{1,0:T(1,128)}, u32[]{:S(2)}) copy-start(s32[1,4]{1,0:T(1,128)} %screen_ref.7) | copy-start | bytes 52
  0.6 11.0 %collective-permute-start.8 = (bf16[1,64,1280]{2,1,0:T(8,128)(2,1)}, bf16[1,64,1280]{2,1,0:T(8,128)(2,1)S(1)}, u32[]{:S(2)}, u32[]{:S(2)}) collective-permute-start(bf16[1,64,1280]{2,1,0:T(8,128)(2,1)} %theta_ref.1), channel_id=1, source_target_pairs={{0,4},{1,5},{2,6},{3,7},{4,8},{5,9},{6,10},{7,11},{8,12},{9,13},{1... | collective-permute-start | bytes 491528 | tf_op jit(solution)/shard_map/ppermute | solution.py:167
  3.7 13.5 %collective-permute-start.4 = (bf16[1,64,1280]{2,1,0:T(8,128)(2,1)}, bf16[1,64,1280]{2,1,0:T(8,128)(2,1)S(1)}, u32[]{:S(2)}, u32[]{:S(2)}) collective-permute-start(bf16[1,64,1280]{2,1,0:T(8,128)(2,1)} %theta_ref.1), channel_id=1, source_target_pairs={{0,8},{1,9},{2,10},{3,11},{4,12},{5,13},{6,14},{7,15},{8,0},{9,1},... | collective-permute-start | bytes 491528 | tf_op jit(solution)/shard_map/ppermute | solution.py:167
  6.3 14.6 %collective-permute-start = (bf16[1,64,1280]{2,1,0:T(8,128)(2,1)}, bf16[1,64,1280]{2,1,0:T(8,128)(2,1)S(1)}, u32[]{:S(2)}, u32[]{:S(2)}) collective-permute-start(bf16[1,64,1280]{2,1,0:T(8,128)(2,1)} %theta_ref.1), channel_id=1, source_target_pairs={{0,12},{1,13},{2,14},{3,15},{4,0},{5,1},{6,2},{7,3},{8,4},{9,5},{1... | collective-permute-start | bytes 491528 | tf_op jit(solution)/shard_map/ppermute | solution.py:167
  7.7 0.9 %copy-start.2 = (bf16[1,64,1280]{2,1,0:T(8,128)(2,1)S(1)}, bf16[1,64,1280]{2,1,0:T(8,128)(2,1)}, u32[]{:S(2)}) copy-start(bf16[1,64,1280]{2,1,0:T(8,128)(2,1)} %theta_ref.1) | copy-start | bytes 491524
  8.6 0.7 %copy-start.3 = (s32[16,4]{0,1:T(4,128)S(1)}, s32[16,4]{0,1:T(4,128)}, u32[]{:S(2)}) copy-start(s32[16,4]{0,1:T(4,128)} %param.7) | copy-start | bytes 772
  10.0 9.5 %collective-permute-start.12 = (bf16[1,64,512]{2,1,0:T(8,128)(2,1)S(1)}, bf16[1,64,512]{2,1,0:T(8,128)(2,1)S(1)}, u32[]{:S(2)}, u32[]{:S(2)}) collective-permute-start(bf16[1,64,512]{2,1,0:T(8,128)(2,1)S(1)} %get-tuple-element.31), channel_id=1, source_target_pairs={{0,1},{1,2},{2,3},{3,0},{4,5},{5,6},{6,7},{7,4},{8,9},{9,10},{10,1... | collective-permute-start | bytes 196616 | tf_op jit(solution)/shard_map/ppermute | solution.py:171
  10.0 9.5 %collective-permute-start.13 = (bf16[1,64,512]{2,1,0:T(8,128)(2,1)S(1)}, bf16[1,64,512]{2,1,0:T(8,128)(2,1)S(1)}, u32[]{:S(2)}, u32[]{:S(2)}) collective-permute-start(bf16[1,64,512]{2,1,0:T(8,128)(2,1)S(1)} %get-tuple-element.32), channel_id=1, source_target_pairs={{0,2},{1,3},{2,0},{3,1},{4,6},{5,7},{6,4},{7,5},{8,10},{9,11},{10,... | collective-permute-start | bytes 196616 | tf_op jit(solution)/shard_map/ppermute | solution.py:171
  11.6 8.4 %collective-permute-start.14 = (bf16[1,64,512]{2,1,0:T(8,128)(2,1)S(1)}, bf16[1,64,512]{2,1,0:T(8,128)(2,1)S(1)}, u32[]{:S(2)}, u32[]{:S(2)}) collective-permute-start(bf16[1,64,512]{2,1,0:T(8,128)(2,1)S(1)} %get-tuple-element.33), channel_id=1, source_target_pairs={{0,3},{1,0},{2,1},{3,2},{4,7},{5,4},{6,5},{7,6},{8,11},{9,8},{10,9... | collective-permute-start | bytes 196616 | tf_op jit(solution)/shard_map/ppermute | solution.py:171
  17.3 4.5 %collective-permute-start.10 = (bf16[1,64,512]{2,1,0:T(8,128)(2,1)S(1)}, bf16[1,64,512]{2,1,0:T(8,128)(2,1)S(1)}, u32[]{:S(2)}, u32[]{:S(2)}) collective-permute-start(bf16[1,64,512]{2,1,0:T(8,128)(2,1)S(1)} %get-tuple-element.28), channel_id=1, source_target_pairs={{0,2},{1,3},{2,0},{3,1},{4,6},{5,7},{6,4},{7,5},{8,10},{9,11},{10,... | collective-permute-start | bytes 196616 | tf_op jit(solution)/shard_map/ppermute | solution.py:171
  19.5 7.8 %collective-permute-start.11 = (bf16[1,64,512]{2,1,0:T(8,128)(2,1)S(1)}, bf16[1,64,512]{2,1,0:T(8,128)(2,1)S(1)}, u32[]{:S(2)}, u32[]{:S(2)}) collective-permute-start(bf16[1,64,512]{2,1,0:T(8,128)(2,1)S(1)} %get-tuple-element.29), channel_id=1, source_target_pairs={{0,3},{1,0},{2,1},{3,2},{4,7},{5,4},{6,5},{7,6},{8,11},{9,8},{10,9... | collective-permute-start | bytes 196616 | tf_op jit(solution)/shard_map/ppermute | solution.py:171
  19.5 7.8 %collective-permute-start.9 = (bf16[1,64,512]{2,1,0:T(8,128)(2,1)S(1)}, bf16[1,64,512]{2,1,0:T(8,128)(2,1)S(1)}, u32[]{:S(2)}, u32[]{:S(2)}) collective-permute-start(bf16[1,64,512]{2,1,0:T(8,128)(2,1)S(1)} %get-tuple-element.27), channel_id=1, source_target_pairs={{0,1},{1,2},{2,3},{3,0},{4,5},{5,6},{6,7},{7,4},{8,9},{9,10},{10,1... | collective-permute-start | bytes 196616 | tf_op jit(solution)/shard_map/ppermute | solution.py:171
  20.0 8.5 %collective-permute-start.5 = (bf16[1,64,512]{2,1,0:T(8,128)(2,1)S(1)}, bf16[1,64,512]{2,1,0:T(8,128)(2,1)S(1)}, u32[]{:S(2)}, u32[]{:S(2)}) collective-permute-start(bf16[1,64,512]{2,1,0:T(8,128)(2,1)S(1)} %get-tuple-element.23), channel_id=1, source_target_pairs={{0,1},{1,2},{2,3},{3,0},{4,5},{5,6},{6,7},{7,4},{8,9},{9,10},{10,1... | collective-permute-start | bytes 196616 | tf_op jit(solution)/shard_map/ppermute | solution.py:171
  20.9 11.0 %collective-permute-start.6 = (bf16[1,64,512]{2,1,0:T(8,128)(2,1)S(1)}, bf16[1,64,512]{2,1,0:T(8,128)(2,1)S(1)}, u32[]{:S(2)}, u32[]{:S(2)}) collective-permute-start(bf16[1,64,512]{2,1,0:T(8,128)(2,1)S(1)} %get-tuple-element.24), channel_id=1, source_target_pairs={{0,2},{1,3},{2,0},{3,1},{4,6},{5,7},{6,4},{7,5},{8,10},{9,11},{10,... | collective-permute-start | bytes 196616 | tf_op jit(solution)/shard_map/ppermute | solution.py:171
  21.7 10.2 %collective-permute-start.7 = (bf16[1,64,512]{2,1,0:T(8,128)(2,1)S(1)}, bf16[1,64,512]{2,1,0:T(8,128)(2,1)S(1)}, u32[]{:S(2)}, u32[]{:S(2)}) collective-permute-start(bf16[1,64,512]{2,1,0:T(8,128)(2,1)S(1)} %get-tuple-element.25), channel_id=1, source_target_pairs={{0,3},{1,0},{2,1},{3,2},{4,7},{5,4},{6,5},{7,6},{8,11},{9,8},{10,9... | collective-permute-start | bytes 196616 | tf_op jit(solution)/shard_map/ppermute | solution.py:171
  22.3 1.6 %copy-start = (bf16[1,4,32,64,128]{4,3,2,1,0:T(8,128)(2,1)S(1)}, bf16[1,4,32,64,128]{4,3,2,1,0:T(8,128)(2,1)}, u32[]{:S(2)}) copy-start(bf16[1,4,32,64,128]{4,3,2,1,0:T(8,128)(2,1)} %chol_ref.7) | copy-start | bytes 6291460
  23.9 0.7 %copy-start.4 = (s32[1,4]{1,0:T(1,128)S(1)}, s32[1,4]{1,0:T(1,128)}, u32[]{:S(2)}) copy-start(s32[1,4]{1,0:T(1,128)} %screen_ref.7) | copy-start | bytes 52
  24.6 5.4 %copy-start.1 = (bf16[1,4,32,64,128]{4,3,2,1,0:T(8,128)(2,1)S(1)}, bf16[1,4,32,64,128]{4,3,2,1,0:T(8,128)(2,1)}, u32[]{:S(2)}) copy-start(bf16[1,4,32,64,128]{4,3,2,1,0:T(8,128)(2,1)} %chol_ref.7) | copy-start | bytes 6291460
  27.2 6.7 %collective-permute-start.1 = (bf16[1,64,512]{2,1,0:T(8,128)(2,1)S(1)}, bf16[1,64,512]{2,1,0:T(8,128)(2,1)S(1)}, u32[]{:S(2)}, u32[]{:S(2)}) collective-permute-start(bf16[1,64,512]{2,1,0:T(8,128)(2,1)S(1)} %get-tuple-element.19), channel_id=1, source_target_pairs={{0,1},{1,2},{2,3},{3,0},{4,5},{5,6},{6,7},{7,4},{8,9},{9,10},{10,1... | collective-permute-start | bytes 196616 | tf_op jit(solution)/shard_map/ppermute | solution.py:171
  27.3 6.6 %collective-permute-start.2 = (bf16[1,64,512]{2,1,0:T(8,128)(2,1)S(1)}, bf16[1,64,512]{2,1,0:T(8,128)(2,1)S(1)}, u32[]{:S(2)}, u32[]{:S(2)}) collective-permute-start(bf16[1,64,512]{2,1,0:T(8,128)(2,1)S(1)} %get-tuple-element.20), channel_id=1, source_target_pairs={{0,2},{1,3},{2,0},{3,1},{4,6},{5,7},{6,4},{7,5},{8,10},{9,11},{10,... | collective-permute-start | bytes 196616 | tf_op jit(solution)/shard_map/ppermute | solution.py:171
  28.6 5.4 %collective-permute-start.3 = (bf16[1,64,512]{2,1,0:T(8,128)(2,1)S(1)}, bf16[1,64,512]{2,1,0:T(8,128)(2,1)S(1)}, u32[]{:S(2)}, u32[]{:S(2)}) collective-permute-start(bf16[1,64,512]{2,1,0:T(8,128)(2,1)S(1)} %get-tuple-element.21), channel_id=1, source_target_pairs={{0,3},{1,0},{2,1},{3,2},{4,7},{5,4},{6,5},{7,6},{8,11},{9,8},{10,9... | collective-permute-start | bytes 196616 | tf_op jit(solution)/shard_map/ppermute | solution.py:171

commit v3 on v2

v3 whole, which is shorter than its diff:
```python
import functools

import jax
import jax.numpy as jnp
from jax import lax
from jax.experimental import pallas as pl
from jax.experimental.pallas import tpu as pltpu
from jax.sharding import PartitionSpec as P

LANES = 128
VMEM_LIMIT = 48 * 1024 * 1024
BATCH = 4
K_STEP = 8
VMEM = pl.BlockSpec(memory_space=pltpu.VMEM)
SMEM = pl.BlockSpec(memory_space=pltpu.SMEM)


def split_axis(groups):
    outer = 1
    while outer * outer * 4 <= groups:
        outer *= 2
    return outer, groups // outer


def pick_kernel(list_ref, *refs, count, inner):
    theta_refs, out_refs = refs[:count], refs[count:]
    listed = list_ref.shape[0]
    width = out_refs[0].shape[2] // listed
    me = lax.axis_index("chol")
    spot = lax.rem(me, inner)
    for t, out_ref in enumerate(out_refs):
        group = me - spot + (spot ^ t)
        for m in range(listed):
            start = pl.multiple_of(list_ref[m, group] * width, width)
            for i, theta_ref in enumerate(theta_refs):
                out_ref[i, :, m * width:(m + 1) * width] = theta_ref[0, :, pl.ds(start, width)]


def pick_tiles(thetas, listing, width, inner):
    count = len(thetas)
    _, occupied, _ = thetas[0].shape
    listed = listing.shape[0]
    piece = jax.ShapeDtypeStruct((count, occupied, listed * width), thetas[0].dtype)
    return pl.pallas_call(
        functools.partial(pick_kernel, count=count, inner=inner),
        in_specs=[SMEM] + [VMEM] * count,
        out_specs=[VMEM] * inner,
        out_shape=[piece] * inner,
        compiler_params=pltpu.CompilerParams(vmem_limit_bytes=VMEM_LIMIT),
        cost_estimate=pl.CostEstimate(
            flops=0, bytes_accessed=4 * count * inner * occupied * listed * width, transcendentals=0
        ),
        name="pick_tiles",
    )(listing, *thetas)


def batch_terms(chol_ref, theta):
    _, listed, vectors, occupied, width = chol_ref.shape
    columns = theta.shape[0]
    walkers = columns // occupied
    tiles = columns // LANES
    contract = (((1,), (1,)), ((), ()))

    lane = lax.broadcasted_iota(jnp.int32, (occupied, LANES), 1)
    low = lane < occupied
    sub8 = lax.broadcasted_iota(jnp.int32, (8, LANES), 0)
    lane8 = lax.broadcasted_iota(jnp.int32, (8, LANES), 1)
    strip = (lane8 % occupied) // 8
    on_diag = lane8 % 8 == sub8

    def diagonal(block):
        merged = block[:8]
        for r in range(1, occupied // 8):
            merged = jnp.where(strip == r, block[8 * r:8 * r + 8], merged)
        return jnp.sum(jnp.where(on_diag, merged, 0.0), axis=0, keepdims=True)

    cross = [jnp.zeros((8, LANES), jnp.float32) for _ in range(tiles)]
    diag_rows = []
    for k0 in range(0, vectors, K_STEP):
        left = jnp.concatenate(
            [chol_ref[0, m, k0:k0 + K_STEP].reshape(K_STEP * occupied, width) for m in range(listed)],
            axis=1,
        )
        inner_mat = lax.dot_general(left, theta, contract, preferred_element_type=jnp.float32)
        flipped = lax.dot_general(theta, left, contract, preferred_element_type=jnp.float32)
        for pair in range(K_STEP // 2):
            tops, bottoms = [], []
            r0 = pair * 2 * occupied
            for t in range(tiles):
                c0 = t * LANES
                top = inner_mat[r0:r0 + occupied, c0:c0 + LANES]
                bottom = inner_mat[r0 + occupied:r0 + 2 * occupied, c0:c0 + LANES]
                f_top = flipped[c0:c0 + occupied, r0:r0 + LANES]
                f_bottom = flipped[c0 + occupied:c0 + 2 * occupied, r0:r0 + LANES]
                swapped = pltpu.roll(jnp.where(low, f_bottom, f_top), occupied, 1)
                product = jnp.where(low, top, bottom) * jnp.where(low, f_top, f_bottom)
                product = product + jnp.where(low, bottom, top) * swapped
                cross[t] = cross[t] + jnp.sum(product.reshape(occupied // 8, 8, LANES), axis=0)
                tops.append(diagonal(top))
                bottoms.append(diagonal(bottom))
            diag_rows.append(jnp.concatenate(tops, axis=1))
            diag_rows.append(jnp.concatenate(bottoms, axis=1))
    cross_row = jnp.concatenate([jnp.sum(c, axis=0, keepdims=True) for c in cross], axis=1)
    rows = jnp.concatenate(diag_rows + [jnp.broadcast_to(cross_row, (8, columns))], axis=0)
    seg_row = lax.broadcasted_iota(jnp.int32, (8, columns), 0)
    seg_col = lax.broadcasted_iota(jnp.int32, (8, columns), 1)
    segment = jnp.where(seg_col // occupied == seg_row, 1.0, 0.0).astype(jnp.float32)
    sums = lax.dot_general(
        segment, rows, contract, precision=lax.Precision.HIGHEST, preferred_element_type=jnp.float32
    )[:walkers]
    bias = sums[:, :vectors]
    energy = jnp.sum(bias * bias, axis=1, keepdims=True) - sums[:, vectors:vectors + 1]
    return bias, energy


def terms_kernel(screen_ref, chol_ref, *refs, shifts, inner, carried):
    piece_refs, rest = refs[:inner], refs[inner:]
    out_ref = rest[-1]
    _, listed, vectors, occupied, width = chol_ref.shape
    depth = listed * width
    me = lax.axis_index("chol")
    spot = lax.rem(me, inner)
    zone = me // inner

    lane = lax.broadcasted_iota(jnp.int32, (1, depth), 1)
    mask = jnp.zeros((1, depth), jnp.float32)
    for m in range(listed):
        keep = screen_ref[0, m].astype(jnp.float32)
        mask = jnp.where((lane >= m * width) & (lane < (m + 1) * width), keep, mask)
    mask = mask.astype(piece_refs[0].dtype)

    if carried:
        out_ref[...] = rest[0][...]
    else:
        out_ref[...] = jnp.zeros(out_ref.shape, out_ref.dtype)
    for i, s in enumerate(shifts):
        for first in range(0, inner, BATCH):
            theta = jnp.concatenate([ref[i] for ref in piece_refs[first:first + BATCH]], axis=0) * mask
            bias, energy = batch_terms(chol_ref, theta)
            for offset in range(BATCH):
                owner = (zone ^ s) * inner + (spot ^ (first + offset))
                out_ref[pl.ds(owner, 1), 0, :vectors] = bias[offset:offset + 1]
                out_ref[pl.ds(owner, 1), 0, vectors:vectors + 1] = energy[offset:offset + 1]


def block_terms(screen, chol_tiles, pieces, carried, shifts, groups, out_width):
    inner = len(pieces)
    count, occupied, depth = pieces[0].shape
    vectors = chol_tiles.shape[2]
    operands = [screen, chol_tiles, *pieces] + ([] if carried is None else [carried])
    return pl.pallas_call(
        functools.partial(terms_kernel, shifts=shifts, inner=inner, carried=carried is not None),
        in_specs=[SMEM] + [VMEM] * (len(operands) - 1),
        out_specs=VMEM,
        out_shape=jax.ShapeDtypeStruct((groups, 1, out_width), jnp.float32),
        compiler_params=pltpu.CompilerParams(vmem_limit_bytes=VMEM_LIMIT),
        cost_estimate=pl.CostEstimate(
            flops=4 * count * inner * vectors * occupied * occupied * depth,
            bytes_accessed=2 * chol_tiles.size,
            transcendentals=0,
        ),
        name="block_terms",
    )(*operands)


def finish_kernel(rows_ref, bias_ref, energy_ref, *, vectors, scale):
    groups = rows_ref.shape[0]
    for d in range(groups):
        bias_ref[:, d * vectors:(d + 1) * vectors] = rows_ref[d, :, :vectors]
    total = jnp.sum(rows_ref[:, 0, :], axis=0, keepdims=True)
    energy_ref[...] = total[:, vectors:vectors + 1] * scale


def finish(rows, vectors, scale):
    groups = rows.shape[0]
    force_bias, energy = pl.pallas_call(
        functools.partial(finish_kernel, vectors=vectors, scale=scale),
        in_specs=[VMEM],
        out_specs=[VMEM, VMEM],
        out_shape=[
            jax.ShapeDtypeStruct((1, groups * vectors), jnp.float32),
            jax.ShapeDtypeStruct((1, 1), jnp.float32),
        ],
        name="finish",
    )(rows)
    return force_bias, energy.reshape(1)


def body(theta, chol_tiles, screen, tile_list):
    groups = lax.axis_size("chol")
    outer, inner = split_axis(groups)
    _, occupied, _ = theta.shape
    width = chol_tiles.shape[-1]
    vectors = chol_tiles.shape[2]
    out_width = LANES * ((vectors + 1 + LANES - 1) // LANES)
    listing = tile_list.T

    def partners(zone_flip, spot_flip):
        return [(i, ((i // inner) ^ zone_flip) * inner + ((i % inner) ^ spot_flip)) for i in range(groups)]

    held = [theta] + [lax.ppermute(theta, "chol", partners(s, 0)) for s in range(1, outer)]
    rows = None
    for first in range(0, outer, outer // 2):
        shifts = list(range(first, first + outer // 2))
        picked = pick_tiles([held[s] for s in shifts], listing, width, inner)
        pieces = [picked[0]] + [lax.ppermute(picked[t], "chol", partners(0, t)) for t in range(1, inner)]
        rows = block_terms(screen, chol_tiles, pieces, rows, shifts, groups, out_width)
    back = lax.all_to_all(rows, "chol", split_axis=0, concat_axis=0, tiled=True)
    return finish(back, vectors, 1.0 / (2.0 * occupied * occupied))


def solution(mesh):
    in_specs = (
        P(("grp", "chol"), None, None),
        P("chol", None, None, None, None),
        P("chol", None),
        P(),
    )
    out_specs = (P(("grp", "chol"), None), P(("grp", "chol")))
    return jax.shard_map(body, mesh=mesh, in_specs=in_specs, out_specs=out_specs, check_vma=False)
```

time: 52 us -> 45.6 us (0.88)
  starting transfers between devices: 17.1 us -> 9.56 us
  waiting for transfers between devices: 3.67 us -> 8.94 us
  between operations: 2.55 us -> 0.69 us
  local copies, waits for them, and re-layouts: 4.57 us -> 3.84 us
  other arithmetic: 0.69 us -> 0 us
    ppermute x15 -> x9, starting transfers between devices: 17.1 us -> 9.56 us  [the longest x3 5.68 us: body(): lax.ppermute(theta, 'chol', partners(s, 0))]
    ppermute x15 -> x9, waiting for transfers between devices: 3.67 us -> 8.94 us  [the longest x3 8.41 us: body(): lax.ppermute(theta, 'chol', partners(s, 0))]
    reduce_sum x1 -> x0, other arithmetic: 0.69 us -> none  [body(): jnp.sum(back[:, 0, vectors]).reshape(1) / (2.0 * occupied * occupied)]
    another operation x1 -> x0, local copies, waits for them, and re-layouts: 0.66 us -> none  [body(): force_bias = back[:, 0, :vectors].reshape(1, groups * vectors)]
    pallas_call x8 -> x5, Pallas kernels: 10.5 us -> 9.98 us  [the longest x2 7.24 us: block_terms(): pl.pallas_call(functools.partial(terms_kernel, shifts=shifts, inner=inner...]
    unnamed x12 -> x8, local copies, waits for them, and re-layouts: 3.89 us -> 3.84 us
  transfers between devices with their start and end apart: 15 -> 9, of which waited for: 1 -> 3; matrix products, arithmetic and copies ran while one was open for 0% -> 0% of each run, Pallas kernels for 17% -> 11%
where the time goes in v3:
time: 45.6 us; the launch traced here: 45.3 us
  blocking collectives  12.3 us (27%)
  Pallas kernels  9.98 us (22%)
  starting transfers between devices  9.56 us (21%)
  waiting for transfers between devices  8.94 us (20%)
  local copies, waits for them, and re-layouts  3.84 us (8%)
  between operations  0.69 us (2%)
    all_to_all x1, blocking collectives, body(): back = lax.all_to_all(rows, 'chol', split_axis=0, concat_axis=0, tiled=True)  12.3 us
    ppermute x3, waiting for transfers between devices, body(): lax.ppermute(theta, 'chol', partners(s, 0))  8.41 us
    pallas_call x2, Pallas kernels, block_terms(): pl.pallas_call(functools.partial(terms_kernel, shifts=shifts, inner=inner...  7.24 us
    ppermute x3, starting transfers between devices, body(): lax.ppermute(theta, 'chol', partners(s, 0))  5.68 us
    ppermute x6, starting transfers between devices, body(): lax.ppermute(picked[t], 'chol', partners(0, t))  3.88 us
    unnamed x8, local copies, waits for them, and re-layouts  3.84 us
    pallas_call x2, Pallas kernels, pick_tiles(): pl.pallas_call(functools.partial(pick_kernel, count=count, inner=inner),...  1.38 us
    pallas_call x1, Pallas kernels, finish(): pl.pallas_call(functools.partial(finish_kernel, vectors=vectors, scale=sc...  1.36 us
  transfers between devices with their start and end apart: 9, of which 3 were waited for; matrix products, arithmetic and copies ran while one was open for 0% of the time, Pallas kernels for 11%

profile of v3, /device:TPU:0, one launch (start us, length us, event | category | flops | bytes accessed | tf_op | source)
XLA Modules:
  0.0 45.3 jit_solution(10550827244631119481)
XLA Ops:
  0.6 3.1 %collective-permute-start.5 = (bf16[1,64,1280]{2,1,0:T(8,128)(2,1)}, bf16[1,64,1280]{2,1,0:T(8,128)(2,1)S(1)}, u32[]{:S(2)}, u32[]{:S(2)}) collective-permute-start(bf16[1,64,1280]{2,1,0:T(8,128)(2,1)} %refs_0_.1), channel_id=1, source_target_pairs={{0,4},{1,5},{2,6},{3,7},{4,0},{5,1},{6,2},{7,3},{8,12},{9,13},{10,... | collective-permute-start | bytes 491528 | tf_op jit(solution)/shard_map/ppermute | solution.py:201
  3.7 2.6 %collective-permute-start = (bf16[1,64,1280]{2,1,0:T(8,128)(2,1)}, bf16[1,64,1280]{2,1,0:T(8,128)(2,1)S(1)}, u32[]{:S(2)}, u32[]{:S(2)}) collective-permute-start(bf16[1,64,1280]{2,1,0:T(8,128)(2,1)} %refs_0_.1), channel_id=1, source_target_pairs={{0,8},{1,9},{2,10},{3,11},{4,12},{5,13},{6,14},{7,15},{8,0},{9,1},... | collective-permute-start | bytes 491528 | tf_op jit(solution)/shard_map/ppermute | solution.py:201
  6.3 0.0 collective-permute-start.1
  6.3 4.3 %collective-permute-done.5.refs_1_ = bf16[1,64,1280]{2,1,0:T(8,128)(2,1)S(1)} collective-permute-done((bf16[1,64,1280]{2,1,0:T(8,128)(2,1)}, bf16[1,64,1280]{2,1,0:T(8,128)(2,1)S(1)}, u32[]{:S(2)}, u32[]{:S(2)}) %collective-permute-start.5) | collective-permute-done | bytes 163872 | tf_op jit(solution)/shard_map/ppermute | solution.py:201
  10.6 0.0 copy-start
  10.6 0.9 %copy-done = bf16[1,64,1280]{2,1,0:T(8,128)(2,1)S(1)} copy-done((bf16[1,64,1280]{2,1,0:T(8,128)(2,1)S(1)}, bf16[1,64,1280]{2,1,0:T(8,128)(2,1)}, u32[]{:S(2)}) %copy-start) | copy-done | bytes 163864
  11.5 0.0 copy-start.1
  11.5 0.7 %copy-done.1 = s32[16,4]{0,1:T(4,128)S(1)} copy-done((s32[16,4]{0,1:T(4,128)S(1)}, s32[16,4]{0,1:T(4,128)}, u32[]{:S(2)}) %copy-start.1) | copy-done | bytes 280
  12.2 0.7 %pick_tiles.3 = (bf16[2,64,512]{2,1,0:T(8,128)(2,1)S(1)}, bf16[2,64,512]{2,1,0:T(8,128)(2,1)S(1)}, bf16[2,64,512]{2,1,0:T(8,128)(2,1)S(1)}, bf16[2,64,512]{2,1,0:T(8,128)(2,1)S(1)}) custom-call(s32[4,16]{1,0:T(4,128)S(1)} %bitcast.2, bf16[1,64,1280]{2,1,0:T(8,128)(2,1)S(1)} %copy-done, bf16[1,64,1280]{2,1,0:T(8,128)(2,1)S(1)} %collective-permute-done.5.refs_1_), custom_call_target="tpu_custom_call" | custom-call | bytes 1048576 | tf_op jit(solution)/shard_map/pick_tiles/pallas_call | solution.py:44
  12.9 0.1 collective-permute-start.6
  13.0 1.8 %collective-permute-start.7 = (bf16[2,64,512]{2,1,0:T(8,128)(2,1)S(1)}, bf16[2,64,512]{2,1,0:T(8,128)(2,1)S(1)}, u32[]{:S(2)}, u32[]{:S(2)}) collective-permute-start(bf16[2,64,512]{2,1,0:T(8,128)(2,1)S(1)} %get-tuple-element.18), channel_id=1, source_target_pairs={{0,2},{1,3},{2,0},{3,1},{4,6},{5,7},{6,4},{7,5},{8,10},{9,11},{10,... | collective-permute-start | bytes 393224 | tf_op jit(solution)/shard_map/ppermute | solution.py:206
  14.8 0.1 collective-permute-start.8
  14.9 4.1 %collective-permute-done.refs_0_ = bf16[1,64,1280]{2,1,0:T(8,128)(2,1)S(1)} collective-permute-done((bf16[1,64,1280]{2,1,0:T(8,128)(2,1)}, bf16[1,64,1280]{2,1,0:T(8,128)(2,1)S(1)}, u32[]{:S(2)}, u32[]{:S(2)}) %collective-permute-start) | collective-permute-done | bytes 163872 | tf_op jit(solution)/shard_map/ppermute | solution.py:201
  19.0 0.0 collective-permute-done.1.refs_1_
  19.0 0.7 %pick_tiles.2 = (bf16[2,64,512]{2,1,0:T(8,128)(2,1)S(1)}, bf16[2,64,512]{2,1,0:T(8,128)(2,1)S(1)}, bf16[2,64,512]{2,1,0:T(8,128)(2,1)S(1)}, bf16[2,64,512]{2,1,0:T(8,128)(2,1)S(1)}) custom-call(s32[4,16]{1,0:T(4,128)S(1)} %bitcast.3, bf16[1,64,1280]{2,1,0:T(8,128)(2,1)S(1)} %collective-permute-done.refs_0_, ...), custom_call_target="tpu_custom_call" | custom-call | bytes 1048576 | tf_op jit(solution)/shard_map/pick_tiles/pallas_call | solution.py:44
  19.7 0.1 collective-permute-start.2
  19.8 1.6 %collective-permute-start.3 = (bf16[2,64,512]{2,1,0:T(8,128)(2,1)S(1)}, bf16[2,64,512]{2,1,0:T(8,128)(2,1)S(1)}, u32[]{:S(2)}, u32[]{:S(2)}) collective-permute-start(bf16[2,64,512]{2,1,0:T(8,128)(2,1)S(1)} %get-tuple-element.14), channel_id=1, source_target_pairs={{0,2},{1,3},{2,0},{3,1},{4,6},{5,7},{6,4},{7,5},{8,10},{9,11},{10,... | collective-permute-start | bytes 393224 | tf_op jit(solution)/shard_map/ppermute | solution.py:206
  21.3 0.0 collective-permute-done.6.refs_1_
  21.3 0.3 collective-permute-start.4
  21.6 0.0 collective-permute-done.7.refs_2_
  21.6 0.0 collective-permute-done.8.refs_3_
  21.6 0.0 copy-start.2
  21.6 1.6 %copy-done.2 = bf16[1,4,32,64,128]{4,3,2,1,0:T(8,128)(2,1)S(1)} copy-done((bf16[1,4,32,64,128]{4,3,2,1,0:T(8,128)(2,1)S(1)}, bf16[1,4,32,64,128]{4,3,2,1,0:T(8,128)(2,1)}, u32[]{:S(2)}) %copy-start.2) | copy-done | bytes 2097176
  23.2 0.0 copy-start.3
  23.2 0.7 %copy-done.3 = s32[1,4]{1,0:T(1,128)S(1)} copy-done((s32[1,4]{1,0:T(1,128)S(1)}, s32[1,4]{1,0:T(1,128)}, u32[]{:S(2)}) %copy-start.3) | copy-done | bytes 40
  23.9 3.6 %block_terms.2.refs_4_ = f32[16,1,128]{2,1,0:T(1,128)S(1)} custom-call(s32[1,4]{1,0:T(1,128)S(1)} %copy-done.3, bf16[1,4,32,64,128]{4,3,2,1,0:T(8,128)(2,1)S(1)} %copy-done.2, bf16[2,64,512]{2,1,0:T(8,128)(2,1)S(1)} %get-tuple-element.16.refs_0_, bf16[2,64,512]{2,1,0:T(8,128)(2,1)S(1)} %collective-permute-done.6.refs_1_, ...), custom_call_target="tpu_custom_call" | custom-call | flops 2147483648 | bytes 2097152 | tf_op jit(solution)/shard_map/block_terms/pallas_call | solution.py:151
  27.5 0.0 collective-permute-done.2.refs_1_
  27.5 0.0 collective-permute-done.3.refs_2_
  27.5 0.5 %collective-permute-done.4.refs_3_ = bf16[2,64,512]{2,1,0:T(8,128)(2,1)S(1)} collective-permute-done((bf16[2,64,512]{2,1,0:T(8,128)(2,1)S(1)}, bf16[2,64,512]{2,1,0:T(8,128)(2,1)S(1)}, u32[]{:S(2)}, u32[]{:S(2)}) %collective-permute-start.4) | collective-permute-done | bytes 131104 | tf_op jit(solution)/shard_map/ppermute | solution.py:206
  28.0 3.6 %block_terms.3 = f32[16,1,128]{2,1,0:T(1,128)S(1)} custom-call(s32[1,4]{1,0:T(1,128)S(1)} %copy-done.3, bf16[1,4,32,64,128]{4,3,2,1,0:T(8,128)(2,1)S(1)} %copy-done.2, bf16[2,64,512]{2,1,0:T(8,128)(2,1)S(1)} %get-tuple-element.12.refs_0_, bf16[2,64,512]{2,1,0:T(8,128)(2,1)S(1)} %collective-permute-done.2.refs_1_, ...), custom_call_target="tpu_custom_call" | custom-call | flops 2147483648 | bytes 2097152 | tf_op jit(solution)/shard_map/block_terms/pallas_call | solution.py:151
  31.7 12.3 %all_to_all.5.rows_ref = f32[16,1,128]{2,1,0:T(1,128)} all-to-all(f32[16,1,128]{2,1,0:T(1,128)S(1)} %block_terms.3), channel_id=1, replica_groups=mesh['grp'=2,'chol'=16] {'chol'}, dimensions={0} | all-to-all | bytes 16384 | tf_op jit(solution)/shard_map/all_to_all | solution.py:208
  44.0 1.4 %finish.1 = (f32[1,512]{1,0:T(1,128)}, f32[1,1]{1,0:T(1,128)}) custom-call(f32[16,1,128]{2,1,0:T(1,128)} %all_to_all.5.rows_ref), custom_call_target="tpu_custom_call" | custom-call | tf_op jit(solution)/shard_map/finish/pallas_call | solution.py:176
Async XLA Ops:
  0.6 10.0 %collective-permute-start.5 = (bf16[1,64,1280]{2,1,0:T(8,128)(2,1)}, bf16[1,64,1280]{2,1,0:T(8,128)(2,1)S(1)}, u32[]{:S(2)}, u32[]{:S(2)}) collective-permute-start(bf16[1,64,1280]{2,1,0:T(8,128)(2,1)} %refs_0_.1), channel_id=1, source_target_pairs={{0,4},{1,5},{2,6},{3,7},{4,0},{5,1},{6,2},{7,3},{8,12},{9,13},{10,... | collective-permute-start | bytes 491528 | tf_op jit(solution)/shard_map/ppermute | solution.py:201
  3.7 15.3 %collective-permute-start = (bf16[1,64,1280]{2,1,0:T(8,128)(2,1)}, bf16[1,64,1280]{2,1,0:T(8,128)(2,1)S(1)}, u32[]{:S(2)}, u32[]{:S(2)}) collective-permute-start(bf16[1,64,1280]{2,1,0:T(8,128)(2,1)} %refs_0_.1), channel_id=1, source_target_pairs={{0,8},{1,9},{2,10},{3,11},{4,12},{5,13},{6,14},{7,15},{8,0},{9,1},... | collective-permute-start | bytes 491528 | tf_op jit(solution)/shard_map/ppermute | solution.py:201
  6.3 12.7 %collective-permute-start.1 = (bf16[1,64,1280]{2,1,0:T(8,128)(2,1)}, bf16[1,64,1280]{2,1,0:T(8,128)(2,1)S(1)}, u32[]{:S(2)}, u32[]{:S(2)}) collective-permute-start(bf16[1,64,1280]{2,1,0:T(8,128)(2,1)} %refs_0_.1), channel_id=1, source_target_pairs={{0,12},{1,13},{2,14},{3,15},{4,8},{5,9},{6,10},{7,11},{8,4},{9,5},... | collective-permute-start | bytes 491528 | tf_op jit(solution)/shard_map/ppermute | solution.py:201
  10.6 0.9 %copy-start = (bf16[1,64,1280]{2,1,0:T(8,128)(2,1)S(1)}, bf16[1,64,1280]{2,1,0:T(8,128)(2,1)}, u32[]{:S(2)}) copy-start(bf16[1,64,1280]{2,1,0:T(8,128)(2,1)} %refs_0_.1) | copy-start | bytes 491524
  11.5 0.7 %copy-start.1 = (s32[16,4]{0,1:T(4,128)S(1)}, s32[16,4]{0,1:T(4,128)}, u32[]{:S(2)}) copy-start(s32[16,4]{0,1:T(4,128)} %param.7) | copy-start | bytes 772
  12.9 8.4 %collective-permute-start.6 = (bf16[2,64,512]{2,1,0:T(8,128)(2,1)S(1)}, bf16[2,64,512]{2,1,0:T(8,128)(2,1)S(1)}, u32[]{:S(2)}, u32[]{:S(2)}) collective-permute-start(bf16[2,64,512]{2,1,0:T(8,128)(2,1)S(1)} %get-tuple-element.17), channel_id=1, source_target_pairs={{0,1},{1,0},{2,3},{3,2},{4,5},{5,4},{6,7},{7,6},{8,9},{9,8},{10,11... | collective-permute-start | bytes 393224 | tf_op jit(solution)/shard_map/ppermute | solution.py:206
  13.0 8.7 %collective-permute-start.7 = (bf16[2,64,512]{2,1,0:T(8,128)(2,1)S(1)}, bf16[2,64,512]{2,1,0:T(8,128)(2,1)S(1)}, u32[]{:S(2)}, u32[]{:S(2)}) collective-permute-start(bf16[2,64,512]{2,1,0:T(8,128)(2,1)S(1)} %get-tuple-element.18), channel_id=1, source_target_pairs={{0,2},{1,3},{2,0},{3,1},{4,6},{5,7},{6,4},{7,5},{8,10},{9,11},{10,... | collective-permute-start | bytes 393224 | tf_op jit(solution)/shard_map/ppermute | solution.py:206
  14.8 6.8 %collective-permute-start.8 = (bf16[2,64,512]{2,1,0:T(8,128)(2,1)S(1)}, bf16[2,64,512]{2,1,0:T(8,128)(2,1)S(1)}, u32[]{:S(2)}, u32[]{:S(2)}) collective-permute-start(bf16[2,64,512]{2,1,0:T(8,128)(2,1)S(1)} %get-tuple-element.19), channel_id=1, source_target_pairs={{0,3},{1,2},{2,1},{3,0},{4,7},{5,6},{6,5},{7,4},{8,11},{9,10},{10,... | collective-permute-start | bytes 393224 | tf_op jit(solution)/shard_map/ppermute | solution.py:206
  19.7 7.8 %collective-permute-start.2 = (bf16[2,64,512]{2,1,0:T(8,128)(2,1)S(1)}, bf16[2,64,512]{2,1,0:T(8,128)(2,1)S(1)}, u32[]{:S(2)}, u32[]{:S(2)}) collective-permute-start(bf16[2,64,512]{2,1,0:T(8,128)(2,1)S(1)} %get-tuple-element.13), channel_id=1, source_target_pairs={{0,1},{1,0},{2,3},{3,2},{4,5},{5,4},{6,7},{7,6},{8,9},{9,8},{10,11... | collective-permute-start | bytes 393224 | tf_op jit(solution)/shard_map/ppermute | solution.py:206
  19.8 7.8 %collective-permute-start.3 = (bf16[2,64,512]{2,1,0:T(8,128)(2,1)S(1)}, bf16[2,64,512]{2,1,0:T(8,128)(2,1)S(1)}, u32[]{:S(2)}, u32[]{:S(2)}) collective-permute-start(bf16[2,64,512]{2,1,0:T(8,128)(2,1)S(1)} %get-tuple-element.14), channel_id=1, source_target_pairs={{0,2},{1,3},{2,0},{3,1},{4,6},{5,7},{6,4},{7,5},{8,10},{9,11},{10,... | collective-permute-start | bytes 393224 | tf_op jit(solution)/shard_map/ppermute | solution.py:206
  21.3 6.7 %collective-permute-start.4 = (bf16[2,64,512]{2,1,0:T(8,128)(2,1)S(1)}, bf16[2,64,512]{2,1,0:T(8,128)(2,1)S(1)}, u32[]{:S(2)}, u32[]{:S(2)}) collective-permute-start(bf16[2,64,512]{2,1,0:T(8,128)(2,1)S(1)} %get-tuple-element.15), channel_id=1, source_target_pairs={{0,3},{1,2},{2,1},{3,0},{4,7},{5,6},{6,5},{7,4},{8,11},{9,10},{10,... | collective-permute-start | bytes 393224 | tf_op jit(solution)/shard_map/ppermute | solution.py:206
  21.6 1.6 %copy-start.2 = (bf16[1,4,32,64,128]{4,3,2,1,0:T(8,128)(2,1)S(1)}, bf16[1,4,32,64,128]{4,3,2,1,0:T(8,128)(2,1)}, u32[]{:S(2)}) copy-start(bf16[1,4,32,64,128]{4,3,2,1,0:T(8,128)(2,1)} %chol_ref.3) | copy-start | bytes 6291460
  23.2 0.7 %copy-start.3 = (s32[1,4]{1,0:T(1,128)S(1)}, s32[1,4]{1,0:T(1,128)}, u32[]{:S(2)}) copy-start(s32[1,4]{1,0:T(1,128)} %screen_ref.3) | copy-start | bytes 52

commit v4 on v0

v4 whole, which is shorter than its diff:
```python
import functools

import jax
import jax.numpy as jnp
from jax import lax
from jax.experimental import pallas as pl
from jax.experimental.pallas import tpu as pltpu
from jax.sharding import PartitionSpec as P

LANES = 128
CORES = 2
VMEM_LIMIT = 32 * 1024 * 1024
K_STEP = 8
VMEM = pl.BlockSpec(memory_space=pltpu.VMEM)
SMEM = pl.BlockSpec(memory_space=pltpu.SMEM)
PARAMS = pltpu.CompilerParams(vmem_limit_bytes=VMEM_LIMIT)
CONTRACT = (((1,), (1,)), ((), ()))


def screen_kernel(screen_ref, chol_ref, out_ref):
    _, listed, vectors, occupied, width = chol_ref.shape
    for m in range(listed):
        keep = jnp.full((1, width), screen_ref[0, m].astype(jnp.float32)).astype(chol_ref.dtype)
        out_ref[:, m * width:(m + 1) * width] = chol_ref[0, m].reshape(vectors * occupied, width) * keep


def screened_block(screen, chol_tiles):
    _, listed, vectors, occupied, width = chol_tiles.shape
    return pl.pallas_call(
        screen_kernel,
        in_specs=[SMEM, VMEM],
        out_specs=VMEM,
        out_shape=jax.ShapeDtypeStruct((vectors * occupied, listed * width), chol_tiles.dtype),
        compiler_params=PARAMS,
        cost_estimate=pl.CostEstimate(flops=0, bytes_accessed=4 * chol_tiles.size, transcendentals=0),
        name="screen_block",
    )(screen, chol_tiles)


def batch_terms(block_ref, theta, vectors, occupied):
    columns = theta.shape[0]
    walkers = columns // occupied
    tiles = columns // LANES

    lane = lax.broadcasted_iota(jnp.int32, (occupied, LANES), 1)
    low = lane < occupied
    sub8 = lax.broadcasted_iota(jnp.int32, (8, LANES), 0)
    lane8 = lax.broadcasted_iota(jnp.int32, (8, LANES), 1)
    strip = (lane8 % occupied) // 8
    on_diag = lane8 % 8 == sub8

    def diagonal(block):
        merged = block[:8]
        for r in range(1, occupied // 8):
            merged = jnp.where(strip == r, block[8 * r:8 * r + 8], merged)
        return jnp.where(on_diag, merged, 0.0)

    cross = [jnp.zeros((8, LANES), jnp.float32) for _ in range(tiles)]
    diagonals = []
    for k0 in range(0, vectors, K_STEP):
        left = block_ref[k0 * occupied:(k0 + K_STEP) * occupied, :]
        inner_mat = lax.dot_general(left, theta, CONTRACT, preferred_element_type=jnp.float32)
        flipped = lax.dot_general(theta, left, CONTRACT, preferred_element_type=jnp.float32)
        for pair in range(K_STEP // 2):
            tops, bottoms = [], []
            r0 = pair * 2 * occupied
            for t in range(tiles):
                c0 = t * LANES
                top = inner_mat[r0:r0 + occupied, c0:c0 + LANES]
                bottom = inner_mat[r0 + occupied:r0 + 2 * occupied, c0:c0 + LANES]
                f_top = flipped[c0:c0 + occupied, r0:r0 + LANES]
                f_bottom = flipped[c0 + occupied:c0 + 2 * occupied, r0:r0 + LANES]
                swapped = pltpu.roll(jnp.where(low, f_bottom, f_top), occupied, 1)
                product = jnp.where(low, top, bottom) * jnp.where(low, f_top, f_bottom)
                product = product + jnp.where(low, bottom, top) * swapped
                cross[t] = cross[t] + jnp.sum(product.reshape(occupied // 8, 8, LANES), axis=0)
                tops.append(diagonal(top))
                bottoms.append(diagonal(bottom))
            diagonals.append(jnp.concatenate(tops, axis=1))
            diagonals.append(jnp.concatenate(bottoms, axis=1))
    diagonals.append(jnp.concatenate(cross, axis=1))
    stacked = jnp.concatenate(diagonals, axis=0).reshape(vectors + 1, 8, columns)
    rows = jnp.sum(stacked, axis=1)
    seg_row = lax.broadcasted_iota(jnp.int32, (8, columns), 0)
    seg_col = lax.broadcasted_iota(jnp.int32, (8, columns), 1)
    segment = jnp.where(seg_col // occupied == seg_row, 1.0, 0.0).astype(jnp.float32)
    sums = lax.dot_general(
        segment, rows, CONTRACT, precision=lax.Precision.HIGHEST, preferred_element_type=jnp.float32
    )[:walkers]
    return sums[:, :vectors], sums[:, vectors:vectors + 1]


def terms_kernel(list_ref, own_ref, other_ref, *refs, first, pairs, vectors, carried):
    theta_refs, rest = refs[:2 * pairs], refs[2 * pairs:]
    out_ref, picked_ref = rest[-2], rest[-1]
    listed = list_ref.shape[0]
    _, occupied, _ = theta_refs[0].shape
    width = own_ref.shape[1] // listed
    me = lax.axis_index("chol")
    core = lax.rem(me, CORES)
    chip = me // CORES
    spot = lax.rem(chip, 2)
    zone = chip // 2

    for b, group in enumerate((me, me ^ 1)):
        for m in range(listed):
            start = pl.multiple_of(list_ref[m, group] * width, width)
            for i, ref in enumerate(theta_refs):
                picked_ref[b, i * occupied:(i + 1) * occupied, m * width:(m + 1) * width] = ref[0, :, pl.ds(start, width)]

    if carried:
        out_ref[...] = rest[0][...]
    else:
        out_ref[...] = jnp.zeros(out_ref.shape, out_ref.dtype)

    def one_batch(pair, count):
        start = pair * 2 * occupied
        rows = pl.ds(start if isinstance(pair, int) else pl.multiple_of(start, 2 * occupied), count * 2 * occupied)
        own_bias, own_cross = batch_terms(own_ref, picked_ref[0, rows, :], vectors, occupied)
        other_bias, other_cross = batch_terms(other_ref, picked_ref[1, rows, :], vectors, occupied)
        both = jnp.where(
            core == 0,
            jnp.concatenate([own_bias, other_bias], axis=1),
            jnp.concatenate([other_bias, own_bias], axis=1),
        )
        energy = jnp.sum(both * both, axis=1, keepdims=True) - (own_cross + other_cross)
        for i in range(2 * count):
            owner = (zone ^ (first + pair + i // 2)) * 2 + (spot ^ (i % 2))
            out_ref[pl.ds(owner, 1), 0, :CORES * vectors] = both[i:i + 1]
            out_ref[pl.ds(owner, 1), 0, CORES * vectors:CORES * vectors + 1] = energy[i:i + 1]

    if pairs <= 2:
        one_batch(0, pairs)
    else:
        @pl.loop(0, pairs // 2)
        def _(step):
            one_batch(step * 2, 2)


def pair_terms(listing, own, other, thetas, carried, first, vectors, out_width):
    pairs = len(thetas) // 2
    _, occupied, _ = thetas[0].shape
    chips = listing.shape[1] // CORES
    depth = own.shape[1]
    operands = [listing, own, other, *thetas] + ([] if carried is None else [carried])
    return pl.pallas_call(
        functools.partial(terms_kernel, first=first, pairs=pairs, vectors=vectors, carried=carried is not None),
        in_specs=[SMEM] + [VMEM] * (len(operands) - 1),
        out_specs=VMEM,
        out_shape=jax.ShapeDtypeStruct((chips, 1, out_width), jnp.float32),
        scratch_shapes=[pltpu.VMEM((CORES, 2 * pairs * occupied, depth), own.dtype)],
        compiler_params=PARAMS,
        cost_estimate=pl.CostEstimate(
            flops=16 * pairs * vectors * occupied * occupied * depth,
            bytes_accessed=4 * own.size,
            transcendentals=0,
        ),
        name="pair_terms",
    )(*operands)


def finish_kernel(rows_ref, bias_ref, energy_ref, *, used, scale):
    chips = rows_ref.shape[0]
    for d in range(chips):
        bias_ref[:, d * used:(d + 1) * used] = rows_ref[d, :, :used]
    total = jnp.sum(rows_ref[:, 0, :], axis=0, keepdims=True)
    energy_ref[...] = total[:, used:used + 1] * scale


def finish(rows, used, scale):
    chips = rows.shape[0]
    force_bias, energy = pl.pallas_call(
        functools.partial(finish_kernel, used=used, scale=scale),
        in_specs=[VMEM],
        out_specs=[VMEM, VMEM],
        out_shape=[
            jax.ShapeDtypeStruct((1, chips * used), jnp.float32),
            jax.ShapeDtypeStruct((1, 1), jnp.float32),
        ],
        name="finish",
    )(rows)
    return force_bias, energy.reshape(1)


def body(theta, chol_tiles, screen, tile_list):
    groups = lax.axis_size("chol")
    chips = groups // CORES
    zones = chips // 2
    _, occupied, _ = theta.shape
    vectors = chol_tiles.shape[2]
    used = CORES * vectors
    out_width = LANES * ((used + 1 + LANES - 1) // LANES)
    listing = tile_list.T

    def flipped(x, flip):
        return lax.ppermute(x, "chol", [(i, i ^ flip) for i in range(groups)])

    held = {0: theta}
    bit = zones // 2
    while bit:
        for s in sorted(held):
            held[s ^ bit] = flipped(held[s], bit * 2 * CORES)
        bit //= 2
    own = screened_block(screen, chol_tiles)
    other = flipped(own, 1)
    beside = {s: flipped(held[s], CORES) for s in range(zones)}

    rows = None
    for first, last in ((0, 1), (1, zones - 1), (zones - 1, zones)):
        thetas = [x for s in range(first, last) for x in (held[s], beside[s])]
        rows = pair_terms(listing, own, other, thetas, rows, first, vectors, out_width)
    same_core = [list(range(core, groups, CORES)) for core in range(CORES)]
    back = lax.all_to_all(rows, "chol", split_axis=0, concat_axis=0, tiled=True, axis_index_groups=same_core)
    return finish(back, used, 1.0 / (2.0 * occupied * occupied))


def solution(mesh):
    in_specs = (
        P(("grp", "chol"), None, None),
        P("chol", None, None, None, None),
        P("chol", None),
        P(),
    )
    out_specs = (P(("grp", "chol"), None), P(("grp", "chol")))
    return jax.shard_map(body, mesh=mesh, in_specs=in_specs, out_specs=out_specs, check_vma=False)
```

time: 154 us -> 52.1 us (0.34)
  waiting for transfers between devices: 48.1 us -> 12.3 us
  local copies, waits for them, and re-layouts: 24.8 us -> 2.25 us
  blocking collectives: 33.8 us -> 11.8 us
  other arithmetic: 17.7 us -> 0 us
  between operations: 15.9 us -> 0.66 us
  Pallas kernels: 0 us -> 13.5 us
  matrix products: 9.69 us -> 0 us
  starting transfers between devices: 3.51 us -> 11.3 us
    all_gather x1 -> x0, waiting for transfers between devices: 47.4 us -> none  [body(): walker_piece = lax.all_gather(theta, 'chol', axis=0, tiled=True)]
    unnamed x1 -> x0, blocking collectives: 33.8 us -> none
    dot_general x1 -> x0, local copies, waits for them, and re-layouts: 17.5 us -> none  [block_terms(): jnp.einsum('bmkaq,ncmq->nbkac', masked, selected, preferred_element_type=...]
    reduce_sum x2 -> x0, other arithmetic: 16.3 us -> none  [the longest x1 15.5 us: block_terms(): cross_sum = jnp.sum(inner_mat * jnp.swapaxes(inner_mat, 3, 4), axis=(3, 4))]
    pallas_call x0 -> x5, Pallas kernels: none -> 13.5 us  [the longest x3 11.3 us: pair_terms(): pl.pallas_call(functools.partial(terms_kernel, first=first, pairs=pairs,...]
    ppermute x0 -> x8, waiting for transfers between devices: none -> 12.3 us  [flipped(): return lax.ppermute(x, 'chol', [(i, i ^ flip) for i in range(groups)])]
    all_to_all x0 -> x1, blocking collectives: none -> 11.8 us  [body(): lax.all_to_all(rows, 'chol', split_axis=0, concat_axis=0, tiled=True, axi...]
    ppermute x0 -> x8, starting transfers between devices: none -> 11.3 us  [flipped(): return lax.ppermute(x, 'chol', [(i, i ^ flip) for i in range(groups)])]
  transfers between devices with their start and end apart: 2 -> 8, of which waited for: 1 -> 4; matrix products, arithmetic and copies ran while one was open for 2% -> 0% of each run, Pallas kernels for 0% -> 14%
where the time goes in v4:
time: 52.1 us; the launch traced here: 51.8 us
  Pallas kernels  13.5 us (26%)
  waiting for transfers between devices  12.3 us (24%)
  blocking collectives  11.8 us (23%)
  starting transfers between devices  11.3 us (22%)
  local copies, waits for them, and re-layouts  2.25 us (4%)
  between operations  0.66 us (1%)
    ppermute x8, waiting for transfers between devices, flipped(): return lax.ppermute(x, 'chol', [(i, i ^ flip) for i in range(groups)])  12.3 us
    all_to_all x1, blocking collectives, body(): lax.all_to_all(rows, 'chol', split_axis=0, concat_axis=0, tiled=True, axi...  11.8 us
    ppermute x8, starting transfers between devices, flipped(): return lax.ppermute(x, 'chol', [(i, i ^ flip) for i in range(groups)])  11.3 us
    pallas_call x3, Pallas kernels, pair_terms(): pl.pallas_call(functools.partial(terms_kernel, first=first, pairs=pairs,...  11.3 us
    unnamed x8, local copies, waits for them, and re-layouts  2.25 us
    pallas_call x1, Pallas kernels, finish(): pl.pallas_call(functools.partial(finish_kernel, used=used, scale=scale),...  1.32 us
  transfers between devices with their start and end apart: 8, of which 4 were waited for; matrix products, arithmetic and copies ran while one was open for 0% of the time, Pallas kernels for 14%

profile of v4, /device:TPU:0, one launch (start us, length us, event | category | flops | bytes accessed | tf_op | source)
XLA Modules:
  0.0 51.8 jit_solution(17417455547517597607)
XLA Ops:
  0.6 0.0 copy-start
  0.6 1.6 %copy-done = bf16[1,4,32,64,128]{4,3,2,1,0:T(8,128)(2,1)S(1)} copy-done((bf16[1,4,32,64,128]{4,3,2,1,0:T(8,128)(2,1)S(1)}, bf16[1,4,32,64,128]{4,3,2,1,0:T(8,128)(2,1)}, u32[]{:S(2)}) %copy-start) | copy-done | bytes 2097176
  2.2 0.0 copy-start.3
  2.2 0.7 %copy-done.3 = s32[1,4]{1,0:T(1,128)S(1)} copy-done((s32[1,4]{1,0:T(1,128)S(1)}, s32[1,4]{1,0:T(1,128)}, u32[]{:S(2)}) %copy-start.3) | copy-done | bytes 40
  2.9 0.0 copy-start.1
  2.9 0.0 copy-start.2
  2.9 0.9 %screen_block.1.own_ref = bf16[2048,512]{1,0:T(8,128)(2,1)S(1)} custom-call(s32[1,4]{1,0:T(1,128)S(1)} %copy-done.3, bf16[1,4,32,64,128]{4,3,2,1,0:T(8,128)(2,1)S(1)} %copy-done), custom_call_target="tpu_custom_call" | custom-call | bytes 4194304 | tf_op jit(solution)/shard_map/screen_block/pallas_call | solution.py:29
  3.8 0.5 collective-permute-start
  4.3 0.0 copy-done.1
  4.3 3.7 %collective-permute-start.1 = (bf16[1,64,1280]{2,1,0:T(8,128)(2,1)S(1)}, bf16[1,64,1280]{2,1,0:T(8,128)(2,1)S(1)}, u32[]{:S(2)}, u32[]{:S(2)}) collective-permute-start(bf16[1,64,1280]{2,1,0:T(8,128)(2,1)S(1)} %copy-done.1), channel_id=1, source_target_pairs={{0,8},{1,9},{2,10},{3,11},{4,12},{5,13},{6,14},{7,15},{8,0},{9,1},... | collective-permute-start | bytes 491528 | tf_op jit(solution)/shard_map/ppermute | solution.py:196
  8.0 1.6 %collective-permute-start.4 = (bf16[1,64,1280]{2,1,0:T(8,128)(2,1)S(1)}, bf16[1,64,1280]{2,1,0:T(8,128)(2,1)S(1)}, u32[]{:S(2)}, u32[]{:S(2)}) collective-permute-start(bf16[1,64,1280]{2,1,0:T(8,128)(2,1)S(1)} %copy-done.1), channel_id=1, source_target_pairs={{0,4},{1,5},{2,6},{3,7},{4,0},{5,1},{6,2},{7,3},{8,12},{9,13},{10,... | collective-permute-start | bytes 491528 | tf_op jit(solution)/shard_map/ppermute | solution.py:196
  9.6 6.8 %collective-permute-done.1.refs_2_ = bf16[1,64,1280]{2,1,0:T(8,128)(2,1)S(1)} collective-permute-done((bf16[1,64,1280]{2,1,0:T(8,128)(2,1)S(1)}, bf16[1,64,1280]{2,1,0:T(8,128)(2,1)S(1)}, u32[]{:S(2)}, u32[]{:S(2)}) %collective-permute-start.1) | collective-permute-done | bytes 163872 | tf_op jit(solution)/shard_map/ppermute | solution.py:196
  16.4 0.6 %collective-permute-start.2 = (bf16[1,64,1280]{2,1,0:T(8,128)(2,1)S(1)}, bf16[1,64,1280]{2,1,0:T(8,128)(2,1)S(1)}, u32[]{:S(2)}, u32[]{:S(2)}) collective-permute-start(bf16[1,64,1280]{2,1,0:T(8,128)(2,1)S(1)} %collective-permute-done.1.refs_2_), channel_id=1, source_target_pairs={{0,4},{1,5},{2,6},{3,7},{4,0},{5,1},{6,2},{7,3},{8,12},{9,13},{10,... | collective-permute-start | bytes 491528 | tf_op jit(solution)/shard_map/ppermute | solution.py:196
  17.0 1.5 %collective-permute-start.7 = (bf16[1,64,1280]{2,1,0:T(8,128)(2,1)S(1)}, bf16[1,64,1280]{2,1,0:T(8,128)(2,1)S(1)}, u32[]{:S(2)}, u32[]{:S(2)}) collective-permute-start(bf16[1,64,1280]{2,1,0:T(8,128)(2,1)S(1)} %copy-done.1), channel_id=1, source_target_pairs={{0,2},{1,3},{2,0},{3,1},{4,6},{5,7},{6,4},{7,5},{8,10},{9,11},{10,... | collective-permute-start | bytes 491528 | tf_op jit(solution)/shard_map/ppermute | solution.py:196
  18.6 0.5 collective-permute-start.6
  19.1 0.0 collective-permute-done.4.refs_0_
  19.1 1.5 %collective-permute-start.5 = (bf16[1,64,1280]{2,1,0:T(8,128)(2,1)S(1)}, bf16[1,64,1280]{2,1,0:T(8,128)(2,1)S(1)}, u32[]{:S(2)}, u32[]{:S(2)}) collective-permute-start(bf16[1,64,1280]{2,1,0:T(8,128)(2,1)S(1)} %collective-permute-done.4.refs_0_), channel_id=1, source_target_pairs={{0,2},{1,3},{2,0},{3,1},{4,6},{5,7},{6,4},{7,5},{8,10},{9,11},{10,... | collective-permute-start | bytes 491528 | tf_op jit(solution)/shard_map/ppermute | solution.py:196
  20.6 1.7 %collective-permute-done.2.refs_0_ = bf16[1,64,1280]{2,1,0:T(8,128)(2,1)S(1)} collective-permute-done((bf16[1,64,1280]{2,1,0:T(8,128)(2,1)S(1)}, bf16[1,64,1280]{2,1,0:T(8,128)(2,1)S(1)}, u32[]{:S(2)}, u32[]{:S(2)}) %collective-permute-start.2) | collective-permute-done | bytes 163872 | tf_op jit(solution)/shard_map/ppermute | solution.py:196
  22.3 1.4 %collective-permute-start.3 = (bf16[1,64,1280]{2,1,0:T(8,128)(2,1)S(1)}, bf16[1,64,1280]{2,1,0:T(8,128)(2,1)S(1)}, u32[]{:S(2)}, u32[]{:S(2)}) collective-permute-start(bf16[1,64,1280]{2,1,0:T(8,128)(2,1)S(1)} %collective-permute-done.2.refs_0_), channel_id=1, source_target_pairs={{0,2},{1,3},{2,0},{3,1},{4,6},{5,7},{6,4},{7,5},{8,10},{9,11},{10,... | collective-permute-start | bytes 491528 | tf_op jit(solution)/shard_map/ppermute | solution.py:196
  23.7 0.5 collective-permute-done.7.refs_1_
  24.1 0.0 collective-permute-done.other_ref
  24.1 0.0 copy-done.2
  24.1 3.7 %pair_terms.3.refs_4_ = f32[8,1,128]{2,1,0:T(1,128)S(1)} custom-call(s32[4,16]{1,0:T(4,128)S(1)} %bitcast.2, bf16[2048,512]{1,0:T(8,128)(2,1)S(1)} %screen_block.1.own_ref, bf16[2048,512]{1,0:T(8,128)(2,1)S(1)} %collective-permute-done.other_ref, bf16[1,64,1280]{2,1,0:T(8,128)(2,1)S(1)} %copy-done.1, bf16[1,64,1280]{2,1,0:T(8,128)(2,1)S(1)} %collective-permute-done.7.refs_1_), custom_call_target="tpu_custom_call" | custom-call | flops 1073741824 | bytes 4194304 | tf_op jit(solution)/shard_map/pair_terms/pallas_call | solution.py:146
  27.9 0.0 collective-permute-done.6.refs_3_
  27.9 3.3 %collective-permute-done.5.refs_1_ = bf16[1,64,1280]{2,1,0:T(8,128)(2,1)S(1)} collective-permute-done((bf16[1,64,1280]{2,1,0:T(8,128)(2,1)S(1)}, bf16[1,64,1280]{2,1,0:T(8,128)(2,1)S(1)}, u32[]{:S(2)}, u32[]{:S(2)}) %collective-permute-start.5) | collective-permute-done | bytes 163872 | tf_op jit(solution)/shard_map/ppermute | solution.py:196
  31.2 3.8 %pair_terms.4.refs_2_ = f32[8,1,128]{2,1,0:T(1,128)S(1)} custom-call(s32[4,16]{1,0:T(4,128)S(1)} %bitcast.3, bf16[2048,512]{1,0:T(8,128)(2,1)S(1)} %screen_block.1.own_ref, bf16[2048,512]{1,0:T(8,128)(2,1)S(1)} %collective-permute-done.other_ref, bf16[1,64,1280]{2,1,0:T(8,128)(2,1)S(1)} %collective-permute-done.4.refs_0_, ...), custom_call_target="tpu_custom_call" | custom-call | flops 2147483648 | bytes 4194304 | tf_op jit(solution)/shard_map/pair_terms/pallas_call | solution.py:146
  34.9 0.0 collective-permute-done.3.refs_1_
  34.9 3.8 %pair_terms.5 = f32[8,1,128]{2,1,0:T(1,128)S(1)} custom-call(s32[4,16]{1,0:T(4,128)S(1)} %bitcast.4, bf16[2048,512]{1,0:T(8,128)(2,1)S(1)} %screen_block.1.own_ref, bf16[2048,512]{1,0:T(8,128)(2,1)S(1)} %collective-permute-done.other_ref, bf16[1,64,1280]{2,1,0:T(8,128)(2,1)S(1)} %collective-permute-done.2.refs_0_, ...), custom_call_target="tpu_custom_call" | custom-call | flops 1073741824 | bytes 4194304 | tf_op jit(solution)/shard_map/pair_terms/pallas_call | solution.py:146
  38.7 11.8 %all_to_all.5.rows_ref = f32[8,1,128]{2,1,0:T(1,128)} all-to-all(f32[8,1,128]{2,1,0:T(1,128)S(1)} %pair_terms.5), channel_id=1, replica_groups={{0,2,4,6,8,10,12,14},{1,3,5,7,9,11,13,15},{16,18,20,22,24,26,28,30},{17..., dimensions={0} | all-to-all | bytes 8192 | tf_op jit(solution)/shard_map/all_to_all | solution.py:213
  50.5 1.3 %finish.1 = (f32[1,512]{1,0:T(1,128)}, f32[1,1]{1,0:T(1,128)}) custom-call(f32[8,1,128]{2,1,0:T(1,128)} %all_to_all.5.rows_ref), custom_call_target="tpu_custom_call" | custom-call | tf_op jit(solution)/shard_map/finish/pallas_call | solution.py:172
Async XLA Ops:
  0.6 1.6 %copy-start = (bf16[1,4,32,64,128]{4,3,2,1,0:T(8,128)(2,1)S(1)}, bf16[1,4,32,64,128]{4,3,2,1,0:T(8,128)(2,1)}, u32[]{:S(2)}) copy-start(bf16[1,4,32,64,128]{4,3,2,1,0:T(8,128)(2,1)} %chol_ref.1) | copy-start | bytes 6291460
  2.2 0.7 %copy-start.3 = (s32[1,4]{1,0:T(1,128)S(1)}, s32[1,4]{1,0:T(1,128)}, u32[]{:S(2)}) copy-start(s32[1,4]{1,0:T(1,128)} %screen_ref.1) | copy-start | bytes 52
  2.9 1.4 %copy-start.1 = (bf16[1,64,1280]{2,1,0:T(8,128)(2,1)S(1)}, bf16[1,64,1280]{2,1,0:T(8,128)(2,1)}, u32[]{:S(2)}) copy-start(bf16[1,64,1280]{2,1,0:T(8,128)(2,1)} %refs_0_.1) | copy-start | bytes 491524
  2.9 21.3 %copy-start.2 = (s32[16,4]{0,1:T(4,128)S(1)}, s32[16,4]{0,1:T(4,128)}, u32[]{:S(2)}) copy-start(s32[16,4]{0,1:T(4,128)} %param.7) | copy-start | bytes 772
  3.8 20.3 %collective-permute-start = (bf16[2048,512]{1,0:T(8,128)(2,1)S(1)}, bf16[2048,512]{1,0:T(8,128)(2,1)S(1)}, u32[]{:S(2)}, u32[]{:S(2)}) collective-permute-start(bf16[2048,512]{1,0:T(8,128)(2,1)S(1)} %screen_block.1.own_ref), channel_id=1, source_target_pairs={{0,1},{1,0},{2,3},{3,2},{4,5},{5,4},{6,7},{7,6},{8,9},{9,8},{10,11... | collective-permute-start | bytes 6291464 | tf_op jit(solution)/shard_map/ppermute | solution.py:196
  4.3 12.1 %collective-permute-start.1 = (bf16[1,64,1280]{2,1,0:T(8,128)(2,1)S(1)}, bf16[1,64,1280]{2,1,0:T(8,128)(2,1)S(1)}, u32[]{:S(2)}, u32[]{:S(2)}) collective-permute-start(bf16[1,64,1280]{2,1,0:T(8,128)(2,1)S(1)} %copy-done.1), channel_id=1, source_target_pairs={{0,8},{1,9},{2,10},{3,11},{4,12},{5,13},{6,14},{7,15},{8,0},{9,1},... | collective-permute-start | bytes 491528 | tf_op jit(solution)/shard_map/ppermute | solution.py:196
  8.0 11.1 %collective-permute-start.4 = (bf16[1,64,1280]{2,1,0:T(8,128)(2,1)S(1)}, bf16[1,64,1280]{2,1,0:T(8,128)(2,1)S(1)}, u32[]{:S(2)}, u32[]{:S(2)}) collective-permute-start(bf16[1,64,1280]{2,1,0:T(8,128)(2,1)S(1)} %copy-done.1), channel_id=1, source_target_pairs={{0,4},{1,5},{2,6},{3,7},{4,0},{5,1},{6,2},{7,3},{8,12},{9,13},{10,... | collective-permute-start | bytes 491528 | tf_op jit(solution)/shard_map/ppermute | solution.py:196
  16.4 5.9 %collective-permute-start.2 = (bf16[1,64,1280]{2,1,0:T(8,128)(2,1)S(1)}, bf16[1,64,1280]{2,1,0:T(8,128)(2,1)S(1)}, u32[]{:S(2)}, u32[]{:S(2)}) collective-permute-start(bf16[1,64,1280]{2,1,0:T(8,128)(2,1)S(1)} %collective-permute-done.1.refs_2_), channel_id=1, source_target_pairs={{0,4},{1,5},{2,6},{3,7},{4,0},{5,1},{6,2},{7,3},{8,12},{9,13},{10,... | collective-permute-start | bytes 491528 | tf_op jit(solution)/shard_map/ppermute | solution.py:196
  17.0 7.1 %collective-permute-start.7 = (bf16[1,64,1280]{2,1,0:T(8,128)(2,1)S(1)}, bf16[1,64,1280]{2,1,0:T(8,128)(2,1)S(1)}, u32[]{:S(2)}, u32[]{:S(2)}) collective-permute-start(bf16[1,64,1280]{2,1,0:T(8,128)(2,1)S(1)} %copy-done.1), channel_id=1, source_target_pairs={{0,2},{1,3},{2,0},{3,1},{4,6},{5,7},{6,4},{7,5},{8,10},{9,11},{10,... | collective-permute-start | bytes 491528 | tf_op jit(solution)/shard_map/ppermute | solution.py:196
  18.6 9.3 %collective-permute-start.6 = (bf16[1,64,1280]{2,1,0:T(8,128)(2,1)S(1)}, bf16[1,64,1280]{2,1,0:T(8,128)(2,1)S(1)}, u32[]{:S(2)}, u32[]{:S(2)}) collective-permute-start(bf16[1,64,1280]{2,1,0:T(8,128)(2,1)S(1)} %collective-permute-done.1.refs_2_), channel_id=1, source_target_pairs={{0,2},{1,3},{2,0},{3,1},{4,6},{5,7},{6,4},{7,5},{8,10},{9,11},{10,... | collective-permute-start | bytes 491528 | tf_op jit(solution)/shard_map/ppermute | solution.py:196
  19.1 12.1 %collective-permute-start.5 = (bf16[1,64,1280]{2,1,0:T(8,128)(2,1)S(1)}, bf16[1,64,1280]{2,1,0:T(8,128)(2,1)S(1)}, u32[]{:S(2)}, u32[]{:S(2)}) collective-permute-start(bf16[1,64,1280]{2,1,0:T(8,128)(2,1)S(1)} %collective-permute-done.4.refs_0_), channel_id=1, source_target_pairs={{0,2},{1,3},{2,0},{3,1},{4,6},{5,7},{6,4},{7,5},{8,10},{9,11},{10,... | collective-permute-start | bytes 491528 | tf_op jit(solution)/shard_map/ppermute | solution.py:196
  22.3 12.7 %collective-permute-start.3 = (bf16[1,64,1280]{2,1,0:T(8,128)(2,1)S(1)}, bf16[1,64,1280]{2,1,0:T(8,128)(2,1)S(1)}, u32[]{:S(2)}, u32[]{:S(2)}) collective-permute-start(bf16[1,64,1280]{2,1,0:T(8,128)(2,1)S(1)} %collective-permute-done.2.refs_0_), channel_id=1, source_target_pairs={{0,2},{1,3},{2,0},{3,1},{4,6},{5,7},{6,4},{7,5},{8,10},{9,11},{10,... | collective-permute-start | bytes 491528 | tf_op jit(solution)/shard_map/ppermute | solution.py:196

commit v5 on v3

v5 whole, which is shorter than its diff:
```python
import functools

import jax
import jax.numpy as jnp
from jax import lax
from jax.experimental import pallas as pl
from jax.experimental.pallas import tpu as pltpu
from jax.sharding import PartitionSpec as P

LANES = 128
VMEM_LIMIT = 32 * 1024 * 1024
K_STEP = 8
BATCH = 8
VMEM = pl.BlockSpec(memory_space=pltpu.VMEM)
SMEM = pl.BlockSpec(memory_space=pltpu.SMEM)
ANY = pl.BlockSpec(memory_space=pl.ANY)
PARAMS = pltpu.CompilerParams(vmem_limit_bytes=VMEM_LIMIT)
NT = (((1,), (1,)), ((), ()))
NN = (((1,), (0,)), ((), ()))


def split_axis(groups):
    outer = 1
    while outer * outer * 4 <= groups:
        outer *= 2
    return outer, groups // outer


def prepare_kernel(screen_ref, chol_ref, block_ref, turned_ref):
    _, listed, vectors, occupied, width = chol_ref.shape
    for m in range(listed):
        keep = jnp.full((1, width), screen_ref[0, m].astype(jnp.float32)).astype(chol_ref.dtype)
        tile = chol_ref[0, m].reshape(vectors * occupied, width) * keep
        block_ref[:, m * width:(m + 1) * width] = tile
        turned_ref[m * width:(m + 1) * width, :] = tile.T


def prepare_block(screen, chol_tiles):
    _, listed, vectors, occupied, width = chol_tiles.shape
    rows, depth = vectors * occupied, listed * width
    return pl.pallas_call(
        prepare_kernel,
        in_specs=[SMEM, VMEM],
        out_specs=[VMEM, VMEM],
        out_shape=[
            jax.ShapeDtypeStruct((rows, depth), chol_tiles.dtype),
            jax.ShapeDtypeStruct((depth, rows), chol_tiles.dtype),
        ],
        compiler_params=PARAMS,
        cost_estimate=pl.CostEstimate(flops=0, bytes_accessed=6 * chol_tiles.size, transcendentals=0),
        name="prepare_block",
    )(screen, chol_tiles)


def pick_kernel(list_ref, *refs, count, inner):
    theta_refs, out_refs = refs[:count], refs[count:]
    listed = list_ref.shape[0]
    width = out_refs[0].shape[2] // listed
    me = lax.axis_index("chol")
    for t, out_ref in enumerate(out_refs):
        group = (me // inner) * inner + (lax.rem(me, inner) ^ t)
        for m in range(listed):
            start = pl.multiple_of(list_ref[m, group] * width, width)
            for i, theta_ref in enumerate(theta_refs):
                out_ref[i, :, m * width:(m + 1) * width] = theta_ref[0, :, pl.ds(start, width)]


def pick_tiles(thetas, listing, width, inner):
    count = len(thetas)
    _, occupied, _ = thetas[0].shape
    listed = listing.shape[0]
    piece = jax.ShapeDtypeStruct((count, occupied, listed * width), thetas[0].dtype)
    return pl.pallas_call(
        functools.partial(pick_kernel, count=count, inner=inner),
        in_specs=[SMEM] + [VMEM] * count,
        out_specs=[VMEM] * inner,
        out_shape=[piece] * inner,
        compiler_params=PARAMS,
        cost_estimate=pl.CostEstimate(
            flops=0, bytes_accessed=4 * count * inner * occupied * listed * width, transcendentals=0
        ),
        name="pick_tiles",
    )(listing, *thetas)


def batch_terms(block_ref, turned_ref, theta, vectors, occupied):
    columns = theta.shape[0]
    walkers = columns // occupied
    tiles = columns // LANES

    lane = lax.broadcasted_iota(jnp.int32, (occupied, LANES), 1)
    low = lane < occupied
    sub8 = lax.broadcasted_iota(jnp.int32, (8, LANES), 0)
    lane8 = lax.broadcasted_iota(jnp.int32, (8, LANES), 1)
    strip = (lane8 % occupied) // 8
    on_diag = lane8 % 8 == sub8

    def diagonal(block):
        merged = block[:8]
        for r in range(1, occupied // 8):
            merged = jnp.where(strip == r, block[8 * r:8 * r + 8], merged)
        return jnp.where(on_diag, merged, 0.0)

    cross = [jnp.zeros((8, LANES), jnp.float32) for _ in range(tiles)]
    diagonals = []
    for k0 in range(0, vectors, K_STEP):
        span = slice(k0 * occupied, (k0 + K_STEP) * occupied)
        inner_mat = lax.dot_general(block_ref[span, :], theta, NT, preferred_element_type=jnp.float32)
        flipped = lax.dot_general(theta, turned_ref[:, span], NN, preferred_element_type=jnp.float32)
        for pair in range(K_STEP // 2):
            tops, bottoms = [], []
            r0 = pair * 2 * occupied
            for t in range(tiles):
                c0 = t * LANES
                top = inner_mat[r0:r0 + occupied, c0:c0 + LANES]
                bottom = inner_mat[r0 + occupied:r0 + 2 * occupied, c0:c0 + LANES]
                f_top = flipped[c0:c0 + occupied, r0:r0 + LANES]
                f_bottom = flipped[c0 + occupied:c0 + 2 * occupied, r0:r0 + LANES]
                swapped = pltpu.roll(jnp.where(low, f_bottom, f_top), occupied, 1)
                product = jnp.where(low, top, bottom) * jnp.where(low, f_top, f_bottom)
                product = product + jnp.where(low, bottom, top) * swapped
                cross[t] = cross[t] + jnp.sum(product.reshape(occupied // 8, 8, LANES), axis=0)
                tops.append(diagonal(top))
                bottoms.append(diagonal(bottom))
            diagonals.append(jnp.concatenate(tops, axis=1))
            diagonals.append(jnp.concatenate(bottoms, axis=1))
    diagonals.append(jnp.concatenate(cross, axis=1))
    stacked = jnp.concatenate(diagonals, axis=0).reshape(vectors + 1, 8, columns)
    rows = jnp.sum(stacked, axis=1)
    seg_row = lax.broadcasted_iota(jnp.int32, (8, columns), 0)
    seg_col = lax.broadcasted_iota(jnp.int32, (8, columns), 1)
    segment = jnp.where(seg_col // occupied == seg_row, 1.0, 0.0).astype(jnp.float32)
    sums = lax.dot_general(
        segment, rows, NT, precision=lax.Precision.HIGHEST, preferred_element_type=jnp.float32
    )[:walkers]
    bias = sums[:, :vectors]
    return bias, jnp.sum(bias * bias, axis=1, keepdims=True) - sums[:, vectors:vectors + 1]


def terms_kernel(block_ref, turned_ref, *refs, parts, inner, vectors, carried):
    piece_refs, rest = refs[:inner * len(parts)], refs[inner * len(parts):]
    out_ref, theta_ref = rest[-2], rest[-1]
    _, occupied, _ = piece_refs[0].shape
    me = lax.axis_index("chol")
    spot = lax.rem(me, inner)
    zone = me // inner
    shifts = [s for part in parts for s in part]
    walkers = len(shifts) * inner

    row = 0
    for p, part in enumerate(parts):
        for i in range(len(part)):
            for ref in piece_refs[p * inner:(p + 1) * inner]:
                theta_ref[row:row + occupied, :] = ref[i]
                row += occupied
    if carried:
        out_ref[...] = rest[0][...]
    else:
        out_ref[...] = jnp.zeros(out_ref.shape, out_ref.dtype)

    def one_batch(first, count):
        start = first * occupied
        rows = pl.ds(start if isinstance(first, int) else pl.multiple_of(start, count * occupied), count * occupied)
        bias, energy = batch_terms(block_ref, turned_ref, theta_ref[rows, :], vectors, occupied)
        for j in range(count):
            index = first + j
            owner = (zone ^ (shifts[0] + index // inner)) * inner + (spot ^ lax.rem(index, inner))
            out_ref[pl.ds(owner, 1), 0, :vectors] = bias[j:j + 1]
            out_ref[pl.ds(owner, 1), 0, vectors:vectors + 1] = energy[j:j + 1]

    if walkers <= BATCH:
        one_batch(0, walkers)
    else:
        @pl.loop(0, walkers // BATCH)
        def _(step):
            one_batch(step * BATCH, BATCH)


def block_terms(block, turned, pieces, carried, parts, vectors, groups, out_width):
    inner = len(pieces[0])
    count = sum(len(part) for part in parts)
    _, occupied, depth = pieces[0][0].shape
    operands = [block, turned] + [p for part in pieces for p in part] + ([] if carried is None else [carried])
    return pl.pallas_call(
        functools.partial(
            terms_kernel, parts=parts, inner=inner, vectors=vectors, carried=carried is not None
        ),
        in_specs=[VMEM] * len(operands),
        out_specs=VMEM,
        out_shape=jax.ShapeDtypeStruct((groups, 1, out_width), jnp.float32),
        scratch_shapes=[pltpu.VMEM((count * inner * occupied, depth), block.dtype)],
        compiler_params=PARAMS,
        cost_estimate=pl.CostEstimate(
            flops=4 * count * inner * vectors * occupied * occupied * depth,
            bytes_accessed=4 * block.size,
            transcendentals=0,
        ),
        name="block_terms",
    )(*operands)


def finish_kernel(rows_ref, bias_ref, energy_ref, bias_buf, energy_buf, sems, *, vectors, scale):
    groups = rows_ref.shape[0]
    total = jnp.sum(rows_ref[:, 0, :], axis=0, keepdims=True)
    energy_buf[...] = total[:, vectors:vectors + 1] * scale
    energy_copy = pltpu.make_async_copy(energy_buf, energy_ref, sems.at[1])
    energy_copy.start()
    for d in range(groups):
        bias_buf[:, d * vectors:(d + 1) * vectors] = rows_ref[d, :, :vectors]
    bias_copy = pltpu.make_async_copy(bias_buf, bias_ref, sems.at[0])
    bias_copy.start()
    energy_copy.wait()
    bias_copy.wait()


def finish(rows, vectors, scale):
    groups = rows.shape[0]
    shapes = [(1, groups * vectors), (1, 1)]
    force_bias, energy = pl.pallas_call(
        functools.partial(finish_kernel, vectors=vectors, scale=scale),
        in_specs=[VMEM],
        out_specs=[ANY, ANY],
        out_shape=[jax.ShapeDtypeStruct(s, jnp.float32) for s in shapes],
        scratch_shapes=[pltpu.VMEM(s, jnp.float32) for s in shapes] + [pltpu.SemaphoreType.DMA((2,))],
        name="finish",
    )(rows)
    return force_bias, energy.reshape(1)


def body(theta, chol_tiles, screen, tile_list):
    groups = lax.axis_size("chol")
    outer, inner = split_axis(groups)
    _, occupied, _ = theta.shape
    width = chol_tiles.shape[-1]
    vectors = chol_tiles.shape[2]
    out_width = LANES * ((vectors + 1 + LANES - 1) // LANES)
    listing = tile_list.T

    def partners(zone_flip, spot_flip):
        return [(i, ((i // inner) ^ zone_flip) * inner + ((i % inner) ^ spot_flip)) for i in range(groups)]

    def flipped(x, zone_flip, spot_flip=0):
        return lax.ppermute(x, "chol", partners(zone_flip, spot_flip))

    held = [theta] + [None] * (outer - 1)
    bit = outer // 2
    while bit:
        for s in range(0, outer, 2 * bit):
            held[s + bit] = flipped(held[s], bit)
        bit //= 2
    block, turned = prepare_block(screen, chol_tiles)

    def neighbourhood(shifts):
        picked = pick_tiles([held[s] for s in shifts], listing, width, inner)
        return [picked[0]] + [flipped(picked[t], 0, t) for t in range(1, inner)]

    rows = None
    for parts in ([[0, 1]], [list(range(2, outer - 1)), [outer - 1]]):
        pieces = [neighbourhood(shifts) for shifts in parts]
        rows = block_terms(block, turned, pieces, rows, parts, vectors, groups, out_width)
    back = lax.all_to_all(rows, "chol", split_axis=0, concat_axis=0, tiled=True)
    return finish(back, vectors, 1.0 / (2.0 * occupied * occupied))


def solution(mesh):
    in_specs = (
        P(("grp", "chol"), None, None),
        P("chol", None, None, None, None),
        P("chol", None),
        P(),
    )
    out_specs = (P(("grp", "chol"), None), P(("grp", "chol")))
    return jax.shard_map(body, mesh=mesh, in_specs=in_specs, out_specs=out_specs, check_vma=False)
```

time: 45.6 us -> 46.8 us (1.026)
  starting transfers between devices: 9.56 us -> 12.5 us
  blocking collectives: 12.3 us -> 10.8 us
  waiting for transfers between devices: 8.94 us -> 8.35 us
    ppermute x9 -> x12, starting transfers between devices: 9.56 us -> 12.5 us  [flipped(): return lax.ppermute(x, 'chol', partners(zone_flip, spot_flip))]
    all_to_all x1, blocking collectives: 12.3 us -> 10.8 us  [body(): back = lax.all_to_all(rows, 'chol', split_axis=0, concat_axis=0, tiled=True)]
    pallas_call x2 -> x3, Pallas kernels: 1.38 us -> 1.99 us  [pick_tiles(): pl.pallas_call(functools.partial(pick_kernel, count=count, inner=inner),...]
    ppermute x9 -> x12, waiting for transfers between devices: 8.94 us -> 8.35 us  [flipped(): return lax.ppermute(x, 'chol', partners(zone_flip, spot_flip))]
    pallas_call x2 -> x3, Pallas kernels: 7.24 us -> 6.88 us  [the longest x2 5.59 us: block_terms(): pl.pallas_call(functools.partial(terms_kernel, parts=parts, inner=inner,...]
    unnamed x8 -> x10, local copies, waits for them, and re-layouts: 3.84 us -> 3.84 us
  transfers between devices with their start and end apart: 9 -> 12, of which waited for: 3 -> 3; matrix products, arithmetic and copies ran while one was open for 0% -> 0% of each run, Pallas kernels for 11% -> 13%
where the time goes in v5:
time: 46.8 us; the launch traced here: 46.5 us
  starting transfers between devices  12.5 us (27%)
  blocking collectives  10.8 us (23%)
  Pallas kernels  10.2 us (22%)
  waiting for transfers between devices  8.35 us (18%)
  local copies, waits for them, and re-layouts  3.84 us (8%)
  between operations  0.73 us (2%)
    ppermute x12, starting transfers between devices, flipped(): return lax.ppermute(x, 'chol', partners(zone_flip, spot_flip))  12.5 us
    all_to_all x1, blocking collectives, body(): back = lax.all_to_all(rows, 'chol', split_axis=0, concat_axis=0, tiled=True)  10.8 us
    ppermute x12, waiting for transfers between devices, flipped(): return lax.ppermute(x, 'chol', partners(zone_flip, spot_flip))  8.35 us
    pallas_call x2, Pallas kernels, block_terms(): pl.pallas_call(functools.partial(terms_kernel, parts=parts, inner=inner,...  5.59 us
    unnamed x10, local copies, waits for them, and re-layouts  3.84 us
    pallas_call x3, Pallas kernels, pick_tiles(): pl.pallas_call(functools.partial(pick_kernel, count=count, inner=inner),...  1.99 us
    pallas_call x1, Pallas kernels, finish(): pl.pallas_call(functools.partial(finish_kernel, vectors=vectors, scale=sc...  1.38 us
    pallas_call x1, Pallas kernels, prepare_block(): pl.pallas_call(prepare_kernel, in_specs=[SMEM, VMEM], out_specs=[VMEM, VM...  1.29 us
  transfers between devices with their start and end apart: 12, of which 3 were waited for; matrix products, arithmetic and copies ran while one was open for 0% of the time, Pallas kernels for 13%

profile of v5, /device:TPU:0, one launch (start us, length us, event | category | flops | bytes accessed | tf_op | source)
XLA Modules:
  0.0 46.5 jit_solution(7682382591014255111)
XLA Ops:
  0.6 4.1 %collective-permute-start = (bf16[1,64,1280]{2,1,0:T(8,128)(2,1)}, bf16[1,64,1280]{2,1,0:T(8,128)(2,1)S(1)}, u32[]{:S(2)}, u32[]{:S(2)}) collective-permute-start(bf16[1,64,1280]{2,1,0:T(8,128)(2,1)} %refs_0_.1), channel_id=1, source_target_pairs={{0,8},{1,9},{2,10},{3,11},{4,12},{5,13},{6,14},{7,15},{8,0},{9,1},... | collective-permute-start | bytes 491528 | tf_op jit(solution)/shard_map/ppermute | solution.py:243
  4.7 1.6 %collective-permute-start.8 = (bf16[1,64,1280]{2,1,0:T(8,128)(2,1)}, bf16[1,64,1280]{2,1,0:T(8,128)(2,1)S(1)}, u32[]{:S(2)}, u32[]{:S(2)}) collective-permute-start(bf16[1,64,1280]{2,1,0:T(8,128)(2,1)} %refs_0_.1), channel_id=1, source_target_pairs={{0,4},{1,5},{2,6},{3,7},{4,0},{5,1},{6,2},{7,3},{8,12},{9,13},{10,... | collective-permute-start | bytes 491528 | tf_op jit(solution)/shard_map/ppermute | solution.py:243
  6.3 6.4 %collective-permute-done.refs_0_ = bf16[1,64,1280]{2,1,0:T(8,128)(2,1)S(1)} collective-permute-done((bf16[1,64,1280]{2,1,0:T(8,128)(2,1)}, bf16[1,64,1280]{2,1,0:T(8,128)(2,1)S(1)}, u32[]{:S(2)}, u32[]{:S(2)}) %collective-permute-start) | collective-permute-done | bytes 163872 | tf_op jit(solution)/shard_map/ppermute | solution.py:243
  12.8 0.7 %collective-permute-start.4 = (bf16[1,64,1280]{2,1,0:T(8,128)(2,1)S(1)}, bf16[1,64,1280]{2,1,0:T(8,128)(2,1)S(1)}, u32[]{:S(2)}, u32[]{:S(2)}) collective-permute-start(bf16[1,64,1280]{2,1,0:T(8,128)(2,1)S(1)} %collective-permute-done.refs_0_), channel_id=1, source_target_pairs={{0,4},{1,5},{2,6},{3,7},{4,0},{5,1},{6,2},{7,3},{8,12},{9,13},{10,... | collective-permute-start | bytes 491528 | tf_op jit(solution)/shard_map/ppermute | solution.py:243
  13.5 0.0 collective-permute-done.8.refs_1_
  13.5 0.9 %copy-done.1 = bf16[1,64,1280]{2,1,0:T(8,128)(2,1)S(1)} copy-done((bf16[1,64,1280]{2,1,0:T(8,128)(2,1)S(1)}, bf16[1,64,1280]{2,1,0:T(8,128)(2,1)}, u32[]{:S(2)}) %copy-start.1) | copy-done | bytes 163864
  14.4 0.7 %copy-done.2 = s32[16,4]{0,1:T(4,128)S(1)} copy-done((s32[16,4]{0,1:T(4,128)S(1)}, s32[16,4]{0,1:T(4,128)}, u32[]{:S(2)}) %copy-start.2) | copy-done | bytes 280
  15.1 0.7 %pick_tiles.5 = (bf16[2,64,512]{2,1,0:T(8,128)(2,1)S(1)}, bf16[2,64,512]{2,1,0:T(8,128)(2,1)S(1)}, bf16[2,64,512]{2,1,0:T(8,128)(2,1)S(1)}, bf16[2,64,512]{2,1,0:T(8,128)(2,1)S(1)}) custom-call(s32[4,16]{1,0:T(4,128)S(1)} %bitcast.2, bf16[1,64,1280]{2,1,0:T(8,128)(2,1)S(1)} %copy-done.1, bf16[1,64,1280]{2,1,0:T(8,128)(2,1)S(1)} %collective-permute-done.8.refs_1_), custom_call_target="tpu_custom_call" | custom-call | bytes 1048576 | tf_op jit(solution)/shard_map/pick_tiles/pallas_call | solution.py:73
  15.8 1.6 %collective-permute-start.10 = (bf16[2,64,512]{2,1,0:T(8,128)(2,1)S(1)}, bf16[2,64,512]{2,1,0:T(8,128)(2,1)S(1)}, u32[]{:S(2)}, u32[]{:S(2)}) collective-permute-start(bf16[2,64,512]{2,1,0:T(8,128)(2,1)S(1)} %get-tuple-element.30), channel_id=1, source_target_pairs={{0,2},{1,3},{2,0},{3,1},{4,6},{5,7},{6,4},{7,5},{8,10},{9,11},{10,... | collective-permute-start | bytes 393224 | tf_op jit(solution)/shard_map/ppermute | solution.py:243
  17.4 0.0 collective-permute-start.11
  17.4 0.6 %collective-permute-start.9 = (bf16[2,64,512]{2,1,0:T(8,128)(2,1)S(1)}, bf16[2,64,512]{2,1,0:T(8,128)(2,1)S(1)}, u32[]{:S(2)}, u32[]{:S(2)}) collective-permute-start(bf16[2,64,512]{2,1,0:T(8,128)(2,1)S(1)} %get-tuple-element.29), channel_id=1, source_target_pairs={{0,1},{1,0},{2,3},{3,2},{4,5},{5,4},{6,7},{7,6},{8,9},{9,8},{10,11... | collective-permute-start | bytes 393224 | tf_op jit(solution)/shard_map/ppermute | solution.py:243
  18.0 0.6 %pick_tiles.3 = (bf16[1,64,512]{2,1,0:T(8,128)(2,1)S(1)}, bf16[1,64,512]{2,1,0:T(8,128)(2,1)S(1)}, bf16[1,64,512]{2,1,0:T(8,128)(2,1)S(1)}, bf16[1,64,512]{2,1,0:T(8,128)(2,1)S(1)}) custom-call(s32[4,16]{1,0:T(4,128)S(1)} %bitcast.3, bf16[1,64,1280]{2,1,0:T(8,128)(2,1)S(1)} %collective-permute-done.refs_0_), custom_call_target="tpu_custom_call" | custom-call | bytes 524288 | tf_op jit(solution)/shard_map/pick_tiles/pallas_call | solution.py:73
  18.7 0.1 collective-permute-start.1
  18.7 0.0 copy-start
  18.7 1.6 %copy-done = bf16[1,4,32,64,128]{4,3,2,1,0:T(8,128)(2,1)S(1)} copy-done((bf16[1,4,32,64,128]{4,3,2,1,0:T(8,128)(2,1)S(1)}, bf16[1,4,32,64,128]{4,3,2,1,0:T(8,128)(2,1)}, u32[]{:S(2)}) %copy-start) | copy-done | bytes 2097176
  20.3 0.7 %copy-done.4 = s32[1,4]{1,0:T(1,128)S(1)} copy-done((s32[1,4]{1,0:T(1,128)S(1)}, s32[1,4]{1,0:T(1,128)}, u32[]{:S(2)}) %copy-start.4) | copy-done | bytes 40
  21.0 1.3 %prepare_block.1 = (bf16[2048,512]{1,0:T(8,128)(2,1)S(1)}, bf16[512,2048]{1,0:T(8,128)(2,1)S(1)}) custom-call(s32[1,4]{1,0:T(1,128)S(1)} %copy-done.4, bf16[1,4,32,64,128]{4,3,2,1,0:T(8,128)(2,1)S(1)} %copy-done), custom_call_target="tpu_custom_call" | custom-call | bytes 6291456 | tf_op jit(solution)/shard_map/prepare_block/pallas_call | solution.py:41
  22.3 0.0 collective-permute-done.4.refs_0_
  22.3 1.6 %collective-permute-start.2 = (bf16[1,64,512]{2,1,0:T(8,128)(2,1)S(1)}, bf16[1,64,512]{2,1,0:T(8,128)(2,1)S(1)}, u32[]{:S(2)}, u32[]{:S(2)}) collective-permute-start(bf16[1,64,512]{2,1,0:T(8,128)(2,1)S(1)} %get-tuple-element.22), channel_id=1, source_target_pairs={{0,2},{1,3},{2,0},{3,1},{4,6},{5,7},{6,4},{7,5},{8,10},{9,11},{10,... | collective-permute-start | bytes 196616 | tf_op jit(solution)/shard_map/ppermute | solution.py:243
  23.9 0.7 %pick_tiles.4 = (bf16[1,64,512]{2,1,0:T(8,128)(2,1)S(1)}, bf16[1,64,512]{2,1,0:T(8,128)(2,1)S(1)}, bf16[1,64,512]{2,1,0:T(8,128)(2,1)S(1)}, bf16[1,64,512]{2,1,0:T(8,128)(2,1)S(1)}) custom-call(s32[4,16]{1,0:T(4,128)S(1)} %bitcast.4, bf16[1,64,1280]{2,1,0:T(8,128)(2,1)S(1)} %collective-permute-done.4.refs_0_), custom_call_target="tpu_custom_call" | custom-call | bytes 524288 | tf_op jit(solution)/shard_map/pick_tiles/pallas_call | solution.py:73
  24.5 0.0 collective-permute-done.1.refs_1_
  24.5 0.4 collective-permute-start.3
  24.9 0.3 collective-permute-start.5
  25.2 1.5 %collective-permute-start.6 = (bf16[1,64,512]{2,1,0:T(8,128)(2,1)S(1)}, bf16[1,64,512]{2,1,0:T(8,128)(2,1)S(1)}, u32[]{:S(2)}, u32[]{:S(2)}) collective-permute-start(bf16[1,64,512]{2,1,0:T(8,128)(2,1)S(1)} %get-tuple-element.26), channel_id=1, source_target_pairs={{0,2},{1,3},{2,0},{3,1},{4,6},{5,7},{6,4},{7,5},{8,10},{9,11},{10,... | collective-permute-start | bytes 196616 | tf_op jit(solution)/shard_map/ppermute | solution.py:243
  26.8 0.0 collective-permute-start.7
  26.8 2.8 %block_terms.2.refs_8_ = f32[16,1,128]{2,1,0:T(1,128)S(1)} custom-call(bf16[2048,512]{1,0:T(8,128)(2,1)S(1)} %get-tuple-element.18.block_ref, bf16[512,2048]{1,0:T(8,128)(2,1)S(1)} %get-tuple-element.19.turned_ref, bf16[2,64,512]{2,1,0:T(8,128)(2,1)S(1)} %get-tuple-element.28.refs_0_, bf16[2,64,512]{2,1,0:T(8,128)(2,1)S(1)} %collective-permute-done.9.refs_1_, ...), custom_call_target="tpu_custom_call" | custom-call | flops 2147483648 | bytes 4194304 | tf_op jit(solution)/shard_map/block_terms/pallas_call | solution.py:184
  29.6 0.0 collective-permute-done.2.refs_2_
  29.6 1.1 %collective-permute-done.6.refs_6_ = bf16[1,64,512]{2,1,0:T(8,128)(2,1)S(1)} collective-permute-done((bf16[1,64,512]{2,1,0:T(8,128)(2,1)S(1)}, bf16[1,64,512]{2,1,0:T(8,128)(2,1)S(1)}, u32[]{:S(2)}, u32[]{:S(2)}) %collective-permute-start.6) | collective-permute-done | bytes 65568 | tf_op jit(solution)/shard_map/ppermute | solution.py:243
  30.7 0.8 %collective-permute-done.7.refs_7_ = bf16[1,64,512]{2,1,0:T(8,128)(2,1)S(1)} collective-permute-done((bf16[1,64,512]{2,1,0:T(8,128)(2,1)S(1)}, bf16[1,64,512]{2,1,0:T(8,128)(2,1)S(1)}, u32[]{:S(2)}, u32[]{:S(2)}) %collective-permute-start.7) | collective-permute-done | bytes 65568 | tf_op jit(solution)/shard_map/ppermute | solution.py:243
  31.5 2.8 %block_terms.3 = f32[16,1,128]{2,1,0:T(1,128)S(1)} custom-call(bf16[2048,512]{1,0:T(8,128)(2,1)S(1)} %get-tuple-element.18.block_ref, bf16[512,2048]{1,0:T(8,128)(2,1)S(1)} %get-tuple-element.19.turned_ref, bf16[1,64,512]{2,1,0:T(8,128)(2,1)S(1)} %get-tuple-element.20.refs_0_, bf16[1,64,512]{2,1,0:T(8,128)(2,1)S(1)} %collective-permute-done.1.refs_1_, ...), custom_call_target="tpu_custom_call" | custom-call | flops 2147483648 | bytes 4194304 | tf_op jit(solution)/shard_map/block_terms/pallas_call | solution.py:184
  34.3 10.8 %all_to_all.5.rows_ref = f32[16,1,128]{2,1,0:T(1,128)} all-to-all(f32[16,1,128]{2,1,0:T(1,128)S(1)} %block_terms.3), channel_id=1, replica_groups=mesh['grp'=2,'chol'=16] {'chol'}, dimensions={0} | all-to-all | bytes 16384 | tf_op jit(solution)/shard_map/all_to_all | solution.py:261
  45.1 1.4 %finish.1 = (f32[1,512]{1,0:T(1,128)}, f32[1,1]{1,0:T(1,128)}) custom-call(f32[16,1,128]{2,1,0:T(1,128)} %all_to_all.5.rows_ref), custom_call_target="tpu_custom_call" | custom-call | tf_op jit(solution)/shard_map/finish/pallas_call | solution.py:219
  (10 shorter events, 0.0 us)
Async XLA Ops:
  0.6 12.1 %collective-permute-start = (bf16[1,64,1280]{2,1,0:T(8,128)(2,1)}, bf16[1,64,1280]{2,1,0:T(8,128)(2,1)S(1)}, u32[]{:S(2)}, u32[]{:S(2)}) collective-permute-start(bf16[1,64,1280]{2,1,0:T(8,128)(2,1)} %refs_0_.1), channel_id=1, source_target_pairs={{0,8},{1,9},{2,10},{3,11},{4,12},{5,13},{6,14},{7,15},{8,0},{9,1},... | collective-permute-start | bytes 491528 | tf_op jit(solution)/shard_map/ppermute | solution.py:243
  4.7 8.8 %collective-permute-start.8 = (bf16[1,64,1280]{2,1,0:T(8,128)(2,1)}, bf16[1,64,1280]{2,1,0:T(8,128)(2,1)S(1)}, u32[]{:S(2)}, u32[]{:S(2)}) collective-permute-start(bf16[1,64,1280]{2,1,0:T(8,128)(2,1)} %refs_0_.1), channel_id=1, source_target_pairs={{0,4},{1,5},{2,6},{3,7},{4,0},{5,1},{6,2},{7,3},{8,12},{9,13},{10,... | collective-permute-start | bytes 491528 | tf_op jit(solution)/shard_map/ppermute | solution.py:243
  12.8 9.5 %collective-permute-start.4 = (bf16[1,64,1280]{2,1,0:T(8,128)(2,1)S(1)}, bf16[1,64,1280]{2,1,0:T(8,128)(2,1)S(1)}, u32[]{:S(2)}, u32[]{:S(2)}) collective-permute-start(bf16[1,64,1280]{2,1,0:T(8,128)(2,1)S(1)} %collective-permute-done.refs_0_), channel_id=1, source_target_pairs={{0,4},{1,5},{2,6},{3,7},{4,0},{5,1},{6,2},{7,3},{8,12},{9,13},{10,... | collective-permute-start | bytes 491528 | tf_op jit(solution)/shard_map/ppermute | solution.py:243
  13.5 0.9 %copy-start.1 = (bf16[1,64,1280]{2,1,0:T(8,128)(2,1)S(1)}, bf16[1,64,1280]{2,1,0:T(8,128)(2,1)}, u32[]{:S(2)}) copy-start(bf16[1,64,1280]{2,1,0:T(8,128)(2,1)} %refs_0_.1) | copy-start | bytes 491524
  14.4 0.7 %copy-start.2 = (s32[16,4]{0,1:T(4,128)S(1)}, s32[16,4]{0,1:T(4,128)}, u32[]{:S(2)}) copy-start(s32[16,4]{0,1:T(4,128)} %param.7) | copy-start | bytes 772
  15.1 8.8 %copy-start.3 = (s32[16,4]{0,1:T(4,128)S(1)}, s32[16,4]{0,1:T(4,128)}, u32[]{:S(2)}) copy-start(s32[16,4]{0,1:T(4,128)} %param.7) | copy-start | bytes 772
  15.8 9.2 %collective-permute-start.10 = (bf16[2,64,512]{2,1,0:T(8,128)(2,1)S(1)}, bf16[2,64,512]{2,1,0:T(8,128)(2,1)S(1)}, u32[]{:S(2)}, u32[]{:S(2)}) collective-permute-start(bf16[2,64,512]{2,1,0:T(8,128)(2,1)S(1)} %get-tuple-element.30), channel_id=1, source_target_pairs={{0,2},{1,3},{2,0},{3,1},{4,6},{5,7},{6,4},{7,5},{8,10},{9,11},{10,... | collective-permute-start | bytes 393224 | tf_op jit(solution)/shard_map/ppermute | solution.py:243
  17.4 7.9 %collective-permute-start.11 = (bf16[2,64,512]{2,1,0:T(8,128)(2,1)S(1)}, bf16[2,64,512]{2,1,0:T(8,128)(2,1)S(1)}, u32[]{:S(2)}, u32[]{:S(2)}) collective-permute-start(bf16[2,64,512]{2,1,0:T(8,128)(2,1)S(1)} %get-tuple-element.31), channel_id=1, source_target_pairs={{0,3},{1,2},{2,1},{3,0},{4,7},{5,6},{6,5},{7,4},{8,11},{9,10},{10,... | collective-permute-start | bytes 393224 | tf_op jit(solution)/shard_map/ppermute | solution.py:243
  17.4 9.4 %collective-permute-start.9 = (bf16[2,64,512]{2,1,0:T(8,128)(2,1)S(1)}, bf16[2,64,512]{2,1,0:T(8,128)(2,1)S(1)}, u32[]{:S(2)}, u32[]{:S(2)}) collective-permute-start(bf16[2,64,512]{2,1,0:T(8,128)(2,1)S(1)} %get-tuple-element.29), channel_id=1, source_target_pairs={{0,1},{1,0},{2,3},{3,2},{4,5},{5,4},{6,7},{7,6},{8,9},{9,8},{10,11... | collective-permute-start | bytes 393224 | tf_op jit(solution)/shard_map/ppermute | solution.py:243
  18.7 5.9 %collective-permute-start.1 = (bf16[1,64,512]{2,1,0:T(8,128)(2,1)S(1)}, bf16[1,64,512]{2,1,0:T(8,128)(2,1)S(1)}, u32[]{:S(2)}, u32[]{:S(2)}) collective-permute-start(bf16[1,64,512]{2,1,0:T(8,128)(2,1)S(1)} %get-tuple-element.21), channel_id=1, source_target_pairs={{0,1},{1,0},{2,3},{3,2},{4,5},{5,4},{6,7},{7,6},{8,9},{9,8},{10,11... | collective-permute-start | bytes 196616 | tf_op jit(solution)/shard_map/ppermute | solution.py:243
  18.7 1.6 %copy-start = (bf16[1,4,32,64,128]{4,3,2,1,0:T(8,128)(2,1)S(1)}, bf16[1,4,32,64,128]{4,3,2,1,0:T(8,128)(2,1)}, u32[]{:S(2)}) copy-start(bf16[1,4,32,64,128]{4,3,2,1,0:T(8,128)(2,1)} %chol_ref.1) | copy-start | bytes 6291460
  20.3 0.7 %copy-start.4 = (s32[1,4]{1,0:T(1,128)S(1)}, s32[1,4]{1,0:T(1,128)}, u32[]{:S(2)}) copy-start(s32[1,4]{1,0:T(1,128)} %screen_ref.1) | copy-start | bytes 52
  22.3 7.3 %collective-permute-start.2 = (bf16[1,64,512]{2,1,0:T(8,128)(2,1)S(1)}, bf16[1,64,512]{2,1,0:T(8,128)(2,1)S(1)}, u32[]{:S(2)}, u32[]{:S(2)}) collective-permute-start(bf16[1,64,512]{2,1,0:T(8,128)(2,1)S(1)} %get-tuple-element.22), channel_id=1, source_target_pairs={{0,2},{1,3},{2,0},{3,1},{4,6},{5,7},{6,4},{7,5},{8,10},{9,11},{10,... | collective-permute-start | bytes 196616 | tf_op jit(solution)/shard_map/ppermute | solution.py:243
  24.5 5.1 %collective-permute-start.3 = (bf16[1,64,512]{2,1,0:T(8,128)(2,1)S(1)}, bf16[1,64,512]{2,1,0:T(8,128)(2,1)S(1)}, u32[]{:S(2)}, u32[]{:S(2)}) collective-permute-start(bf16[1,64,512]{2,1,0:T(8,128)(2,1)S(1)} %get-tuple-element.23), channel_id=1, source_target_pairs={{0,3},{1,2},{2,1},{3,0},{4,7},{5,6},{6,5},{7,4},{8,11},{9,10},{10,... | collective-permute-start | bytes 196616 | tf_op jit(solution)/shard_map/ppermute | solution.py:243
  24.9 4.7 %collective-permute-start.5 = (bf16[1,64,512]{2,1,0:T(8,128)(2,1)S(1)}, bf16[1,64,512]{2,1,0:T(8,128)(2,1)S(1)}, u32[]{:S(2)}, u32[]{:S(2)}) collective-permute-start(bf16[1,64,512]{2,1,0:T(8,128)(2,1)S(1)} %get-tuple-element.25), channel_id=1, source_target_pairs={{0,1},{1,0},{2,3},{3,2},{4,5},{5,4},{6,7},{7,6},{8,9},{9,8},{10,11... | collective-permute-start | bytes 196616 | tf_op jit(solution)/shard_map/ppermute | solution.py:243
  25.2 5.5 %collective-permute-start.6 = (bf16[1,64,512]{2,1,0:T(8,128)(2,1)S(1)}, bf16[1,64,512]{2,1,0:T(8,128)(2,1)S(1)}, u32[]{:S(2)}, u32[]{:S(2)}) collective-permute-start(bf16[1,64,512]{2,1,0:T(8,128)(2,1)S(1)} %get-tuple-element.26), channel_id=1, source_target_pairs={{0,2},{1,3},{2,0},{3,1},{4,6},{5,7},{6,4},{7,5},{8,10},{9,11},{10,... | collective-permute-start | bytes 196616 | tf_op jit(solution)/shard_map/ppermute | solution.py:243
  26.8 4.7 %collective-permute-start.7 = (bf16[1,64,512]{2,1,0:T(8,128)(2,1)S(1)}, bf16[1,64,512]{2,1,0:T(8,128)(2,1)S(1)}, u32[]{:S(2)}, u32[]{:S(2)}) collective-permute-start(bf16[1,64,512]{2,1,0:T(8,128)(2,1)S(1)} %get-tuple-element.27), channel_id=1, source_target_pairs={{0,3},{1,2},{2,1},{3,0},{4,7},{5,6},{6,5},{7,4},{8,11},{9,10},{10,... | collective-permute-start | bytes 196616 | tf_op jit(solution)/shard_map/ppermute | solution.py:243

commit v6 on v4

v6 whole, which is shorter than its diff:
```python
import functools

import jax
import jax.numpy as jnp
from jax import lax
from jax.experimental import pallas as pl
from jax.experimental.pallas import tpu as pltpu
from jax.sharding import PartitionSpec as P

LANES = 128
CORES = 2
VMEM_LIMIT = 32 * 1024 * 1024
K_STEP = 8
BATCH = 4
VMEM = pl.BlockSpec(memory_space=pltpu.VMEM)
SMEM = pl.BlockSpec(memory_space=pltpu.SMEM)
PARAMS = pltpu.CompilerParams(vmem_limit_bytes=VMEM_LIMIT)
NT = (((1,), (1,)), ((), ()))
NN = (((1,), (0,)), ((), ()))


def prepare_kernel(screen_ref, chol_ref, block_ref, turned_ref):
    _, listed, vectors, occupied, width = chol_ref.shape
    for m in range(listed):
        keep = jnp.full((1, width), screen_ref[0, m].astype(jnp.float32)).astype(chol_ref.dtype)
        tile = chol_ref[0, m].reshape(vectors * occupied, width) * keep
        block_ref[:, m * width:(m + 1) * width] = tile
        turned_ref[m * width:(m + 1) * width, :] = tile.T


def prepare_block(screen, chol_tiles):
    _, listed, vectors, occupied, width = chol_tiles.shape
    rows, depth = vectors * occupied, listed * width
    return pl.pallas_call(
        prepare_kernel,
        in_specs=[SMEM, VMEM],
        out_specs=[VMEM, VMEM],
        out_shape=[
            jax.ShapeDtypeStruct((rows, depth), chol_tiles.dtype),
            jax.ShapeDtypeStruct((depth, rows), chol_tiles.dtype),
        ],
        compiler_params=PARAMS,
        cost_estimate=pl.CostEstimate(flops=0, bytes_accessed=6 * chol_tiles.size, transcendentals=0),
        name="prepare_block",
    )(screen, chol_tiles)


def batch_terms(block_ref, turned_ref, theta, vectors, occupied):
    columns = theta.shape[0]
    walkers = columns // occupied
    tiles = columns // LANES

    lane = lax.broadcasted_iota(jnp.int32, (occupied, LANES), 1)
    low = lane < occupied
    sub8 = lax.broadcasted_iota(jnp.int32, (8, LANES), 0)
    lane8 = lax.broadcasted_iota(jnp.int32, (8, LANES), 1)
    strip = (lane8 % occupied) // 8
    on_diag = lane8 % 8 == sub8

    def diagonal(block):
        merged = block[:8]
        for r in range(1, occupied // 8):
            merged = jnp.where(strip == r, block[8 * r:8 * r + 8], merged)
        return jnp.where(on_diag, merged, 0.0)

    cross = [jnp.zeros((8, LANES), jnp.float32) for _ in range(tiles)]
    diagonals = []
    for k0 in range(0, vectors, K_STEP):
        span = slice(k0 * occupied, (k0 + K_STEP) * occupied)
        inner_mat = lax.dot_general(block_ref[span, :], theta, NT, preferred_element_type=jnp.float32)
        flipped = lax.dot_general(theta, turned_ref[:, span], NN, preferred_element_type=jnp.float32)
        for pair in range(K_STEP // 2):
            tops, bottoms = [], []
            r0 = pair * 2 * occupied
            for t in range(tiles):
                c0 = t * LANES
                top = inner_mat[r0:r0 + occupied, c0:c0 + LANES]
                bottom = inner_mat[r0 + occupied:r0 + 2 * occupied, c0:c0 + LANES]
                f_top = flipped[c0:c0 + occupied, r0:r0 + LANES]
                f_bottom = flipped[c0 + occupied:c0 + 2 * occupied, r0:r0 + LANES]
                swapped = pltpu.roll(jnp.where(low, f_bottom, f_top), occupied, 1)
                product = jnp.where(low, top, bottom) * jnp.where(low, f_top, f_bottom)
                product = product + jnp.where(low, bottom, top) * swapped
                cross[t] = cross[t] + jnp.sum(product.reshape(occupied // 8, 8, LANES), axis=0)
                tops.append(diagonal(top))
                bottoms.append(diagonal(bottom))
            diagonals.append(jnp.concatenate(tops, axis=1))
            diagonals.append(jnp.concatenate(bottoms, axis=1))
    diagonals.append(jnp.concatenate(cross, axis=1))
    stacked = jnp.concatenate(diagonals, axis=0).reshape(vectors + 1, 8, columns)
    rows = jnp.sum(stacked, axis=1)
    seg_row = lax.broadcasted_iota(jnp.int32, (8, columns), 0)
    seg_col = lax.broadcasted_iota(jnp.int32, (8, columns), 1)
    segment = jnp.where(seg_col // occupied == seg_row, 1.0, 0.0).astype(jnp.float32)
    sums = lax.dot_general(
        segment, rows, NT, precision=lax.Precision.HIGHEST, preferred_element_type=jnp.float32
    )[:walkers]
    return sums[:, :vectors], sums[:, vectors:vectors + 1]


def terms_kernel(list_ref, own_ref, own_turned_ref, other_ref, other_turned_ref, *refs, first, count, vectors, carried):
    theta_refs, rest = refs[:count], refs[count:]
    out_ref, picked_ref = rest[-2], rest[-1]
    listed = list_ref.shape[0]
    _, occupied, _ = theta_refs[0].shape
    width = own_ref.shape[1] // listed
    me = lax.axis_index("chol")
    core = lax.rem(me, CORES)
    chip = me // CORES

    for b, group in enumerate((me, me ^ 1)):
        for m in range(listed):
            start = pl.multiple_of(list_ref[m, group] * width, width)
            for i, ref in enumerate(theta_refs):
                picked_ref[b, i * occupied:(i + 1) * occupied, m * width:(m + 1) * width] = ref[0, :, pl.ds(start, width)]

    if carried:
        out_ref[...] = rest[0][...]
    else:
        out_ref[...] = jnp.zeros(out_ref.shape, out_ref.dtype)

    def one_batch(index, walkers):
        start = index * occupied
        rows = pl.ds(start if isinstance(index, int) else pl.multiple_of(start, walkers * occupied), walkers * occupied)
        own_bias, own_cross = batch_terms(own_ref, own_turned_ref, picked_ref[0, rows, :], vectors, occupied)
        other_bias, other_cross = batch_terms(other_ref, other_turned_ref, picked_ref[1, rows, :], vectors, occupied)
        both = jnp.where(
            core == 0,
            jnp.concatenate([own_bias, other_bias], axis=1),
            jnp.concatenate([other_bias, own_bias], axis=1),
        )
        energy = jnp.sum(both * both, axis=1, keepdims=True) - (own_cross + other_cross)
        for i in range(walkers):
            owner = chip ^ (first + index + i)
            out_ref[pl.ds(owner, 1), 0, :CORES * vectors] = both[i:i + 1]
            out_ref[pl.ds(owner, 1), 0, CORES * vectors:CORES * vectors + 1] = energy[i:i + 1]

    if count <= BATCH:
        one_batch(0, count)
    else:
        @pl.loop(0, count // BATCH)
        def _(step):
            one_batch(step * BATCH, BATCH)


def chip_terms(listing, blocks, thetas, carried, first, vectors, out_width):
    count = len(thetas)
    _, occupied, _ = thetas[0].shape
    chips = listing.shape[1] // CORES
    depth = blocks[0].shape[1]
    operands = [listing, *blocks, *thetas] + ([] if carried is None else [carried])
    return pl.pallas_call(
        functools.partial(terms_kernel, first=first, count=count, vectors=vectors, carried=carried is not None),
        in_specs=[SMEM] + [VMEM] * (len(operands) - 1),
        out_specs=VMEM,
        out_shape=jax.ShapeDtypeStruct((chips, 1, out_width), jnp.float32),
        scratch_shapes=[pltpu.VMEM((CORES, count * occupied, depth), thetas[0].dtype)],
        compiler_params=PARAMS,
        cost_estimate=pl.CostEstimate(
            flops=8 * count * vectors * occupied * occupied * depth,
            bytes_accessed=8 * blocks[0].size,
            transcendentals=0,
        ),
        name="chip_terms",
    )(*operands)


def finish_kernel(rows_ref, bias_ref, energy_ref, *, used, scale):
    chips, _, width = rows_ref.shape
    total = rows_ref[0]
    for d in range(1, chips):
        total = total + rows_ref[d]
    energy_ref[...] = total[:, used:used + 1] * scale
    lane = lax.broadcasted_iota(jnp.int32, (1, width), 1)
    fit = LANES // used if width == LANES else 0
    if fit and chips % fit == 0:
        for d in range(0, chips, fit):
            packed = rows_ref[d]
            for i in range(1, fit):
                packed = jnp.where(lane < i * used, packed, pltpu.roll(rows_ref[d + i], i * used, 1))
            bias_ref[:, d * used:(d + fit) * used] = packed
    else:
        for d in range(chips):
            bias_ref[:, d * used:(d + 1) * used] = rows_ref[d, :, :used]


def finish(rows, used, scale):
    chips = rows.shape[0]
    force_bias, energy = pl.pallas_call(
        functools.partial(finish_kernel, used=used, scale=scale),
        in_specs=[VMEM],
        out_specs=[VMEM, VMEM],
        out_shape=[
            jax.ShapeDtypeStruct((1, chips * used), jnp.float32),
            jax.ShapeDtypeStruct((1, 1), jnp.float32),
        ],
        name="finish",
    )(rows)
    return force_bias, energy.reshape(1)


def body(theta, chol_tiles, screen, tile_list):
    groups = lax.axis_size("chol")
    chips = groups // CORES
    half = chips // 2
    _, occupied, _ = theta.shape
    vectors = chol_tiles.shape[2]
    used = CORES * vectors
    out_width = LANES * ((used + 1 + LANES - 1) // LANES)
    listing = tile_list.T

    def to_chip(x, offset):
        return lax.ppermute(x, "chol", [(i, i ^ (offset * CORES)) for i in range(groups)])

    def to_core(x):
        return lax.ppermute(x, "chol", [(i, i ^ 1) for i in range(groups)])

    far = to_chip(theta, half)
    near = [theta] + [to_chip(theta, offset) for offset in range(1, half)]
    beyond = [far] + [to_chip(far, offset) for offset in range(1, half)]
    blocks = [*prepare_block(screen, chol_tiles), *prepare_block(to_core(screen), to_core(chol_tiles))]

    rows = chip_terms(listing, blocks, near, None, 0, vectors, out_width)
    rows = chip_terms(listing, blocks, beyond, rows, half, vectors, out_width)
    same_core = [list(range(core, groups, CORES)) for core in range(CORES)]
    back = lax.all_to_all(rows, "chol", split_axis=0, concat_axis=0, tiled=True, axis_index_groups=same_core)
    return finish(back, used, 1.0 / (2.0 * occupied * occupied))


def solution(mesh):
    in_specs = (
        P(("grp", "chol"), None, None),
        P("chol", None, None, None, None),
        P("chol", None),
        P(),
    )
    out_specs = (P(("grp", "chol"), None), P(("grp", "chol")))
    return jax.shard_map(body, mesh=mesh, in_specs=in_specs, out_specs=out_specs, check_vma=False)
```

time: 52.1 us -> 41.9 us (0.80)
  waiting for transfers between devices: 12.3 us -> 4.83 us
  Pallas kernels: 13.5 us -> 11.7 us
  blocking collectives: 11.8 us -> 11 us
    ppermute x8 -> x9, waiting for transfers between devices: 12.3 us -> 4.83 us  [the longest x7 3.58 us: to_chip(): lax.ppermute(x, 'chol', [(i, i ^ offset * CORES) for i in range(groups)])]
    pallas_call x4, Pallas kernels: 12.2 us -> 10.4 us  [the longest x2 7.79 us: chip_terms(): pl.pallas_call(functools.partial(terms_kernel, first=first, count=count,...]
    all_to_all x1, blocking collectives: 11.8 us -> 11 us  [body(): lax.all_to_all(rows, 'chol', split_axis=0, concat_axis=0, tiled=True, axi...]
    ppermute x8 -> x9, starting transfers between devices: 11.3 us -> 11.2 us  [the longest x7 10.7 us: to_chip(): lax.ppermute(x, 'chol', [(i, i ^ offset * CORES) for i in range(groups)])]
  transfers between devices with their start and end apart: 8 -> 9, of which waited for: 4 -> 5; matrix products, arithmetic and copies ran while one was open for 0% -> 0% of each run, Pallas kernels for 14% -> 16%
where the time goes in v6:
time: 41.9 us; the launch traced here: 41.7 us
  Pallas kernels  11.7 us (28%)
  starting transfers between devices  11.2 us (27%)
  blocking collectives  11 us (26%)
  waiting for transfers between devices  4.83 us (12%)
  local copies, waits for them, and re-layouts  2.25 us (5%)
  between operations  0.67 us (2%)
    all_to_all x1, blocking collectives, body(): lax.all_to_all(rows, 'chol', split_axis=0, concat_axis=0, tiled=True, axi...  11 us
    ppermute x7, starting transfers between devices, to_chip(): lax.ppermute(x, 'chol', [(i, i ^ offset * CORES) for i in range(groups)])  10.7 us
    pallas_call x2, Pallas kernels, chip_terms(): pl.pallas_call(functools.partial(terms_kernel, first=first, count=count,...  7.79 us
    ppermute x7, waiting for transfers between devices, to_chip(): lax.ppermute(x, 'chol', [(i, i ^ offset * CORES) for i in range(groups)])  3.58 us
    pallas_call x2, Pallas kernels, prepare_block(): pl.pallas_call(prepare_kernel, in_specs=[SMEM, VMEM], out_specs=[VMEM, VM...  2.58 us
    unnamed x8, local copies, waits for them, and re-layouts  2.25 us
    pallas_call x1, Pallas kernels, finish(): pl.pallas_call(functools.partial(finish_kernel, used=used, scale=scale),...  1.33 us
    ppermute x2, waiting for transfers between devices, to_core(): return lax.ppermute(x, 'chol', [(i, i ^ 1) for i in range(groups)])  1.26 us
  transfers between devices with their start and end apart: 9, of which 5 were waited for; matrix products, arithmetic and copies ran while one was open for 0% of the time, Pallas kernels for 16%

profile of v6, /device:TPU:0, one launch (start us, length us, event | category | flops | bytes accessed | tf_op | source)
XLA Modules:
  0.0 41.7 jit_solution(11560060429198224342)
XLA Ops:
  0.6 0.5 %collective-permute-start.1 = (bf16[1,4,32,64,128]{4,3,2,1,0:T(8,128)(2,1)}, bf16[1,4,32,64,128]{4,3,2,1,0:T(8,128)(2,1)S(1)}, u32[]{:S(2)}, u32[]{:S(2)}) collective-permute-start(bf16[1,4,32,64,128]{4,3,2,1,0:T(8,128)(2,1)} %chol_ref.1), channel_id=1, source_target_pairs={{0,1},{1,0},{2,3},{3,2},{4,5},{5,4},{6,7},{7,6},{8,9},{9,8},{10,11... | collective-permute-start | bytes 6291464 | tf_op jit(solution)/shard_map/ppermute | solution.py:216
  1.1 3.7 %collective-permute-start.2 = (bf16[1,64,1280]{2,1,0:T(8,128)(2,1)}, bf16[1,64,1280]{2,1,0:T(8,128)(2,1)S(1)}, u32[]{:S(2)}, u32[]{:S(2)}) collective-permute-start(bf16[1,64,1280]{2,1,0:T(8,128)(2,1)} %refs_0_.1), channel_id=1, source_target_pairs={{0,8},{1,9},{2,10},{3,11},{4,12},{5,13},{6,14},{7,15},{8,0},{9,1},... | collective-permute-start | bytes 491528 | tf_op jit(solution)/shard_map/ppermute | solution.py:213
  4.8 1.5 %collective-permute-start.6 = (bf16[1,64,1280]{2,1,0:T(8,128)(2,1)}, bf16[1,64,1280]{2,1,0:T(8,128)(2,1)S(1)}, u32[]{:S(2)}, u32[]{:S(2)}) collective-permute-start(bf16[1,64,1280]{2,1,0:T(8,128)(2,1)} %refs_0_.1), channel_id=1, source_target_pairs={{0,2},{1,3},{2,0},{3,1},{4,6},{5,7},{6,4},{7,5},{8,10},{9,11},{10,... | collective-permute-start | bytes 491528 | tf_op jit(solution)/shard_map/ppermute | solution.py:213
  6.3 1.6 %collective-permute-start.7 = (bf16[1,64,1280]{2,1,0:T(8,128)(2,1)}, bf16[1,64,1280]{2,1,0:T(8,128)(2,1)S(1)}, u32[]{:S(2)}, u32[]{:S(2)}) collective-permute-start(bf16[1,64,1280]{2,1,0:T(8,128)(2,1)} %refs_0_.1), channel_id=1, source_target_pairs={{0,4},{1,5},{2,6},{3,7},{4,0},{5,1},{6,2},{7,3},{8,12},{9,13},{10,... | collective-permute-start | bytes 491528 | tf_op jit(solution)/shard_map/ppermute | solution.py:213
  7.9 0.0 collective-permute-start
  7.9 1.3 %collective-permute-done.screen_ref = s32[1,4]{1,0:T(1,128)S(1)} collective-permute-done((s32[1,4]{1,0:T(1,128)}, s32[1,4]{1,0:T(1,128)S(1)}, u32[]{:S(2)}, u32[]{:S(2)}) %collective-permute-start) | collective-permute-done | bytes 48 | tf_op jit(solution)/shard_map/ppermute | solution.py:216
  9.2 0.4 collective-permute-start.8
  9.6 0.0 copy-start
  9.6 1.6 %copy-done = bf16[1,4,32,64,128]{4,3,2,1,0:T(8,128)(2,1)S(1)} copy-done((bf16[1,4,32,64,128]{4,3,2,1,0:T(8,128)(2,1)S(1)}, bf16[1,4,32,64,128]{4,3,2,1,0:T(8,128)(2,1)}, u32[]{:S(2)}) %copy-start) | copy-done | bytes 2097176
  11.1 0.0 copy-start.3
  11.2 0.7 %copy-done.3 = s32[1,4]{1,0:T(1,128)S(1)} copy-done((s32[1,4]{1,0:T(1,128)S(1)}, s32[1,4]{1,0:T(1,128)}, u32[]{:S(2)}) %copy-start.3) | copy-done | bytes 40
  11.8 0.0 copy-start.1
  11.8 0.0 copy-start.2
  11.8 1.3 %prepare_block.2 = (bf16[2048,512]{1,0:T(8,128)(2,1)S(1)}, bf16[512,2048]{1,0:T(8,128)(2,1)S(1)}) custom-call(s32[1,4]{1,0:T(1,128)S(1)} %copy-done.3, bf16[1,4,32,64,128]{4,3,2,1,0:T(8,128)(2,1)S(1)} %copy-done), custom_call_target="tpu_custom_call" | custom-call | bytes 6291456 | tf_op jit(solution)/shard_map/prepare_block/pallas_call | solution.py:34
  13.1 0.3 collective-permute-done.2.refs_0_
  13.4 1.6 %collective-permute-start.3 = (bf16[1,64,1280]{2,1,0:T(8,128)(2,1)S(1)}, bf16[1,64,1280]{2,1,0:T(8,128)(2,1)S(1)}, u32[]{:S(2)}, u32[]{:S(2)}) collective-permute-start(bf16[1,64,1280]{2,1,0:T(8,128)(2,1)S(1)} %collective-permute-done.2.refs_0_), channel_id=1, source_target_pairs={{0,2},{1,3},{2,0},{3,1},{4,6},{5,7},{6,4},{7,5},{8,10},{9,11},{10,... | collective-permute-start | bytes 491528 | tf_op jit(solution)/shard_map/ppermute | solution.py:213
  15.0 0.0 collective-permute-done.1.chol_ref
  15.0 1.3 %collective-permute-start.4 = (bf16[1,64,1280]{2,1,0:T(8,128)(2,1)S(1)}, bf16[1,64,1280]{2,1,0:T(8,128)(2,1)S(1)}, u32[]{:S(2)}, u32[]{:S(2)}) collective-permute-start(bf16[1,64,1280]{2,1,0:T(8,128)(2,1)S(1)} %collective-permute-done.2.refs_0_), channel_id=1, source_target_pairs={{0,4},{1,5},{2,6},{3,7},{4,0},{5,1},{6,2},{7,3},{8,12},{9,13},{10,... | collective-permute-start | bytes 491528 | tf_op jit(solution)/shard_map/ppermute | solution.py:213
  16.3 1.3 %prepare_block.3 = (bf16[2048,512]{1,0:T(8,128)(2,1)S(1)}, bf16[512,2048]{1,0:T(8,128)(2,1)S(1)}) custom-call(s32[1,4]{1,0:T(1,128)S(1)} %collective-permute-done.screen_ref, bf16[1,4,32,64,128]{4,3,2,1,0:T(8,128)(2,1)S(1)} %collective-permute-done.1.chol_ref), custom_call_target="tpu_custom_call" | custom-call | bytes 6291456 | tf_op jit(solution)/shard_map/prepare_block/pallas_call | solution.py:34
  17.6 0.0 collective-permute-done.6.refs_1_
  17.6 0.7 %collective-permute-start.5 = (bf16[1,64,1280]{2,1,0:T(8,128)(2,1)S(1)}, bf16[1,64,1280]{2,1,0:T(8,128)(2,1)S(1)}, u32[]{:S(2)}, u32[]{:S(2)}) collective-permute-start(bf16[1,64,1280]{2,1,0:T(8,128)(2,1)S(1)} %collective-permute-done.2.refs_0_), channel_id=1, source_target_pairs={{0,6},{1,7},{2,4},{3,5},{4,2},{5,3},{6,0},{7,1},{8,14},{9,15},{10,... | collective-permute-start | bytes 491528 | tf_op jit(solution)/shard_map/ppermute | solution.py:213
  18.3 0.0 collective-permute-done.7.refs_2_
  18.3 0.5 %collective-permute-done.8.refs_3_ = bf16[1,64,1280]{2,1,0:T(8,128)(2,1)S(1)} collective-permute-done((bf16[1,64,1280]{2,1,0:T(8,128)(2,1)}, bf16[1,64,1280]{2,1,0:T(8,128)(2,1)S(1)}, u32[]{:S(2)}, u32[]{:S(2)}) %collective-permute-start.8) | collective-permute-done | bytes 163872 | tf_op jit(solution)/shard_map/ppermute | solution.py:213
  18.8 0.0 copy-done.1
  18.8 0.0 copy-done.2
  18.8 3.9 %chip_terms.2.refs_4_ = f32[8,1,128]{2,1,0:T(1,128)S(1)} custom-call(s32[4,16]{1,0:T(4,128)S(1)} %bitcast.2, bf16[2048,512]{1,0:T(8,128)(2,1)S(1)} %get-tuple-element.8.own_ref, bf16[512,2048]{1,0:T(8,128)(2,1)S(1)} %get-tuple-element.9.own_turned_ref, bf16[2048,512]{1,0:T(8,128)(2,1)S(1)} %get-tuple-element.10.other_ref, ...), custom_call_target="tpu_custom_call" | custom-call | flops 2147483648 | bytes 8388608 | tf_op jit(solution)/shard_map/chip_terms/pallas_call | solution.py:152
  22.7 0.0 collective-permute-done.3.refs_1_
  22.7 0.3 collective-permute-done.4.refs_2_
  23.0 2.4 %collective-permute-done.5.refs_3_ = bf16[1,64,1280]{2,1,0:T(8,128)(2,1)S(1)} collective-permute-done((bf16[1,64,1280]{2,1,0:T(8,128)(2,1)S(1)}, bf16[1,64,1280]{2,1,0:T(8,128)(2,1)S(1)}, u32[]{:S(2)}, u32[]{:S(2)}) %collective-permute-start.5) | collective-permute-done | bytes 163872 | tf_op jit(solution)/shard_map/ppermute | solution.py:213
  25.4 3.9 %chip_terms.3 = f32[8,1,128]{2,1,0:T(1,128)S(1)} custom-call(s32[4,16]{1,0:T(4,128)S(1)} %bitcast.3, bf16[2048,512]{1,0:T(8,128)(2,1)S(1)} %get-tuple-element.8.own_ref, bf16[512,2048]{1,0:T(8,128)(2,1)S(1)} %get-tuple-element.9.own_turned_ref, bf16[2048,512]{1,0:T(8,128)(2,1)S(1)} %get-tuple-element.10.other_ref, ...), custom_call_target="tpu_custom_call" | custom-call | flops 2147483648 | bytes 8388608 | tf_op jit(solution)/shard_map/chip_terms/pallas_call | solution.py:152
  29.3 11.0 %all_to_all.5.rows_ref = f32[8,1,128]{2,1,0:T(1,128)} all-to-all(f32[8,1,128]{2,1,0:T(1,128)S(1)} %chip_terms.3), channel_id=1, replica_groups={{0,2,4,6,8,10,12,14},{1,3,5,7,9,11,13,15},{16,18,20,22,24,26,28,30},{17..., dimensions={0} | all-to-all | bytes 8192 | tf_op jit(solution)/shard_map/all_to_all | solution.py:226
  40.3 1.3 %finish.1 = (f32[1,512]{1,0:T(1,128)}, f32[1,1]{1,0:T(1,128)}) custom-call(f32[8,1,128]{2,1,0:T(1,128)} %all_to_all.5.rows_ref), custom_call_target="tpu_custom_call" | custom-call | tf_op jit(solution)/shard_map/finish/pallas_call | solution.py:189
Async XLA Ops:
  0.6 14.4 %collective-permute-start.1 = (bf16[1,4,32,64,128]{4,3,2,1,0:T(8,128)(2,1)}, bf16[1,4,32,64,128]{4,3,2,1,0:T(8,128)(2,1)S(1)}, u32[]{:S(2)}, u32[]{:S(2)}) collective-permute-start(bf16[1,4,32,64,128]{4,3,2,1,0:T(8,128)(2,1)} %chol_ref.1), channel_id=1, source_target_pairs={{0,1},{1,0},{2,3},{3,2},{4,5},{5,4},{6,7},{7,6},{8,9},{9,8},{10,11... | collective-permute-start | bytes 6291464 | tf_op jit(solution)/shard_map/ppermute | solution.py:216
  1.1 12.3 %collective-permute-start.2 = (bf16[1,64,1280]{2,1,0:T(8,128)(2,1)}, bf16[1,64,1280]{2,1,0:T(8,128)(2,1)S(1)}, u32[]{:S(2)}, u32[]{:S(2)}) collective-permute-start(bf16[1,64,1280]{2,1,0:T(8,128)(2,1)} %refs_0_.1), channel_id=1, source_target_pairs={{0,8},{1,9},{2,10},{3,11},{4,12},{5,13},{6,14},{7,15},{8,0},{9,1},... | collective-permute-start | bytes 491528 | tf_op jit(solution)/shard_map/ppermute | solution.py:213
  4.8 12.8 %collective-permute-start.6 = (bf16[1,64,1280]{2,1,0:T(8,128)(2,1)}, bf16[1,64,1280]{2,1,0:T(8,128)(2,1)S(1)}, u32[]{:S(2)}, u32[]{:S(2)}) collective-permute-start(bf16[1,64,1280]{2,1,0:T(8,128)(2,1)} %refs_0_.1), channel_id=1, source_target_pairs={{0,2},{1,3},{2,0},{3,1},{4,6},{5,7},{6,4},{7,5},{8,10},{9,11},{10,... | collective-permute-start | bytes 491528 | tf_op jit(solution)/shard_map/ppermute | solution.py:213
  6.3 12.0 %collective-permute-start.7 = (bf16[1,64,1280]{2,1,0:T(8,128)(2,1)}, bf16[1,64,1280]{2,1,0:T(8,128)(2,1)S(1)}, u32[]{:S(2)}, u32[]{:S(2)}) collective-permute-start(bf16[1,64,1280]{2,1,0:T(8,128)(2,1)} %refs_0_.1), channel_id=1, source_target_pairs={{0,4},{1,5},{2,6},{3,7},{4,0},{5,1},{6,2},{7,3},{8,12},{9,13},{10,... | collective-permute-start | bytes 491528 | tf_op jit(solution)/shard_map/ppermute | solution.py:213
  7.9 1.3 %collective-permute-start = (s32[1,4]{1,0:T(1,128)}, s32[1,4]{1,0:T(1,128)S(1)}, u32[]{:S(2)}, u32[]{:S(2)}) collective-permute-start(s32[1,4]{1,0:T(1,128)} %screen_ref.1), channel_id=1, source_target_pairs={{0,1},{1,0},{2,3},{3,2},{4,5},{5,4},{6,7},{7,6},{8,9},{9,8},{10,11... | collective-permute-start | bytes 56 | tf_op jit(solution)/shard_map/ppermute | solution.py:216
  9.2 9.6 %collective-permute-start.8 = (bf16[1,64,1280]{2,1,0:T(8,128)(2,1)}, bf16[1,64,1280]{2,1,0:T(8,128)(2,1)S(1)}, u32[]{:S(2)}, u32[]{:S(2)}) collective-permute-start(bf16[1,64,1280]{2,1,0:T(8,128)(2,1)} %refs_0_.1), channel_id=1, source_target_pairs={{0,6},{1,7},{2,4},{3,5},{4,2},{5,3},{6,0},{7,1},{8,14},{9,15},{10,... | collective-permute-start | bytes 491528 | tf_op jit(solution)/shard_map/ppermute | solution.py:213
  9.6 1.6 %copy-start = (bf16[1,4,32,64,128]{4,3,2,1,0:T(8,128)(2,1)S(1)}, bf16[1,4,32,64,128]{4,3,2,1,0:T(8,128)(2,1)}, u32[]{:S(2)}) copy-start(bf16[1,4,32,64,128]{4,3,2,1,0:T(8,128)(2,1)} %chol_ref.1) | copy-start | bytes 6291460
  11.1 0.7 %copy-start.3 = (s32[1,4]{1,0:T(1,128)S(1)}, s32[1,4]{1,0:T(1,128)}, u32[]{:S(2)}) copy-start(s32[1,4]{1,0:T(1,128)} %screen_ref.1) | copy-start | bytes 52
  11.8 7.0 %copy-start.1 = (bf16[1,64,1280]{2,1,0:T(8,128)(2,1)S(1)}, bf16[1,64,1280]{2,1,0:T(8,128)(2,1)}, u32[]{:S(2)}) copy-start(bf16[1,64,1280]{2,1,0:T(8,128)(2,1)} %refs_0_.1) | copy-start | bytes 491524
  11.8 7.0 %copy-start.2 = (s32[16,4]{0,1:T(4,128)S(1)}, s32[16,4]{0,1:T(4,128)}, u32[]{:S(2)}) copy-start(s32[16,4]{0,1:T(4,128)} %param.7) | copy-start | bytes 772
  13.4 9.3 %collective-permute-start.3 = (bf16[1,64,1280]{2,1,0:T(8,128)(2,1)S(1)}, bf16[1,64,1280]{2,1,0:T(8,128)(2,1)S(1)}, u32[]{:S(2)}, u32[]{:S(2)}) collective-permute-start(bf16[1,64,1280]{2,1,0:T(8,128)(2,1)S(1)} %collective-permute-done.2.refs_0_), channel_id=1, source_target_pairs={{0,2},{1,3},{2,0},{3,1},{4,6},{5,7},{6,4},{7,5},{8,10},{9,11},{10,... | collective-permute-start | bytes 491528 | tf_op jit(solution)/shard_map/ppermute | solution.py:213
  15.0 8.0 %collective-permute-start.4 = (bf16[1,64,1280]{2,1,0:T(8,128)(2,1)S(1)}, bf16[1,64,1280]{2,1,0:T(8,128)(2,1)S(1)}, u32[]{:S(2)}, u32[]{:S(2)}) collective-permute-start(bf16[1,64,1280]{2,1,0:T(8,128)(2,1)S(1)} %collective-permute-done.2.refs_0_), channel_id=1, source_target_pairs={{0,4},{1,5},{2,6},{3,7},{4,0},{5,1},{6,2},{7,3},{8,12},{9,13},{10,... | collective-permute-start | bytes 491528 | tf_op jit(solution)/shard_map/ppermute | solution.py:213
  17.6 7.9 %collective-permute-start.5 = (bf16[1,64,1280]{2,1,0:T(8,128)(2,1)S(1)}, bf16[1,64,1280]{2,1,0:T(8,128)(2,1)S(1)}, u32[]{:S(2)}, u32[]{:S(2)}) collective-permute-start(bf16[1,64,1280]{2,1,0:T(8,128)(2,1)S(1)} %collective-permute-done.2.refs_0_), channel_id=1, source_target_pairs={{0,6},{1,7},{2,4},{3,5},{4,2},{5,3},{6,0},{7,1},{8,14},{9,15},{10,... | collective-permute-start | bytes 491528 | tf_op jit(solution)/shard_map/ppermute | solution.py:213

commit v7 on v6

v7 whole, which is shorter than its diff:
```python
import functools

import jax
import jax.numpy as jnp
from jax import lax
from jax.experimental import pallas as pl
from jax.experimental.pallas import tpu as pltpu
from jax.sharding import PartitionSpec as P

LANES = 128
CORES = 2
VMEM_LIMIT = 32 * 1024 * 1024
K_STEP = 16
BATCH = 4
VMEM = pl.BlockSpec(memory_space=pltpu.VMEM)
SMEM = pl.BlockSpec(memory_space=pltpu.SMEM)
PARAMS = pltpu.CompilerParams(vmem_limit_bytes=VMEM_LIMIT)
SMALL = pl.CostEstimate(flops=0, bytes_accessed=0, transcendentals=0)
NT = (((1,), (1,)), ((), ()))
NN = (((1,), (0,)), ((), ()))


def prepare_kernel(chol_ref, block_ref, turned_ref):
    _, listed, vectors, occupied, width = chol_ref.shape
    for m in range(listed):
        tile = chol_ref[0, m].reshape(vectors * occupied, width)
        block_ref[:, m * width:(m + 1) * width] = tile
        turned_ref[m * width:(m + 1) * width, :] = tile.T


def prepare_block(chol_tiles):
    _, listed, vectors, occupied, width = chol_tiles.shape
    rows, depth = vectors * occupied, listed * width
    return pl.pallas_call(
        prepare_kernel,
        in_specs=[VMEM],
        out_specs=[VMEM, VMEM],
        out_shape=[
            jax.ShapeDtypeStruct((rows, depth), chol_tiles.dtype),
            jax.ShapeDtypeStruct((depth, rows), chol_tiles.dtype),
        ],
        compiler_params=PARAMS,
        cost_estimate=SMALL,
        name="prepare_block",
    )(chol_tiles)


def fold_rows(blocks, sub):
    high = sub < 4
    pairs = []
    for i in range(4):
        a, b = blocks[i], blocks[i + 4]
        pairs.append(jnp.where(high, a, b) + pltpu.roll(jnp.where(high, b, a), 4, 0))
    for shift in (2, 1):
        first = sub % (2 * shift) < shift
        half = len(pairs) // 2
        pairs = [
            jnp.where(
                first,
                pairs[i] + pltpu.roll(pairs[i], 8 - shift, 0),
                pairs[i + half] + pltpu.roll(pairs[i + half], shift, 0),
            )
            for i in range(half)
        ]
    return pairs[0]


def batch_terms(block_ref, turned_ref, theta, cross, store_rows, vectors, occupied):
    columns = theta.shape[0]
    tiles = columns // LANES

    low = lax.broadcasted_iota(jnp.int32, (occupied, LANES), 1) < occupied
    sub8 = lax.broadcasted_iota(jnp.int32, (8, LANES), 0)
    lane8 = lax.broadcasted_iota(jnp.int32, (8, LANES), 1)
    strip = (lane8 % occupied) // 8
    on_diag = lane8 % 8 == sub8

    def diagonal(block):
        merged = block[:8]
        for r in range(1, occupied // 8):
            merged = jnp.where(strip == r, block[8 * r:8 * r + 8], merged)
        return jnp.where(on_diag, merged, 0.0)

    for k0 in range(0, vectors, K_STEP):
        span = slice(k0 * occupied, (k0 + K_STEP) * occupied)
        inner_mat = lax.dot_general(block_ref[span, :], theta, NT, preferred_element_type=jnp.float32)
        flipped = lax.dot_general(theta, turned_ref[:, span], NN, preferred_element_type=jnp.float32)
        for k8 in range(0, K_STEP, 8):
            for t in range(tiles):
                c0 = t * LANES
                diagonals = []
                for k in range(k8, k8 + 8, 2):
                    r0 = k * occupied
                    top = inner_mat[r0:r0 + occupied, c0:c0 + LANES]
                    bottom = inner_mat[r0 + occupied:r0 + 2 * occupied, c0:c0 + LANES]
                    f_top = flipped[c0:c0 + occupied, r0:r0 + LANES]
                    f_bottom = flipped[c0 + occupied:c0 + 2 * occupied, r0:r0 + LANES]
                    swapped = pltpu.roll(jnp.where(low, f_bottom, f_top), occupied, 1)
                    product = jnp.where(low, top, bottom) * jnp.where(low, f_top, f_bottom)
                    product = product + jnp.where(low, bottom, top) * swapped
                    cross[t] = cross[t] + jnp.sum(product.reshape(occupied // 8, 8, LANES), axis=0)
                    diagonals.append(diagonal(top))
                    diagonals.append(diagonal(bottom))
                store_rows(k0 + k8, t, fold_rows(diagonals, sub8))


def terms_kernel(list_ref, *refs, first, count, vectors, batch, carried):
    screen_refs, block_refs, theta_refs, rest = refs[:2], refs[2:6], refs[6:6 + count], refs[6 + count:]
    out_ref, picked_ref, rows_ref = rest[-3:]
    listed = list_ref.shape[0]
    _, occupied, _ = theta_refs[0].shape
    width = block_refs[0].shape[1] // listed
    used = CORES * vectors
    columns = batch * occupied
    tiles = columns // LANES
    out_width = out_ref.shape[2]
    me = lax.axis_index("chol")
    core = lax.rem(me, CORES)
    chip = me // CORES

    for b, group in enumerate((me, me ^ 1)):
        for m in range(listed):
            start = pl.multiple_of(list_ref[m, group] * width, width)
            keep = jnp.full((1, width), screen_refs[b][0, m].astype(jnp.float32)).astype(picked_ref.dtype)
            for i, ref in enumerate(theta_refs):
                picked_ref[b, i * occupied:(i + 1) * occupied, m * width:(m + 1) * width] = (
                    ref[0, :, pl.ds(start, width)] * keep
                )

    if carried:
        out_ref[...] = rest[0][...]
    else:
        out_ref[...] = jnp.zeros(out_ref.shape, out_ref.dtype)

    def one_batch(index):
        start = index * occupied
        rows = pl.ds(start if isinstance(index, int) else pl.multiple_of(start, columns), columns)
        cross = [jnp.zeros((8, LANES), jnp.float32) for _ in range(tiles)]
        for b in range(CORES):
            place = (core ^ b) * vectors

            def store_rows(k, t, value, place=place):
                rows_ref[pl.ds(pl.multiple_of(place + k, 8), 8), t * LANES:(t + 1) * LANES] = value

            batch_terms(
                block_refs[2 * b], block_refs[2 * b + 1], picked_ref[b, rows, :], cross, store_rows, vectors, occupied
            )
        for t in range(tiles):
            rows_ref[used:used + 8, t * LANES:(t + 1) * LANES] = cross[t]
        values = rows_ref[...]
        parts = []
        for _ in range(3):
            part = values.astype(jnp.bfloat16)
            parts.append(part)
            values = values - part.astype(jnp.float32)
        seg_row = lax.broadcasted_iota(jnp.int32, (8, columns), 0)
        seg_col = lax.broadcasted_iota(jnp.int32, (8, columns), 1)
        segment = jnp.where(seg_col // occupied == seg_row, 1.0, 0.0).astype(jnp.bfloat16)
        sums = sum(
            lax.dot_general(segment, part, NT, preferred_element_type=jnp.float32) for part in parts
        )
        bias = sums[:, :used]
        energy = jnp.sum(bias * bias, axis=1, keepdims=True) - jnp.sum(
            sums[:, used:used + 8], axis=1, keepdims=True
        )
        for i in range(batch):
            owner = chip ^ (first + index + i)
            out_ref[pl.ds(owner, 1), 0, :used] = bias[i:i + 1]
            out_ref[pl.ds(owner, 1), 0, used:used + 1] = energy[i:i + 1]

    if count == batch:
        one_batch(0)
    else:
        @pl.loop(0, count // batch)
        def _(step):
            one_batch(step * batch)


def chip_terms(listing, screens, blocks, thetas, carried, first, vectors, out_width):
    count = len(thetas)
    batch = min(count, BATCH)
    _, occupied, _ = thetas[0].shape
    chips = listing.shape[1] // CORES
    depth = blocks[0].shape[1]
    operands = [listing, *screens, *blocks, *thetas] + ([] if carried is None else [carried])
    return pl.pallas_call(
        functools.partial(
            terms_kernel, first=first, count=count, vectors=vectors, batch=batch, carried=carried is not None
        ),
        in_specs=[SMEM] * 3 + [VMEM] * (len(operands) - 3),
        out_specs=VMEM,
        out_shape=jax.ShapeDtypeStruct((chips, 1, out_width), jnp.float32),
        scratch_shapes=[
            pltpu.VMEM((CORES, count * occupied, depth), thetas[0].dtype),
            pltpu.VMEM((CORES * vectors + 8, batch * occupied), jnp.float32),
        ],
        compiler_params=PARAMS,
        cost_estimate=SMALL,
        name="chip_terms",
    )(*operands)


def finish_kernel(rows_ref, bias_ref, energy_ref, bias_buf, energy_buf, sems, *, used, scale):
    chips, _, width = rows_ref.shape
    fit = LANES // used if width == LANES else 0
    lane = lax.broadcasted_iota(jnp.int32, (1, width), 1)
    if fit and chips % fit == 0:
        for d in range(0, chips, fit):
            packed = rows_ref[d]
            for i in range(1, fit):
                packed = jnp.where(lane < i * used, packed, pltpu.roll(rows_ref[d + i], i * used, 1))
            bias_buf[:, d * used:(d + fit) * used] = packed
    else:
        for d in range(chips):
            bias_buf[:, d * used:(d + 1) * used] = rows_ref[d, :, :used]
    bias_copy = pltpu.make_async_copy(bias_buf, bias_ref, sems.at[0])
    bias_copy.start()
    total = rows_ref[0]
    for d in range(1, chips):
        total = total + rows_ref[d]
    energy_buf[...] = total[:, used:used + 1] * scale
    energy_copy = pltpu.make_async_copy(energy_buf, energy_ref, sems.at[1])
    energy_copy.start()
    bias_copy.wait()
    energy_copy.wait()


def finish(rows, used, scale):
    chips = rows.shape[0]
    shapes = [(1, chips * used), (1, 1)]
    force_bias, energy = pl.pallas_call(
        functools.partial(finish_kernel, used=used, scale=scale),
        in_specs=[VMEM],
        out_specs=[pl.BlockSpec(memory_space=pl.ANY)] * 2,
        out_shape=[jax.ShapeDtypeStruct(s, jnp.float32) for s in shapes],
        scratch_shapes=[pltpu.VMEM(s, jnp.float32) for s in shapes] + [pltpu.SemaphoreType.DMA((2,))],
        name="finish",
    )(rows)
    return force_bias, energy.reshape(1)


def body(theta, chol_tiles, screen, tile_list):
    groups = lax.axis_size("chol")
    chips = groups // CORES
    half = chips // 2
    _, occupied, _ = theta.shape
    vectors = chol_tiles.shape[2]
    used = CORES * vectors
    out_width = LANES * ((used + 1 + LANES - 1) // LANES)
    listing = tile_list.T

    def to_chip(x, offset):
        return lax.ppermute(x, "chol", [(i, i ^ (offset * CORES)) for i in range(groups)])

    def to_core(x):
        return lax.ppermute(x, "chol", [(i, i ^ 1) for i in range(groups)])

    far = to_chip(theta, half)
    near = [theta] + [to_chip(theta, offset) for offset in range(1, half)]
    own, own_turned = prepare_block(chol_tiles)
    far, own = lax.optimization_barrier((far, own))
    beyond = [far] + [to_chip(far, offset) for offset in range(1, half)]
    other, other_turned = prepare_block(to_core(chol_tiles))
    other, late_screen = lax.optimization_barrier((other, screen))
    screens = [screen, to_core(late_screen)]
    blocks = [own, own_turned, other, other_turned]

    rows = chip_terms(listing, screens, blocks, near, None, 0, vectors, out_width)
    rows = chip_terms(listing, screens, blocks, beyond, rows, half, vectors, out_width)
    same_core = [list(range(core, groups, CORES)) for core in range(CORES)]
    back = lax.all_to_all(rows, "chol", split_axis=0, concat_axis=0, tiled=True, axis_index_groups=same_core)
    return finish(back, used, 1.0 / (2.0 * occupied * occupied))


def solution(mesh):
    in_specs = (
        P(("grp", "chol"), None, None),
        P("chol", None, None, None, None),
        P("chol", None),
        P(),
    )
    out_specs = (P(("grp", "chol"), None), P(("grp", "chol")))
    return jax.shard_map(body, mesh=mesh, in_specs=in_specs, out_specs=out_specs, check_vma=False)
```

time: 41.9 us -> 41.1 us (0.981)
  Pallas kernels: 11.7 us -> 9.53 us
  waiting for transfers between devices: 4.83 us -> 6.69 us
  local copies, waits for them, and re-layouts: 2.25 us -> 1.6 us
    ppermute x7, waiting for transfers between devices: 3.58 us -> 6.68 us  [to_chip(): lax.ppermute(x, 'chol', [(i, i ^ offset * CORES) for i in range(groups)])]
    ppermute x2, waiting for transfers between devices: 1.26 us -> 0.01 us  [to_core(): return lax.ppermute(x, 'chol', [(i, i ^ 1) for i in range(groups)])]
    pallas_call x2, Pallas kernels: 2.58 us -> 1.43 us  [prepare_block(): pl.pallas_call(prepare_kernel, in_specs=[VMEM], out_specs=[VMEM, VMEM], o...]
    pallas_call x2, Pallas kernels: 7.79 us -> 6.76 us  [chip_terms(): pl.pallas_call(functools.partial(terms_kernel, first=first, count=count,...]
    unnamed x8, local copies, waits for them, and re-layouts: 2.25 us -> 1.6 us
  transfers between devices with their start and end apart: 9 -> 9, of which waited for: 5 -> 5; matrix products, arithmetic and copies ran while one was open for 0% -> 0% of each run, Pallas kernels for 16% -> 12%
where the time goes in v7:
time: 41.1 us; the launch traced here: 40.9 us
  starting transfers between devices  11.4 us (28%)
  blocking collectives  11 us (27%)
  Pallas kernels  9.53 us (23%)
  waiting for transfers between devices  6.69 us (16%)
  local copies, waits for them, and re-layouts  1.6 us (4%)
  between operations  0.68 us (2%)
    all_to_all x1, blocking collectives, body(): lax.all_to_all(rows, 'chol', split_axis=0, concat_axis=0, tiled=True, axi...  11 us
    ppermute x7, starting transfers between devices, to_chip(): lax.ppermute(x, 'chol', [(i, i ^ offset * CORES) for i in range(groups)])  10.8 us
    pallas_call x2, Pallas kernels, chip_terms(): pl.pallas_call(functools.partial(terms_kernel, first=first, count=count,...  6.76 us
    ppermute x7, waiting for transfers between devices, to_chip(): lax.ppermute(x, 'chol', [(i, i ^ offset * CORES) for i in range(groups)])  6.68 us
    unnamed x8, local copies, waits for them, and re-layouts  1.6 us
    pallas_call x2, Pallas kernels, prepare_block(): pl.pallas_call(prepare_kernel, in_specs=[VMEM], out_specs=[VMEM, VMEM], o...  1.43 us
    pallas_call x1, Pallas kernels, finish(): pl.pallas_call(functools.partial(finish_kernel, used=used, scale=scale),...  1.34 us
  transfers between devices with their start and end apart: 9, of which 5 were waited for; matrix products, arithmetic and copies ran while one was open for 0% of the time, Pallas kernels for 12%

profile of v7, /device:TPU:0, one launch (start us, length us, event | category | flops | bytes accessed | tf_op | source)
XLA Modules:
  0.0 40.9 jit_solution(9899999712764079142)
XLA Ops:
  0.6 0.5 %collective-permute-start = (bf16[1,4,32,64,128]{4,3,2,1,0:T(8,128)(2,1)}, bf16[1,4,32,64,128]{4,3,2,1,0:T(8,128)(2,1)S(1)}, u32[]{:S(2)}, u32[]{:S(2)}) collective-permute-start(bf16[1,4,32,64,128]{4,3,2,1,0:T(8,128)(2,1)} %chol_ref.1), channel_id=1, source_target_pairs={{0,1},{1,0},{2,3},{3,2},{4,5},{5,4},{6,7},{7,6},{8,9},{9,8},{10,11... | collective-permute-start | bytes 6291464 | tf_op jit(solution)/shard_map/ppermute | solution.py:256
  1.1 3.7 %collective-permute-start.2 = (bf16[1,64,1280]{2,1,0:T(8,128)(2,1)}, bf16[1,64,1280]{2,1,0:T(8,128)(2,1)S(1)}, u32[]{:S(2)}, u32[]{:S(2)}) collective-permute-start(bf16[1,64,1280]{2,1,0:T(8,128)(2,1)} %refs_6_.1), channel_id=1, source_target_pairs={{0,8},{1,9},{2,10},{3,11},{4,12},{5,13},{6,14},{7,15},{8,0},{9,1},... | collective-permute-start | bytes 491528 | tf_op jit(solution)/shard_map/ppermute | solution.py:253
  4.8 1.6 %collective-permute-start.7 = (bf16[1,64,1280]{2,1,0:T(8,128)(2,1)}, bf16[1,64,1280]{2,1,0:T(8,128)(2,1)S(1)}, u32[]{:S(2)}, u32[]{:S(2)}) collective-permute-start(bf16[1,64,1280]{2,1,0:T(8,128)(2,1)} %refs_6_.1), channel_id=1, source_target_pairs={{0,4},{1,5},{2,6},{3,7},{4,0},{5,1},{6,2},{7,3},{8,12},{9,13},{10,... | collective-permute-start | bytes 491528 | tf_op jit(solution)/shard_map/ppermute | solution.py:253
  6.4 1.5 %collective-permute-start.6 = (bf16[1,64,1280]{2,1,0:T(8,128)(2,1)}, bf16[1,64,1280]{2,1,0:T(8,128)(2,1)S(1)}, u32[]{:S(2)}, u32[]{:S(2)}) collective-permute-start(bf16[1,64,1280]{2,1,0:T(8,128)(2,1)} %refs_6_.1), channel_id=1, source_target_pairs={{0,2},{1,3},{2,0},{3,1},{4,6},{5,7},{6,4},{7,5},{8,10},{9,11},{10,... | collective-permute-start | bytes 491528 | tf_op jit(solution)/shard_map/ppermute | solution.py:253
  7.9 0.4 collective-permute-start.8
  8.3 0.0 copy-start
  8.3 1.6 %copy-done = bf16[1,4,32,64,128]{4,3,2,1,0:T(8,128)(2,1)S(1)} copy-done((bf16[1,4,32,64,128]{4,3,2,1,0:T(8,128)(2,1)S(1)}, bf16[1,4,32,64,128]{4,3,2,1,0:T(8,128)(2,1)}, u32[]{:S(2)}) %copy-start) | copy-done | bytes 2097176
  9.9 0.0 copy-start.3
  9.9 0.0 copy-start.1
  9.9 0.0 copy-start.2
  9.9 0.7 %prepare_block.3 = (bf16[2048,512]{1,0:T(8,128)(2,1)S(1)}, bf16[512,2048]{1,0:T(8,128)(2,1)S(1)}) custom-call(bf16[1,4,32,64,128]{4,3,2,1,0:T(8,128)(2,1)S(1)} %copy-done), custom_call_target="tpu_custom_call" | custom-call | tf_op jit(solution)/shard_map/prepare_block/pallas_call | solution.py:34
  10.6 2.8 %collective-permute-done.2.refs_6_ = bf16[1,64,1280]{2,1,0:T(8,128)(2,1)S(1)} collective-permute-done((bf16[1,64,1280]{2,1,0:T(8,128)(2,1)}, bf16[1,64,1280]{2,1,0:T(8,128)(2,1)S(1)}, u32[]{:S(2)}, u32[]{:S(2)}) %collective-permute-start.2) | collective-permute-done | bytes 163872 | tf_op jit(solution)/shard_map/ppermute | solution.py:253
  13.4 1.7 %collective-permute-start.5 = (bf16[1,64,1280]{2,1,0:T(8,128)(2,1)S(1)}, bf16[1,64,1280]{2,1,0:T(8,128)(2,1)S(1)}, u32[]{:S(2)}, u32[]{:S(2)}) collective-permute-start(bf16[1,64,1280]{2,1,0:T(8,128)(2,1)S(1)} %collective-permute-done.2.refs_6_), channel_id=1, source_target_pairs={{0,6},{1,7},{2,4},{3,5},{4,2},{5,3},{6,0},{7,1},{8,14},{9,15},{10,... | collective-permute-start | bytes 491528 | tf_op jit(solution)/shard_map/ppermute | solution.py:253
  15.2 0.0 collective-permute-done.7.refs_8_
  15.2 1.3 %collective-permute-start.4 = (bf16[1,64,1280]{2,1,0:T(8,128)(2,1)S(1)}, bf16[1,64,1280]{2,1,0:T(8,128)(2,1)S(1)}, u32[]{:S(2)}, u32[]{:S(2)}) collective-permute-start(bf16[1,64,1280]{2,1,0:T(8,128)(2,1)S(1)} %collective-permute-done.2.refs_6_), channel_id=1, source_target_pairs={{0,4},{1,5},{2,6},{3,7},{4,0},{5,1},{6,2},{7,3},{8,12},{9,13},{10,... | collective-permute-start | bytes 491528 | tf_op jit(solution)/shard_map/ppermute | solution.py:253
  16.5 0.0 collective-permute-done.chol_ref
  16.5 0.6 %collective-permute-start.3 = (bf16[1,64,1280]{2,1,0:T(8,128)(2,1)S(1)}, bf16[1,64,1280]{2,1,0:T(8,128)(2,1)S(1)}, u32[]{:S(2)}, u32[]{:S(2)}) collective-permute-start(bf16[1,64,1280]{2,1,0:T(8,128)(2,1)S(1)} %collective-permute-done.2.refs_6_), channel_id=1, source_target_pairs={{0,2},{1,3},{2,0},{3,1},{4,6},{5,7},{6,4},{7,5},{8,10},{9,11},{10,... | collective-permute-start | bytes 491528 | tf_op jit(solution)/shard_map/ppermute | solution.py:253
  17.1 0.7 %prepare_block.2 = (bf16[2048,512]{1,0:T(8,128)(2,1)S(1)}, bf16[512,2048]{1,0:T(8,128)(2,1)S(1)}) custom-call(bf16[1,4,32,64,128]{4,3,2,1,0:T(8,128)(2,1)S(1)} %collective-permute-done.chol_ref), custom_call_target="tpu_custom_call" | custom-call | tf_op jit(solution)/shard_map/prepare_block/pallas_call | solution.py:34
  17.8 0.0 collective-permute-done.6.refs_7_
  17.8 0.0 copy-done.3
  17.8 0.1 collective-permute-start.1
  17.9 1.1 %collective-permute-done.8.refs_9_ = bf16[1,64,1280]{2,1,0:T(8,128)(2,1)S(1)} collective-permute-done((bf16[1,64,1280]{2,1,0:T(8,128)(2,1)}, bf16[1,64,1280]{2,1,0:T(8,128)(2,1)S(1)}, u32[]{:S(2)}, u32[]{:S(2)}) %collective-permute-start.8) | collective-permute-done | bytes 163872 | tf_op jit(solution)/shard_map/ppermute | solution.py:253
  19.0 0.0 collective-permute-done.1.refs_1_
  19.0 0.0 copy-done.1
  19.0 0.0 copy-done.2
  19.0 3.4 %chip_terms.2.refs_10_ = f32[8,1,128]{2,1,0:T(1,128)S(1)} custom-call(s32[4,16]{1,0:T(4,128)S(1)} %bitcast.2, s32[1,4]{1,0:T(1,128)S(1)} %copy-done.3, s32[1,4]{1,0:T(1,128)S(1)} %collective-permute-done.1.refs_1_, bf16[2048,512]{1,0:T(8,128)(2,1)S(1)} %get-tuple-element.15.refs_2_, bf16[512,2048]{1,0:T(8,128)(2,1)S(1)} %get-tuple-element.16.refs_3_, ...), custom_call_target="tpu_custom_call" | custom-call | tf_op jit(solution)/shard_map/chip_terms/pallas_call | solution.py:186
  22.4 0.1 collective-permute-done.5.refs_9_
  22.5 1.7 %collective-permute-done.4.refs_8_ = bf16[1,64,1280]{2,1,0:T(8,128)(2,1)S(1)} collective-permute-done((bf16[1,64,1280]{2,1,0:T(8,128)(2,1)S(1)}, bf16[1,64,1280]{2,1,0:T(8,128)(2,1)S(1)}, u32[]{:S(2)}, u32[]{:S(2)}) %collective-permute-start.4) | collective-permute-done | bytes 163872 | tf_op jit(solution)/shard_map/ppermute | solution.py:253
  24.2 1.0 %collective-permute-done.3.refs_7_ = bf16[1,64,1280]{2,1,0:T(8,128)(2,1)S(1)} collective-permute-done((bf16[1,64,1280]{2,1,0:T(8,128)(2,1)S(1)}, bf16[1,64,1280]{2,1,0:T(8,128)(2,1)S(1)}, u32[]{:S(2)}, u32[]{:S(2)}) %collective-permute-start.3) | collective-permute-done | bytes 163872 | tf_op jit(solution)/shard_map/ppermute | solution.py:253
  25.2 3.4 %chip_terms.3 = f32[8,1,128]{2,1,0:T(1,128)S(1)} custom-call(s32[4,16]{1,0:T(4,128)S(1)} %bitcast.3, s32[1,4]{1,0:T(1,128)S(1)} %copy-done.3, s32[1,4]{1,0:T(1,128)S(1)} %collective-permute-done.1.refs_1_, bf16[2048,512]{1,0:T(8,128)(2,1)S(1)} %get-tuple-element.15.refs_2_, bf16[512,2048]{1,0:T(8,128)(2,1)S(1)} %get-tuple-element.16.refs_3_, ...), custom_call_target="tpu_custom_call" | custom-call | tf_op jit(solution)/shard_map/chip_terms/pallas_call | solution.py:186
  28.6 11.0 %all_to_all.5.rows_ref = f32[8,1,128]{2,1,0:T(1,128)} all-to-all(f32[8,1,128]{2,1,0:T(1,128)S(1)} %chip_terms.3), channel_id=1, replica_groups={{0,2,4,6,8,10,12,14},{1,3,5,7,9,11,13,15},{16,18,20,22,24,26,28,30},{17..., dimensions={0} | all-to-all | bytes 8192 | tf_op jit(solution)/shard_map/all_to_all | solution.py:271
  39.5 1.3 %finish.1 = (f32[1,512]{1,0:T(1,128)}, f32[1,1]{1,0:T(1,128)}) custom-call(f32[8,1,128]{2,1,0:T(1,128)} %all_to_all.5.rows_ref), custom_call_target="tpu_custom_call" | custom-call | tf_op jit(solution)/shard_map/finish/pallas_call | solution.py:231
Async XLA Ops:
  0.6 15.9 %collective-permute-start = (bf16[1,4,32,64,128]{4,3,2,1,0:T(8,128)(2,1)}, bf16[1,4,32,64,128]{4,3,2,1,0:T(8,128)(2,1)S(1)}, u32[]{:S(2)}, u32[]{:S(2)}) collective-permute-start(bf16[1,4,32,64,128]{4,3,2,1,0:T(8,128)(2,1)} %chol_ref.1), channel_id=1, source_target_pairs={{0,1},{1,0},{2,3},{3,2},{4,5},{5,4},{6,7},{7,6},{8,9},{9,8},{10,11... | collective-permute-start | bytes 6291464 | tf_op jit(solution)/shard_map/ppermute | solution.py:256
  1.1 12.3 %collective-permute-start.2 = (bf16[1,64,1280]{2,1,0:T(8,128)(2,1)}, bf16[1,64,1280]{2,1,0:T(8,128)(2,1)S(1)}, u32[]{:S(2)}, u32[]{:S(2)}) collective-permute-start(bf16[1,64,1280]{2,1,0:T(8,128)(2,1)} %refs_6_.1), channel_id=1, source_target_pairs={{0,8},{1,9},{2,10},{3,11},{4,12},{5,13},{6,14},{7,15},{8,0},{9,1},... | collective-permute-start | bytes 491528 | tf_op jit(solution)/shard_map/ppermute | solution.py:253
  4.8 10.4 %collective-permute-start.7 = (bf16[1,64,1280]{2,1,0:T(8,128)(2,1)}, bf16[1,64,1280]{2,1,0:T(8,128)(2,1)S(1)}, u32[]{:S(2)}, u32[]{:S(2)}) collective-permute-start(bf16[1,64,1280]{2,1,0:T(8,128)(2,1)} %refs_6_.1), channel_id=1, source_target_pairs={{0,4},{1,5},{2,6},{3,7},{4,0},{5,1},{6,2},{7,3},{8,12},{9,13},{10,... | collective-permute-start | bytes 491528 | tf_op jit(solution)/shard_map/ppermute | solution.py:253
  6.4 11.4 %collective-permute-start.6 = (bf16[1,64,1280]{2,1,0:T(8,128)(2,1)}, bf16[1,64,1280]{2,1,0:T(8,128)(2,1)S(1)}, u32[]{:S(2)}, u32[]{:S(2)}) collective-permute-start(bf16[1,64,1280]{2,1,0:T(8,128)(2,1)} %refs_6_.1), channel_id=1, source_target_pairs={{0,2},{1,3},{2,0},{3,1},{4,6},{5,7},{6,4},{7,5},{8,10},{9,11},{10,... | collective-permute-start | bytes 491528 | tf_op jit(solution)/shard_map/ppermute | solution.py:253
  7.9 11.1 %collective-permute-start.8 = (bf16[1,64,1280]{2,1,0:T(8,128)(2,1)}, bf16[1,64,1280]{2,1,0:T(8,128)(2,1)S(1)}, u32[]{:S(2)}, u32[]{:S(2)}) collective-permute-start(bf16[1,64,1280]{2,1,0:T(8,128)(2,1)} %refs_6_.1), channel_id=1, source_target_pairs={{0,6},{1,7},{2,4},{3,5},{4,2},{5,3},{6,0},{7,1},{8,14},{9,15},{10,... | collective-permute-start | bytes 491528 | tf_op jit(solution)/shard_map/ppermute | solution.py:253
  8.3 1.6 %copy-start = (bf16[1,4,32,64,128]{4,3,2,1,0:T(8,128)(2,1)S(1)}, bf16[1,4,32,64,128]{4,3,2,1,0:T(8,128)(2,1)}, u32[]{:S(2)}) copy-start(bf16[1,4,32,64,128]{4,3,2,1,0:T(8,128)(2,1)} %chol_ref.1) | copy-start | bytes 6291460
  9.9 7.9 %copy-start.3 = (s32[1,4]{1,0:T(1,128)S(1)}, s32[1,4]{1,0:T(1,128)}, u32[]{:S(2)}) copy-start(s32[1,4]{1,0:T(1,128)} %refs_0_.3) | copy-start | bytes 52
  9.9 9.1 %copy-start.1 = (bf16[1,64,1280]{2,1,0:T(8,128)(2,1)S(1)}, bf16[1,64,1280]{2,1,0:T(8,128)(2,1)}, u32[]{:S(2)}) copy-start(bf16[1,64,1280]{2,1,0:T(8,128)(2,1)} %refs_6_.1) | copy-start | bytes 491524
  9.9 9.1 %copy-start.2 = (s32[16,4]{0,1:T(4,128)S(1)}, s32[16,4]{0,1:T(4,128)}, u32[]{:S(2)}) copy-start(s32[16,4]{0,1:T(4,128)} %param.7) | copy-start | bytes 772
  13.4 9.1 %collective-permute-start.5 = (bf16[1,64,1280]{2,1,0:T(8,128)(2,1)S(1)}, bf16[1,64,1280]{2,1,0:T(8,128)(2,1)S(1)}, u32[]{:S(2)}, u32[]{:S(2)}) collective-permute-start(bf16[1,64,1280]{2,1,0:T(8,128)(2,1)S(1)} %collective-permute-done.2.refs_6_), channel_id=1, source_target_pairs={{0,6},{1,7},{2,4},{3,5},{4,2},{5,3},{6,0},{7,1},{8,14},{9,15},{10,... | collective-permute-start | bytes 491528 | tf_op jit(solution)/shard_map/ppermute | solution.py:253
  15.2 9.0 %collective-permute-start.4 = (bf16[1,64,1280]{2,1,0:T(8,128)(2,1)S(1)}, bf16[1,64,1280]{2,1,0:T(8,128)(2,1)S(1)}, u32[]{:S(2)}, u32[]{:S(2)}) collective-permute-start(bf16[1,64,1280]{2,1,0:T(8,128)(2,1)S(1)} %collective-permute-done.2.refs_6_), channel_id=1, source_target_pairs={{0,4},{1,5},{2,6},{3,7},{4,0},{5,1},{6,2},{7,3},{8,12},{9,13},{10,... | collective-permute-start | bytes 491528 | tf_op jit(solution)/shard_map/ppermute | solution.py:253
  16.5 8.7 %collective-permute-start.3 = (bf16[1,64,1280]{2,1,0:T(8,128)(2,1)S(1)}, bf16[1,64,1280]{2,1,0:T(8,128)(2,1)S(1)}, u32[]{:S(2)}, u32[]{:S(2)}) collective-permute-start(bf16[1,64,1280]{2,1,0:T(8,128)(2,1)S(1)} %collective-permute-done.2.refs_6_), channel_id=1, source_target_pairs={{0,2},{1,3},{2,0},{3,1},{4,6},{5,7},{6,4},{7,5},{8,10},{9,11},{10,... | collective-permute-start | bytes 491528 | tf_op jit(solution)/shard_map/ppermute | solution.py:253
  17.8 1.2 %collective-permute-start.1 = (s32[1,4]{1,0:T(1,128)S(1)}, s32[1,4]{1,0:T(1,128)S(1)}, u32[]{:S(2)}, u32[]{:S(2)}) collective-permute-start(s32[1,4]{1,0:T(1,128)S(1)} %copy-done.3), channel_id=1, source_target_pairs={{0,1},{1,0},{2,3},{3,2},{4,5},{5,4},{6,7},{7,6},{8,9},{9,8},{10,11... | collective-permute-start | bytes 56 | tf_op jit(solution)/shard_map/ppermute | solution.py:256

commit v8 on v7

--- a/solution.py
+++ b/solution.py
@@ -11,6 +11,7 @@
 CORES = 2
 VMEM_LIMIT = 32 * 1024 * 1024
 K_STEP = 16
+TURNED = 8
 BATCH = 4
 VMEM = pl.BlockSpec(memory_space=pltpu.VMEM)
 SMEM = pl.BlockSpec(memory_space=pltpu.SMEM)
@@ -20,29 +21,33 @@
 NN = (((1,), (0,)), ((), ()))
 
 
-def prepare_kernel(chol_ref, block_ref, turned_ref):
+def prepare_kernel(screen_ref, chol_ref, block_ref, turned_ref):
     _, listed, vectors, occupied, width = chol_ref.shape
+    span = TURNED * occupied
     for m in range(listed):
-        tile = chol_ref[0, m].reshape(vectors * occupied, width)
+        keep = jnp.full((1, width), screen_ref[0, m].astype(jnp.float32)).astype(chol_ref.dtype)
+        tile = chol_ref[0, m].reshape(vectors * occupied, width) * keep
         block_ref[:, m * width:(m + 1) * width] = tile
-        turned_ref[m * width:(m + 1) * width, :] = tile.T
-
-
-def prepare_block(chol_tiles):
+        for c in range(vectors // K_STEP):
+            start = c * K_STEP * occupied
+            turned_ref[m * width:(m + 1) * width, c * span:(c + 1) * span] = tile[start:start + span].T
+
+
+def prepare_block(screen, chol_tiles):
     _, listed, vectors, occupied, width = chol_tiles.shape
     rows, depth = vectors * occupied, listed * width
     return pl.pallas_call(
         prepare_kernel,
-        in_specs=[VMEM],
+        in_specs=[SMEM, VMEM],
         out_specs=[VMEM, VMEM],
         out_shape=[
             jax.ShapeDtypeStruct((rows, depth), chol_tiles.dtype),
-            jax.ShapeDtypeStruct((depth, rows), chol_tiles.dtype),
+            jax.ShapeDtypeStruct((depth, rows // K_STEP * TURNED), chol_tiles.dtype),
         ],
         compiler_params=PARAMS,
         cost_estimate=SMALL,
         name="prepare_block",
-    )(chol_tiles)
+    )(screen, chol_tiles)
 
 
 def fold_rows(blocks, sub):
@@ -84,7 +89,8 @@
     for k0 in range(0, vectors, K_STEP):
         span = slice(k0 * occupied, (k0 + K_STEP) * occupied)
         inner_mat = lax.dot_general(block_ref[span, :], theta, NT, preferred_element_type=jnp.float32)
-        flipped = lax.dot_general(theta, turned_ref[:, span], NN, preferred_element_type=jnp.float32)
+        turned = slice(k0 // K_STEP * TURNED * occupied, (k0 // K_STEP + 1) * TURNED * occupied)
+        flipped = lax.dot_general(theta, turned_ref[:, turned], NN, preferred_element_type=jnp.float32)
         for k8 in range(0, K_STEP, 8):
             for t in range(tiles):
                 c0 = t * LANES
@@ -93,8 +99,11 @@
                     r0 = k * occupied
                     top = inner_mat[r0:r0 + occupied, c0:c0 + LANES]
                     bottom = inner_mat[r0 + occupied:r0 + 2 * occupied, c0:c0 + LANES]
-                    f_top = flipped[c0:c0 + occupied, r0:r0 + LANES]
-                    f_bottom = flipped[c0 + occupied:c0 + 2 * occupied, r0:r0 + LANES]
+                    if k < TURNED:
+                        other = flipped[c0:c0 + LANES, r0:r0 + LANES]
+                    else:
+                        other = inner_mat[r0:r0 + LANES, c0:c0 + LANES].T
+                    f_top, f_bottom = other[:occupied], other[occupied:]
                     swapped = pltpu.roll(jnp.where(low, f_bottom, f_top), occupied, 1)
                     product = jnp.where(low, top, bottom) * jnp.where(low, f_top, f_bottom)
                     product = product + jnp.where(low, bottom, top) * swapped
@@ -104,8 +113,8 @@
                 store_rows(k0 + k8, t, fold_rows(diagonals, sub8))
 
 
-def terms_kernel(list_ref, *refs, first, count, vectors, batch, carried):
-    screen_refs, block_refs, theta_refs, rest = refs[:2], refs[2:6], refs[6:6 + count], refs[6 + count:]
+def terms_kernel(list_ref, *refs, first, count, falling, vectors, batch, carried):
+    block_refs, theta_refs, rest = refs[:4], refs[4:4 + count], refs[4 + count:]
     out_ref, picked_ref, rows_ref = rest[-3:]
     listed = list_ref.shape[0]
     _, occupied, _ = theta_refs[0].shape
@@ -121,11 +130,8 @@
     for b, group in enumerate((me, me ^ 1)):
         for m in range(listed):
             start = pl.multiple_of(list_ref[m, group] * width, width)
-            keep = jnp.full((1, width), screen_refs[b][0, m].astype(jnp.float32)).astype(picked_ref.dtype)
             for i, ref in enumerate(theta_refs):
-                picked_ref[b, i * occupied:(i + 1) * occupied, m * width:(m + 1) * width] = (
-                    ref[0, :, pl.ds(start, width)] * keep
-                )
+                picked_ref[b, i * occupied:(i + 1) * occupied, m * width:(m + 1) * width] = ref[0, :, pl.ds(start, width)]
 
     if carried:
         out_ref[...] = rest[0][...]
@@ -164,7 +170,8 @@
             sums[:, used:used + 8], axis=1, keepdims=True
         )
         for i in range(batch):
-            owner = chip ^ (first + index + i)
+            place = lax.rem(count - index - i, count) if falling else index + i
+            owner = chip ^ (first + place)
             out_ref[pl.ds(owner, 1), 0, :used] = bias[i:i + 1]
             out_ref[pl.ds(owner, 1), 0, used:used + 1] = energy[i:i + 1]
 
@@ -176,18 +183,21 @@
             one_batch(step * batch)
 
 
-def chip_terms(listing, screens, blocks, thetas, carried, first, vectors, out_width):
+def chip_terms(listing, blocks, thetas, carried, first, falling, vectors, out_width):
     count = len(thetas)
+    if falling:
+        thetas = thetas[:1] + thetas[:0:-1]
     batch = min(count, BATCH)
     _, occupied, _ = thetas[0].shape
     chips = listing.shape[1] // CORES
     depth = blocks[0].shape[1]
-    operands = [listing, *screens, *blocks, *thetas] + ([] if carried is None else [carried])
+    operands = [listing, *blocks, *thetas] + ([] if carried is None else [carried])
     return pl.pallas_call(
         functools.partial(
-            terms_kernel, first=first, count=count, vectors=vectors, batch=batch, carried=carried is not None
+            terms_kernel, first=first, count=count, falling=falling, vectors=vectors, batch=batch,
+            carried=carried is not None,
         ),
-        in_specs=[SMEM] * 3 + [VMEM] * (len(operands) - 3),
+        in_specs=[SMEM] + [VMEM] * (len(operands) - 1),
         out_specs=VMEM,
         out_shape=jax.ShapeDtypeStruct((chips, 1, out_width), jnp.float32),
         scratch_shapes=[
@@ -257,16 +267,15 @@
 
     far = to_chip(theta, half)
     near = [theta] + [to_chip(theta, offset) for offset in range(1, half)]
-    own, own_turned = prepare_block(chol_tiles)
-    far, own = lax.optimization_barrier((far, own))
+    own, own_turned = prepare_block(screen, chol_tiles)
+    near[1], near[2], own, far = lax.optimization_barrier((near[1], near[2], own, far))
     beyond = [far] + [to_chip(far, offset) for offset in range(1, half)]
-    other, other_turned = prepare_block(to_core(chol_tiles))
-    other, late_screen = lax.optimization_barrier((other, screen))
-    screens = [screen, to_core(late_screen)]
+    other_chol, late_screen, near[-1] = lax.optimization_barrier((to_core(chol_tiles), screen, near[-1]))
+    other, other_turned = prepare_block(to_core(late_screen), other_chol)
     blocks = [own, own_turned, other, other_turned]
 
-    rows = chip_terms(listing, screens, blocks, near, None, 0, vectors, out_width)
-    rows = chip_terms(listing, screens, blocks, beyond, rows, half, vectors, out_width)
+    rows = chip_terms(listing, blocks, near, None, 0, False, vectors, out_width)
+    rows = chip_terms(listing, blocks, beyond, rows, half, True, vectors, out_width)
     same_core = [list(range(core, groups, CORES)) for core in range(CORES)]
     back = lax.all_to_all(rows, "chol", split_axis=0, concat_axis=0, tiled=True, axis_index_groups=same_core)
     return finish(back, used, 1.0 / (2.0 * occupied * occupied))

time: 41.1 us -> 41.3 us (level)
  waiting for transfers between devices: 6.69 us -> 5.71 us
  local copies, waits for them, and re-layouts: 1.6 us -> 2.25 us
  Pallas kernels: 9.53 us -> 9.99 us
    ppermute x7, waiting for transfers between devices: 6.68 us -> 4.59 us  [to_chip(): lax.ppermute(x, 'chol', [(i, i ^ offset * CORES) for i in range(groups)])]
    ppermute x2, waiting for transfers between devices: 0.01 us -> 1.12 us  [to_core(): return lax.ppermute(x, 'chol', [(i, i ^ 1) for i in range(groups)])]
    pallas_call x2, Pallas kernels: 1.43 us -> 2.12 us  [prepare_block(): pl.pallas_call(prepare_kernel, in_specs=[SMEM, VMEM], out_specs=[VMEM, VM...]
    unnamed x8, local copies, waits for them, and re-layouts: 1.6 us -> 2.25 us
  transfers between devices with their start and end apart: 9 -> 9, of which waited for: 5 -> 5; matrix products, arithmetic and copies ran while one was open for 0% -> 0% of each run, Pallas kernels for 12% -> 13%
where the time goes in v8:
time: 41.3 us; the launch traced here: 41 us
  starting transfers between devices  11.2 us (27%)
  blocking collectives  11.2 us (27%)
  Pallas kernels  9.99 us (24%)
  waiting for transfers between devices  5.71 us (14%)
  local copies, waits for them, and re-layouts  2.25 us (5%)
  between operations  0.68 us (2%)
    all_to_all x1, blocking collectives, body(): lax.all_to_all(rows, 'chol', split_axis=0, concat_axis=0, tiled=True, axi...  11.2 us
    ppermute x7, starting transfers between devices, to_chip(): lax.ppermute(x, 'chol', [(i, i ^ offset * CORES) for i in range(groups)])  10.6 us
    pallas_call x2, Pallas kernels, chip_terms(): pl.pallas_call(functools.partial(terms_kernel, first=first, count=count,...  6.53 us
    ppermute x7, waiting for transfers between devices, to_chip(): lax.ppermute(x, 'chol', [(i, i ^ offset * CORES) for i in range(groups)])  4.59 us
    unnamed x8, local copies, waits for them, and re-layouts  2.25 us
    pallas_call x2, Pallas kernels, prepare_block(): pl.pallas_call(prepare_kernel, in_specs=[SMEM, VMEM], out_specs=[VMEM, VM...  2.12 us
    pallas_call x1, Pallas kernels, finish(): pl.pallas_call(functools.partial(finish_kernel, used=used, scale=scale),...  1.34 us
    ppermute x2, waiting for transfers between devices, to_core(): return lax.ppermute(x, 'chol', [(i, i ^ 1) for i in range(groups)])  1.12 us
  transfers between devices with their start and end apart: 9, of which 5 were waited for; matrix products, arithmetic and copies ran while one was open for 0% of the time, Pallas kernels for 13%

profile of v8, /device:TPU:0, one launch (start us, length us, event | category | flops | bytes accessed | tf_op | source)
XLA Modules:
  0.0 41.0 jit_solution(10846016014952905499)
XLA Ops:
  0.6 0.5 %collective-permute-start.3 = (bf16[1,4,32,64,128]{4,3,2,1,0:T(8,128)(2,1)}, bf16[1,4,32,64,128]{4,3,2,1,0:T(8,128)(2,1)S(1)}, u32[]{:S(2)}, u32[]{:S(2)}) collective-permute-start(bf16[1,4,32,64,128]{4,3,2,1,0:T(8,128)(2,1)} %chol_ref.1), channel_id=1, source_target_pairs={{0,1},{1,0},{2,3},{3,2},{4,5},{5,4},{6,7},{7,6},{8,9},{9,8},{10,11... | collective-permute-start | bytes 6291464 | tf_op jit(solution)/shard_map/ppermute | solution.py:266
  1.1 3.7 %collective-permute-start.2 = (bf16[1,64,1280]{2,1,0:T(8,128)(2,1)}, bf16[1,64,1280]{2,1,0:T(8,128)(2,1)S(1)}, u32[]{:S(2)}, u32[]{:S(2)}) collective-permute-start(bf16[1,64,1280]{2,1,0:T(8,128)(2,1)} %refs_4_.1), channel_id=1, source_target_pairs={{0,8},{1,9},{2,10},{3,11},{4,12},{5,13},{6,14},{7,15},{8,0},{9,1},... | collective-permute-start | bytes 491528 | tf_op jit(solution)/shard_map/ppermute | solution.py:263
  4.8 1.6 %collective-permute-start.1 = (bf16[1,64,1280]{2,1,0:T(8,128)(2,1)}, bf16[1,64,1280]{2,1,0:T(8,128)(2,1)S(1)}, u32[]{:S(2)}, u32[]{:S(2)}) collective-permute-start(bf16[1,64,1280]{2,1,0:T(8,128)(2,1)} %refs_4_.1), channel_id=1, source_target_pairs={{0,4},{1,5},{2,6},{3,7},{4,0},{5,1},{6,2},{7,3},{8,12},{9,13},{10,... | collective-permute-start | bytes 491528 | tf_op jit(solution)/shard_map/ppermute | solution.py:263
  6.4 1.5 %collective-permute-start = (bf16[1,64,1280]{2,1,0:T(8,128)(2,1)}, bf16[1,64,1280]{2,1,0:T(8,128)(2,1)S(1)}, u32[]{:S(2)}, u32[]{:S(2)}) collective-permute-start(bf16[1,64,1280]{2,1,0:T(8,128)(2,1)} %refs_4_.1), channel_id=1, source_target_pairs={{0,2},{1,3},{2,0},{3,1},{4,6},{5,7},{6,4},{7,5},{8,10},{9,11},{10,... | collective-permute-start | bytes 491528 | tf_op jit(solution)/shard_map/ppermute | solution.py:263
  7.9 0.4 collective-permute-start.4
  8.3 0.0 copy-start
  8.3 1.6 %copy-done = bf16[1,4,32,64,128]{4,3,2,1,0:T(8,128)(2,1)S(1)} copy-done((bf16[1,4,32,64,128]{4,3,2,1,0:T(8,128)(2,1)S(1)}, bf16[1,4,32,64,128]{4,3,2,1,0:T(8,128)(2,1)}, u32[]{:S(2)}) %copy-start) | copy-done | bytes 2097176
  9.9 0.0 copy-start.3
  9.9 0.7 %copy-done.3 = s32[1,4]{1,0:T(1,128)S(1)} copy-done((s32[1,4]{1,0:T(1,128)S(1)}, s32[1,4]{1,0:T(1,128)}, u32[]{:S(2)}) %copy-start.3) | copy-done | bytes 40
  10.5 0.0 copy-start.1
  10.5 0.0 copy-start.2
  10.6 1.1 %prepare_block.2 = (bf16[2048,512]{1,0:T(8,128)(2,1)S(1)}, bf16[512,1024]{1,0:T(8,128)(2,1)S(1)}) custom-call(s32[1,4]{1,0:T(1,128)S(1)} %copy-done.3, bf16[1,4,32,64,128]{4,3,2,1,0:T(8,128)(2,1)S(1)} %copy-done), custom_call_target="tpu_custom_call" | custom-call | tf_op jit(solution)/shard_map/prepare_block/pallas_call | solution.py:39
  11.6 1.8 %collective-permute-done.2.refs_4_ = bf16[1,64,1280]{2,1,0:T(8,128)(2,1)S(1)} collective-permute-done((bf16[1,64,1280]{2,1,0:T(8,128)(2,1)}, bf16[1,64,1280]{2,1,0:T(8,128)(2,1)S(1)}, u32[]{:S(2)}, u32[]{:S(2)}) %collective-permute-start.2) | collective-permute-done | bytes 163872 | tf_op jit(solution)/shard_map/ppermute | solution.py:263
  13.4 1.0 %collective-permute-done.1.refs_6_ = bf16[1,64,1280]{2,1,0:T(8,128)(2,1)S(1)} collective-permute-done((bf16[1,64,1280]{2,1,0:T(8,128)(2,1)}, bf16[1,64,1280]{2,1,0:T(8,128)(2,1)S(1)}, u32[]{:S(2)}, u32[]{:S(2)}) %collective-permute-start.1) | collective-permute-done | bytes 163872 | tf_op jit(solution)/shard_map/ppermute | solution.py:263
  14.4 0.0 collective-permute-done.refs_5_
  14.4 1.6 %collective-permute-start.8 = (bf16[1,64,1280]{2,1,0:T(8,128)(2,1)S(1)}, bf16[1,64,1280]{2,1,0:T(8,128)(2,1)S(1)}, u32[]{:S(2)}, u32[]{:S(2)}) collective-permute-start(bf16[1,64,1280]{2,1,0:T(8,128)(2,1)S(1)} %collective-permute-done.2.refs_4_), channel_id=1, source_target_pairs={{0,2},{1,3},{2,0},{3,1},{4,6},{5,7},{6,4},{7,5},{8,10},{9,11},{10,... | collective-permute-start | bytes 491528 | tf_op jit(solution)/shard_map/ppermute | solution.py:263
  16.0 1.1 %collective-permute-start.7 = (bf16[1,64,1280]{2,1,0:T(8,128)(2,1)S(1)}, bf16[1,64,1280]{2,1,0:T(8,128)(2,1)S(1)}, u32[]{:S(2)}, u32[]{:S(2)}) collective-permute-start(bf16[1,64,1280]{2,1,0:T(8,128)(2,1)S(1)} %collective-permute-done.2.refs_4_), channel_id=1, source_target_pairs={{0,4},{1,5},{2,6},{3,7},{4,0},{5,1},{6,2},{7,3},{8,12},{9,13},{10,... | collective-permute-start | bytes 491528 | tf_op jit(solution)/shard_map/ppermute | solution.py:263
  17.1 0.8 %collective-permute-start.6 = (bf16[1,64,1280]{2,1,0:T(8,128)(2,1)S(1)}, bf16[1,64,1280]{2,1,0:T(8,128)(2,1)S(1)}, u32[]{:S(2)}, u32[]{:S(2)}) collective-permute-start(bf16[1,64,1280]{2,1,0:T(8,128)(2,1)S(1)} %collective-permute-done.2.refs_4_), channel_id=1, source_target_pairs={{0,6},{1,7},{2,4},{3,5},{4,2},{5,3},{6,0},{7,1},{8,14},{9,15},{10,... | collective-permute-start | bytes 491528 | tf_op jit(solution)/shard_map/ppermute | solution.py:263
  17.9 1.0 %collective-permute-done.4.refs_7_ = bf16[1,64,1280]{2,1,0:T(8,128)(2,1)S(1)} collective-permute-done((bf16[1,64,1280]{2,1,0:T(8,128)(2,1)}, bf16[1,64,1280]{2,1,0:T(8,128)(2,1)S(1)}, u32[]{:S(2)}, u32[]{:S(2)}) %collective-permute-start.4) | collective-permute-done | bytes 163872 | tf_op jit(solution)/shard_map/ppermute | solution.py:263
  18.9 0.0 collective-permute-done.3.chol_ref
  18.9 0.0 collective-permute-start.5
  18.9 1.1 %collective-permute-done.5.screen_ref = s32[1,4]{1,0:T(1,128)S(1)} collective-permute-done((s32[1,4]{1,0:T(1,128)S(1)}, s32[1,4]{1,0:T(1,128)S(1)}, u32[]{:S(2)}, u32[]{:S(2)}) %collective-permute-start.5) | collective-permute-done | bytes 48 | tf_op jit(solution)/shard_map/ppermute | solution.py:266
  20.1 1.1 %prepare_block.3 = (bf16[2048,512]{1,0:T(8,128)(2,1)S(1)}, bf16[512,1024]{1,0:T(8,128)(2,1)S(1)}) custom-call(s32[1,4]{1,0:T(1,128)S(1)} %collective-permute-done.5.screen_ref, bf16[1,4,32,64,128]{4,3,2,1,0:T(8,128)(2,1)S(1)} %collective-permute-done.3.chol_ref), custom_call_target="tpu_custom_call" | custom-call | tf_op jit(solution)/shard_map/prepare_block/pallas_call | solution.py:39
  21.1 0.0 copy-done.1
  21.2 0.0 copy-done.2
  21.2 3.3 %chip_terms.2.refs_8_ = f32[8,1,128]{2,1,0:T(1,128)S(1)} custom-call(s32[4,16]{1,0:T(4,128)S(1)} %bitcast.2, bf16[2048,512]{1,0:T(8,128)(2,1)S(1)} %get-tuple-element.16.refs_0_, bf16[512,1024]{1,0:T(8,128)(2,1)S(1)} %get-tuple-element.17.refs_1_, bf16[2048,512]{1,0:T(8,128)(2,1)S(1)} %get-tuple-element.20.refs_2_, ...), custom_call_target="tpu_custom_call" | custom-call | tf_op jit(solution)/shard_map/chip_terms/pallas_call | solution.py:195
  24.4 0.0 collective-permute-done.8.refs_7_
  24.4 0.0 collective-permute-done.7.refs_6_
  24.5 0.7 %collective-permute-done.6.refs_5_ = bf16[1,64,1280]{2,1,0:T(8,128)(2,1)S(1)} collective-permute-done((bf16[1,64,1280]{2,1,0:T(8,128)(2,1)S(1)}, bf16[1,64,1280]{2,1,0:T(8,128)(2,1)S(1)}, u32[]{:S(2)}, u32[]{:S(2)}) %collective-permute-start.6) | collective-permute-done | bytes 163872 | tf_op jit(solution)/shard_map/ppermute | solution.py:263
  25.2 3.3 %chip_terms.3 = f32[8,1,128]{2,1,0:T(1,128)S(1)} custom-call(s32[4,16]{1,0:T(4,128)S(1)} %bitcast.3, bf16[2048,512]{1,0:T(8,128)(2,1)S(1)} %get-tuple-element.16.refs_0_, bf16[512,1024]{1,0:T(8,128)(2,1)S(1)} %get-tuple-element.17.refs_1_, bf16[2048,512]{1,0:T(8,128)(2,1)S(1)} %get-tuple-element.20.refs_2_, bf16[512,1024]{1,0:T(8,128)(2,1)S(1)} %get-tuple-element.21.refs_3_, ...), custom_call_target="tpu_custom_call" | custom-call | tf_op jit(solution)/shard_map/chip_terms/pallas_call | solution.py:195
  28.5 11.2 %all_to_all.5.rows_ref = f32[8,1,128]{2,1,0:T(1,128)} all-to-all(f32[8,1,128]{2,1,0:T(1,128)S(1)} %chip_terms.3), channel_id=1, replica_groups={{0,2,4,6,8,10,12,14},{1,3,5,7,9,11,13,15},{16,18,20,22,24,26,28,30},{17..., dimensions={0} | all-to-all | bytes 8192 | tf_op jit(solution)/shard_map/all_to_all | solution.py:280
  39.7 1.3 %finish.1 = (f32[1,512]{1,0:T(1,128)}, f32[1,1]{1,0:T(1,128)}) custom-call(f32[8,1,128]{2,1,0:T(1,128)} %all_to_all.5.rows_ref), custom_call_target="tpu_custom_call" | custom-call | tf_op jit(solution)/shard_map/finish/pallas_call | solution.py:241
Async XLA Ops:
  0.6 18.3 %collective-permute-start.3 = (bf16[1,4,32,64,128]{4,3,2,1,0:T(8,128)(2,1)}, bf16[1,4,32,64,128]{4,3,2,1,0:T(8,128)(2,1)S(1)}, u32[]{:S(2)}, u32[]{:S(2)}) collective-permute-start(bf16[1,4,32,64,128]{4,3,2,1,0:T(8,128)(2,1)} %chol_ref.1), channel_id=1, source_target_pairs={{0,1},{1,0},{2,3},{3,2},{4,5},{5,4},{6,7},{7,6},{8,9},{9,8},{10,11... | collective-permute-start | bytes 6291464 | tf_op jit(solution)/shard_map/ppermute | solution.py:266
  1.1 12.3 %collective-permute-start.2 = (bf16[1,64,1280]{2,1,0:T(8,128)(2,1)}, bf16[1,64,1280]{2,1,0:T(8,128)(2,1)S(1)}, u32[]{:S(2)}, u32[]{:S(2)}) collective-permute-start(bf16[1,64,1280]{2,1,0:T(8,128)(2,1)} %refs_4_.1), channel_id=1, source_target_pairs={{0,8},{1,9},{2,10},{3,11},{4,12},{5,13},{6,14},{7,15},{8,0},{9,1},... | collective-permute-start | bytes 491528 | tf_op jit(solution)/shard_map/ppermute | solution.py:263
  4.8 9.6 %collective-permute-start.1 = (bf16[1,64,1280]{2,1,0:T(8,128)(2,1)}, bf16[1,64,1280]{2,1,0:T(8,128)(2,1)S(1)}, u32[]{:S(2)}, u32[]{:S(2)}) collective-permute-start(bf16[1,64,1280]{2,1,0:T(8,128)(2,1)} %refs_4_.1), channel_id=1, source_target_pairs={{0,4},{1,5},{2,6},{3,7},{4,0},{5,1},{6,2},{7,3},{8,12},{9,13},{10,... | collective-permute-start | bytes 491528 | tf_op jit(solution)/shard_map/ppermute | solution.py:263
  6.4 8.0 %collective-permute-start = (bf16[1,64,1280]{2,1,0:T(8,128)(2,1)}, bf16[1,64,1280]{2,1,0:T(8,128)(2,1)S(1)}, u32[]{:S(2)}, u32[]{:S(2)}) collective-permute-start(bf16[1,64,1280]{2,1,0:T(8,128)(2,1)} %refs_4_.1), channel_id=1, source_target_pairs={{0,2},{1,3},{2,0},{3,1},{4,6},{5,7},{6,4},{7,5},{8,10},{9,11},{10,... | collective-permute-start | bytes 491528 | tf_op jit(solution)/shard_map/ppermute | solution.py:263
  7.9 11.0 %collective-permute-start.4 = (bf16[1,64,1280]{2,1,0:T(8,128)(2,1)}, bf16[1,64,1280]{2,1,0:T(8,128)(2,1)S(1)}, u32[]{:S(2)}, u32[]{:S(2)}) collective-permute-start(bf16[1,64,1280]{2,1,0:T(8,128)(2,1)} %refs_4_.1), channel_id=1, source_target_pairs={{0,6},{1,7},{2,4},{3,5},{4,2},{5,3},{6,0},{7,1},{8,14},{9,15},{10,... | collective-permute-start | bytes 491528 | tf_op jit(solution)/shard_map/ppermute | solution.py:263
  8.3 1.6 %copy-start = (bf16[1,4,32,64,128]{4,3,2,1,0:T(8,128)(2,1)S(1)}, bf16[1,4,32,64,128]{4,3,2,1,0:T(8,128)(2,1)}, u32[]{:S(2)}) copy-start(bf16[1,4,32,64,128]{4,3,2,1,0:T(8,128)(2,1)} %chol_ref.1) | copy-start | bytes 6291460
  9.9 0.7 %copy-start.3 = (s32[1,4]{1,0:T(1,128)S(1)}, s32[1,4]{1,0:T(1,128)}, u32[]{:S(2)}) copy-start(s32[1,4]{1,0:T(1,128)} %screen_ref.1) | copy-start | bytes 52
  10.5 10.6 %copy-start.1 = (bf16[1,64,1280]{2,1,0:T(8,128)(2,1)S(1)}, bf16[1,64,1280]{2,1,0:T(8,128)(2,1)}, u32[]{:S(2)}) copy-start(bf16[1,64,1280]{2,1,0:T(8,128)(2,1)} %refs_4_.1) | copy-start | bytes 491524
  10.5 10.6 %copy-start.2 = (s32[16,4]{0,1:T(4,128)S(1)}, s32[16,4]{0,1:T(4,128)}, u32[]{:S(2)}) copy-start(s32[16,4]{0,1:T(4,128)} %param.7) | copy-start | bytes 772
  14.4 10.0 %collective-permute-start.8 = (bf16[1,64,1280]{2,1,0:T(8,128)(2,1)S(1)}, bf16[1,64,1280]{2,1,0:T(8,128)(2,1)S(1)}, u32[]{:S(2)}, u32[]{:S(2)}) collective-permute-start(bf16[1,64,1280]{2,1,0:T(8,128)(2,1)S(1)} %collective-permute-done.2.refs_4_), channel_id=1, source_target_pairs={{0,2},{1,3},{2,0},{3,1},{4,6},{5,7},{6,4},{7,5},{8,10},{9,11},{10,... | collective-permute-start | bytes 491528 | tf_op jit(solution)/shard_map/ppermute | solution.py:263
  16.0 8.5 %collective-permute-start.7 = (bf16[1,64,1280]{2,1,0:T(8,128)(2,1)S(1)}, bf16[1,64,1280]{2,1,0:T(8,128)(2,1)S(1)}, u32[]{:S(2)}, u32[]{:S(2)}) collective-permute-start(bf16[1,64,1280]{2,1,0:T(8,128)(2,1)S(1)} %collective-permute-done.2.refs_4_), channel_id=1, source_target_pairs={{0,4},{1,5},{2,6},{3,7},{4,0},{5,1},{6,2},{7,3},{8,12},{9,13},{10,... | collective-permute-start | bytes 491528 | tf_op jit(solution)/shard_map/ppermute | solution.py:263
  17.1 8.1 %collective-permute-start.6 = (bf16[1,64,1280]{2,1,0:T(8,128)(2,1)S(1)}, bf16[1,64,1280]{2,1,0:T(8,128)(2,1)S(1)}, u32[]{:S(2)}, u32[]{:S(2)}) collective-permute-start(bf16[1,64,1280]{2,1,0:T(8,128)(2,1)S(1)} %collective-permute-done.2.refs_4_), channel_id=1, source_target_pairs={{0,6},{1,7},{2,4},{3,5},{4,2},{5,3},{6,0},{7,1},{8,14},{9,15},{10,... | collective-permute-start | bytes 491528 | tf_op jit(solution)/shard_map/ppermute | solution.py:263
  18.9 1.1 %collective-permute-start.5 = (s32[1,4]{1,0:T(1,128)S(1)}, s32[1,4]{1,0:T(1,128)S(1)}, u32[]{:S(2)}, u32[]{:S(2)}) collective-permute-start(s32[1,4]{1,0:T(1,128)S(1)} %copy-done.3), channel_id=1, source_target_pairs={{0,1},{1,0},{2,3},{3,2},{4,5},{5,4},{6,7},{7,6},{8,9},{9,8},{10,11... | collective-permute-start | bytes 56 | tf_op jit(solution)/shard_map/ppermute | solution.py:266

commit v9 on v8

--- a/solution.py
+++ b/solution.py
@@ -10,8 +10,8 @@
 LANES = 128
 CORES = 2
 VMEM_LIMIT = 32 * 1024 * 1024
-K_STEP = 16
-TURNED = 8
+K_STEP = 32
+TURNED = 16
 BATCH = 4
 VMEM = pl.BlockSpec(memory_space=pltpu.VMEM)
 SMEM = pl.BlockSpec(memory_space=pltpu.SMEM)
@@ -266,16 +266,18 @@
         return lax.ppermute(x, "chol", [(i, i ^ 1) for i in range(groups)])
 
     far = to_chip(theta, half)
-    near = [theta] + [to_chip(theta, offset) for offset in range(1, half)]
+    near = [theta] + [to_chip(theta, offset) for offset in range(1, half - 1)]
     own, own_turned = prepare_block(screen, chol_tiles)
-    near[1], near[2], own, far = lax.optimization_barrier((near[1], near[2], own, far))
+    near[1], own, late_theta = lax.optimization_barrier((near[1], own, theta))
+    near.append(to_chip(late_theta, half - 1))
+    far, near[2] = lax.optimization_barrier((far, near[2]))
     beyond = [far] + [to_chip(far, offset) for offset in range(1, half)]
     other_chol, late_screen, near[-1] = lax.optimization_barrier((to_core(chol_tiles), screen, near[-1]))
     other, other_turned = prepare_block(to_core(late_screen), other_chol)
     blocks = [own, own_turned, other, other_turned]
 
     rows = chip_terms(listing, blocks, near, None, 0, False, vectors, out_width)
-    rows = chip_terms(listing, blocks, beyond, rows, half, True, vectors, out_width)
+    rows = chip_terms(listing, blocks, beyond, rows, half, False, vectors, out_width)
     same_core = [list(range(core, groups, CORES)) for core in range(CORES)]
     back = lax.all_to_all(rows, "chol", split_axis=0, concat_axis=0, tiled=True, axis_index_groups=same_core)
     return finish(back, used, 1.0 / (2.0 * occupied * occupied))

time: 41.3 us -> 42.4 us (1.027)
  blocking collectives: 11.2 us -> 11.9 us
  Pallas kernels: 9.99 us -> 10.5 us
    all_to_all x1, blocking collectives: 11.2 us -> 11.9 us  [body(): lax.all_to_all(rows, 'chol', split_axis=0, concat_axis=0, tiled=True, axi...]
    pallas_call x2, Pallas kernels: 6.53 us -> 7.07 us  [chip_terms(): pl.pallas_call(functools.partial(terms_kernel, first=first, count=count,...]
where the time goes in v9:
time: 42.4 us; the launch traced here: 42.1 us
  blocking collectives  11.9 us (28%)
  starting transfers between devices  11.3 us (27%)
  Pallas kernels  10.5 us (25%)
  waiting for transfers between devices  5.47 us (13%)
  local copies, waits for them, and re-layouts  2.25 us (5%)
  between operations  0.69 us (2%)
    all_to_all x1, blocking collectives, body(): lax.all_to_all(rows, 'chol', split_axis=0, concat_axis=0, tiled=True, axi...  11.9 us
    ppermute x7, starting transfers between devices, to_chip(): lax.ppermute(x, 'chol', [(i, i ^ offset * CORES) for i in range(groups)])  10.8 us
    pallas_call x2, Pallas kernels, chip_terms(): pl.pallas_call(functools.partial(terms_kernel, first=first, count=count,...  7.07 us
    ppermute x7, waiting for transfers between devices, to_chip(): lax.ppermute(x, 'chol', [(i, i ^ offset * CORES) for i in range(groups)])  4.34 us
    unnamed x8, local copies, waits for them, and re-layouts  2.25 us
    pallas_call x2, Pallas kernels, prepare_block(): pl.pallas_call(prepare_kernel, in_specs=[SMEM, VMEM], out_specs=[VMEM, VM...  2.12 us
    pallas_call x1, Pallas kernels, finish(): pl.pallas_call(functools.partial(finish_kernel, used=used, scale=scale),...  1.34 us
    ppermute x2, waiting for transfers between devices, to_core(): return lax.ppermute(x, 'chol', [(i, i ^ 1) for i in range(groups)])  1.12 us
  transfers between devices with their start and end apart: 9, of which 5 were waited for; matrix products, arithmetic and copies ran while one was open for 0% of the time, Pallas kernels for 13%

profile of v9, /device:TPU:0, one launch (start us, length us, event | category | flops | bytes accessed | tf_op | source)
XLA Modules:
  0.0 42.1 jit_solution(10794970429531077869)
XLA Ops:
  0.6 0.5 %collective-permute-start.1 = (bf16[1,4,32,64,128]{4,3,2,1,0:T(8,128)(2,1)}, bf16[1,4,32,64,128]{4,3,2,1,0:T(8,128)(2,1)S(1)}, u32[]{:S(2)}, u32[]{:S(2)}) collective-permute-start(bf16[1,4,32,64,128]{4,3,2,1,0:T(8,128)(2,1)} %chol_ref.1), channel_id=1, source_target_pairs={{0,1},{1,0},{2,3},{3,2},{4,5},{5,4},{6,7},{7,6},{8,9},{9,8},{10,11... | collective-permute-start | bytes 6291464 | tf_op jit(solution)/shard_map/ppermute | solution.py:266
  1.1 2.6 %collective-permute-start = (bf16[1,64,1280]{2,1,0:T(8,128)(2,1)}, bf16[1,64,1280]{2,1,0:T(8,128)(2,1)S(1)}, u32[]{:S(2)}, u32[]{:S(2)}) collective-permute-start(bf16[1,64,1280]{2,1,0:T(8,128)(2,1)} %refs_4_.1), channel_id=1, source_target_pairs={{0,2},{1,3},{2,0},{3,1},{4,6},{5,7},{6,4},{7,5},{8,10},{9,11},{10,... | collective-permute-start | bytes 491528 | tf_op jit(solution)/shard_map/ppermute | solution.py:263
  3.7 2.6 %collective-permute-start.4 = (bf16[1,64,1280]{2,1,0:T(8,128)(2,1)}, bf16[1,64,1280]{2,1,0:T(8,128)(2,1)S(1)}, u32[]{:S(2)}, u32[]{:S(2)}) collective-permute-start(bf16[1,64,1280]{2,1,0:T(8,128)(2,1)} %refs_4_.1), channel_id=1, source_target_pairs={{0,8},{1,9},{2,10},{3,11},{4,12},{5,13},{6,14},{7,15},{8,0},{9,1},... | collective-permute-start | bytes 491528 | tf_op jit(solution)/shard_map/ppermute | solution.py:263
  6.3 1.6 %collective-permute-start.5 = (bf16[1,64,1280]{2,1,0:T(8,128)(2,1)}, bf16[1,64,1280]{2,1,0:T(8,128)(2,1)S(1)}, u32[]{:S(2)}, u32[]{:S(2)}) collective-permute-start(bf16[1,64,1280]{2,1,0:T(8,128)(2,1)} %refs_4_.1), channel_id=1, source_target_pairs={{0,4},{1,5},{2,6},{3,7},{4,0},{5,1},{6,2},{7,3},{8,12},{9,13},{10,... | collective-permute-start | bytes 491528 | tf_op jit(solution)/shard_map/ppermute | solution.py:263
  7.9 0.0 copy-start
  7.9 1.6 %copy-done = bf16[1,4,32,64,128]{4,3,2,1,0:T(8,128)(2,1)S(1)} copy-done((bf16[1,4,32,64,128]{4,3,2,1,0:T(8,128)(2,1)S(1)}, bf16[1,4,32,64,128]{4,3,2,1,0:T(8,128)(2,1)}, u32[]{:S(2)}) %copy-start) | copy-done | bytes 2097176
  9.5 0.0 copy-start.3
  9.5 0.7 %copy-done.3 = s32[1,4]{1,0:T(1,128)S(1)} copy-done((s32[1,4]{1,0:T(1,128)S(1)}, s32[1,4]{1,0:T(1,128)}, u32[]{:S(2)}) %copy-start.3) | copy-done | bytes 40
  10.2 0.0 copy-start.1
  10.2 0.0 copy-start.2
  10.2 1.1 %prepare_block.2 = (bf16[2048,512]{1,0:T(8,128)(2,1)S(1)}, bf16[512,1024]{1,0:T(8,128)(2,1)S(1)}) custom-call(s32[1,4]{1,0:T(1,128)S(1)} %copy-done.3, bf16[1,4,32,64,128]{4,3,2,1,0:T(8,128)(2,1)S(1)} %copy-done), custom_call_target="tpu_custom_call" | custom-call | tf_op jit(solution)/shard_map/prepare_block/pallas_call | solution.py:39
  11.2 0.0 collective-permute-done.refs_5_
  11.2 0.0 copy-done.1
  11.2 0.5 %collective-permute-start.2 = (bf16[1,64,1280]{2,1,0:T(8,128)(2,1)S(1)}, bf16[1,64,1280]{2,1,0:T(8,128)(2,1)S(1)}, u32[]{:S(2)}, u32[]{:S(2)}) collective-permute-start(bf16[1,64,1280]{2,1,0:T(8,128)(2,1)S(1)} %copy-done.1), channel_id=1, source_target_pairs={{0,6},{1,7},{2,4},{3,5},{4,2},{5,3},{6,0},{7,1},{8,14},{9,15},{10,... | collective-permute-start | bytes 491528 | tf_op jit(solution)/shard_map/ppermute | solution.py:263
  11.7 3.1 %collective-permute-done.4.refs_4_ = bf16[1,64,1280]{2,1,0:T(8,128)(2,1)S(1)} collective-permute-done((bf16[1,64,1280]{2,1,0:T(8,128)(2,1)}, bf16[1,64,1280]{2,1,0:T(8,128)(2,1)S(1)}, u32[]{:S(2)}, u32[]{:S(2)}) %collective-permute-start.4) | collective-permute-done | bytes 163872 | tf_op jit(solution)/shard_map/ppermute | solution.py:263
  14.8 0.3 collective-permute-done.5.refs_6_
  15.0 0.5 %collective-permute-start.6 = (bf16[1,64,1280]{2,1,0:T(8,128)(2,1)S(1)}, bf16[1,64,1280]{2,1,0:T(8,128)(2,1)S(1)}, u32[]{:S(2)}, u32[]{:S(2)}) collective-permute-start(bf16[1,64,1280]{2,1,0:T(8,128)(2,1)S(1)} %collective-permute-done.4.refs_4_), channel_id=1, source_target_pairs={{0,2},{1,3},{2,0},{3,1},{4,6},{5,7},{6,4},{7,5},{8,10},{9,11},{10,... | collective-permute-start | bytes 491528 | tf_op jit(solution)/shard_map/ppermute | solution.py:263
  15.5 2.1 %collective-permute-start.7 = (bf16[1,64,1280]{2,1,0:T(8,128)(2,1)S(1)}, bf16[1,64,1280]{2,1,0:T(8,128)(2,1)S(1)}, u32[]{:S(2)}, u32[]{:S(2)}) collective-permute-start(bf16[1,64,1280]{2,1,0:T(8,128)(2,1)S(1)} %collective-permute-done.4.refs_4_), channel_id=1, source_target_pairs={{0,4},{1,5},{2,6},{3,7},{4,0},{5,1},{6,2},{7,3},{8,12},{9,13},{10,... | collective-permute-start | bytes 491528 | tf_op jit(solution)/shard_map/ppermute | solution.py:263
  17.6 1.0 %collective-permute-start.8 = (bf16[1,64,1280]{2,1,0:T(8,128)(2,1)S(1)}, bf16[1,64,1280]{2,1,0:T(8,128)(2,1)S(1)}, u32[]{:S(2)}, u32[]{:S(2)}) collective-permute-start(bf16[1,64,1280]{2,1,0:T(8,128)(2,1)S(1)} %collective-permute-done.4.refs_4_), channel_id=1, source_target_pairs={{0,6},{1,7},{2,4},{3,5},{4,2},{5,3},{6,0},{7,1},{8,14},{9,15},{10,... | collective-permute-start | bytes 491528 | tf_op jit(solution)/shard_map/ppermute | solution.py:263
  18.6 0.2 collective-permute-done.2.refs_7_
  18.8 0.0 collective-permute-done.1.chol_ref
  18.8 0.0 collective-permute-start.3
  18.8 1.1 %collective-permute-done.3.screen_ref = s32[1,4]{1,0:T(1,128)S(1)} collective-permute-done((s32[1,4]{1,0:T(1,128)S(1)}, s32[1,4]{1,0:T(1,128)S(1)}, u32[]{:S(2)}, u32[]{:S(2)}) %collective-permute-start.3) | collective-permute-done | bytes 48 | tf_op jit(solution)/shard_map/ppermute | solution.py:266
  20.0 1.1 %prepare_block.3 = (bf16[2048,512]{1,0:T(8,128)(2,1)S(1)}, bf16[512,1024]{1,0:T(8,128)(2,1)S(1)}) custom-call(s32[1,4]{1,0:T(1,128)S(1)} %collective-permute-done.3.screen_ref, bf16[1,4,32,64,128]{4,3,2,1,0:T(8,128)(2,1)S(1)} %collective-permute-done.1.chol_ref), custom_call_target="tpu_custom_call" | custom-call | tf_op jit(solution)/shard_map/prepare_block/pallas_call | solution.py:39
  21.0 0.0 copy-done.2
  21.0 3.5 %chip_terms.2.refs_8_ = f32[8,1,128]{2,1,0:T(1,128)S(1)} custom-call(s32[4,16]{1,0:T(4,128)S(1)} %bitcast.2, bf16[2048,512]{1,0:T(8,128)(2,1)S(1)} %get-tuple-element.17.refs_0_, bf16[512,1024]{1,0:T(8,128)(2,1)S(1)} %get-tuple-element.18.refs_1_, bf16[2048,512]{1,0:T(8,128)(2,1)S(1)} %get-tuple-element.22.refs_2_, ...), custom_call_target="tpu_custom_call" | custom-call | tf_op jit(solution)/shard_map/chip_terms/pallas_call | solution.py:195
  24.6 0.0 collective-permute-done.6.refs_5_
  24.6 0.0 collective-permute-done.7.refs_6_
  24.6 0.7 %collective-permute-done.8.refs_7_ = bf16[1,64,1280]{2,1,0:T(8,128)(2,1)S(1)} collective-permute-done((bf16[1,64,1280]{2,1,0:T(8,128)(2,1)S(1)}, bf16[1,64,1280]{2,1,0:T(8,128)(2,1)S(1)}, u32[]{:S(2)}, u32[]{:S(2)}) %collective-permute-start.8) | collective-permute-done | bytes 163872 | tf_op jit(solution)/shard_map/ppermute | solution.py:263
  25.4 3.5 %chip_terms.3 = f32[8,1,128]{2,1,0:T(1,128)S(1)} custom-call(s32[4,16]{1,0:T(4,128)S(1)} %bitcast.3, bf16[2048,512]{1,0:T(8,128)(2,1)S(1)} %get-tuple-element.17.refs_0_, bf16[512,1024]{1,0:T(8,128)(2,1)S(1)} %get-tuple-element.18.refs_1_, bf16[2048,512]{1,0:T(8,128)(2,1)S(1)} %get-tuple-element.22.refs_2_, bf16[512,1024]{1,0:T(8,128)(2,1)S(1)} %get-tuple-element.23.refs_3_, ...), custom_call_target="tpu_custom_call" | custom-call | tf_op jit(solution)/shard_map/chip_terms/pallas_call | solution.py:195
  28.9 11.9 %all_to_all.5.rows_ref = f32[8,1,128]{2,1,0:T(1,128)} all-to-all(f32[8,1,128]{2,1,0:T(1,128)S(1)} %chip_terms.3), channel_id=1, replica_groups={{0,2,4,6,8,10,12,14},{1,3,5,7,9,11,13,15},{16,18,20,22,24,26,28,30},{17..., dimensions={0} | all-to-all | bytes 8192 | tf_op jit(solution)/shard_map/all_to_all | solution.py:282
  40.8 1.3 %finish.1 = (f32[1,512]{1,0:T(1,128)}, f32[1,1]{1,0:T(1,128)}) custom-call(f32[8,1,128]{2,1,0:T(1,128)} %all_to_all.5.rows_ref), custom_call_target="tpu_custom_call" | custom-call | tf_op jit(solution)/shard_map/finish/pallas_call | solution.py:241
Async XLA Ops:
  0.6 18.2 %collective-permute-start.1 = (bf16[1,4,32,64,128]{4,3,2,1,0:T(8,128)(2,1)}, bf16[1,4,32,64,128]{4,3,2,1,0:T(8,128)(2,1)S(1)}, u32[]{:S(2)}, u32[]{:S(2)}) collective-permute-start(bf16[1,4,32,64,128]{4,3,2,1,0:T(8,128)(2,1)} %chol_ref.1), channel_id=1, source_target_pairs={{0,1},{1,0},{2,3},{3,2},{4,5},{5,4},{6,7},{7,6},{8,9},{9,8},{10,11... | collective-permute-start | bytes 6291464 | tf_op jit(solution)/shard_map/ppermute | solution.py:266
  1.1 10.1 %collective-permute-start = (bf16[1,64,1280]{2,1,0:T(8,128)(2,1)}, bf16[1,64,1280]{2,1,0:T(8,128)(2,1)S(1)}, u32[]{:S(2)}, u32[]{:S(2)}) collective-permute-start(bf16[1,64,1280]{2,1,0:T(8,128)(2,1)} %refs_4_.1), channel_id=1, source_target_pairs={{0,2},{1,3},{2,0},{3,1},{4,6},{5,7},{6,4},{7,5},{8,10},{9,11},{10,... | collective-permute-start | bytes 491528 | tf_op jit(solution)/shard_map/ppermute | solution.py:263
  3.7 11.0 %collective-permute-start.4 = (bf16[1,64,1280]{2,1,0:T(8,128)(2,1)}, bf16[1,64,1280]{2,1,0:T(8,128)(2,1)S(1)}, u32[]{:S(2)}, u32[]{:S(2)}) collective-permute-start(bf16[1,64,1280]{2,1,0:T(8,128)(2,1)} %refs_4_.1), channel_id=1, source_target_pairs={{0,8},{1,9},{2,10},{3,11},{4,12},{5,13},{6,14},{7,15},{8,0},{9,1},... | collective-permute-start | bytes 491528 | tf_op jit(solution)/shard_map/ppermute | solution.py:263
  6.3 8.7 %collective-permute-start.5 = (bf16[1,64,1280]{2,1,0:T(8,128)(2,1)}, bf16[1,64,1280]{2,1,0:T(8,128)(2,1)S(1)}, u32[]{:S(2)}, u32[]{:S(2)}) collective-permute-start(bf16[1,64,1280]{2,1,0:T(8,128)(2,1)} %refs_4_.1), channel_id=1, source_target_pairs={{0,4},{1,5},{2,6},{3,7},{4,0},{5,1},{6,2},{7,3},{8,12},{9,13},{10,... | collective-permute-start | bytes 491528 | tf_op jit(solution)/shard_map/ppermute | solution.py:263
  7.9 1.6 %copy-start = (bf16[1,4,32,64,128]{4,3,2,1,0:T(8,128)(2,1)S(1)}, bf16[1,4,32,64,128]{4,3,2,1,0:T(8,128)(2,1)}, u32[]{:S(2)}) copy-start(bf16[1,4,32,64,128]{4,3,2,1,0:T(8,128)(2,1)} %chol_ref.1) | copy-start | bytes 6291460
  9.5 0.7 %copy-start.3 = (s32[1,4]{1,0:T(1,128)S(1)}, s32[1,4]{1,0:T(1,128)}, u32[]{:S(2)}) copy-start(s32[1,4]{1,0:T(1,128)} %screen_ref.1) | copy-start | bytes 52
  10.2 1.1 %copy-start.1 = (bf16[1,64,1280]{2,1,0:T(8,128)(2,1)S(1)}, bf16[1,64,1280]{2,1,0:T(8,128)(2,1)}, u32[]{:S(2)}) copy-start(bf16[1,64,1280]{2,1,0:T(8,128)(2,1)} %refs_4_.1) | copy-start | bytes 491524
  10.2 10.9 %copy-start.2 = (s32[16,4]{0,1:T(4,128)S(1)}, s32[16,4]{0,1:T(4,128)}, u32[]{:S(2)}) copy-start(s32[16,4]{0,1:T(4,128)} %param.7) | copy-start | bytes 772
  11.2 7.6 %collective-permute-start.2 = (bf16[1,64,1280]{2,1,0:T(8,128)(2,1)S(1)}, bf16[1,64,1280]{2,1,0:T(8,128)(2,1)S(1)}, u32[]{:S(2)}, u32[]{:S(2)}) collective-permute-start(bf16[1,64,1280]{2,1,0:T(8,128)(2,1)S(1)} %copy-done.1), channel_id=1, source_target_pairs={{0,6},{1,7},{2,4},{3,5},{4,2},{5,3},{6,0},{7,1},{8,14},{9,15},{10,... | collective-permute-start | bytes 491528 | tf_op jit(solution)/shard_map/ppermute | solution.py:263
  15.0 9.5 %collective-permute-start.6 = (bf16[1,64,1280]{2,1,0:T(8,128)(2,1)S(1)}, bf16[1,64,1280]{2,1,0:T(8,128)(2,1)S(1)}, u32[]{:S(2)}, u32[]{:S(2)}) collective-permute-start(bf16[1,64,1280]{2,1,0:T(8,128)(2,1)S(1)} %collective-permute-done.4.refs_4_), channel_id=1, source_target_pairs={{0,2},{1,3},{2,0},{3,1},{4,6},{5,7},{6,4},{7,5},{8,10},{9,11},{10,... | collective-permute-start | bytes 491528 | tf_op jit(solution)/shard_map/ppermute | solution.py:263
  15.5 9.1 %collective-permute-start.7 = (bf16[1,64,1280]{2,1,0:T(8,128)(2,1)S(1)}, bf16[1,64,1280]{2,1,0:T(8,128)(2,1)S(1)}, u32[]{:S(2)}, u32[]{:S(2)}) collective-permute-start(bf16[1,64,1280]{2,1,0:T(8,128)(2,1)S(1)} %collective-permute-done.4.refs_4_), channel_id=1, source_target_pairs={{0,4},{1,5},{2,6},{3,7},{4,0},{5,1},{6,2},{7,3},{8,12},{9,13},{10,... | collective-permute-start | bytes 491528 | tf_op jit(solution)/shard_map/ppermute | solution.py:263
  17.6 7.7 %collective-permute-start.8 = (bf16[1,64,1280]{2,1,0:T(8,128)(2,1)S(1)}, bf16[1,64,1280]{2,1,0:T(8,128)(2,1)S(1)}, u32[]{:S(2)}, u32[]{:S(2)}) collective-permute-start(bf16[1,64,1280]{2,1,0:T(8,128)(2,1)S(1)} %collective-permute-done.4.refs_4_), channel_id=1, source_target_pairs={{0,6},{1,7},{2,4},{3,5},{4,2},{5,3},{6,0},{7,1},{8,14},{9,15},{10,... | collective-permute-start | bytes 491528 | tf_op jit(solution)/shard_map/ppermute | solution.py:263
  18.8 1.1 %collective-permute-start.3 = (s32[1,4]{1,0:T(1,128)S(1)}, s32[1,4]{1,0:T(1,128)S(1)}, u32[]{:S(2)}, u32[]{:S(2)}) collective-permute-start(s32[1,4]{1,0:T(1,128)S(1)} %copy-done.3), channel_id=1, source_target_pairs={{0,1},{1,0},{2,3},{3,2},{4,5},{5,4},{6,7},{7,6},{8,9},{9,8},{10,11... | collective-permute-start | bytes 56 | tf_op jit(solution)/shard_map/ppermute | solution.py:266

commit v10 on v8

--- a/solution.py
+++ b/solution.py
@@ -113,11 +113,12 @@
                 store_rows(k0 + k8, t, fold_rows(diagonals, sub8))
 
 
-def terms_kernel(list_ref, *refs, first, count, falling, vectors, batch, carried):
-    block_refs, theta_refs, rest = refs[:4], refs[4:4 + count], refs[4 + count:]
+def terms_kernel(list_ref, *refs, first, jump, count, places, vectors, batch, carried):
+    held = len(places)
+    block_refs, theta_refs, rest = refs[:4], refs[4:4 + held], refs[4 + held:]
     out_ref, picked_ref, rows_ref = rest[-3:]
     listed = list_ref.shape[0]
-    _, occupied, _ = theta_refs[0].shape
+    occupied = block_refs[0].shape[0] // vectors
     width = block_refs[0].shape[1] // listed
     used = CORES * vectors
     columns = batch * occupied
@@ -130,8 +131,8 @@
     for b, group in enumerate((me, me ^ 1)):
         for m in range(listed):
             start = pl.multiple_of(list_ref[m, group] * width, width)
-            for i, ref in enumerate(theta_refs):
-                picked_ref[b, i * occupied:(i + 1) * occupied, m * width:(m + 1) * width] = ref[0, :, pl.ds(start, width)]
+            for row, ref in zip(places, theta_refs):
+                picked_ref[b, row:row + ref.shape[1], m * width:(m + 1) * width] = ref[0, :, pl.ds(start, width)]
 
     if carried:
         out_ref[...] = rest[0][...]
@@ -170,8 +171,8 @@
             sums[:, used:used + 8], axis=1, keepdims=True
         )
         for i in range(batch):
-            place = lax.rem(count - index - i, count) if falling else index + i
-            owner = chip ^ (first + place)
+            place = jnp.int32(index + i)
+            owner = chip ^ (first + place + (place >= jump).astype(jnp.int32))
             out_ref[pl.ds(owner, 1), 0, :used] = bias[i:i + 1]
             out_ref[pl.ds(owner, 1), 0, used:used + 1] = energy[i:i + 1]
 
@@ -183,18 +184,24 @@
             one_batch(step * batch)
 
 
-def chip_terms(listing, blocks, thetas, carried, first, falling, vectors, out_width):
+def chip_terms(listing, blocks, thetas, carried, first, jump, vectors, out_width):
     count = len(thetas)
-    if falling:
-        thetas = thetas[:1] + thetas[:0:-1]
+    occupied = sum(part.shape[1] for part in thetas[0])
+    pieces = []
+    for walker, parts in enumerate(thetas):
+        row = walker * occupied
+        for index, part in enumerate(parts):
+            pieces.append((index, row, part))
+            row += part.shape[1]
+    pieces.sort(key=lambda piece: piece[0])
+    places, thetas = [piece[1] for piece in pieces], [piece[2] for piece in pieces]
     batch = min(count, BATCH)
-    _, occupied, _ = thetas[0].shape
     chips = listing.shape[1] // CORES
     depth = blocks[0].shape[1]
     operands = [listing, *blocks, *thetas] + ([] if carried is None else [carried])
     return pl.pallas_call(
         functools.partial(
-            terms_kernel, first=first, count=count, falling=falling, vectors=vectors, batch=batch,
+            terms_kernel, first=first, jump=jump, count=count, places=places, vectors=vectors, batch=batch,
             carried=carried is not None,
         ),
         in_specs=[SMEM] + [VMEM] * (len(operands) - 1),
@@ -265,17 +272,23 @@
     def to_core(x):
         return lax.ppermute(x, "chol", [(i, i ^ 1) for i in range(groups)])
 
-    far = to_chip(theta, half)
-    near = [theta] + [to_chip(theta, offset) for offset in range(1, half)]
+    middle = occupied // 2
+    far = [to_chip(theta[:, :middle], half), to_chip(theta[:, middle:], half)]
+    near = [theta] + [to_chip(theta, offset) for offset in range(1, half - 1)]
     own, own_turned = prepare_block(screen, chol_tiles)
-    near[1], near[2], own, far = lax.optimization_barrier((near[1], near[2], own, far))
-    beyond = [far] + [to_chip(far, offset) for offset in range(1, half)]
-    other_chol, late_screen, near[-1] = lax.optimization_barrier((to_core(chol_tiles), screen, near[-1]))
-    other, other_turned = prepare_block(to_core(late_screen), other_chol)
+    near[1], own, late_screen = lax.optimization_barrier((near[1], own, screen))
+    far[0], near[2], other_screen, other_chol, late_theta = lax.optimization_barrier(
+        (far[0], near[2], to_core(late_screen), to_core(chol_tiles), theta)
+    )
+    sent = [to_chip(far[0], offset) for offset in range(1, half)]
+    far[1], far[0] = lax.optimization_barrier((far[1], far[0]))
+    beyond = [[sent[offset - 1], to_chip(far[1], offset)] for offset in range(1, half)]
+    last = to_chip(late_theta, half - 1)
+    other, other_turned = prepare_block(other_screen, other_chol)
     blocks = [own, own_turned, other, other_turned]
 
-    rows = chip_terms(listing, blocks, near, None, 0, False, vectors, out_width)
-    rows = chip_terms(listing, blocks, beyond, rows, half, True, vectors, out_width)
+    rows = chip_terms(listing, blocks, [[x] for x in near] + [far], None, 0, half - 1, vectors, out_width)
+    rows = chip_terms(listing, blocks, [[last]] + beyond, rows, half - 1, 1, vectors, out_width)
     same_core = [list(range(core, groups, CORES)) for core in range(CORES)]
     back = lax.all_to_all(rows, "chol", split_axis=0, concat_axis=0, tiled=True, axis_index_groups=same_core)
     return finish(back, used, 1.0 / (2.0 * occupied * occupied))

time: 41.3 us -> 46.1 us (1.12)
  starting transfers between devices: 11.2 us -> 17.7 us
  waiting for transfers between devices: 5.71 us -> 2.07 us
  local copies, waits for them, and re-layouts: 2.25 us -> 3.22 us
  blocking collectives: 11.2 us -> 12 us
    ppermute x7 -> x11, starting transfers between devices: 10.6 us -> 17.2 us  [to_chip(): lax.ppermute(x, 'chol', [(i, i ^ offset * CORES) for i in range(groups)])]
    ppermute x7 -> x11, waiting for transfers between devices: 4.59 us -> 0.98 us  [to_chip(): lax.ppermute(x, 'chol', [(i, i ^ offset * CORES) for i in range(groups)])]
    slice x0 -> x1, local copies, waits for them, and re-layouts: none -> 0.97 us  [body(): far = [to_chip(theta[:, :middle], half), to_chip(theta[:, middle:], half)]]
    all_to_all x1, blocking collectives: 11.2 us -> 12 us  [body(): lax.all_to_all(rows, 'chol', split_axis=0, concat_axis=0, tiled=True, axi...]
  transfers between devices with their start and end apart: 9 -> 13, of which waited for: 5 -> 2; matrix products, arithmetic and copies ran while one was open for 0% -> 2% of each run, Pallas kernels for 13% -> 12%
where the time goes in v10:
time: 46.1 us; the launch traced here: 45.8 us
  starting transfers between devices  17.7 us (38%)
  blocking collectives  12 us (26%)
  Pallas kernels  10 us (22%)
  local copies, waits for them, and re-layouts  3.22 us (7%)
  waiting for transfers between devices  2.07 us (4%)
  between operations  0.73 us (2%)
    ppermute x11, starting transfers between devices, to_chip(): lax.ppermute(x, 'chol', [(i, i ^ offset * CORES) for i in range(groups)])  17.2 us
    all_to_all x1, blocking collectives, body(): lax.all_to_all(rows, 'chol', split_axis=0, concat_axis=0, tiled=True, axi...  12 us
    pallas_call x2, Pallas kernels, chip_terms(): pl.pallas_call(functools.partial(terms_kernel, first=first, jump=jump, co...  6.54 us
    unnamed x8, local copies, waits for them, and re-layouts  2.25 us
    pallas_call x2, Pallas kernels, prepare_block(): pl.pallas_call(prepare_kernel, in_specs=[SMEM, VMEM], out_specs=[VMEM, VM...  2.12 us
    pallas_call x1, Pallas kernels, finish(): pl.pallas_call(functools.partial(finish_kernel, used=used, scale=scale),...  1.35 us
    ppermute x2, waiting for transfers between devices, to_core(): return lax.ppermute(x, 'chol', [(i, i ^ 1) for i in range(groups)])  1.09 us
    ppermute x11, waiting for transfers between devices, to_chip(): lax.ppermute(x, 'chol', [(i, i ^ offset * CORES) for i in range(groups)])  0.98 us
  transfers between devices with their start and end apart: 13, of which 2 were waited for; matrix products, arithmetic and copies ran while one was open for 2% of the time, Pallas kernels for 12%

profile of v10, /device:TPU:0, one launch (start us, length us, event | category | flops | bytes accessed | tf_op | source)
XLA Modules:
  0.0 45.8 jit_solution(11905113474281161387)
XLA Ops:
  0.6 0.5 %collective-permute-start.4 = (bf16[1,4,32,64,128]{4,3,2,1,0:T(8,128)(2,1)}, bf16[1,4,32,64,128]{4,3,2,1,0:T(8,128)(2,1)S(1)}, u32[]{:S(2)}, u32[]{:S(2)}) collective-permute-start(bf16[1,4,32,64,128]{4,3,2,1,0:T(8,128)(2,1)} %chol_ref.1), channel_id=1, source_target_pairs={{0,1},{1,0},{2,3},{3,2},{4,5},{5,4},{6,7},{7,6},{8,9},{9,8},{10,11... | collective-permute-start | bytes 6291464 | tf_op jit(solution)/shard_map/ppermute | solution.py:273
  1.2 2.6 %collective-permute-start = (bf16[1,64,1280]{2,1,0:T(8,128)(2,1)}, bf16[1,64,1280]{2,1,0:T(8,128)(2,1)S(1)}, u32[]{:S(2)}, u32[]{:S(2)}) collective-permute-start(bf16[1,64,1280]{2,1,0:T(8,128)(2,1)} %refs_4_.1), channel_id=1, source_target_pairs={{0,2},{1,3},{2,0},{3,1},{4,6},{5,7},{6,4},{7,5},{8,10},{9,11},{10,... | collective-permute-start | bytes 491528 | tf_op jit(solution)/shard_map/ppermute | solution.py:270
  3.8 1.6 %collective-permute-start.2 = (bf16[1,64,1280]{2,1,0:T(8,128)(2,1)}, bf16[1,64,1280]{2,1,0:T(8,128)(2,1)S(1)}, u32[]{:S(2)}, u32[]{:S(2)}) collective-permute-start(bf16[1,64,1280]{2,1,0:T(8,128)(2,1)} %refs_4_.1), channel_id=1, source_target_pairs={{0,4},{1,5},{2,6},{3,7},{4,0},{5,1},{6,2},{7,3},{8,12},{9,13},{10,... | collective-permute-start | bytes 491528 | tf_op jit(solution)/shard_map/ppermute | solution.py:270
  5.3 1.0 %fusion = (bf16[1,32,1280]{2,1,0:T(8,128)(2,1)S(1)}, bf16[1,32,1280]{2,1,0:T(8,128)(2,1)S(1)}) fusion(bf16[1,64,1280]{2,1,0:T(8,128)(2,1)} %refs_4_.1), kind=kLoop, calls=%fused_computation | loop fusion | bytes 327680 | tf_op jit(solution)/shard_map/slice | solution.py:276
  6.3 2.7 %collective-permute-start.1 = (bf16[1,32,1280]{2,1,0:T(8,128)(2,1)S(1)}, bf16[1,32,1280]{2,1,0:T(8,128)(2,1)S(1)}, u32[]{:S(2)}, u32[]{:S(2)}) collective-permute-start(bf16[1,32,1280]{2,1,0:T(8,128)(2,1)S(1)} %get-tuple-element.35), channel_id=1, source_target_pairs={{0,8},{1,9},{2,10},{3,11},{4,12},{5,13},{6,14},{7,15},{8,0},{9,1},... | collective-permute-start | bytes 245768 | tf_op jit(solution)/shard_map/ppermute | solution.py:270
  9.0 0.3 collective-permute-start.9
  9.3 1.6 %copy-done = bf16[1,4,32,64,128]{4,3,2,1,0:T(8,128)(2,1)S(1)} copy-done((bf16[1,4,32,64,128]{4,3,2,1,0:T(8,128)(2,1)S(1)}, bf16[1,4,32,64,128]{4,3,2,1,0:T(8,128)(2,1)}, u32[]{:S(2)}) %copy-start) | copy-done | bytes 2097176
  10.9 0.7 %copy-done.3 = s32[1,4]{1,0:T(1,128)S(1)} copy-done((s32[1,4]{1,0:T(1,128)S(1)}, s32[1,4]{1,0:T(1,128)}, u32[]{:S(2)}) %copy-start.3) | copy-done | bytes 40
  11.5 1.1 %prepare_block.2 = (bf16[2048,512]{1,0:T(8,128)(2,1)S(1)}, bf16[512,1024]{1,0:T(8,128)(2,1)S(1)}) custom-call(s32[1,4]{1,0:T(1,128)S(1)} %copy-done.3, bf16[1,4,32,64,128]{4,3,2,1,0:T(8,128)(2,1)S(1)} %copy-done), custom_call_target="tpu_custom_call" | custom-call | tf_op jit(solution)/shard_map/prepare_block/pallas_call | solution.py:39
  12.6 0.0 collective-permute-done.refs_5_
  12.6 0.1 collective-permute-start.3
  12.7 0.0 collective-permute-done.1.refs_7_
  12.7 0.0 collective-permute-done.2.refs_6_
  12.7 1.1 %collective-permute-done.3.screen_ref = s32[1,4]{1,0:T(1,128)S(1)} collective-permute-done((s32[1,4]{1,0:T(1,128)S(1)}, s32[1,4]{1,0:T(1,128)S(1)}, u32[]{:S(2)}, u32[]{:S(2)}) %collective-permute-start.3) | collective-permute-done | bytes 48 | tf_op jit(solution)/shard_map/ppermute | solution.py:273
  13.8 0.0 collective-permute-done.4.chol_ref
  13.8 0.5 %collective-permute-start.6 = (bf16[1,32,1280]{2,1,0:T(8,128)(2,1)S(1)}, bf16[1,32,1280]{2,1,0:T(8,128)(2,1)S(1)}, u32[]{:S(2)}, u32[]{:S(2)}) collective-permute-start(bf16[1,32,1280]{2,1,0:T(8,128)(2,1)S(1)} %collective-permute-done.1.refs_7_), channel_id=1, source_target_pairs={{0,2},{1,3},{2,0},{3,1},{4,6},{5,7},{6,4},{7,5},{8,10},{9,11},{10,... | collective-permute-start | bytes 245768 | tf_op jit(solution)/shard_map/ppermute | solution.py:270
  14.3 1.9 %collective-permute-start.7 = (bf16[1,32,1280]{2,1,0:T(8,128)(2,1)S(1)}, bf16[1,32,1280]{2,1,0:T(8,128)(2,1)S(1)}, u32[]{:S(2)}, u32[]{:S(2)}) collective-permute-start(bf16[1,32,1280]{2,1,0:T(8,128)(2,1)S(1)} %collective-permute-done.1.refs_7_), channel_id=1, source_target_pairs={{0,4},{1,5},{2,6},{3,7},{4,0},{5,1},{6,2},{7,3},{8,12},{9,13},{10,... | collective-permute-start | bytes 245768 | tf_op jit(solution)/shard_map/ppermute | solution.py:270
  16.2 1.1 %collective-permute-start.5 = (bf16[1,64,1280]{2,1,0:T(8,128)(2,1)S(1)}, bf16[1,64,1280]{2,1,0:T(8,128)(2,1)S(1)}, u32[]{:S(2)}, u32[]{:S(2)}) collective-permute-start(bf16[1,64,1280]{2,1,0:T(8,128)(2,1)S(1)} %copy-done.1), channel_id=1, source_target_pairs={{0,6},{1,7},{2,4},{3,5},{4,2},{5,3},{6,0},{7,1},{8,14},{9,15},{10,... | collective-permute-start | bytes 491528 | tf_op jit(solution)/shard_map/ppermute | solution.py:270
  17.3 1.8 %collective-permute-start.8 = (bf16[1,32,1280]{2,1,0:T(8,128)(2,1)S(1)}, bf16[1,32,1280]{2,1,0:T(8,128)(2,1)S(1)}, u32[]{:S(2)}, u32[]{:S(2)}) collective-permute-start(bf16[1,32,1280]{2,1,0:T(8,128)(2,1)S(1)} %collective-permute-done.1.refs_7_), channel_id=1, source_target_pairs={{0,6},{1,7},{2,4},{3,5},{4,2},{5,3},{6,0},{7,1},{8,14},{9,15},{10,... | collective-permute-start | bytes 245768 | tf_op jit(solution)/shard_map/ppermute | solution.py:270
  19.1 1.5 %collective-permute-start.10 = (bf16[1,32,1280]{2,1,0:T(8,128)(2,1)S(1)}, bf16[1,32,1280]{2,1,0:T(8,128)(2,1)S(1)}, u32[]{:S(2)}, u32[]{:S(2)}) collective-permute-start(bf16[1,32,1280]{2,1,0:T(8,128)(2,1)S(1)} %collective-permute-done.9.refs_8_), channel_id=1, source_target_pairs={{0,2},{1,3},{2,0},{3,1},{4,6},{5,7},{6,4},{7,5},{8,10},{9,11},{10,... | collective-permute-start | bytes 245768 | tf_op jit(solution)/shard_map/ppermute | solution.py:270
  20.6 0.0 collective-permute-done.6.refs_5_
  20.6 3.2 %collective-permute-start.11 = (bf16[1,32,1280]{2,1,0:T(8,128)(2,1)S(1)}, bf16[1,32,1280]{2,1,0:T(8,128)(2,1)S(1)}, u32[]{:S(2)}, u32[]{:S(2)}) collective-permute-start(bf16[1,32,1280]{2,1,0:T(8,128)(2,1)S(1)} %collective-permute-done.9.refs_8_), channel_id=1, source_target_pairs={{0,4},{1,5},{2,6},{3,7},{4,0},{5,1},{6,2},{7,3},{8,12},{9,13},{10,... | collective-permute-start | bytes 245768 | tf_op jit(solution)/shard_map/ppermute | solution.py:270
  23.8 0.0 collective-permute-done.7.refs_6_
  23.8 0.0 collective-permute-start.12
  23.8 1.1 %prepare_block.3 = (bf16[2048,512]{1,0:T(8,128)(2,1)S(1)}, bf16[512,1024]{1,0:T(8,128)(2,1)S(1)}) custom-call(s32[1,4]{1,0:T(1,128)S(1)} %collective-permute-done.3.screen_ref, bf16[1,4,32,64,128]{4,3,2,1,0:T(8,128)(2,1)S(1)} %collective-permute-done.4.chol_ref), custom_call_target="tpu_custom_call" | custom-call | tf_op jit(solution)/shard_map/prepare_block/pallas_call | solution.py:39
  24.9 3.3 %chip_terms.2.refs_11_ = f32[8,1,128]{2,1,0:T(1,128)S(1)} custom-call(s32[4,16]{1,0:T(4,128)S(1)} %bitcast.2, bf16[2048,512]{1,0:T(8,128)(2,1)S(1)} %get-tuple-element.19.refs_0_, bf16[512,1024]{1,0:T(8,128)(2,1)S(1)} %get-tuple-element.20.refs_1_, bf16[2048,512]{1,0:T(8,128)(2,1)S(1)} %get-tuple-element.24.refs_2_, ...), custom_call_target="tpu_custom_call" | custom-call | tf_op jit(solution)/shard_map/chip_terms/pallas_call | solution.py:202
  28.2 0.0 collective-permute-done.8.refs_7_
  28.2 0.0 collective-permute-done.10.refs_8_
  28.2 0.9 %collective-permute-done.12.refs_10_ = bf16[1,32,1280]{2,1,0:T(8,128)(2,1)S(1)} collective-permute-done((bf16[1,32,1280]{2,1,0:T(8,128)(2,1)S(1)}, bf16[1,32,1280]{2,1,0:T(8,128)(2,1)S(1)}, u32[]{:S(2)}, u32[]{:S(2)}) %collective-permute-start.12) | collective-permute-done | bytes 81952 | tf_op jit(solution)/shard_map/ppermute | solution.py:270
  29.2 3.3 %chip_terms.3 = f32[8,1,128]{2,1,0:T(1,128)S(1)} custom-call(s32[4,16]{1,0:T(4,128)S(1)} %bitcast.3, bf16[2048,512]{1,0:T(8,128)(2,1)S(1)} %get-tuple-element.19.refs_0_, bf16[512,1024]{1,0:T(8,128)(2,1)S(1)} %get-tuple-element.20.refs_1_, bf16[2048,512]{1,0:T(8,128)(2,1)S(1)} %get-tuple-element.24.refs_2_, bf16[512,1024]{1,0:T(8,128)(2,1)S(1)} %get-tuple-element.25.refs_3_, ...), custom_call_target="tpu_custom_call" | custom-call | tf_op jit(solution)/shard_map/chip_terms/pallas_call | solution.py:202
  32.4 12.0 %all_to_all.5.rows_ref = f32[8,1,128]{2,1,0:T(1,128)} all-to-all(f32[8,1,128]{2,1,0:T(1,128)S(1)} %chip_terms.3), channel_id=1, replica_groups={{0,2,4,6,8,10,12,14},{1,3,5,7,9,11,13,15},{16,18,20,22,24,26,28,30},{17..., dimensions={0} | all-to-all | bytes 8192 | tf_op jit(solution)/shard_map/all_to_all | solution.py:293
  44.4 1.3 %finish.1 = (f32[1,512]{1,0:T(1,128)}, f32[1,1]{1,0:T(1,128)}) custom-call(f32[8,1,128]{2,1,0:T(1,128)} %all_to_all.5.rows_ref), custom_call_target="tpu_custom_call" | custom-call | tf_op jit(solution)/shard_map/finish/pallas_call | solution.py:248
  (9 shorter events, 0.0 us)
Async XLA Ops:
  0.6 15.5 %copy-start.1 = (bf16[1,64,1280]{2,1,0:T(8,128)(2,1)S(1)}, bf16[1,64,1280]{2,1,0:T(8,128)(2,1)}, u32[]{:S(2)}) copy-start(bf16[1,64,1280]{2,1,0:T(8,128)(2,1)} %refs_4_.1) | copy-start | bytes 491524
  0.6 13.2 %collective-permute-start.4 = (bf16[1,4,32,64,128]{4,3,2,1,0:T(8,128)(2,1)}, bf16[1,4,32,64,128]{4,3,2,1,0:T(8,128)(2,1)S(1)}, u32[]{:S(2)}, u32[]{:S(2)}) collective-permute-start(bf16[1,4,32,64,128]{4,3,2,1,0:T(8,128)(2,1)} %chol_ref.1), channel_id=1, source_target_pairs={{0,1},{1,0},{2,3},{3,2},{4,5},{5,4},{6,7},{7,6},{8,9},{9,8},{10,11... | collective-permute-start | bytes 6291464 | tf_op jit(solution)/shard_map/ppermute | solution.py:273
  1.2 11.5 %collective-permute-start = (bf16[1,64,1280]{2,1,0:T(8,128)(2,1)}, bf16[1,64,1280]{2,1,0:T(8,128)(2,1)S(1)}, u32[]{:S(2)}, u32[]{:S(2)}) collective-permute-start(bf16[1,64,1280]{2,1,0:T(8,128)(2,1)} %refs_4_.1), channel_id=1, source_target_pairs={{0,2},{1,3},{2,0},{3,1},{4,6},{5,7},{6,4},{7,5},{8,10},{9,11},{10,... | collective-permute-start | bytes 491528 | tf_op jit(solution)/shard_map/ppermute | solution.py:270
  3.8 9.0 %collective-permute-start.2 = (bf16[1,64,1280]{2,1,0:T(8,128)(2,1)}, bf16[1,64,1280]{2,1,0:T(8,128)(2,1)S(1)}, u32[]{:S(2)}, u32[]{:S(2)}) collective-permute-start(bf16[1,64,1280]{2,1,0:T(8,128)(2,1)} %refs_4_.1), channel_id=1, source_target_pairs={{0,4},{1,5},{2,6},{3,7},{4,0},{5,1},{6,2},{7,3},{8,12},{9,13},{10,... | collective-permute-start | bytes 491528 | tf_op jit(solution)/shard_map/ppermute | solution.py:270
  6.3 6.4 %collective-permute-start.1 = (bf16[1,32,1280]{2,1,0:T(8,128)(2,1)S(1)}, bf16[1,32,1280]{2,1,0:T(8,128)(2,1)S(1)}, u32[]{:S(2)}, u32[]{:S(2)}) collective-permute-start(bf16[1,32,1280]{2,1,0:T(8,128)(2,1)S(1)} %get-tuple-element.35), channel_id=1, source_target_pairs={{0,8},{1,9},{2,10},{3,11},{4,12},{5,13},{6,14},{7,15},{8,0},{9,1},... | collective-permute-start | bytes 245768 | tf_op jit(solution)/shard_map/ppermute | solution.py:270
  9.0 10.2 %collective-permute-start.9 = (bf16[1,32,1280]{2,1,0:T(8,128)(2,1)S(1)}, bf16[1,32,1280]{2,1,0:T(8,128)(2,1)S(1)}, u32[]{:S(2)}, u32[]{:S(2)}) collective-permute-start(bf16[1,32,1280]{2,1,0:T(8,128)(2,1)S(1)} %get-tuple-element.34), channel_id=1, source_target_pairs={{0,8},{1,9},{2,10},{3,11},{4,12},{5,13},{6,14},{7,15},{8,0},{9,1},... | collective-permute-start | bytes 245768 | tf_op jit(solution)/shard_map/ppermute | solution.py:270
  9.3 1.6 %copy-start = (bf16[1,4,32,64,128]{4,3,2,1,0:T(8,128)(2,1)S(1)}, bf16[1,4,32,64,128]{4,3,2,1,0:T(8,128)(2,1)}, u32[]{:S(2)}) copy-start(bf16[1,4,32,64,128]{4,3,2,1,0:T(8,128)(2,1)} %chol_ref.1) | copy-start | bytes 6291460
  10.9 0.7 %copy-start.3 = (s32[1,4]{1,0:T(1,128)S(1)}, s32[1,4]{1,0:T(1,128)}, u32[]{:S(2)}) copy-start(s32[1,4]{1,0:T(1,128)} %screen_ref.1) | copy-start | bytes 52
  11.5 13.4 %copy-start.2 = (s32[16,4]{0,1:T(4,128)S(1)}, s32[16,4]{0,1:T(4,128)}, u32[]{:S(2)}) copy-start(s32[16,4]{0,1:T(4,128)} %param.7) | copy-start | bytes 772
  12.6 1.2 %collective-permute-start.3 = (s32[1,4]{1,0:T(1,128)S(1)}, s32[1,4]{1,0:T(1,128)S(1)}, u32[]{:S(2)}, u32[]{:S(2)}) collective-permute-start(s32[1,4]{1,0:T(1,128)S(1)} %copy-done.3), channel_id=1, source_target_pairs={{0,1},{1,0},{2,3},{3,2},{4,5},{5,4},{6,7},{7,6},{8,9},{9,8},{10,11... | collective-permute-start | bytes 56 | tf_op jit(solution)/shard_map/ppermute | solution.py:273
  13.8 6.8 %collective-permute-start.6 = (bf16[1,32,1280]{2,1,0:T(8,128)(2,1)S(1)}, bf16[1,32,1280]{2,1,0:T(8,128)(2,1)S(1)}, u32[]{:S(2)}, u32[]{:S(2)}) collective-permute-start(bf16[1,32,1280]{2,1,0:T(8,128)(2,1)S(1)} %collective-permute-done.1.refs_7_), channel_id=1, source_target_pairs={{0,2},{1,3},{2,0},{3,1},{4,6},{5,7},{6,4},{7,5},{8,10},{9,11},{10,... | collective-permute-start | bytes 245768 | tf_op jit(solution)/shard_map/ppermute | solution.py:270
  14.3 9.5 %collective-permute-start.7 = (bf16[1,32,1280]{2,1,0:T(8,128)(2,1)S(1)}, bf16[1,32,1280]{2,1,0:T(8,128)(2,1)S(1)}, u32[]{:S(2)}, u32[]{:S(2)}) collective-permute-start(bf16[1,32,1280]{2,1,0:T(8,128)(2,1)S(1)} %collective-permute-done.1.refs_7_), channel_id=1, source_target_pairs={{0,4},{1,5},{2,6},{3,7},{4,0},{5,1},{6,2},{7,3},{8,12},{9,13},{10,... | collective-permute-start | bytes 245768 | tf_op jit(solution)/shard_map/ppermute | solution.py:270
  16.2 13.0 %collective-permute-start.5 = (bf16[1,64,1280]{2,1,0:T(8,128)(2,1)S(1)}, bf16[1,64,1280]{2,1,0:T(8,128)(2,1)S(1)}, u32[]{:S(2)}, u32[]{:S(2)}) collective-permute-start(bf16[1,64,1280]{2,1,0:T(8,128)(2,1)S(1)} %copy-done.1), channel_id=1, source_target_pairs={{0,6},{1,7},{2,4},{3,5},{4,2},{5,3},{6,0},{7,1},{8,14},{9,15},{10,... | collective-permute-start | bytes 491528 | tf_op jit(solution)/shard_map/ppermute | solution.py:270
  17.3 10.9 %collective-permute-start.8 = (bf16[1,32,1280]{2,1,0:T(8,128)(2,1)S(1)}, bf16[1,32,1280]{2,1,0:T(8,128)(2,1)S(1)}, u32[]{:S(2)}, u32[]{:S(2)}) collective-permute-start(bf16[1,32,1280]{2,1,0:T(8,128)(2,1)S(1)} %collective-permute-done.1.refs_7_), channel_id=1, source_target_pairs={{0,6},{1,7},{2,4},{3,5},{4,2},{5,3},{6,0},{7,1},{8,14},{9,15},{10,... | collective-permute-start | bytes 245768 | tf_op jit(solution)/shard_map/ppermute | solution.py:270
  19.1 9.1 %collective-permute-start.10 = (bf16[1,32,1280]{2,1,0:T(8,128)(2,1)S(1)}, bf16[1,32,1280]{2,1,0:T(8,128)(2,1)S(1)}, u32[]{:S(2)}, u32[]{:S(2)}) collective-permute-start(bf16[1,32,1280]{2,1,0:T(8,128)(2,1)S(1)} %collective-permute-done.9.refs_8_), channel_id=1, source_target_pairs={{0,2},{1,3},{2,0},{3,1},{4,6},{5,7},{6,4},{7,5},{8,10},{9,11},{10,... | collective-permute-start | bytes 245768 | tf_op jit(solution)/shard_map/ppermute | solution.py:270
  20.6 7.6 %collective-permute-start.11 = (bf16[1,32,1280]{2,1,0:T(8,128)(2,1)S(1)}, bf16[1,32,1280]{2,1,0:T(8,128)(2,1)S(1)}, u32[]{:S(2)}, u32[]{:S(2)}) collective-permute-start(bf16[1,32,1280]{2,1,0:T(8,128)(2,1)S(1)} %collective-permute-done.9.refs_8_), channel_id=1, source_target_pairs={{0,4},{1,5},{2,6},{3,7},{4,0},{5,1},{6,2},{7,3},{8,12},{9,13},{10,... | collective-permute-start | bytes 245768 | tf_op jit(solution)/shard_map/ppermute | solution.py:270
  23.8 5.3 %collective-permute-start.12 = (bf16[1,32,1280]{2,1,0:T(8,128)(2,1)S(1)}, bf16[1,32,1280]{2,1,0:T(8,128)(2,1)S(1)}, u32[]{:S(2)}, u32[]{:S(2)}) collective-permute-start(bf16[1,32,1280]{2,1,0:T(8,128)(2,1)S(1)} %collective-permute-done.9.refs_8_), channel_id=1, source_target_pairs={{0,6},{1,7},{2,4},{3,5},{4,2},{5,3},{6,0},{7,1},{8,14},{9,15},{10,... | collective-permute-start | bytes 245768 | tf_op jit(solution)/shard_map/ppermute | solution.py:270

commit v11 on v8

--- a/solution.py
+++ b/solution.py
@@ -165,15 +165,10 @@
         sums = sum(
             lax.dot_general(segment, part, NT, preferred_element_type=jnp.float32) for part in parts
         )
-        bias = sums[:, :used]
-        energy = jnp.sum(bias * bias, axis=1, keepdims=True) - jnp.sum(
-            sums[:, used:used + 8], axis=1, keepdims=True
-        )
         for i in range(batch):
             place = lax.rem(count - index - i, count) if falling else index + i
             owner = chip ^ (first + place)
-            out_ref[pl.ds(owner, 1), 0, :used] = bias[i:i + 1]
-            out_ref[pl.ds(owner, 1), 0, used:used + 1] = energy[i:i + 1]
+            out_ref[pl.ds(owner, 1), 0, :used + 8] = sums[i:i + 1]
 
     if count == batch:
         one_batch(0)
@@ -210,8 +205,19 @@
     )(*operands)
 
 
-def finish_kernel(rows_ref, bias_ref, energy_ref, bias_buf, energy_buf, sems, *, used, scale):
+def own_kernel(rows_ref, out_ref, *, used):
+    chip = lax.axis_index("chol") // CORES
+    out_ref[...] = energy_terms(rows_ref[pl.ds(chip, 1), 0, :], used)
+
+
+def energy_terms(rows, used):
+    lane = lax.broadcasted_iota(jnp.int32, rows.shape, 1)
+    return jnp.where(lane < used, rows * rows, jnp.where(lane < used + 8, -rows, 0.0))
+
+
+def finish_kernel(rows_ref, own_ref, bias_ref, energy_ref, bias_buf, energy_buf, sems, *, used, scale):
     chips, _, width = rows_ref.shape
+    chip = lax.axis_index("chol") // CORES
     fit = LANES // used if width == LANES else 0
     lane = lax.broadcasted_iota(jnp.int32, (1, width), 1)
     if fit and chips % fit == 0:
@@ -225,27 +231,35 @@
             bias_buf[:, d * used:(d + 1) * used] = rows_ref[d, :, :used]
     bias_copy = pltpu.make_async_copy(bias_buf, bias_ref, sems.at[0])
     bias_copy.start()
-    total = rows_ref[0]
-    for d in range(1, chips):
-        total = total + rows_ref[d]
-    energy_buf[...] = total[:, used:used + 1] * scale
+    total = own_ref[...]
+    for d in range(chips):
+        total = total + jnp.where(chip == d, 0.0, energy_terms(rows_ref[d], used))
+    energy_buf[...] = jnp.sum(total, axis=1, keepdims=True) * scale
     energy_copy = pltpu.make_async_copy(energy_buf, energy_ref, sems.at[1])
     energy_copy.start()
     bias_copy.wait()
     energy_copy.wait()
 
 
-def finish(rows, used, scale):
-    chips = rows.shape[0]
+def finish(back, rows, used, scale):
+    chips, _, width = rows.shape
+    own = pl.pallas_call(
+        functools.partial(own_kernel, used=used),
+        in_specs=[VMEM],
+        out_specs=VMEM,
+        out_shape=jax.ShapeDtypeStruct((1, width), jnp.float32),
+        cost_estimate=pl.CostEstimate(flops=0, bytes_accessed=1 << 20, transcendentals=0),
+        name="own_terms",
+    )(rows)
     shapes = [(1, chips * used), (1, 1)]
     force_bias, energy = pl.pallas_call(
         functools.partial(finish_kernel, used=used, scale=scale),
-        in_specs=[VMEM],
+        in_specs=[VMEM, VMEM],
         out_specs=[pl.BlockSpec(memory_space=pl.ANY)] * 2,
         out_shape=[jax.ShapeDtypeStruct(s, jnp.float32) for s in shapes],
         scratch_shapes=[pltpu.VMEM(s, jnp.float32) for s in shapes] + [pltpu.SemaphoreType.DMA((2,))],
         name="finish",
-    )(rows)
+    )(back, own)
     return force_bias, energy.reshape(1)
 
 
@@ -256,7 +270,7 @@
     _, occupied, _ = theta.shape
     vectors = chol_tiles.shape[2]
     used = CORES * vectors
-    out_width = LANES * ((used + 1 + LANES - 1) // LANES)
+    out_width = LANES * ((used + 8 + LANES - 1) // LANES)
     listing = tile_list.T
 
     def to_chip(x, offset):
@@ -278,7 +292,7 @@
     rows = chip_terms(listing, blocks, beyond, rows, half, True, vectors, out_width)
     same_core = [list(range(core, groups, CORES)) for core in range(CORES)]
     back = lax.all_to_all(rows, "chol", split_axis=0, concat_axis=0, tiled=True, axis_index_groups=same_core)
-    return finish(back, used, 1.0 / (2.0 * occupied * occupied))
+    return finish(back, rows, used, 1.0 / (2.0 * occupied * occupied))
 
 
 def solution(mesh):

time: 41.3 us -> 42.5 us (1.029)
  blocking collectives: 11.2 us -> 0 us
  waiting for transfers between devices: 5.71 us -> 11 us
  starting transfers between devices: 11.2 us -> 16 us
  Pallas kernels: 9.99 us -> 11.7 us
  local copies, waits for them, and re-layouts: 2.25 us -> 2.84 us
    all_to_all x1 -> x0, blocking collectives: 11.2 us -> none  [body(): lax.all_to_all(rows, 'chol', split_axis=0, concat_axis=0, tiled=True, axi...]
    all_to_all x0 -> x1, waiting for transfers between devices: none -> 5.16 us  [body(): lax.all_to_all(rows, 'chol', split_axis=0, concat_axis=0, tiled=True, axi...]
    all_to_all x0 -> x1, starting transfers between devices: none -> 4.84 us  [body(): lax.all_to_all(rows, 'chol', split_axis=0, concat_axis=0, tiled=True, axi...]
    pallas_call x0 -> x1, Pallas kernels: none -> 1.3 us  [finish(): pl.pallas_call(functools.partial(own_kernel, used=used), in_specs=[VMEM],...]
    unnamed x8 -> x10, local copies, waits for them, and re-layouts: 2.25 us -> 2.84 us
  transfers between devices with their start and end apart: 9 -> 10, of which waited for: 5 -> 6; matrix products, arithmetic and copies ran while one was open for 0% -> 0% of each run, Pallas kernels for 13% -> 16%
where the time goes in v11:
time: 42.5 us; the launch traced here: 42.2 us
  starting transfers between devices  16 us (38%)
  Pallas kernels  11.7 us (28%)
  waiting for transfers between devices  11 us (26%)
  local copies, waits for them, and re-layouts  2.84 us (7%)
  between operations  0.7 us (2%)
    ppermute x7, starting transfers between devices, to_chip(): lax.ppermute(x, 'chol', [(i, i ^ offset * CORES) for i in range(groups)])  10.6 us
    pallas_call x2, Pallas kernels, chip_terms(): pl.pallas_call(functools.partial(terms_kernel, first=first, count=count,...  6.88 us
    all_to_all x1, waiting for transfers between devices, body(): lax.all_to_all(rows, 'chol', split_axis=0, concat_axis=0, tiled=True, axi...  5.16 us
    all_to_all x1, starting transfers between devices, body(): lax.all_to_all(rows, 'chol', split_axis=0, concat_axis=0, tiled=True, axi...  4.84 us
    ppermute x7, waiting for transfers between devices, to_chip(): lax.ppermute(x, 'chol', [(i, i ^ offset * CORES) for i in range(groups)])  4.7 us
    unnamed x10, local copies, waits for them, and re-layouts  2.84 us
    pallas_call x2, Pallas kernels, prepare_block(): pl.pallas_call(prepare_kernel, in_specs=[SMEM, VMEM], out_specs=[VMEM, VM...  2.12 us
    pallas_call x1, Pallas kernels, finish(): pl.pallas_call(functools.partial(finish_kernel, used=used, scale=scale),...  1.37 us
  transfers between devices with their start and end apart: 10, of which 6 were waited for; matrix products, arithmetic and copies ran while one was open for 0% of the time, Pallas kernels for 16%

profile of v11, /device:TPU:0, one launch (start us, length us, event | category | flops | bytes accessed | tf_op | source)
XLA Modules:
  0.0 42.2 jit_solution(159204131200581636)
XLA Ops:
  0.6 0.5 %collective-permute-start.3 = (bf16[1,4,32,64,128]{4,3,2,1,0:T(8,128)(2,1)}, bf16[1,4,32,64,128]{4,3,2,1,0:T(8,128)(2,1)S(1)}, u32[]{:S(2)}, u32[]{:S(2)}) collective-permute-start(bf16[1,4,32,64,128]{4,3,2,1,0:T(8,128)(2,1)} %chol_ref.1), channel_id=1, source_target_pairs={{0,1},{1,0},{2,3},{3,2},{4,5},{5,4},{6,7},{7,6},{8,9},{9,8},{10,11... | collective-permute-start | bytes 6291464 | tf_op jit(solution)/shard_map/ppermute | solution.py:280
  1.1 3.7 %collective-permute-start.2 = (bf16[1,64,1280]{2,1,0:T(8,128)(2,1)}, bf16[1,64,1280]{2,1,0:T(8,128)(2,1)S(1)}, u32[]{:S(2)}, u32[]{:S(2)}) collective-permute-start(bf16[1,64,1280]{2,1,0:T(8,128)(2,1)} %refs_4_.1), channel_id=1, source_target_pairs={{0,8},{1,9},{2,10},{3,11},{4,12},{5,13},{6,14},{7,15},{8,0},{9,1},... | collective-permute-start | bytes 491528 | tf_op jit(solution)/shard_map/ppermute | solution.py:277
  4.8 1.6 %collective-permute-start.1 = (bf16[1,64,1280]{2,1,0:T(8,128)(2,1)}, bf16[1,64,1280]{2,1,0:T(8,128)(2,1)S(1)}, u32[]{:S(2)}, u32[]{:S(2)}) collective-permute-start(bf16[1,64,1280]{2,1,0:T(8,128)(2,1)} %refs_4_.1), channel_id=1, source_target_pairs={{0,4},{1,5},{2,6},{3,7},{4,0},{5,1},{6,2},{7,3},{8,12},{9,13},{10,... | collective-permute-start | bytes 491528 | tf_op jit(solution)/shard_map/ppermute | solution.py:277
  6.4 1.5 %collective-permute-start = (bf16[1,64,1280]{2,1,0:T(8,128)(2,1)}, bf16[1,64,1280]{2,1,0:T(8,128)(2,1)S(1)}, u32[]{:S(2)}, u32[]{:S(2)}) collective-permute-start(bf16[1,64,1280]{2,1,0:T(8,128)(2,1)} %refs_4_.1), channel_id=1, source_target_pairs={{0,2},{1,3},{2,0},{3,1},{4,6},{5,7},{6,4},{7,5},{8,10},{9,11},{10,... | collective-permute-start | bytes 491528 | tf_op jit(solution)/shard_map/ppermute | solution.py:277
  7.9 0.4 collective-permute-start.4
  8.3 0.0 copy-start
  8.3 1.6 %copy-done = bf16[1,4,32,64,128]{4,3,2,1,0:T(8,128)(2,1)S(1)} copy-done((bf16[1,4,32,64,128]{4,3,2,1,0:T(8,128)(2,1)S(1)}, bf16[1,4,32,64,128]{4,3,2,1,0:T(8,128)(2,1)}, u32[]{:S(2)}) %copy-start) | copy-done | bytes 2097176
  9.9 0.7 %copy-done.3 = s32[1,4]{1,0:T(1,128)S(1)} copy-done((s32[1,4]{1,0:T(1,128)S(1)}, s32[1,4]{1,0:T(1,128)}, u32[]{:S(2)}) %copy-start.3) | copy-done | bytes 40
  10.6 1.1 %prepare_block.2 = (bf16[2048,512]{1,0:T(8,128)(2,1)S(1)}, bf16[512,1024]{1,0:T(8,128)(2,1)S(1)}) custom-call(s32[1,4]{1,0:T(1,128)S(1)} %copy-done.3, bf16[1,4,32,64,128]{4,3,2,1,0:T(8,128)(2,1)S(1)} %copy-done), custom_call_target="tpu_custom_call" | custom-call | tf_op jit(solution)/shard_map/prepare_block/pallas_call | solution.py:39
  11.6 1.8 %collective-permute-done.2.refs_4_ = bf16[1,64,1280]{2,1,0:T(8,128)(2,1)S(1)} collective-permute-done((bf16[1,64,1280]{2,1,0:T(8,128)(2,1)}, bf16[1,64,1280]{2,1,0:T(8,128)(2,1)S(1)}, u32[]{:S(2)}, u32[]{:S(2)}) %collective-permute-start.2) | collective-permute-done | bytes 163872 | tf_op jit(solution)/shard_map/ppermute | solution.py:277
  13.4 1.0 %collective-permute-done.1.refs_6_ = bf16[1,64,1280]{2,1,0:T(8,128)(2,1)S(1)} collective-permute-done((bf16[1,64,1280]{2,1,0:T(8,128)(2,1)}, bf16[1,64,1280]{2,1,0:T(8,128)(2,1)S(1)}, u32[]{:S(2)}, u32[]{:S(2)}) %collective-permute-start.1) | collective-permute-done | bytes 163872 | tf_op jit(solution)/shard_map/ppermute | solution.py:277
  14.4 0.0 collective-permute-done.refs_5_
  14.4 1.6 %collective-permute-start.8 = (bf16[1,64,1280]{2,1,0:T(8,128)(2,1)S(1)}, bf16[1,64,1280]{2,1,0:T(8,128)(2,1)S(1)}, u32[]{:S(2)}, u32[]{:S(2)}) collective-permute-start(bf16[1,64,1280]{2,1,0:T(8,128)(2,1)S(1)} %collective-permute-done.2.refs_4_), channel_id=1, source_target_pairs={{0,2},{1,3},{2,0},{3,1},{4,6},{5,7},{6,4},{7,5},{8,10},{9,11},{10,... | collective-permute-start | bytes 491528 | tf_op jit(solution)/shard_map/ppermute | solution.py:277
  16.0 1.1 %collective-permute-start.7 = (bf16[1,64,1280]{2,1,0:T(8,128)(2,1)S(1)}, bf16[1,64,1280]{2,1,0:T(8,128)(2,1)S(1)}, u32[]{:S(2)}, u32[]{:S(2)}) collective-permute-start(bf16[1,64,1280]{2,1,0:T(8,128)(2,1)S(1)} %collective-permute-done.2.refs_4_), channel_id=1, source_target_pairs={{0,4},{1,5},{2,6},{3,7},{4,0},{5,1},{6,2},{7,3},{8,12},{9,13},{10,... | collective-permute-start | bytes 491528 | tf_op jit(solution)/shard_map/ppermute | solution.py:277
  17.1 0.8 %collective-permute-start.6 = (bf16[1,64,1280]{2,1,0:T(8,128)(2,1)S(1)}, bf16[1,64,1280]{2,1,0:T(8,128)(2,1)S(1)}, u32[]{:S(2)}, u32[]{:S(2)}) collective-permute-start(bf16[1,64,1280]{2,1,0:T(8,128)(2,1)S(1)} %collective-permute-done.2.refs_4_), channel_id=1, source_target_pairs={{0,6},{1,7},{2,4},{3,5},{4,2},{5,3},{6,0},{7,1},{8,14},{9,15},{10,... | collective-permute-start | bytes 491528 | tf_op jit(solution)/shard_map/ppermute | solution.py:277
  17.9 1.0 %collective-permute-done.4.refs_7_ = bf16[1,64,1280]{2,1,0:T(8,128)(2,1)S(1)} collective-permute-done((bf16[1,64,1280]{2,1,0:T(8,128)(2,1)}, bf16[1,64,1280]{2,1,0:T(8,128)(2,1)S(1)}, u32[]{:S(2)}, u32[]{:S(2)}) %collective-permute-start.4) | collective-permute-done | bytes 163872 | tf_op jit(solution)/shard_map/ppermute | solution.py:277
  18.9 0.0 collective-permute-done.3.chol_ref
  18.9 0.0 collective-permute-start.5
  18.9 1.1 %collective-permute-done.5.screen_ref = s32[1,4]{1,0:T(1,128)S(1)} collective-permute-done((s32[1,4]{1,0:T(1,128)S(1)}, s32[1,4]{1,0:T(1,128)S(1)}, u32[]{:S(2)}, u32[]{:S(2)}) %collective-permute-start.5) | collective-permute-done | bytes 48 | tf_op jit(solution)/shard_map/ppermute | solution.py:280
  20.1 1.1 %prepare_block.3 = (bf16[2048,512]{1,0:T(8,128)(2,1)S(1)}, bf16[512,1024]{1,0:T(8,128)(2,1)S(1)}) custom-call(s32[1,4]{1,0:T(1,128)S(1)} %collective-permute-done.5.screen_ref, bf16[1,4,32,64,128]{4,3,2,1,0:T(8,128)(2,1)S(1)} %collective-permute-done.3.chol_ref), custom_call_target="tpu_custom_call" | custom-call | tf_op jit(solution)/shard_map/prepare_block/pallas_call | solution.py:39
  21.1 0.0 copy-done.1
  21.2 0.0 copy-done.2
  21.2 3.1 %chip_terms.2.refs_8_ = f32[8,1,128]{2,1,0:T(1,128)S(1)} custom-call(s32[4,16]{1,0:T(4,128)S(1)} %bitcast.2, bf16[2048,512]{1,0:T(8,128)(2,1)S(1)} %get-tuple-element.16.refs_0_, bf16[512,1024]{1,0:T(8,128)(2,1)S(1)} %get-tuple-element.17.refs_1_, bf16[2048,512]{1,0:T(8,128)(2,1)S(1)} %get-tuple-element.20.refs_2_, ...), custom_call_target="tpu_custom_call" | custom-call | tf_op jit(solution)/shard_map/chip_terms/pallas_call | solution.py:190
  24.3 0.0 collective-permute-done.8.refs_7_
  24.3 0.0 collective-permute-done.7.refs_6_
  24.3 0.8 %collective-permute-done.6.refs_5_ = bf16[1,64,1280]{2,1,0:T(8,128)(2,1)S(1)} collective-permute-done((bf16[1,64,1280]{2,1,0:T(8,128)(2,1)S(1)}, bf16[1,64,1280]{2,1,0:T(8,128)(2,1)S(1)}, u32[]{:S(2)}, u32[]{:S(2)}) %collective-permute-start.6) | collective-permute-done | bytes 163872 | tf_op jit(solution)/shard_map/ppermute | solution.py:277
  25.2 3.7 %chip_terms.3.rows_ref = f32[8,1,128]{2,1,0:T(1,128)} custom-call(s32[4,16]{1,0:T(4,128)S(1)} %bitcast.3, bf16[2048,512]{1,0:T(8,128)(2,1)S(1)} %get-tuple-element.16.refs_0_, bf16[512,1024]{1,0:T(8,128)(2,1)S(1)} %get-tuple-element.17.refs_1_, bf16[2048,512]{1,0:T(8,128)(2,1)S(1)} %get-tuple-element.20.refs_2_, ...), custom_call_target="tpu_custom_call" | custom-call | tf_op jit(solution)/shard_map/chip_terms/pallas_call | solution.py:190
  28.9 4.8 %all-to-all-start = ((f32[8,1,128]{2,1,0:T(1,128)}), f32[8,1,128]{2,1,0:T(1,128)S(1)}, u32[]{:S(2)}, u32[]{:S(2)}) async-start(f32[8,1,128]{2,1,0:T(1,128)} %chip_terms.3.rows_ref), calls=%async_computation | async-start | bytes 8192 | tf_op jit(solution)/shard_map/all_to_all | solution.py:294
  33.8 1.3 %own_terms.1.own_ref = f32[1,128]{1,0:T(1,128)} custom-call(f32[8,1,128]{2,1,0:T(1,128)} %chip_terms.3.rows_ref), custom_call_target="tpu_custom_call" | custom-call | bytes 1048576 | tf_op jit(solution)/shard_map/own_terms/pallas_call | solution.py:246
  35.1 5.2 %all-to-all-done.rows_ref = f32[8,1,128]{2,1,0:T(1,128)S(1)} async-done(((f32[8,1,128]{2,1,0:T(1,128)}), f32[8,1,128]{2,1,0:T(1,128)S(1)}, u32[]{:S(2)}, u32[]{:S(2)}) %all-to-all-start) | async-done | bytes 4128 | tf_op jit(solution)/shard_map/all_to_all | solution.py:294
  40.2 0.6 %copy-done.4 = f32[8,1,128]{2,1,0:T(1,128)} copy-done((f32[8,1,128]{2,1,0:T(1,128)}, f32[8,1,128]{2,1,0:T(1,128)S(1)}, u32[]{:S(2)}) %copy-start.4) | copy-done | bytes 4120
  40.8 1.4 %finish.1 = (f32[1,512]{1,0:T(1,128)}, f32[1,1]{1,0:T(1,128)}) custom-call(f32[8,1,128]{2,1,0:T(1,128)} %copy-done.4, f32[1,128]{1,0:T(1,128)} %own_terms.1.own_ref), custom_call_target="tpu_custom_call" | custom-call | tf_op jit(solution)/shard_map/finish/pallas_call | solution.py:255
  (4 shorter events, 0.0 us)
Async XLA Ops:
  0.6 18.3 %collective-permute-start.3 = (bf16[1,4,32,64,128]{4,3,2,1,0:T(8,128)(2,1)}, bf16[1,4,32,64,128]{4,3,2,1,0:T(8,128)(2,1)S(1)}, u32[]{:S(2)}, u32[]{:S(2)}) collective-permute-start(bf16[1,4,32,64,128]{4,3,2,1,0:T(8,128)(2,1)} %chol_ref.1), channel_id=1, source_target_pairs={{0,1},{1,0},{2,3},{3,2},{4,5},{5,4},{6,7},{7,6},{8,9},{9,8},{10,11... | collective-permute-start | bytes 6291464 | tf_op jit(solution)/shard_map/ppermute | solution.py:280
  1.1 12.3 %collective-permute-start.2 = (bf16[1,64,1280]{2,1,0:T(8,128)(2,1)}, bf16[1,64,1280]{2,1,0:T(8,128)(2,1)S(1)}, u32[]{:S(2)}, u32[]{:S(2)}) collective-permute-start(bf16[1,64,1280]{2,1,0:T(8,128)(2,1)} %refs_4_.1), channel_id=1, source_target_pairs={{0,8},{1,9},{2,10},{3,11},{4,12},{5,13},{6,14},{7,15},{8,0},{9,1},... | collective-permute-start | bytes 491528 | tf_op jit(solution)/shard_map/ppermute | solution.py:277
  4.8 9.6 %collective-permute-start.1 = (bf16[1,64,1280]{2,1,0:T(8,128)(2,1)}, bf16[1,64,1280]{2,1,0:T(8,128)(2,1)S(1)}, u32[]{:S(2)}, u32[]{:S(2)}) collective-permute-start(bf16[1,64,1280]{2,1,0:T(8,128)(2,1)} %refs_4_.1), channel_id=1, source_target_pairs={{0,4},{1,5},{2,6},{3,7},{4,0},{5,1},{6,2},{7,3},{8,12},{9,13},{10,... | collective-permute-start | bytes 491528 | tf_op jit(solution)/shard_map/ppermute | solution.py:277
  6.4 8.0 %collective-permute-start = (bf16[1,64,1280]{2,1,0:T(8,128)(2,1)}, bf16[1,64,1280]{2,1,0:T(8,128)(2,1)S(1)}, u32[]{:S(2)}, u32[]{:S(2)}) collective-permute-start(bf16[1,64,1280]{2,1,0:T(8,128)(2,1)} %refs_4_.1), channel_id=1, source_target_pairs={{0,2},{1,3},{2,0},{3,1},{4,6},{5,7},{6,4},{7,5},{8,10},{9,11},{10,... | collective-permute-start | bytes 491528 | tf_op jit(solution)/shard_map/ppermute | solution.py:277
  7.9 11.0 %collective-permute-start.4 = (bf16[1,64,1280]{2,1,0:T(8,128)(2,1)}, bf16[1,64,1280]{2,1,0:T(8,128)(2,1)S(1)}, u32[]{:S(2)}, u32[]{:S(2)}) collective-permute-start(bf16[1,64,1280]{2,1,0:T(8,128)(2,1)} %refs_4_.1), channel_id=1, source_target_pairs={{0,6},{1,7},{2,4},{3,5},{4,2},{5,3},{6,0},{7,1},{8,14},{9,15},{10,... | collective-permute-start | bytes 491528 | tf_op jit(solution)/shard_map/ppermute | solution.py:277
  8.3 1.6 %copy-start = (bf16[1,4,32,64,128]{4,3,2,1,0:T(8,128)(2,1)S(1)}, bf16[1,4,32,64,128]{4,3,2,1,0:T(8,128)(2,1)}, u32[]{:S(2)}) copy-start(bf16[1,4,32,64,128]{4,3,2,1,0:T(8,128)(2,1)} %chol_ref.1) | copy-start | bytes 6291460
  9.9 0.7 %copy-start.3 = (s32[1,4]{1,0:T(1,128)S(1)}, s32[1,4]{1,0:T(1,128)}, u32[]{:S(2)}) copy-start(s32[1,4]{1,0:T(1,128)} %screen_ref.1) | copy-start | bytes 52
  10.5 10.6 %copy-start.1 = (bf16[1,64,1280]{2,1,0:T(8,128)(2,1)S(1)}, bf16[1,64,1280]{2,1,0:T(8,128)(2,1)}, u32[]{:S(2)}) copy-start(bf16[1,64,1280]{2,1,0:T(8,128)(2,1)} %refs_4_.1) | copy-start | bytes 491524
  10.5 10.6 %copy-start.2 = (s32[16,4]{0,1:T(4,128)S(1)}, s32[16,4]{0,1:T(4,128)}, u32[]{:S(2)}) copy-start(s32[16,4]{0,1:T(4,128)} %param.7) | copy-start | bytes 772
  14.4 9.9 %collective-permute-start.8 = (bf16[1,64,1280]{2,1,0:T(8,128)(2,1)S(1)}, bf16[1,64,1280]{2,1,0:T(8,128)(2,1)S(1)}, u32[]{:S(2)}, u32[]{:S(2)}) collective-permute-start(bf16[1,64,1280]{2,1,0:T(8,128)(2,1)S(1)} %collective-permute-done.2.refs_4_), channel_id=1, source_target_pairs={{0,2},{1,3},{2,0},{3,1},{4,6},{5,7},{6,4},{7,5},{8,10},{9,11},{10,... | collective-permute-start | bytes 491528 | tf_op jit(solution)/shard_map/ppermute | solution.py:277
  16.0 8.3 %collective-permute-start.7 = (bf16[1,64,1280]{2,1,0:T(8,128)(2,1)S(1)}, bf16[1,64,1280]{2,1,0:T(8,128)(2,1)S(1)}, u32[]{:S(2)}, u32[]{:S(2)}) collective-permute-start(bf16[1,64,1280]{2,1,0:T(8,128)(2,1)S(1)} %collective-permute-done.2.refs_4_), channel_id=1, source_target_pairs={{0,4},{1,5},{2,6},{3,7},{4,0},{5,1},{6,2},{7,3},{8,12},{9,13},{10,... | collective-permute-start | bytes 491528 | tf_op jit(solution)/shard_map/ppermute | solution.py:277
  17.1 8.1 %collective-permute-start.6 = (bf16[1,64,1280]{2,1,0:T(8,128)(2,1)S(1)}, bf16[1,64,1280]{2,1,0:T(8,128)(2,1)S(1)}, u32[]{:S(2)}, u32[]{:S(2)}) collective-permute-start(bf16[1,64,1280]{2,1,0:T(8,128)(2,1)S(1)} %collective-permute-done.2.refs_4_), channel_id=1, source_target_pairs={{0,6},{1,7},{2,4},{3,5},{4,2},{5,3},{6,0},{7,1},{8,14},{9,15},{10,... | collective-permute-start | bytes 491528 | tf_op jit(solution)/shard_map/ppermute | solution.py:277
  18.9 1.1 %collective-permute-start.5 = (s32[1,4]{1,0:T(1,128)S(1)}, s32[1,4]{1,0:T(1,128)S(1)}, u32[]{:S(2)}, u32[]{:S(2)}) collective-permute-start(s32[1,4]{1,0:T(1,128)S(1)} %copy-done.3), channel_id=1, source_target_pairs={{0,1},{1,0},{2,3},{3,2},{4,5},{5,4},{6,7},{7,6},{8,9},{9,8},{10,11... | collective-permute-start | bytes 56 | tf_op jit(solution)/shard_map/ppermute | solution.py:280
  28.9 11.3 %all-to-all-start = ((f32[8,1,128]{2,1,0:T(1,128)}), f32[8,1,128]{2,1,0:T(1,128)S(1)}, u32[]{:S(2)}, u32[]{:S(2)}) async-start(f32[8,1,128]{2,1,0:T(1,128)} %chip_terms.3.rows_ref), calls=%async_computation | async-start | bytes 8192 | tf_op jit(solution)/shard_map/all_to_all | solution.py:294
  40.2 0.6 %copy-start.4 = (f32[8,1,128]{2,1,0:T(1,128)}, f32[8,1,128]{2,1,0:T(1,128)S(1)}, u32[]{:S(2)}) copy-start(f32[8,1,128]{2,1,0:T(1,128)S(1)} %all-to-all-done.rows_ref) | copy-start | bytes 12292

commit v12 on v8

v12 whole, which is shorter than its diff:
```python
import functools

import jax
import jax.numpy as jnp
from jax import lax
from jax.experimental import pallas as pl
from jax.experimental.pallas import tpu as pltpu
from jax.sharding import PartitionSpec as P

LANES = 128
CORES = 2
VMEM_LIMIT = 32 * 1024 * 1024
WIDE = ((16, 8),)
NARROW = ((8, 8), (8, 0))
BATCH = 4
VMEM = pl.BlockSpec(memory_space=pltpu.VMEM)
SMEM = pl.BlockSpec(memory_space=pltpu.SMEM)
PARAMS = pltpu.CompilerParams(vmem_limit_bytes=VMEM_LIMIT)
SMALL = pl.CostEstimate(flops=0, bytes_accessed=0, transcendentals=0)
NT = (((1,), (1,)), ((), ()))
NN = (((1,), (0,)), ((), ()))


def prepare_kernel(screen_ref, chol_ref, block_ref, turned_ref):
    _, listed, vectors, occupied, width = chol_ref.shape
    for m in range(listed):
        keep = jnp.full((1, width), screen_ref[0, m].astype(jnp.float32)).astype(chol_ref.dtype)
        tile = chol_ref[0, m].reshape(vectors * occupied, width) * keep
        block_ref[:, m * width:(m + 1) * width] = tile
        turned_ref[m * width:(m + 1) * width, :] = tile.T


def prepare_block(screen, chol_tiles):
    _, listed, vectors, occupied, width = chol_tiles.shape
    rows, depth = vectors * occupied, listed * width
    return pl.pallas_call(
        prepare_kernel,
        in_specs=[SMEM, VMEM],
        out_specs=[VMEM, VMEM],
        out_shape=[
            jax.ShapeDtypeStruct((rows, depth), chol_tiles.dtype),
            jax.ShapeDtypeStruct((depth, rows), chol_tiles.dtype),
        ],
        compiler_params=PARAMS,
        cost_estimate=SMALL,
        name="prepare_block",
    )(screen, chol_tiles)


def pick_kernel(list_ref, theta_ref, *out_refs):
    listed = list_ref.shape[0]
    width = out_refs[0].shape[2] // listed
    me = lax.axis_index("chol")
    for offset, out_ref in enumerate(out_refs):
        device = me ^ (offset * CORES)
        for b, group in enumerate((device, device ^ 1)):
            for m in range(listed):
                start = pl.multiple_of(list_ref[m, group] * width, width)
                out_ref[b, :, m * width:(m + 1) * width] = theta_ref[0, :, pl.ds(start, width)]


def pick_tiles(listing, theta, depth, count):
    piece = jax.ShapeDtypeStruct((CORES, theta.shape[1], depth), theta.dtype)
    return pl.pallas_call(
        pick_kernel,
        in_specs=[SMEM, VMEM],
        out_specs=[VMEM] * count,
        out_shape=[piece] * count,
        compiler_params=PARAMS,
        cost_estimate=SMALL,
        name="pick_tiles",
    )(listing, theta)


def fold_rows(blocks, sub):
    high = sub < 4
    pairs = []
    for i in range(4):
        a, b = blocks[i], blocks[i + 4]
        pairs.append(jnp.where(high, a, b) + pltpu.roll(jnp.where(high, b, a), 4, 0))
    for shift in (2, 1):
        first = sub % (2 * shift) < shift
        half = len(pairs) // 2
        pairs = [
            jnp.where(
                first,
                pairs[i] + pltpu.roll(pairs[i], 8 - shift, 0),
                pairs[i + half] + pltpu.roll(pairs[i + half], shift, 0),
            )
            for i in range(half)
        ]
    return pairs[0]


def batch_terms(block_ref, turned_ref, theta, cross, store_rows, chunks, vectors, occupied):
    columns = theta.shape[0]
    tiles = columns // LANES

    low = lax.broadcasted_iota(jnp.int32, (occupied, LANES), 1) < occupied
    sub8 = lax.broadcasted_iota(jnp.int32, (8, LANES), 0)
    lane8 = lax.broadcasted_iota(jnp.int32, (8, LANES), 1)
    strip = (lane8 % occupied) // 8
    on_diag = lane8 % 8 == sub8

    def diagonal(block):
        merged = block[:8]
        for r in range(1, occupied // 8):
            merged = jnp.where(strip == r, block[8 * r:8 * r + 8], merged)
        return jnp.where(on_diag, merged, 0.0)

    k0 = 0
    while k0 < vectors:
        for size, by_matmul in chunks:
            span = slice(k0 * occupied, (k0 + size) * occupied)
            inner_mat = lax.dot_general(block_ref[span, :], theta, NT, preferred_element_type=jnp.float32)
            if by_matmul:
                turned = slice(k0 * occupied, (k0 + by_matmul) * occupied)
                flipped = lax.dot_general(theta, turned_ref[:, turned], NN, preferred_element_type=jnp.float32)
            for k8 in range(0, size, 8):
                for t in range(tiles):
                    c0 = t * LANES
                    diagonals = []
                    for k in range(k8, k8 + 8, 2):
                        r0 = k * occupied
                        top = inner_mat[r0:r0 + occupied, c0:c0 + LANES]
                        bottom = inner_mat[r0 + occupied:r0 + 2 * occupied, c0:c0 + LANES]
                        if k < by_matmul:
                            other = flipped[c0:c0 + LANES, r0:r0 + LANES]
                        else:
                            other = inner_mat[r0:r0 + LANES, c0:c0 + LANES].T
                        f_top, f_bottom = other[:occupied], other[occupied:]
                        swapped = pltpu.roll(jnp.where(low, f_bottom, f_top), occupied, 1)
                        product = jnp.where(low, top, bottom) * jnp.where(low, f_top, f_bottom)
                        product = product + jnp.where(low, bottom, top) * swapped
                        cross[t] = cross[t] + jnp.sum(product.reshape(occupied // 8, 8, LANES), axis=0)
                        diagonals.append(diagonal(top))
                        diagonals.append(diagonal(bottom))
                    store_rows(k0 + k8, t, fold_rows(diagonals, sub8))
            k0 += size


def terms_kernel(*refs, first, count, picked, chunks, vectors, batch, carried):
    if not picked:
        list_ref, refs = refs[0], refs[1:]
    block_refs, theta_refs, rest = refs[:4], refs[4:4 + count], refs[4 + count:]
    out_ref, picked_ref, rows_ref = rest[-3:]
    occupied = block_refs[0].shape[0] // vectors
    depth = block_refs[0].shape[1]
    used = CORES * vectors
    columns = batch * occupied
    tiles = columns // LANES
    me = lax.axis_index("chol")
    core = lax.rem(me, CORES)
    chip = me // CORES

    for b, group in enumerate((me, me ^ 1)):
        if picked:
            for i, ref in enumerate(theta_refs):
                picked_ref[b, i * occupied:(i + 1) * occupied, :] = ref[b]
        else:
            listed = list_ref.shape[0]
            width = depth // listed
            for m in range(listed):
                start = pl.multiple_of(list_ref[m, group] * width, width)
                for i, ref in enumerate(theta_refs):
                    picked_ref[b, i * occupied:(i + 1) * occupied, m * width:(m + 1) * width] = (
                        ref[0, :, pl.ds(start, width)]
                    )

    if carried:
        out_ref[...] = rest[0][...]
    else:
        out_ref[...] = jnp.zeros(out_ref.shape, out_ref.dtype)

    def one_batch(index):
        start = index * occupied
        rows = pl.ds(start if isinstance(index, int) else pl.multiple_of(start, columns), columns)
        cross = [jnp.zeros((8, LANES), jnp.float32) for _ in range(tiles)]
        for b in range(CORES):
            place = (core ^ b) * vectors

            def store_rows(k, t, value, place=place):
                rows_ref[pl.ds(pl.multiple_of(place + k, 8), 8), t * LANES:(t + 1) * LANES] = value

            batch_terms(
                block_refs[2 * b], block_refs[2 * b + 1], picked_ref[b, rows, :], cross, store_rows, chunks,
                vectors, occupied,
            )
        for t in range(tiles):
            rows_ref[used:used + 8, t * LANES:(t + 1) * LANES] = cross[t]
        values = rows_ref[...]
        parts = []
        for _ in range(3):
            part = values.astype(jnp.bfloat16)
            parts.append(part)
            values = values - part.astype(jnp.float32)
        seg_row = lax.broadcasted_iota(jnp.int32, (8, columns), 0)
        seg_col = lax.broadcasted_iota(jnp.int32, (8, columns), 1)
        segment = jnp.where(seg_col // occupied == seg_row, 1.0, 0.0).astype(jnp.bfloat16)
        sums = sum(
            lax.dot_general(segment, part, NT, preferred_element_type=jnp.float32) for part in parts
        )
        for i in range(batch):
            owner = chip ^ (first + index + i)
            out_ref[pl.ds(owner, 1), 0, :used + 8] = sums[i:i + 1]

    if count == batch:
        one_batch(0)
    else:
        @pl.loop(0, count // batch)
        def _(step):
            one_batch(step * batch)


def chip_terms(listing, blocks, thetas, carried, first, chunks, vectors, chips, out_width):
    count = len(thetas)
    batch = min(count, BATCH)
    rows, depth = blocks[0].shape
    occupied = rows // vectors
    operands = [*blocks, *thetas] + ([] if carried is None else [carried])
    in_specs = [VMEM] * len(operands)
    if listing is not None:
        operands, in_specs = [listing, *operands], [SMEM, *in_specs]
    return pl.pallas_call(
        functools.partial(
            terms_kernel, first=first, count=count, picked=listing is None, chunks=chunks, vectors=vectors, batch=batch,
            carried=carried is not None,
        ),
        in_specs=in_specs,
        out_specs=VMEM,
        out_shape=jax.ShapeDtypeStruct((chips, 1, out_width), jnp.float32),
        scratch_shapes=[
            pltpu.VMEM((CORES, count * occupied, depth), thetas[0].dtype),
            pltpu.VMEM((CORES * vectors + 8, batch * occupied), jnp.float32),
        ],
        compiler_params=PARAMS,
        cost_estimate=SMALL,
        name="chip_terms",
    )(*operands)


def energy_terms(rows, used):
    lane = lax.broadcasted_iota(jnp.int32, rows.shape, 1)
    return jnp.where(lane < used, rows * rows, jnp.where(lane < used + 8, -rows, 0.0))


def finish_kernel(rows_ref, bias_ref, energy_ref, bias_buf, energy_buf, sems, *, used, scale):
    chips, _, width = rows_ref.shape
    fit = LANES // used if width == LANES else 0
    lane = lax.broadcasted_iota(jnp.int32, (1, width), 1)
    if fit and chips % fit == 0:
        for d in range(0, chips, fit):
            packed = rows_ref[d]
            for i in range(1, fit):
                packed = jnp.where(lane < i * used, packed, pltpu.roll(rows_ref[d + i], i * used, 1))
            bias_buf[:, d * used:(d + fit) * used] = packed
    else:
        for d in range(chips):
            bias_buf[:, d * used:(d + 1) * used] = rows_ref[d, :, :used]
    bias_copy = pltpu.make_async_copy(bias_buf, bias_ref, sems.at[0])
    bias_copy.start()
    total = energy_terms(rows_ref[0], used)
    for d in range(1, chips):
        total = total + energy_terms(rows_ref[d], used)
    energy_buf[...] = jnp.sum(total, axis=1, keepdims=True) * scale
    energy_copy = pltpu.make_async_copy(energy_buf, energy_ref, sems.at[1])
    energy_copy.start()
    bias_copy.wait()
    energy_copy.wait()


def finish(rows, used, scale):
    chips = rows.shape[0]
    shapes = [(1, chips * used), (1, 1)]
    force_bias, energy = pl.pallas_call(
        functools.partial(finish_kernel, used=used, scale=scale),
        in_specs=[VMEM],
        out_specs=[pl.BlockSpec(memory_space=pl.ANY)] * 2,
        out_shape=[jax.ShapeDtypeStruct(s, jnp.float32) for s in shapes],
        scratch_shapes=[pltpu.VMEM(s, jnp.float32) for s in shapes] + [pltpu.SemaphoreType.DMA((2,))],
        name="finish",
    )(rows)
    return force_bias, energy.reshape(1)


def body(theta, chol_tiles, screen, tile_list):
    groups = lax.axis_size("chol")
    chips = groups // CORES
    half = chips // 2
    _, occupied, _ = theta.shape
    vectors = chol_tiles.shape[2]
    used = CORES * vectors
    out_width = LANES * ((used + 8 + LANES - 1) // LANES)
    listing = tile_list.T

    def to_chip(x, offset):
        return lax.ppermute(x, "chol", [(i, i ^ (offset * CORES)) for i in range(groups)])

    def to_core(x):
        return lax.ppermute(x, "chol", [(i, i ^ 1) for i in range(groups)])

    far = to_chip(theta, half)
    near = [theta] + [to_chip(theta, offset) for offset in range(1, half)]
    own, own_turned = prepare_block(screen, chol_tiles)
    near[1], near[2], own, far = lax.optimization_barrier((near[1], near[2], own, far))
    pieces = pick_tiles(listing, far, own.shape[1], half)
    beyond = [pieces[0]] + [to_chip(pieces[offset], offset) for offset in range(1, half)]
    other_chol, late_screen, near[-1] = lax.optimization_barrier((to_core(chol_tiles), screen, near[-1]))
    other, other_turned = prepare_block(to_core(late_screen), other_chol)
    blocks = [own, own_turned, other, other_turned]

    rows = chip_terms(listing, blocks, near, None, 0, WIDE, vectors, chips, out_width)
    rows = chip_terms(None, blocks, beyond, rows, half, NARROW, vectors, chips, out_width)
    same_core = [list(range(core, groups, CORES)) for core in range(CORES)]
    back = lax.all_to_all(rows, "chol", split_axis=0, concat_axis=0, tiled=True, axis_index_groups=same_core)
    return finish(back, used, 1.0 / (2.0 * occupied * occupied))


def solution(mesh):
    in_specs = (
        P(("grp", "chol"), None, None),
        P("chol", None, None, None, None),
        P("chol", None),
        P(),
    )
    out_specs = (P(("grp", "chol"), None), P(("grp", "chol")))
    return jax.shard_map(body, mesh=mesh, in_specs=in_specs, out_specs=out_specs, check_vma=False)
```

time: 41.3 us -> 39.7 us (0.961)
  waiting for transfers between devices: 5.71 us -> 3.73 us
    ppermute x7, waiting for transfers between devices: 4.59 us -> 2.62 us  [to_chip(): lax.ppermute(x, 'chol', [(i, i ^ offset * CORES) for i in range(groups)])]
    pallas_call x2, Pallas kernels: 6.53 us -> 5.52 us  [chip_terms(): pl.pallas_call(functools.partial(terms_kernel, first=first, count=count,...]
    pallas_call x0 -> x1, Pallas kernels: none -> 0.72 us  [pick_tiles(): pl.pallas_call(pick_kernel, in_specs=[SMEM, VMEM], out_specs=[VMEM] * cou...]
    pallas_call x2, Pallas kernels: 2.12 us -> 2.58 us  [prepare_block(): pl.pallas_call(prepare_kernel, in_specs=[SMEM, VMEM], out_specs=[VMEM, VM...]
  transfers between devices with their start and end apart: 9 -> 9, of which waited for: 5 -> 3; matrix products, arithmetic and copies ran while one was open for 0% -> 0% of each run, Pallas kernels for 13% -> 16%
where the time goes in v12:
time: 39.7 us; the launch traced here: 39.5 us
  blocking collectives  11.4 us (29%)
  starting transfers between devices  11.2 us (28%)
  Pallas kernels  10.2 us (26%)
  waiting for transfers between devices  3.73 us (9%)
  local copies, waits for them, and re-layouts  2.25 us (6%)
  between operations  0.71 us (2%)
    all_to_all x1, blocking collectives, body(): lax.all_to_all(rows, 'chol', split_axis=0, concat_axis=0, tiled=True, axi...  11.4 us
    ppermute x7, starting transfers between devices, to_chip(): lax.ppermute(x, 'chol', [(i, i ^ offset * CORES) for i in range(groups)])  10.7 us
    pallas_call x2, Pallas kernels, chip_terms(): pl.pallas_call(functools.partial(terms_kernel, first=first, count=count,...  5.52 us
    ppermute x7, waiting for transfers between devices, to_chip(): lax.ppermute(x, 'chol', [(i, i ^ offset * CORES) for i in range(groups)])  2.62 us
    pallas_call x2, Pallas kernels, prepare_block(): pl.pallas_call(prepare_kernel, in_specs=[SMEM, VMEM], out_specs=[VMEM, VM...  2.58 us
    unnamed x8, local copies, waits for them, and re-layouts  2.25 us
    pallas_call x1, Pallas kernels, finish(): pl.pallas_call(functools.partial(finish_kernel, used=used, scale=scale),...  1.37 us
    ppermute x2, waiting for transfers between devices, to_core(): return lax.ppermute(x, 'chol', [(i, i ^ 1) for i in range(groups)])  1.12 us
  transfers between devices with their start and end apart: 9, of which 3 were waited for; matrix products, arithmetic and copies ran while one was open for 0% of the time, Pallas kernels for 16%

profile of v12, /device:TPU:0, one launch (start us, length us, event | category | flops | bytes accessed | tf_op | source)
XLA Modules:
  0.0 39.5 jit_solution(3427980318095575001)
XLA Ops:
  0.6 0.5 %collective-permute-start.3 = (bf16[1,4,32,64,128]{4,3,2,1,0:T(8,128)(2,1)}, bf16[1,4,32,64,128]{4,3,2,1,0:T(8,128)(2,1)S(1)}, u32[]{:S(2)}, u32[]{:S(2)}) collective-permute-start(bf16[1,4,32,64,128]{4,3,2,1,0:T(8,128)(2,1)} %chol_ref.1), channel_id=1, source_target_pairs={{0,1},{1,0},{2,3},{3,2},{4,5},{5,4},{6,7},{7,6},{8,9},{9,8},{10,11... | collective-permute-start | bytes 6291464 | tf_op jit(solution)/shard_map/ppermute | solution.py:300
  1.1 3.7 %collective-permute-start.2 = (bf16[1,64,1280]{2,1,0:T(8,128)(2,1)}, bf16[1,64,1280]{2,1,0:T(8,128)(2,1)S(1)}, u32[]{:S(2)}, u32[]{:S(2)}) collective-permute-start(bf16[1,64,1280]{2,1,0:T(8,128)(2,1)} %refs_5_.1), channel_id=1, source_target_pairs={{0,8},{1,9},{2,10},{3,11},{4,12},{5,13},{6,14},{7,15},{8,0},{9,1},... | collective-permute-start | bytes 491528 | tf_op jit(solution)/shard_map/ppermute | solution.py:297
  4.8 1.6 %collective-permute-start.1 = (bf16[1,64,1280]{2,1,0:T(8,128)(2,1)}, bf16[1,64,1280]{2,1,0:T(8,128)(2,1)S(1)}, u32[]{:S(2)}, u32[]{:S(2)}) collective-permute-start(bf16[1,64,1280]{2,1,0:T(8,128)(2,1)} %refs_5_.1), channel_id=1, source_target_pairs={{0,4},{1,5},{2,6},{3,7},{4,0},{5,1},{6,2},{7,3},{8,12},{9,13},{10,... | collective-permute-start | bytes 491528 | tf_op jit(solution)/shard_map/ppermute | solution.py:297
  6.4 1.5 %collective-permute-start = (bf16[1,64,1280]{2,1,0:T(8,128)(2,1)}, bf16[1,64,1280]{2,1,0:T(8,128)(2,1)S(1)}, u32[]{:S(2)}, u32[]{:S(2)}) collective-permute-start(bf16[1,64,1280]{2,1,0:T(8,128)(2,1)} %refs_5_.1), channel_id=1, source_target_pairs={{0,2},{1,3},{2,0},{3,1},{4,6},{5,7},{6,4},{7,5},{8,10},{9,11},{10,... | collective-permute-start | bytes 491528 | tf_op jit(solution)/shard_map/ppermute | solution.py:297
  7.9 0.4 collective-permute-start.4
  8.3 1.6 %copy-done = bf16[1,4,32,64,128]{4,3,2,1,0:T(8,128)(2,1)S(1)} copy-done((bf16[1,4,32,64,128]{4,3,2,1,0:T(8,128)(2,1)S(1)}, bf16[1,4,32,64,128]{4,3,2,1,0:T(8,128)(2,1)}, u32[]{:S(2)}) %copy-start) | copy-done | bytes 2097176
  9.9 0.0 copy-start.3
  9.9 0.7 %copy-done.3 = s32[1,4]{1,0:T(1,128)S(1)} copy-done((s32[1,4]{1,0:T(1,128)S(1)}, s32[1,4]{1,0:T(1,128)}, u32[]{:S(2)}) %copy-start.3) | copy-done | bytes 40
  10.5 0.0 copy-start.2
  10.5 0.0 copy-start.1
  10.6 1.3 %prepare_block.2 = (bf16[2048,512]{1,0:T(8,128)(2,1)S(1)}, bf16[512,2048]{1,0:T(8,128)(2,1)S(1)}) custom-call(s32[1,4]{1,0:T(1,128)S(1)} %copy-done.3, bf16[1,4,32,64,128]{4,3,2,1,0:T(8,128)(2,1)S(1)} %copy-done), custom_call_target="tpu_custom_call" | custom-call | tf_op jit(solution)/shard_map/prepare_block/pallas_call | solution.py:36
  11.8 1.6 %collective-permute-done.2.theta_ref = bf16[1,64,1280]{2,1,0:T(8,128)(2,1)S(1)} collective-permute-done((bf16[1,64,1280]{2,1,0:T(8,128)(2,1)}, bf16[1,64,1280]{2,1,0:T(8,128)(2,1)S(1)}, u32[]{:S(2)}, u32[]{:S(2)}) %collective-permute-start.2) | collective-permute-done | bytes 163872 | tf_op jit(solution)/shard_map/ppermute | solution.py:297
  13.4 1.0 %collective-permute-done.1.refs_7_ = bf16[1,64,1280]{2,1,0:T(8,128)(2,1)S(1)} collective-permute-done((bf16[1,64,1280]{2,1,0:T(8,128)(2,1)}, bf16[1,64,1280]{2,1,0:T(8,128)(2,1)S(1)}, u32[]{:S(2)}, u32[]{:S(2)}) %collective-permute-start.1) | collective-permute-done | bytes 163872 | tf_op jit(solution)/shard_map/ppermute | solution.py:297
  14.4 0.0 collective-permute-done.refs_6_
  14.4 0.0 copy-done.2
  14.4 0.7 %pick_tiles.1 = (bf16[2,64,512]{2,1,0:T(8,128)(2,1)S(1)}, bf16[2,64,512]{2,1,0:T(8,128)(2,1)S(1)}, bf16[2,64,512]{2,1,0:T(8,128)(2,1)S(1)}, bf16[2,64,512]{2,1,0:T(8,128)(2,1)S(1)}) custom-call(s32[4,16]{1,0:T(4,128)S(1)} %bitcast.2, bf16[1,64,1280]{2,1,0:T(8,128)(2,1)S(1)} %collective-permute-done.2.theta_ref), custom_call_target="tpu_custom_call" | custom-call | tf_op jit(solution)/shard_map/pick_tiles/pallas_call | solution.py:64
  15.1 1.7 %collective-permute-start.6 = (bf16[2,64,512]{2,1,0:T(8,128)(2,1)S(1)}, bf16[2,64,512]{2,1,0:T(8,128)(2,1)S(1)}, u32[]{:S(2)}, u32[]{:S(2)}) collective-permute-start(bf16[2,64,512]{2,1,0:T(8,128)(2,1)S(1)} %get-tuple-element.28), channel_id=1, source_target_pairs={{0,2},{1,3},{2,0},{3,1},{4,6},{5,7},{6,4},{7,5},{8,10},{9,11},{10,... | collective-permute-start | bytes 393224 | tf_op jit(solution)/shard_map/ppermute | solution.py:297
  16.8 1.1 %collective-permute-start.7 = (bf16[2,64,512]{2,1,0:T(8,128)(2,1)S(1)}, bf16[2,64,512]{2,1,0:T(8,128)(2,1)S(1)}, u32[]{:S(2)}, u32[]{:S(2)}) collective-permute-start(bf16[2,64,512]{2,1,0:T(8,128)(2,1)S(1)} %get-tuple-element.29), channel_id=1, source_target_pairs={{0,4},{1,5},{2,6},{3,7},{4,0},{5,1},{6,2},{7,3},{8,12},{9,13},{10,... | collective-permute-start | bytes 393224 | tf_op jit(solution)/shard_map/ppermute | solution.py:297
  17.9 0.8 %collective-permute-start.8 = (bf16[2,64,512]{2,1,0:T(8,128)(2,1)S(1)}, bf16[2,64,512]{2,1,0:T(8,128)(2,1)S(1)}, u32[]{:S(2)}, u32[]{:S(2)}) collective-permute-start(bf16[2,64,512]{2,1,0:T(8,128)(2,1)S(1)} %get-tuple-element.30), channel_id=1, source_target_pairs={{0,6},{1,7},{2,4},{3,5},{4,2},{5,3},{6,0},{7,1},{8,14},{9,15},{10,... | collective-permute-start | bytes 393224 | tf_op jit(solution)/shard_map/ppermute | solution.py:297
  18.7 0.0 collective-permute-done.4.refs_8_
  18.7 0.0 collective-permute-done.3.chol_ref
  18.7 0.0 collective-permute-start.5
  18.7 1.1 %collective-permute-done.5.screen_ref = s32[1,4]{1,0:T(1,128)S(1)} collective-permute-done((s32[1,4]{1,0:T(1,128)S(1)}, s32[1,4]{1,0:T(1,128)S(1)}, u32[]{:S(2)}, u32[]{:S(2)}) %collective-permute-start.5) | collective-permute-done | bytes 48 | tf_op jit(solution)/shard_map/ppermute | solution.py:300
  19.8 1.3 %prepare_block.3 = (bf16[2048,512]{1,0:T(8,128)(2,1)S(1)}, bf16[512,2048]{1,0:T(8,128)(2,1)S(1)}) custom-call(s32[1,4]{1,0:T(1,128)S(1)} %collective-permute-done.5.screen_ref, bf16[1,4,32,64,128]{4,3,2,1,0:T(8,128)(2,1)S(1)} %collective-permute-done.3.chol_ref), custom_call_target="tpu_custom_call" | custom-call | tf_op jit(solution)/shard_map/prepare_block/pallas_call | solution.py:36
  21.1 0.0 copy-done.1
  21.1 3.0 %chip_terms.2.refs_8_ = f32[8,1,128]{2,1,0:T(1,128)S(1)} custom-call(s32[4,16]{1,0:T(4,128)S(1)} %bitcast.3, bf16[2048,512]{1,0:T(8,128)(2,1)S(1)} %get-tuple-element.20.refs_1_.refs_0_, bf16[512,2048]{1,0:T(8,128)(2,1)S(1)} %get-tuple-element.21.refs_2_.refs_1_, bf16[2048,512]{1,0:T(8,128)(2,1)S(1)} %get-tuple-element.24.refs_3_.refs_2_, ...), custom_call_target="tpu_custom_call" | custom-call | tf_op jit(solution)/shard_map/chip_terms/pallas_call | solution.py:224
  24.2 0.0 collective-permute-done.6.refs_5_
  24.2 0.0 collective-permute-done.7.refs_6_
  24.2 0.0 collective-permute-done.8.refs_7_
  24.2 2.5 %chip_terms.3 = f32[8,1,128]{2,1,0:T(1,128)S(1)} custom-call(bf16[2048,512]{1,0:T(8,128)(2,1)S(1)} %get-tuple-element.20.refs_1_.refs_0_, bf16[512,2048]{1,0:T(8,128)(2,1)S(1)} %get-tuple-element.21.refs_2_.refs_1_, bf16[2048,512]{1,0:T(8,128)(2,1)S(1)} %get-tuple-element.24.refs_3_.refs_2_, bf16[512,2048]{1,0:T(8,128)(2,1)S(1)} %get-tuple-element.25.refs_4_.refs_3_, ...), custom_call_target="tpu_custom_call" | custom-call | tf_op jit(solution)/shard_map/chip_terms/pallas_call | solution.py:224
  26.7 11.4 %all_to_all.5.rows_ref = f32[8,1,128]{2,1,0:T(1,128)} all-to-all(f32[8,1,128]{2,1,0:T(1,128)S(1)} %chip_terms.3), channel_id=1, replica_groups={{0,2,4,6,8,10,12,14},{1,3,5,7,9,11,13,15},{16,18,20,22,24,26,28,30},{17..., dimensions={0} | all-to-all | bytes 8192 | tf_op jit(solution)/shard_map/all_to_all | solution.py:315
  38.1 1.4 %finish.1 = (f32[1,512]{1,0:T(1,128)}, f32[1,1]{1,0:T(1,128)}) custom-call(f32[8,1,128]{2,1,0:T(1,128)} %all_to_all.5.rows_ref), custom_call_target="tpu_custom_call" | custom-call | tf_op jit(solution)/shard_map/finish/pallas_call | solution.py:275
  (1 shorter events, 0.0 us)
Async XLA Ops:
  0.6 18.1 %collective-permute-start.3 = (bf16[1,4,32,64,128]{4,3,2,1,0:T(8,128)(2,1)}, bf16[1,4,32,64,128]{4,3,2,1,0:T(8,128)(2,1)S(1)}, u32[]{:S(2)}, u32[]{:S(2)}) collective-permute-start(bf16[1,4,32,64,128]{4,3,2,1,0:T(8,128)(2,1)} %chol_ref.1), channel_id=1, source_target_pairs={{0,1},{1,0},{2,3},{3,2},{4,5},{5,4},{6,7},{7,6},{8,9},{9,8},{10,11... | collective-permute-start | bytes 6291464 | tf_op jit(solution)/shard_map/ppermute | solution.py:300
  1.1 12.3 %collective-permute-start.2 = (bf16[1,64,1280]{2,1,0:T(8,128)(2,1)}, bf16[1,64,1280]{2,1,0:T(8,128)(2,1)S(1)}, u32[]{:S(2)}, u32[]{:S(2)}) collective-permute-start(bf16[1,64,1280]{2,1,0:T(8,128)(2,1)} %refs_5_.1), channel_id=1, source_target_pairs={{0,8},{1,9},{2,10},{3,11},{4,12},{5,13},{6,14},{7,15},{8,0},{9,1},... | collective-permute-start | bytes 491528 | tf_op jit(solution)/shard_map/ppermute | solution.py:297
  4.8 9.6 %collective-permute-start.1 = (bf16[1,64,1280]{2,1,0:T(8,128)(2,1)}, bf16[1,64,1280]{2,1,0:T(8,128)(2,1)S(1)}, u32[]{:S(2)}, u32[]{:S(2)}) collective-permute-start(bf16[1,64,1280]{2,1,0:T(8,128)(2,1)} %refs_5_.1), channel_id=1, source_target_pairs={{0,4},{1,5},{2,6},{3,7},{4,0},{5,1},{6,2},{7,3},{8,12},{9,13},{10,... | collective-permute-start | bytes 491528 | tf_op jit(solution)/shard_map/ppermute | solution.py:297
  6.4 8.0 %collective-permute-start = (bf16[1,64,1280]{2,1,0:T(8,128)(2,1)}, bf16[1,64,1280]{2,1,0:T(8,128)(2,1)S(1)}, u32[]{:S(2)}, u32[]{:S(2)}) collective-permute-start(bf16[1,64,1280]{2,1,0:T(8,128)(2,1)} %refs_5_.1), channel_id=1, source_target_pairs={{0,2},{1,3},{2,0},{3,1},{4,6},{5,7},{6,4},{7,5},{8,10},{9,11},{10,... | collective-permute-start | bytes 491528 | tf_op jit(solution)/shard_map/ppermute | solution.py:297
  7.9 10.8 %collective-permute-start.4 = (bf16[1,64,1280]{2,1,0:T(8,128)(2,1)}, bf16[1,64,1280]{2,1,0:T(8,128)(2,1)S(1)}, u32[]{:S(2)}, u32[]{:S(2)}) collective-permute-start(bf16[1,64,1280]{2,1,0:T(8,128)(2,1)} %refs_5_.1), channel_id=1, source_target_pairs={{0,6},{1,7},{2,4},{3,5},{4,2},{5,3},{6,0},{7,1},{8,14},{9,15},{10,... | collective-permute-start | bytes 491528 | tf_op jit(solution)/shard_map/ppermute | solution.py:297
  8.3 1.6 %copy-start = (bf16[1,4,32,64,128]{4,3,2,1,0:T(8,128)(2,1)S(1)}, bf16[1,4,32,64,128]{4,3,2,1,0:T(8,128)(2,1)}, u32[]{:S(2)}) copy-start(bf16[1,4,32,64,128]{4,3,2,1,0:T(8,128)(2,1)} %chol_ref.1) | copy-start | bytes 6291460
  9.9 0.7 %copy-start.3 = (s32[1,4]{1,0:T(1,128)S(1)}, s32[1,4]{1,0:T(1,128)}, u32[]{:S(2)}) copy-start(s32[1,4]{1,0:T(1,128)} %screen_ref.1) | copy-start | bytes 52
  10.5 3.9 %copy-start.2 = (s32[16,4]{0,1:T(4,128)S(1)}, s32[16,4]{0,1:T(4,128)}, u32[]{:S(2)}) copy-start(s32[16,4]{0,1:T(4,128)} %param.7) | copy-start | bytes 772
  10.5 10.6 %copy-start.1 = (bf16[1,64,1280]{2,1,0:T(8,128)(2,1)S(1)}, bf16[1,64,1280]{2,1,0:T(8,128)(2,1)}, u32[]{:S(2)}) copy-start(bf16[1,64,1280]{2,1,0:T(8,128)(2,1)} %refs_5_.1) | copy-start | bytes 491524
  15.1 9.0 %collective-permute-start.6 = (bf16[2,64,512]{2,1,0:T(8,128)(2,1)S(1)}, bf16[2,64,512]{2,1,0:T(8,128)(2,1)S(1)}, u32[]{:S(2)}, u32[]{:S(2)}) collective-permute-start(bf16[2,64,512]{2,1,0:T(8,128)(2,1)S(1)} %get-tuple-element.28), channel_id=1, source_target_pairs={{0,2},{1,3},{2,0},{3,1},{4,6},{5,7},{6,4},{7,5},{8,10},{9,11},{10,... | collective-permute-start | bytes 393224 | tf_op jit(solution)/shard_map/ppermute | solution.py:297
  16.8 7.4 %collective-permute-start.7 = (bf16[2,64,512]{2,1,0:T(8,128)(2,1)S(1)}, bf16[2,64,512]{2,1,0:T(8,128)(2,1)S(1)}, u32[]{:S(2)}, u32[]{:S(2)}) collective-permute-start(bf16[2,64,512]{2,1,0:T(8,128)(2,1)S(1)} %get-tuple-element.29), channel_id=1, source_target_pairs={{0,4},{1,5},{2,6},{3,7},{4,0},{5,1},{6,2},{7,3},{8,12},{9,13},{10,... | collective-permute-start | bytes 393224 | tf_op jit(solution)/shard_map/ppermute | solution.py:297
  17.9 6.4 %collective-permute-start.8 = (bf16[2,64,512]{2,1,0:T(8,128)(2,1)S(1)}, bf16[2,64,512]{2,1,0:T(8,128)(2,1)S(1)}, u32[]{:S(2)}, u32[]{:S(2)}) collective-permute-start(bf16[2,64,512]{2,1,0:T(8,128)(2,1)S(1)} %get-tuple-element.30), channel_id=1, source_target_pairs={{0,6},{1,7},{2,4},{3,5},{4,2},{5,3},{6,0},{7,1},{8,14},{9,15},{10,... | collective-permute-start | bytes 393224 | tf_op jit(solution)/shard_map/ppermute | solution.py:297
  18.7 1.1 %collective-permute-start.5 = (s32[1,4]{1,0:T(1,128)S(1)}, s32[1,4]{1,0:T(1,128)S(1)}, u32[]{:S(2)}, u32[]{:S(2)}) collective-permute-start(s32[1,4]{1,0:T(1,128)S(1)} %copy-done.3), channel_id=1, source_target_pairs={{0,1},{1,0},{2,3},{3,2},{4,5},{5,4},{6,7},{7,6},{8,9},{9,8},{10,11... | collective-permute-start | bytes 56 | tf_op jit(solution)/shard_map/ppermute | solution.py:300

commit v13 on v12

--- a/solution.py
+++ b/solution.py
@@ -10,8 +10,8 @@
 LANES = 128
 CORES = 2
 VMEM_LIMIT = 32 * 1024 * 1024
-WIDE = ((16, 8),)
-NARROW = ((8, 8), (8, 0))
+NEAR = ((8, 4),)
+BEYOND = ((8, 8), (8, 0))
 BATCH = 4
 VMEM = pl.BlockSpec(memory_space=pltpu.VMEM)
 SMEM = pl.BlockSpec(memory_space=pltpu.SMEM)
@@ -21,21 +21,20 @@
 NN = (((1,), (0,)), ((), ()))
 
 
-def prepare_kernel(screen_ref, chol_ref, block_ref, turned_ref):
+def prepare_kernel(chol_ref, block_ref, turned_ref):
     _, listed, vectors, occupied, width = chol_ref.shape
     for m in range(listed):
-        keep = jnp.full((1, width), screen_ref[0, m].astype(jnp.float32)).astype(chol_ref.dtype)
-        tile = chol_ref[0, m].reshape(vectors * occupied, width) * keep
+        tile = chol_ref[0, m].reshape(vectors * occupied, width)
         block_ref[:, m * width:(m + 1) * width] = tile
         turned_ref[m * width:(m + 1) * width, :] = tile.T
 
 
-def prepare_block(screen, chol_tiles):
+def prepare_block(chol_tiles):
     _, listed, vectors, occupied, width = chol_tiles.shape
     rows, depth = vectors * occupied, listed * width
     return pl.pallas_call(
         prepare_kernel,
-        in_specs=[SMEM, VMEM],
+        in_specs=[VMEM],
         out_specs=[VMEM, VMEM],
         out_shape=[
             jax.ShapeDtypeStruct((rows, depth), chol_tiles.dtype),
@@ -44,7 +43,7 @@
         compiler_params=PARAMS,
         cost_estimate=SMALL,
         name="prepare_block",
-    )(screen, chol_tiles)
+    )(chol_tiles)
 
 
 def pick_kernel(list_ref, theta_ref, *out_refs):
@@ -92,9 +91,17 @@
     return pairs[0]
 
 
-def batch_terms(block_ref, turned_ref, theta, cross, store_rows, chunks, vectors, occupied):
-    columns = theta.shape[0]
-    tiles = columns // LANES
+def chunk_products(block_ref, turned_ref, theta, occupied, k0, size, by_matmul):
+    span = slice(k0 * occupied, (k0 + size) * occupied)
+    inner_mat = lax.dot_general(block_ref[span, :], theta, NT, preferred_element_type=jnp.float32)
+    if not by_matmul:
+        return inner_mat, None
+    turned = slice(k0 * occupied, (k0 + by_matmul) * occupied)
+    return inner_mat, lax.dot_general(theta, turned_ref[:, turned], NN, preferred_element_type=jnp.float32)
+
+
+def chunk_terms(inner_mat, flipped, cross, store_rows, occupied, k0, size, by_matmul):
+    tiles = inner_mat.shape[1] // LANES
 
     low = lax.broadcasted_iota(jnp.int32, (occupied, LANES), 1) < occupied
     sub8 = lax.broadcasted_iota(jnp.int32, (8, LANES), 0)
@@ -108,42 +115,44 @@
             merged = jnp.where(strip == r, block[8 * r:8 * r + 8], merged)
         return jnp.where(on_diag, merged, 0.0)
 
-    k0 = 0
-    while k0 < vectors:
-        for size, by_matmul in chunks:
-            span = slice(k0 * occupied, (k0 + size) * occupied)
-            inner_mat = lax.dot_general(block_ref[span, :], theta, NT, preferred_element_type=jnp.float32)
-            if by_matmul:
-                turned = slice(k0 * occupied, (k0 + by_matmul) * occupied)
-                flipped = lax.dot_general(theta, turned_ref[:, turned], NN, preferred_element_type=jnp.float32)
-            for k8 in range(0, size, 8):
-                for t in range(tiles):
-                    c0 = t * LANES
-                    diagonals = []
-                    for k in range(k8, k8 + 8, 2):
-                        r0 = k * occupied
-                        top = inner_mat[r0:r0 + occupied, c0:c0 + LANES]
-                        bottom = inner_mat[r0 + occupied:r0 + 2 * occupied, c0:c0 + LANES]
-                        if k < by_matmul:
-                            other = flipped[c0:c0 + LANES, r0:r0 + LANES]
-                        else:
-                            other = inner_mat[r0:r0 + LANES, c0:c0 + LANES].T
-                        f_top, f_bottom = other[:occupied], other[occupied:]
-                        swapped = pltpu.roll(jnp.where(low, f_bottom, f_top), occupied, 1)
-                        product = jnp.where(low, top, bottom) * jnp.where(low, f_top, f_bottom)
-                        product = product + jnp.where(low, bottom, top) * swapped
-                        cross[t] = cross[t] + jnp.sum(product.reshape(occupied // 8, 8, LANES), axis=0)
-                        diagonals.append(diagonal(top))
-                        diagonals.append(diagonal(bottom))
-                    store_rows(k0 + k8, t, fold_rows(diagonals, sub8))
-            k0 += size
-
-
-def terms_kernel(*refs, first, count, picked, chunks, vectors, batch, carried):
-    if not picked:
-        list_ref, refs = refs[0], refs[1:]
+    for k8 in range(0, size, 8):
+        for t in range(tiles):
+            c0 = t * LANES
+            diagonals = []
+            for k in range(k8, k8 + 8, 2):
+                r0 = k * occupied
+                top = inner_mat[r0:r0 + occupied, c0:c0 + LANES]
+                bottom = inner_mat[r0 + occupied:r0 + 2 * occupied, c0:c0 + LANES]
+                if k < by_matmul:
+                    other = flipped[c0:c0 + LANES, r0:r0 + LANES]
+                else:
+                    other = inner_mat[r0:r0 + LANES, c0:c0 + LANES].T
+                f_top, f_bottom = other[:occupied], other[occupied:]
+                swapped = pltpu.roll(jnp.where(low, f_bottom, f_top), occupied, 1)
+                product = jnp.where(low, top, bottom) * jnp.where(low, f_top, f_bottom)
+                product = product + jnp.where(low, bottom, top) * swapped
+                cross[t] = cross[t] + jnp.sum(product.reshape(occupied // 8, 8, LANES), axis=0)
+                diagonals.append(diagonal(top))
+                diagonals.append(diagonal(bottom))
+            store_rows(k0 + k8, t, fold_rows(diagonals, sub8))
+
+
+def mask_kernel_rows(screen_refs, listed, width):
+    return [
+        jnp.concatenate(
+            [jnp.full((1, width), ref[0, m].astype(jnp.float32)) for m in range(listed)], axis=1
+        )
+        for ref in screen_refs
+    ]
+
+
+def terms_kernel(*refs, first, count, picked, chunks, vectors, batch):
+    if picked:
+        mask_ref, carried_ref, refs = refs[0], refs[1], refs[2:]
+    else:
+        list_ref, screen_refs, refs = refs[0], refs[1:3], refs[3:]
     block_refs, theta_refs, rest = refs[:4], refs[4:4 + count], refs[4 + count:]
-    out_ref, picked_ref, rows_ref = rest[-3:]
+    out_ref, picked_ref, rows_ref = rest[0], rest[-2], rest[-1]
     occupied = block_refs[0].shape[0] // vectors
     depth = block_refs[0].shape[1]
     used = CORES * vectors
@@ -153,39 +162,56 @@
     core = lax.rem(me, CORES)
     chip = me // CORES
 
+    if picked:
+        masks = [mask_ref[b:b + 1, :] for b in range(CORES)]
+        out_ref[...] = carried_ref[...]
+    else:
+        listed = list_ref.shape[0]
+        width = depth // listed
+        masks = mask_kernel_rows(screen_refs, listed, width)
+        mask_ref = rest[1]
+        for b in range(CORES):
+            mask_ref[b:b + 1, :] = masks[b]
+        out_ref[...] = jnp.zeros(out_ref.shape, out_ref.dtype)
     for b, group in enumerate((me, me ^ 1)):
+        mask = masks[b].astype(picked_ref.dtype)
         if picked:
             for i, ref in enumerate(theta_refs):
-                picked_ref[b, i * occupied:(i + 1) * occupied, :] = ref[b]
+                picked_ref[b, i * occupied:(i + 1) * occupied, :] = ref[b] * mask
         else:
-            listed = list_ref.shape[0]
-            width = depth // listed
             for m in range(listed):
                 start = pl.multiple_of(list_ref[m, group] * width, width)
+                tile_mask = mask[:, m * width:(m + 1) * width]
                 for i, ref in enumerate(theta_refs):
                     picked_ref[b, i * occupied:(i + 1) * occupied, m * width:(m + 1) * width] = (
-                        ref[0, :, pl.ds(start, width)]
+                        ref[0, :, pl.ds(start, width)] * tile_mask
                     )
-
-    if carried:
-        out_ref[...] = rest[0][...]
-    else:
-        out_ref[...] = jnp.zeros(out_ref.shape, out_ref.dtype)
 
     def one_batch(index):
         start = index * occupied
         rows = pl.ds(start if isinstance(index, int) else pl.multiple_of(start, columns), columns)
         cross = [jnp.zeros((8, LANES), jnp.float32) for _ in range(tiles)]
+        tasks = []
         for b in range(CORES):
+            theta, k0 = picked_ref[b, rows, :], 0
+            while k0 < vectors:
+                for size, by_matmul in chunks:
+                    tasks.append((b, theta, k0, size, by_matmul))
+                    k0 += size
+
+        def products(task):
+            b, theta, k0, size, by_matmul = task
+            return chunk_products(block_refs[2 * b], block_refs[2 * b + 1], theta, occupied, k0, size, by_matmul)
+
+        ahead = products(tasks[0])
+        for i, (b, _, k0, size, by_matmul) in enumerate(tasks):
+            now, ahead = ahead, products(tasks[i + 1]) if i + 1 < len(tasks) else None
             place = (core ^ b) * vectors
 
             def store_rows(k, t, value, place=place):
                 rows_ref[pl.ds(pl.multiple_of(place + k, 8), 8), t * LANES:(t + 1) * LANES] = value
 
-            batch_terms(
-                block_refs[2 * b], block_refs[2 * b + 1], picked_ref[b, rows, :], cross, store_rows, chunks,
-                vectors, occupied,
-            )
+            chunk_terms(*now, cross, store_rows, occupied, k0, size, by_matmul)
         for t in range(tiles):
             rows_ref[used:used + 8, t * LANES:(t + 1) * LANES] = cross[t]
         values = rows_ref[...]
@@ -212,23 +238,22 @@
             one_batch(step * batch)
 
 
-def chip_terms(listing, blocks, thetas, carried, first, chunks, vectors, chips, out_width):
+def chip_terms(scalars, so_far, blocks, thetas, first, chunks, vectors, chips, out_width):
     count = len(thetas)
     batch = min(count, BATCH)
     rows, depth = blocks[0].shape
     occupied = rows // vectors
-    operands = [*blocks, *thetas] + ([] if carried is None else [carried])
-    in_specs = [VMEM] * len(operands)
-    if listing is not None:
-        operands, in_specs = [listing, *operands], [SMEM, *in_specs]
+    vector_operands = [*so_far, *blocks, *thetas]
+    out_shape = [jax.ShapeDtypeStruct((chips, 1, out_width), jnp.float32)]
+    if scalars:
+        out_shape.append(jax.ShapeDtypeStruct((CORES, depth), jnp.float32))
     return pl.pallas_call(
         functools.partial(
-            terms_kernel, first=first, count=count, picked=listing is None, chunks=chunks, vectors=vectors, batch=batch,
-            carried=carried is not None,
+            terms_kernel, first=first, count=count, picked=not scalars, chunks=chunks, vectors=vectors, batch=batch
         ),
-        in_specs=in_specs,
-        out_specs=VMEM,
-        out_shape=jax.ShapeDtypeStruct((chips, 1, out_width), jnp.float32),
+        in_specs=[SMEM] * len(scalars) + [VMEM] * len(vector_operands),
+        out_specs=[VMEM] * len(out_shape),
+        out_shape=out_shape,
         scratch_shapes=[
             pltpu.VMEM((CORES, count * occupied, depth), thetas[0].dtype),
             pltpu.VMEM((CORES * vectors + 8, batch * occupied), jnp.float32),
@@ -236,7 +261,7 @@
         compiler_params=PARAMS,
         cost_estimate=SMALL,
         name="chip_terms",
-    )(*operands)
+    )(*scalars, *vector_operands)
 
 
 def energy_terms(rows, used):
@@ -301,16 +326,17 @@
 
     far = to_chip(theta, half)
     near = [theta] + [to_chip(theta, offset) for offset in range(1, half)]
-    own, own_turned = prepare_block(screen, chol_tiles)
-    near[1], near[2], own, far = lax.optimization_barrier((near[1], near[2], own, far))
+    own, own_turned = prepare_block(chol_tiles)
+    near[2], far, near[1], own = lax.optimization_barrier((near[2], far, near[1], own))
     pieces = pick_tiles(listing, far, own.shape[1], half)
     beyond = [pieces[0]] + [to_chip(pieces[offset], offset) for offset in range(1, half)]
     other_chol, late_screen, near[-1] = lax.optimization_barrier((to_core(chol_tiles), screen, near[-1]))
-    other, other_turned = prepare_block(to_core(late_screen), other_chol)
+    other, other_turned = prepare_block(other_chol)
     blocks = [own, own_turned, other, other_turned]
 
-    rows = chip_terms(listing, blocks, near, None, 0, WIDE, vectors, chips, out_width)
-    rows = chip_terms(None, blocks, beyond, rows, half, NARROW, vectors, chips, out_width)
+    scalars = [listing, screen, to_core(late_screen)]
+    rows, masks = chip_terms(scalars, [], blocks, near, 0, NEAR, vectors, chips, out_width)
+    rows, = chip_terms([], [masks, rows], blocks, beyond, half, BEYOND, vectors, chips, out_width)
     same_core = [list(range(core, groups, CORES)) for core in range(CORES)]
     back = lax.all_to_all(rows, "chol", split_axis=0, concat_axis=0, tiled=True, axis_index_groups=same_core)
     return finish(back, used, 1.0 / (2.0 * occupied * occupied))

time: 39.7 us -> 39.7 us (level)
  waiting for transfers between devices: 3.73 us -> 5.63 us
  Pallas kernels: 10.2 us -> 8.84 us
  local copies, waits for them, and re-layouts: 2.25 us -> 1.6 us
    ppermute x7, waiting for transfers between devices: 2.62 us -> 5.23 us  [to_chip(): lax.ppermute(x, 'chol', [(i, i ^ offset * CORES) for i in range(groups)])]
    pallas_call x2, Pallas kernels: 2.58 us -> 1.43 us  [prepare_block(): pl.pallas_call(prepare_kernel, in_specs=[VMEM], out_specs=[VMEM, VMEM], o...]
    ppermute x2, waiting for transfers between devices: 1.12 us -> 0.39 us  [to_core(): return lax.ppermute(x, 'chol', [(i, i ^ 1) for i in range(groups)])]
    unnamed x8, local copies, waits for them, and re-layouts: 2.25 us -> 1.6 us
  transfers between devices with their start and end apart: 9 -> 9, of which waited for: 3 -> 4; matrix products, arithmetic and copies ran while one was open for 0% -> 0% of each run, Pallas kernels for 16% -> 13%
where the time goes in v13:
time: 39.7 us; the launch traced here: 39.5 us
  blocking collectives  11.4 us (29%)
  starting transfers between devices  11.3 us (28%)
  Pallas kernels  8.84 us (22%)
  waiting for transfers between devices  5.63 us (14%)
  local copies, waits for them, and re-layouts  1.6 us (4%)
  between operations  0.69 us (2%)
    all_to_all x1, blocking collectives, body(): lax.all_to_all(rows, 'chol', split_axis=0, concat_axis=0, tiled=True, axi...  11.4 us
    ppermute x7, starting transfers between devices, to_chip(): lax.ppermute(x, 'chol', [(i, i ^ offset * CORES) for i in range(groups)])  10.7 us
    pallas_call x2, Pallas kernels, chip_terms(): pl.pallas_call(functools.partial(terms_kernel, first=first, count=count,...  5.32 us
    ppermute x7, waiting for transfers between devices, to_chip(): lax.ppermute(x, 'chol', [(i, i ^ offset * CORES) for i in range(groups)])  5.23 us
    unnamed x8, local copies, waits for them, and re-layouts  1.6 us
    pallas_call x2, Pallas kernels, prepare_block(): pl.pallas_call(prepare_kernel, in_specs=[VMEM], out_specs=[VMEM, VMEM], o...  1.43 us
    pallas_call x1, Pallas kernels, finish(): pl.pallas_call(functools.partial(finish_kernel, used=used, scale=scale),...  1.37 us
  transfers between devices with their start and end apart: 9, of which 4 were waited for; matrix products, arithmetic and copies ran while one was open for 0% of the time, Pallas kernels for 13%

profile of v13, /device:TPU:0, one launch (start us, length us, event | category | flops | bytes accessed | tf_op | source)
XLA Modules:
  0.0 39.5 jit_solution(13977018270244385557)
XLA Ops:
  0.6 0.5 %collective-permute-start = (bf16[1,4,32,64,128]{4,3,2,1,0:T(8,128)(2,1)}, bf16[1,4,32,64,128]{4,3,2,1,0:T(8,128)(2,1)S(1)}, u32[]{:S(2)}, u32[]{:S(2)}) collective-permute-start(bf16[1,4,32,64,128]{4,3,2,1,0:T(8,128)(2,1)} %chol_ref.1), channel_id=1, source_target_pairs={{0,1},{1,0},{2,3},{3,2},{4,5},{5,4},{6,7},{7,6},{8,9},{9,8},{10,11... | collective-permute-start | bytes 6291464 | tf_op jit(solution)/shard_map/ppermute | solution.py:325
  1.1 3.7 %collective-permute-start.4 = (bf16[1,64,1280]{2,1,0:T(8,128)(2,1)}, bf16[1,64,1280]{2,1,0:T(8,128)(2,1)S(1)}, u32[]{:S(2)}, u32[]{:S(2)}) collective-permute-start(bf16[1,64,1280]{2,1,0:T(8,128)(2,1)} %refs_7_.1), channel_id=1, source_target_pairs={{0,8},{1,9},{2,10},{3,11},{4,12},{5,13},{6,14},{7,15},{8,0},{9,1},... | collective-permute-start | bytes 491528 | tf_op jit(solution)/shard_map/ppermute | solution.py:322
  4.8 1.6 %collective-permute-start.3 = (bf16[1,64,1280]{2,1,0:T(8,128)(2,1)}, bf16[1,64,1280]{2,1,0:T(8,128)(2,1)S(1)}, u32[]{:S(2)}, u32[]{:S(2)}) collective-permute-start(bf16[1,64,1280]{2,1,0:T(8,128)(2,1)} %refs_7_.1), channel_id=1, source_target_pairs={{0,4},{1,5},{2,6},{3,7},{4,0},{5,1},{6,2},{7,3},{8,12},{9,13},{10,... | collective-permute-start | bytes 491528 | tf_op jit(solution)/shard_map/ppermute | solution.py:322
  6.4 1.5 %collective-permute-start.5 = (bf16[1,64,1280]{2,1,0:T(8,128)(2,1)}, bf16[1,64,1280]{2,1,0:T(8,128)(2,1)S(1)}, u32[]{:S(2)}, u32[]{:S(2)}) collective-permute-start(bf16[1,64,1280]{2,1,0:T(8,128)(2,1)} %refs_7_.1), channel_id=1, source_target_pairs={{0,2},{1,3},{2,0},{3,1},{4,6},{5,7},{6,4},{7,5},{8,10},{9,11},{10,... | collective-permute-start | bytes 491528 | tf_op jit(solution)/shard_map/ppermute | solution.py:322
  7.9 0.4 collective-permute-start.1
  8.3 0.0 copy-start
  8.3 1.6 %copy-done = bf16[1,4,32,64,128]{4,3,2,1,0:T(8,128)(2,1)S(1)} copy-done((bf16[1,4,32,64,128]{4,3,2,1,0:T(8,128)(2,1)S(1)}, bf16[1,4,32,64,128]{4,3,2,1,0:T(8,128)(2,1)}, u32[]{:S(2)}) %copy-start) | copy-done | bytes 2097176
  9.9 0.0 copy-start.3
  9.9 0.0 copy-start.1
  9.9 0.7 %prepare_block.2 = (bf16[2048,512]{1,0:T(8,128)(2,1)S(1)}, bf16[512,2048]{1,0:T(8,128)(2,1)S(1)}) custom-call(bf16[1,4,32,64,128]{4,3,2,1,0:T(8,128)(2,1)S(1)} %copy-done), custom_call_target="tpu_custom_call" | custom-call | tf_op jit(solution)/shard_map/prepare_block/pallas_call | solution.py:35
  10.6 2.8 %collective-permute-done.4.theta_ref = bf16[1,64,1280]{2,1,0:T(8,128)(2,1)S(1)} collective-permute-done((bf16[1,64,1280]{2,1,0:T(8,128)(2,1)}, bf16[1,64,1280]{2,1,0:T(8,128)(2,1)S(1)}, u32[]{:S(2)}, u32[]{:S(2)}) %collective-permute-start.4) | collective-permute-done | bytes 163872 | tf_op jit(solution)/shard_map/ppermute | solution.py:322
  13.4 1.0 %collective-permute-done.3.refs_9_ = bf16[1,64,1280]{2,1,0:T(8,128)(2,1)S(1)} collective-permute-done((bf16[1,64,1280]{2,1,0:T(8,128)(2,1)}, bf16[1,64,1280]{2,1,0:T(8,128)(2,1)S(1)}, u32[]{:S(2)}, u32[]{:S(2)}) %collective-permute-start.3) | collective-permute-done | bytes 163872 | tf_op jit(solution)/shard_map/ppermute | solution.py:322
  14.4 0.0 collective-permute-done.5.refs_8_
  14.4 0.0 copy-done.2
  14.4 0.7 %pick_tiles.1 = (bf16[2,64,512]{2,1,0:T(8,128)(2,1)S(1)}, bf16[2,64,512]{2,1,0:T(8,128)(2,1)S(1)}, bf16[2,64,512]{2,1,0:T(8,128)(2,1)S(1)}, bf16[2,64,512]{2,1,0:T(8,128)(2,1)S(1)}) custom-call(s32[4,16]{1,0:T(4,128)S(1)} %bitcast.2, bf16[1,64,1280]{2,1,0:T(8,128)(2,1)S(1)} %collective-permute-done.4.theta_ref), custom_call_target="tpu_custom_call" | custom-call | tf_op jit(solution)/shard_map/pick_tiles/pallas_call | solution.py:63
  15.1 1.7 %collective-permute-start.6 = (bf16[2,64,512]{2,1,0:T(8,128)(2,1)S(1)}, bf16[2,64,512]{2,1,0:T(8,128)(2,1)S(1)}, u32[]{:S(2)}, u32[]{:S(2)}) collective-permute-start(bf16[2,64,512]{2,1,0:T(8,128)(2,1)S(1)} %get-tuple-element.35), channel_id=1, source_target_pairs={{0,2},{1,3},{2,0},{3,1},{4,6},{5,7},{6,4},{7,5},{8,10},{9,11},{10,... | collective-permute-start | bytes 393224 | tf_op jit(solution)/shard_map/ppermute | solution.py:322
  16.8 1.1 %collective-permute-start.7 = (bf16[2,64,512]{2,1,0:T(8,128)(2,1)S(1)}, bf16[2,64,512]{2,1,0:T(8,128)(2,1)S(1)}, u32[]{:S(2)}, u32[]{:S(2)}) collective-permute-start(bf16[2,64,512]{2,1,0:T(8,128)(2,1)S(1)} %get-tuple-element.36), channel_id=1, source_target_pairs={{0,4},{1,5},{2,6},{3,7},{4,0},{5,1},{6,2},{7,3},{8,12},{9,13},{10,... | collective-permute-start | bytes 393224 | tf_op jit(solution)/shard_map/ppermute | solution.py:322
  17.9 0.8 %collective-permute-start.8 = (bf16[2,64,512]{2,1,0:T(8,128)(2,1)S(1)}, bf16[2,64,512]{2,1,0:T(8,128)(2,1)S(1)}, u32[]{:S(2)}, u32[]{:S(2)}) collective-permute-start(bf16[2,64,512]{2,1,0:T(8,128)(2,1)S(1)} %get-tuple-element.37), channel_id=1, source_target_pairs={{0,6},{1,7},{2,4},{3,5},{4,2},{5,3},{6,0},{7,1},{8,14},{9,15},{10,... | collective-permute-start | bytes 393224 | tf_op jit(solution)/shard_map/ppermute | solution.py:322
  18.7 0.0 collective-permute-done.1.refs_10_
  18.7 0.0 collective-permute-done.chol_ref
  18.7 0.0 copy-done.3
  18.7 0.1 collective-permute-start.2
  18.8 0.7 %prepare_block.3 = (bf16[2048,512]{1,0:T(8,128)(2,1)S(1)}, bf16[512,2048]{1,0:T(8,128)(2,1)S(1)}) custom-call(bf16[1,4,32,64,128]{4,3,2,1,0:T(8,128)(2,1)S(1)} %collective-permute-done.chol_ref), custom_call_target="tpu_custom_call" | custom-call | tf_op jit(solution)/shard_map/prepare_block/pallas_call | solution.py:35
  19.5 0.4 collective-permute-done.2.refs_2_
  19.9 0.0 copy-done.1
  19.9 2.9 %chip_terms.2 = (f32[8,1,128]{2,1,0:T(1,128)S(1)}, f32[2,512]{1,0:T(2,128)S(1)}) custom-call(s32[4,16]{1,0:T(4,128)S(1)} %bitcast.3, s32[1,4]{1,0:T(1,128)S(1)} %copy-done.3, s32[1,4]{1,0:T(1,128)S(1)} %collective-permute-done.2.refs_2_, bf16[2048,512]{1,0:T(8,128)(2,1)S(1)} %get-tuple-element.23.refs_3_.refs_2_, ...), custom_call_target="tpu_custom_call" | custom-call | tf_op jit(solution)/shard_map/chip_terms/pallas_call | solution.py:250
  22.8 0.0 collective-permute-done.6.refs_7_
  22.8 0.0 collective-permute-done.7.refs_8_
  22.8 1.4 %collective-permute-done.8.refs_9_ = bf16[2,64,512]{2,1,0:T(8,128)(2,1)S(1)} collective-permute-done((bf16[2,64,512]{2,1,0:T(8,128)(2,1)S(1)}, bf16[2,64,512]{2,1,0:T(8,128)(2,1)S(1)}, u32[]{:S(2)}, u32[]{:S(2)}) %collective-permute-start.8) | collective-permute-done | bytes 131104 | tf_op jit(solution)/shard_map/ppermute | solution.py:322
  24.2 2.4 %chip_terms.3 = f32[8,1,128]{2,1,0:T(1,128)S(1)} custom-call(f32[2,512]{1,0:T(2,128)S(1)} %get-tuple-element.31.refs_0_, f32[8,1,128]{2,1,0:T(1,128)S(1)} %get-tuple-element.32.refs_1_, bf16[2048,512]{1,0:T(8,128)(2,1)S(1)} %get-tuple-element.23.refs_3_.refs_2_, bf16[512,2048]{1,0:T(8,128)(2,1)S(1)} %get-tuple-element.24.refs_4_.refs_3_, ...), custom_call_target="tpu_custom_call" | custom-call | tf_op jit(solution)/shard_map/chip_terms/pallas_call | solution.py:250
  26.7 11.4 %all_to_all.5.rows_ref = f32[8,1,128]{2,1,0:T(1,128)} all-to-all(f32[8,1,128]{2,1,0:T(1,128)S(1)} %chip_terms.3), channel_id=1, replica_groups={{0,2,4,6,8,10,12,14},{1,3,5,7,9,11,13,15},{16,18,20,22,24,26,28,30},{17..., dimensions={0} | all-to-all | bytes 8192 | tf_op jit(solution)/shard_map/all_to_all | solution.py:341
  38.1 1.4 %finish.1 = (f32[1,512]{1,0:T(1,128)}, f32[1,1]{1,0:T(1,128)}) custom-call(f32[8,1,128]{2,1,0:T(1,128)} %all_to_all.5.rows_ref), custom_call_target="tpu_custom_call" | custom-call | tf_op jit(solution)/shard_map/finish/pallas_call | solution.py:300
  (1 shorter events, 0.0 us)
Async XLA Ops:
  0.6 18.1 %collective-permute-start = (bf16[1,4,32,64,128]{4,3,2,1,0:T(8,128)(2,1)}, bf16[1,4,32,64,128]{4,3,2,1,0:T(8,128)(2,1)S(1)}, u32[]{:S(2)}, u32[]{:S(2)}) collective-permute-start(bf16[1,4,32,64,128]{4,3,2,1,0:T(8,128)(2,1)} %chol_ref.1), channel_id=1, source_target_pairs={{0,1},{1,0},{2,3},{3,2},{4,5},{5,4},{6,7},{7,6},{8,9},{9,8},{10,11... | collective-permute-start | bytes 6291464 | tf_op jit(solution)/shard_map/ppermute | solution.py:325
  1.1 12.3 %collective-permute-start.4 = (bf16[1,64,1280]{2,1,0:T(8,128)(2,1)}, bf16[1,64,1280]{2,1,0:T(8,128)(2,1)S(1)}, u32[]{:S(2)}, u32[]{:S(2)}) collective-permute-start(bf16[1,64,1280]{2,1,0:T(8,128)(2,1)} %refs_7_.1), channel_id=1, source_target_pairs={{0,8},{1,9},{2,10},{3,11},{4,12},{5,13},{6,14},{7,15},{8,0},{9,1},... | collective-permute-start | bytes 491528 | tf_op jit(solution)/shard_map/ppermute | solution.py:322
  4.8 9.6 %collective-permute-start.3 = (bf16[1,64,1280]{2,1,0:T(8,128)(2,1)}, bf16[1,64,1280]{2,1,0:T(8,128)(2,1)S(1)}, u32[]{:S(2)}, u32[]{:S(2)}) collective-permute-start(bf16[1,64,1280]{2,1,0:T(8,128)(2,1)} %refs_7_.1), channel_id=1, source_target_pairs={{0,4},{1,5},{2,6},{3,7},{4,0},{5,1},{6,2},{7,3},{8,12},{9,13},{10,... | collective-permute-start | bytes 491528 | tf_op jit(solution)/shard_map/ppermute | solution.py:322
  6.4 8.0 %collective-permute-start.5 = (bf16[1,64,1280]{2,1,0:T(8,128)(2,1)}, bf16[1,64,1280]{2,1,0:T(8,128)(2,1)S(1)}, u32[]{:S(2)}, u32[]{:S(2)}) collective-permute-start(bf16[1,64,1280]{2,1,0:T(8,128)(2,1)} %refs_7_.1), channel_id=1, source_target_pairs={{0,2},{1,3},{2,0},{3,1},{4,6},{5,7},{6,4},{7,5},{8,10},{9,11},{10,... | collective-permute-start | bytes 491528 | tf_op jit(solution)/shard_map/ppermute | solution.py:322
  7.9 10.8 %collective-permute-start.1 = (bf16[1,64,1280]{2,1,0:T(8,128)(2,1)}, bf16[1,64,1280]{2,1,0:T(8,128)(2,1)S(1)}, u32[]{:S(2)}, u32[]{:S(2)}) collective-permute-start(bf16[1,64,1280]{2,1,0:T(8,128)(2,1)} %refs_7_.1), channel_id=1, source_target_pairs={{0,6},{1,7},{2,4},{3,5},{4,2},{5,3},{6,0},{7,1},{8,14},{9,15},{10,... | collective-permute-start | bytes 491528 | tf_op jit(solution)/shard_map/ppermute | solution.py:322
  8.3 1.6 %copy-start = (bf16[1,4,32,64,128]{4,3,2,1,0:T(8,128)(2,1)S(1)}, bf16[1,4,32,64,128]{4,3,2,1,0:T(8,128)(2,1)}, u32[]{:S(2)}) copy-start(bf16[1,4,32,64,128]{4,3,2,1,0:T(8,128)(2,1)} %chol_ref.1) | copy-start | bytes 6291460
  9.9 4.5 %copy-start.2 = (s32[16,4]{0,1:T(4,128)S(1)}, s32[16,4]{0,1:T(4,128)}, u32[]{:S(2)}) copy-start(s32[16,4]{0,1:T(4,128)} %param.7) | copy-start | bytes 772
  9.9 8.8 %copy-start.3 = (s32[1,4]{1,0:T(1,128)S(1)}, s32[1,4]{1,0:T(1,128)}, u32[]{:S(2)}) copy-start(s32[1,4]{1,0:T(1,128)} %refs_1_.1) | copy-start | bytes 52
  9.9 10.0 %copy-start.1 = (bf16[1,64,1280]{2,1,0:T(8,128)(2,1)S(1)}, bf16[1,64,1280]{2,1,0:T(8,128)(2,1)}, u32[]{:S(2)}) copy-start(bf16[1,64,1280]{2,1,0:T(8,128)(2,1)} %refs_7_.1) | copy-start | bytes 491524
  15.1 7.7 %collective-permute-start.6 = (bf16[2,64,512]{2,1,0:T(8,128)(2,1)S(1)}, bf16[2,64,512]{2,1,0:T(8,128)(2,1)S(1)}, u32[]{:S(2)}, u32[]{:S(2)}) collective-permute-start(bf16[2,64,512]{2,1,0:T(8,128)(2,1)S(1)} %get-tuple-element.35), channel_id=1, source_target_pairs={{0,2},{1,3},{2,0},{3,1},{4,6},{5,7},{6,4},{7,5},{8,10},{9,11},{10,... | collective-permute-start | bytes 393224 | tf_op jit(solution)/shard_map/ppermute | solution.py:322
  16.8 6.0 %collective-permute-start.7 = (bf16[2,64,512]{2,1,0:T(8,128)(2,1)S(1)}, bf16[2,64,512]{2,1,0:T(8,128)(2,1)S(1)}, u32[]{:S(2)}, u32[]{:S(2)}) collective-permute-start(bf16[2,64,512]{2,1,0:T(8,128)(2,1)S(1)} %get-tuple-element.36), channel_id=1, source_target_pairs={{0,4},{1,5},{2,6},{3,7},{4,0},{5,1},{6,2},{7,3},{8,12},{9,13},{10,... | collective-permute-start | bytes 393224 | tf_op jit(solution)/shard_map/ppermute | solution.py:322
  17.9 6.4 %collective-permute-start.8 = (bf16[2,64,512]{2,1,0:T(8,128)(2,1)S(1)}, bf16[2,64,512]{2,1,0:T(8,128)(2,1)S(1)}, u32[]{:S(2)}, u32[]{:S(2)}) collective-permute-start(bf16[2,64,512]{2,1,0:T(8,128)(2,1)S(1)} %get-tuple-element.37), channel_id=1, source_target_pairs={{0,6},{1,7},{2,4},{3,5},{4,2},{5,3},{6,0},{7,1},{8,14},{9,15},{10,... | collective-permute-start | bytes 393224 | tf_op jit(solution)/shard_map/ppermute | solution.py:322
  18.7 1.2 %collective-permute-start.2 = (s32[1,4]{1,0:T(1,128)S(1)}, s32[1,4]{1,0:T(1,128)S(1)}, u32[]{:S(2)}, u32[]{:S(2)}) collective-permute-start(s32[1,4]{1,0:T(1,128)S(1)} %copy-done.3), channel_id=1, source_target_pairs={{0,1},{1,0},{2,3},{3,2},{4,5},{5,4},{6,7},{7,6},{8,9},{9,8},{10,11... | collective-permute-start | bytes 56 | tf_op jit(solution)/shard_map/ppermute | solution.py:325

commit v14 on v13

--- a/solution.py
+++ b/solution.py
@@ -11,7 +11,7 @@
 CORES = 2
 VMEM_LIMIT = 32 * 1024 * 1024
 NEAR = ((8, 4),)
-BEYOND = ((8, 8), (8, 0))
+BEYOND = ((8, 0),)
 BATCH = 4
 VMEM = pl.BlockSpec(memory_space=pltpu.VMEM)
 SMEM = pl.BlockSpec(memory_space=pltpu.SMEM)
@@ -135,6 +135,10 @@
                 diagonals.append(diagonal(top))
                 diagonals.append(diagonal(bottom))
             store_rows(k0 + k8, t, fold_rows(diagonals, sub8))
+
+
+def spread(place, count):
+    return jnp.where(place == 1, 1, jnp.where(place == 2, count - 1, place - 1))
 
 
 def mask_kernel_rows(screen_refs, listed, width):
@@ -227,7 +231,10 @@
             lax.dot_general(segment, part, NT, preferred_element_type=jnp.float32) for part in parts
         )
         for i in range(batch):
-            owner = chip ^ (first + index + i)
+            place = jnp.int32(index + i)
+            if picked:
+                place = jnp.where(place == 0, 0, spread(place, count))
+            owner = chip ^ (first + place)
             out_ref[pl.ds(owner, 1), 0, :used + 8] = sums[i:i + 1]
 
     if count == batch:
@@ -336,6 +343,7 @@
 
     scalars = [listing, screen, to_core(late_screen)]
     rows, masks = chip_terms(scalars, [], blocks, near, 0, NEAR, vectors, chips, out_width)
+    beyond = beyond[:2] + beyond[:1:-1][:1] + beyond[2:-1]
     rows, = chip_terms([], [masks, rows], blocks, beyond, half, BEYOND, vectors, chips, out_width)
     same_core = [list(range(core, groups, CORES)) for core in range(CORES)]
     back = lax.all_to_all(rows, "chol", split_axis=0, concat_axis=0, tiled=True, axis_index_groups=same_core)

time: 39.7 us -> 39.7 us (level)
  blocking collectives: 11.4 us -> 11.9 us
  waiting for transfers between devices: 5.63 us -> 5.17 us
    all_to_all x1, blocking collectives: 11.4 us -> 11.9 us  [body(): lax.all_to_all(rows, 'chol', split_axis=0, concat_axis=0, tiled=True, axi...]
    ppermute x7, waiting for transfers between devices: 5.23 us -> 4.78 us  [to_chip(): lax.ppermute(x, 'chol', [(i, i ^ offset * CORES) for i in range(groups)])]
where the time goes in v14:
time: 39.7 us; the launch traced here: 39.5 us
  blocking collectives  11.9 us (30%)
  starting transfers between devices  11.3 us (28%)
  Pallas kernels  8.84 us (22%)
  waiting for transfers between devices  5.17 us (13%)
  local copies, waits for them, and re-layouts  1.6 us (4%)
  between operations  0.67 us (2%)
    all_to_all x1, blocking collectives, body(): lax.all_to_all(rows, 'chol', split_axis=0, concat_axis=0, tiled=True, axi...  11.9 us
    ppermute x7, starting transfers between devices, to_chip(): lax.ppermute(x, 'chol', [(i, i ^ offset * CORES) for i in range(groups)])  10.7 us
    pallas_call x2, Pallas kernels, chip_terms(): pl.pallas_call(functools.partial(terms_kernel, first=first, count=count,...  5.32 us
    ppermute x7, waiting for transfers between devices, to_chip(): lax.ppermute(x, 'chol', [(i, i ^ offset * CORES) for i in range(groups)])  4.78 us
    unnamed x8, local copies, waits for them, and re-layouts  1.6 us
    pallas_call x2, Pallas kernels, prepare_block(): pl.pallas_call(prepare_kernel, in_specs=[VMEM], out_specs=[VMEM, VMEM], o...  1.43 us
    pallas_call x1, Pallas kernels, finish(): pl.pallas_call(functools.partial(finish_kernel, used=used, scale=scale),...  1.37 us
  transfers between devices with their start and end apart: 9, of which 4 were waited for; matrix products, arithmetic and copies ran while one was open for 0% of the time, Pallas kernels for 13%

profile of v14, /device:TPU:0, one launch (start us, length us, event | category | flops | bytes accessed | tf_op | source)
XLA Modules:
  0.0 39.5 jit_solution(9715417059975199416)
XLA Ops:
  0.6 0.5 %collective-permute-start = (bf16[1,4,32,64,128]{4,3,2,1,0:T(8,128)(2,1)}, bf16[1,4,32,64,128]{4,3,2,1,0:T(8,128)(2,1)S(1)}, u32[]{:S(2)}, u32[]{:S(2)}) collective-permute-start(bf16[1,4,32,64,128]{4,3,2,1,0:T(8,128)(2,1)} %chol_ref.1), channel_id=1, source_target_pairs={{0,1},{1,0},{2,3},{3,2},{4,5},{5,4},{6,7},{7,6},{8,9},{9,8},{10,11... | collective-permute-start | bytes 6291464 | tf_op jit(solution)/shard_map/ppermute | solution.py:332
  1.1 3.7 %collective-permute-start.4 = (bf16[1,64,1280]{2,1,0:T(8,128)(2,1)}, bf16[1,64,1280]{2,1,0:T(8,128)(2,1)S(1)}, u32[]{:S(2)}, u32[]{:S(2)}) collective-permute-start(bf16[1,64,1280]{2,1,0:T(8,128)(2,1)} %refs_7_.1), channel_id=1, source_target_pairs={{0,8},{1,9},{2,10},{3,11},{4,12},{5,13},{6,14},{7,15},{8,0},{9,1},... | collective-permute-start | bytes 491528 | tf_op jit(solution)/shard_map/ppermute | solution.py:329
  4.8 1.6 %collective-permute-start.3 = (bf16[1,64,1280]{2,1,0:T(8,128)(2,1)}, bf16[1,64,1280]{2,1,0:T(8,128)(2,1)S(1)}, u32[]{:S(2)}, u32[]{:S(2)}) collective-permute-start(bf16[1,64,1280]{2,1,0:T(8,128)(2,1)} %refs_7_.1), channel_id=1, source_target_pairs={{0,4},{1,5},{2,6},{3,7},{4,0},{5,1},{6,2},{7,3},{8,12},{9,13},{10,... | collective-permute-start | bytes 491528 | tf_op jit(solution)/shard_map/ppermute | solution.py:329
  6.4 1.5 %collective-permute-start.5 = (bf16[1,64,1280]{2,1,0:T(8,128)(2,1)}, bf16[1,64,1280]{2,1,0:T(8,128)(2,1)S(1)}, u32[]{:S(2)}, u32[]{:S(2)}) collective-permute-start(bf16[1,64,1280]{2,1,0:T(8,128)(2,1)} %refs_7_.1), channel_id=1, source_target_pairs={{0,2},{1,3},{2,0},{3,1},{4,6},{5,7},{6,4},{7,5},{8,10},{9,11},{10,... | collective-permute-start | bytes 491528 | tf_op jit(solution)/shard_map/ppermute | solution.py:329
  7.9 0.4 collective-permute-start.1
  8.3 0.0 copy-start
  8.3 1.6 %copy-done = bf16[1,4,32,64,128]{4,3,2,1,0:T(8,128)(2,1)S(1)} copy-done((bf16[1,4,32,64,128]{4,3,2,1,0:T(8,128)(2,1)S(1)}, bf16[1,4,32,64,128]{4,3,2,1,0:T(8,128)(2,1)}, u32[]{:S(2)}) %copy-start) | copy-done | bytes 2097176
  9.9 0.0 copy-start.2
  9.9 0.0 copy-start.3
  9.9 0.7 %prepare_block.2 = (bf16[2048,512]{1,0:T(8,128)(2,1)S(1)}, bf16[512,2048]{1,0:T(8,128)(2,1)S(1)}) custom-call(bf16[1,4,32,64,128]{4,3,2,1,0:T(8,128)(2,1)S(1)} %copy-done), custom_call_target="tpu_custom_call" | custom-call | tf_op jit(solution)/shard_map/prepare_block/pallas_call | solution.py:35
  10.6 2.8 %collective-permute-done.4.theta_ref = bf16[1,64,1280]{2,1,0:T(8,128)(2,1)S(1)} collective-permute-done((bf16[1,64,1280]{2,1,0:T(8,128)(2,1)}, bf16[1,64,1280]{2,1,0:T(8,128)(2,1)S(1)}, u32[]{:S(2)}, u32[]{:S(2)}) %collective-permute-start.4) | collective-permute-done | bytes 163872 | tf_op jit(solution)/shard_map/ppermute | solution.py:329
  13.4 1.0 %collective-permute-done.3.refs_9_ = bf16[1,64,1280]{2,1,0:T(8,128)(2,1)S(1)} collective-permute-done((bf16[1,64,1280]{2,1,0:T(8,128)(2,1)}, bf16[1,64,1280]{2,1,0:T(8,128)(2,1)S(1)}, u32[]{:S(2)}, u32[]{:S(2)}) %collective-permute-start.3) | collective-permute-done | bytes 163872 | tf_op jit(solution)/shard_map/ppermute | solution.py:329
  14.4 0.0 collective-permute-done.5.refs_8_
  14.4 0.0 copy-done.2
  14.4 0.7 %pick_tiles.1 = (bf16[2,64,512]{2,1,0:T(8,128)(2,1)S(1)}, bf16[2,64,512]{2,1,0:T(8,128)(2,1)S(1)}, bf16[2,64,512]{2,1,0:T(8,128)(2,1)S(1)}, bf16[2,64,512]{2,1,0:T(8,128)(2,1)S(1)}) custom-call(s32[4,16]{1,0:T(4,128)S(1)} %bitcast.2, bf16[1,64,1280]{2,1,0:T(8,128)(2,1)S(1)} %collective-permute-done.4.theta_ref), custom_call_target="tpu_custom_call" | custom-call | tf_op jit(solution)/shard_map/pick_tiles/pallas_call | solution.py:63
  15.1 1.7 %collective-permute-start.6 = (bf16[2,64,512]{2,1,0:T(8,128)(2,1)S(1)}, bf16[2,64,512]{2,1,0:T(8,128)(2,1)S(1)}, u32[]{:S(2)}, u32[]{:S(2)}) collective-permute-start(bf16[2,64,512]{2,1,0:T(8,128)(2,1)S(1)} %get-tuple-element.35), channel_id=1, source_target_pairs={{0,2},{1,3},{2,0},{3,1},{4,6},{5,7},{6,4},{7,5},{8,10},{9,11},{10,... | collective-permute-start | bytes 393224 | tf_op jit(solution)/shard_map/ppermute | solution.py:329
  16.8 1.1 %collective-permute-start.7 = (bf16[2,64,512]{2,1,0:T(8,128)(2,1)S(1)}, bf16[2,64,512]{2,1,0:T(8,128)(2,1)S(1)}, u32[]{:S(2)}, u32[]{:S(2)}) collective-permute-start(bf16[2,64,512]{2,1,0:T(8,128)(2,1)S(1)} %get-tuple-element.36), channel_id=1, source_target_pairs={{0,6},{1,7},{2,4},{3,5},{4,2},{5,3},{6,0},{7,1},{8,14},{9,15},{10,... | collective-permute-start | bytes 393224 | tf_op jit(solution)/shard_map/ppermute | solution.py:329
  17.8 0.8 %collective-permute-start.8 = (bf16[2,64,512]{2,1,0:T(8,128)(2,1)S(1)}, bf16[2,64,512]{2,1,0:T(8,128)(2,1)S(1)}, u32[]{:S(2)}, u32[]{:S(2)}) collective-permute-start(bf16[2,64,512]{2,1,0:T(8,128)(2,1)S(1)} %get-tuple-element.37), channel_id=1, source_target_pairs={{0,4},{1,5},{2,6},{3,7},{4,0},{5,1},{6,2},{7,3},{8,12},{9,13},{10,... | collective-permute-start | bytes 393224 | tf_op jit(solution)/shard_map/ppermute | solution.py:329
  18.7 0.0 collective-permute-done.1.refs_10_
  18.7 0.0 collective-permute-done.chol_ref
  18.7 0.0 copy-done.3
  18.7 0.1 collective-permute-start.2
  18.8 0.7 %prepare_block.3 = (bf16[2048,512]{1,0:T(8,128)(2,1)S(1)}, bf16[512,2048]{1,0:T(8,128)(2,1)S(1)}) custom-call(bf16[1,4,32,64,128]{4,3,2,1,0:T(8,128)(2,1)S(1)} %collective-permute-done.chol_ref), custom_call_target="tpu_custom_call" | custom-call | tf_op jit(solution)/shard_map/prepare_block/pallas_call | solution.py:35
  19.5 0.4 collective-permute-done.2.refs_2_
  19.9 0.0 copy-done.1
  19.9 2.9 %chip_terms.2 = (f32[8,1,128]{2,1,0:T(1,128)S(1)}, f32[2,512]{1,0:T(2,128)S(1)}) custom-call(s32[4,16]{1,0:T(4,128)S(1)} %bitcast.3, s32[1,4]{1,0:T(1,128)S(1)} %copy-done.3, s32[1,4]{1,0:T(1,128)S(1)} %collective-permute-done.2.refs_2_, bf16[2048,512]{1,0:T(8,128)(2,1)S(1)} %get-tuple-element.23.refs_3_.refs_2_, ...), custom_call_target="tpu_custom_call" | custom-call | tf_op jit(solution)/shard_map/chip_terms/pallas_call | solution.py:257
  22.8 1.0 %collective-permute-done.6.refs_7_ = bf16[2,64,512]{2,1,0:T(8,128)(2,1)S(1)} collective-permute-done((bf16[2,64,512]{2,1,0:T(8,128)(2,1)S(1)}, bf16[2,64,512]{2,1,0:T(8,128)(2,1)S(1)}, u32[]{:S(2)}, u32[]{:S(2)}) %collective-permute-start.6) | collective-permute-done | bytes 131104 | tf_op jit(solution)/shard_map/ppermute | solution.py:329
  23.8 0.0 collective-permute-done.7.refs_8_
  23.8 0.0 collective-permute-done.8.refs_9_
  23.8 2.4 %chip_terms.3 = f32[8,1,128]{2,1,0:T(1,128)S(1)} custom-call(f32[2,512]{1,0:T(2,128)S(1)} %get-tuple-element.31.refs_0_, f32[8,1,128]{2,1,0:T(1,128)S(1)} %get-tuple-element.32.refs_1_, bf16[2048,512]{1,0:T(8,128)(2,1)S(1)} %get-tuple-element.23.refs_3_.refs_2_, bf16[512,2048]{1,0:T(8,128)(2,1)S(1)} %get-tuple-element.24.refs_4_.refs_3_, ...), custom_call_target="tpu_custom_call" | custom-call | tf_op jit(solution)/shard_map/chip_terms/pallas_call | solution.py:257
  26.2 11.9 %all_to_all.5.rows_ref = f32[8,1,128]{2,1,0:T(1,128)} all-to-all(f32[8,1,128]{2,1,0:T(1,128)S(1)} %chip_terms.3), channel_id=1, replica_groups={{0,2,4,6,8,10,12,14},{1,3,5,7,9,11,13,15},{16,18,20,22,24,26,28,30},{17..., dimensions={0} | all-to-all | bytes 8192 | tf_op jit(solution)/shard_map/all_to_all | solution.py:349
  38.1 1.4 %finish.1 = (f32[1,512]{1,0:T(1,128)}, f32[1,1]{1,0:T(1,128)}) custom-call(f32[8,1,128]{2,1,0:T(1,128)} %all_to_all.5.rows_ref), custom_call_target="tpu_custom_call" | custom-call | tf_op jit(solution)/shard_map/finish/pallas_call | solution.py:307
  (1 shorter events, 0.0 us)
Async XLA Ops:
  0.6 18.1 %collective-permute-start = (bf16[1,4,32,64,128]{4,3,2,1,0:T(8,128)(2,1)}, bf16[1,4,32,64,128]{4,3,2,1,0:T(8,128)(2,1)S(1)}, u32[]{:S(2)}, u32[]{:S(2)}) collective-permute-start(bf16[1,4,32,64,128]{4,3,2,1,0:T(8,128)(2,1)} %chol_ref.1), channel_id=1, source_target_pairs={{0,1},{1,0},{2,3},{3,2},{4,5},{5,4},{6,7},{7,6},{8,9},{9,8},{10,11... | collective-permute-start | bytes 6291464 | tf_op jit(solution)/shard_map/ppermute | solution.py:332
  1.1 12.3 %collective-permute-start.4 = (bf16[1,64,1280]{2,1,0:T(8,128)(2,1)}, bf16[1,64,1280]{2,1,0:T(8,128)(2,1)S(1)}, u32[]{:S(2)}, u32[]{:S(2)}) collective-permute-start(bf16[1,64,1280]{2,1,0:T(8,128)(2,1)} %refs_7_.1), channel_id=1, source_target_pairs={{0,8},{1,9},{2,10},{3,11},{4,12},{5,13},{6,14},{7,15},{8,0},{9,1},... | collective-permute-start | bytes 491528 | tf_op jit(solution)/shard_map/ppermute | solution.py:329
  4.8 9.6 %collective-permute-start.3 = (bf16[1,64,1280]{2,1,0:T(8,128)(2,1)}, bf16[1,64,1280]{2,1,0:T(8,128)(2,1)S(1)}, u32[]{:S(2)}, u32[]{:S(2)}) collective-permute-start(bf16[1,64,1280]{2,1,0:T(8,128)(2,1)} %refs_7_.1), channel_id=1, source_target_pairs={{0,4},{1,5},{2,6},{3,7},{4,0},{5,1},{6,2},{7,3},{8,12},{9,13},{10,... | collective-permute-start | bytes 491528 | tf_op jit(solution)/shard_map/ppermute | solution.py:329
  6.4 8.0 %collective-permute-start.5 = (bf16[1,64,1280]{2,1,0:T(8,128)(2,1)}, bf16[1,64,1280]{2,1,0:T(8,128)(2,1)S(1)}, u32[]{:S(2)}, u32[]{:S(2)}) collective-permute-start(bf16[1,64,1280]{2,1,0:T(8,128)(2,1)} %refs_7_.1), channel_id=1, source_target_pairs={{0,2},{1,3},{2,0},{3,1},{4,6},{5,7},{6,4},{7,5},{8,10},{9,11},{10,... | collective-permute-start | bytes 491528 | tf_op jit(solution)/shard_map/ppermute | solution.py:329
  7.9 10.8 %collective-permute-start.1 = (bf16[1,64,1280]{2,1,0:T(8,128)(2,1)}, bf16[1,64,1280]{2,1,0:T(8,128)(2,1)S(1)}, u32[]{:S(2)}, u32[]{:S(2)}) collective-permute-start(bf16[1,64,1280]{2,1,0:T(8,128)(2,1)} %refs_7_.1), channel_id=1, source_target_pairs={{0,6},{1,7},{2,4},{3,5},{4,2},{5,3},{6,0},{7,1},{8,14},{9,15},{10,... | collective-permute-start | bytes 491528 | tf_op jit(solution)/shard_map/ppermute | solution.py:329
  8.3 1.6 %copy-start = (bf16[1,4,32,64,128]{4,3,2,1,0:T(8,128)(2,1)S(1)}, bf16[1,4,32,64,128]{4,3,2,1,0:T(8,128)(2,1)}, u32[]{:S(2)}) copy-start(bf16[1,4,32,64,128]{4,3,2,1,0:T(8,128)(2,1)} %chol_ref.1) | copy-start | bytes 6291460
  9.9 4.5 %copy-start.2 = (s32[16,4]{0,1:T(4,128)S(1)}, s32[16,4]{0,1:T(4,128)}, u32[]{:S(2)}) copy-start(s32[16,4]{0,1:T(4,128)} %param.7) | copy-start | bytes 772
  9.9 8.8 %copy-start.3 = (s32[1,4]{1,0:T(1,128)S(1)}, s32[1,4]{1,0:T(1,128)}, u32[]{:S(2)}) copy-start(s32[1,4]{1,0:T(1,128)} %refs_1_.1) | copy-start | bytes 52
  9.9 10.0 %copy-start.1 = (bf16[1,64,1280]{2,1,0:T(8,128)(2,1)S(1)}, bf16[1,64,1280]{2,1,0:T(8,128)(2,1)}, u32[]{:S(2)}) copy-start(bf16[1,64,1280]{2,1,0:T(8,128)(2,1)} %refs_7_.1) | copy-start | bytes 491524
  15.1 8.6 %collective-permute-start.6 = (bf16[2,64,512]{2,1,0:T(8,128)(2,1)S(1)}, bf16[2,64,512]{2,1,0:T(8,128)(2,1)S(1)}, u32[]{:S(2)}, u32[]{:S(2)}) collective-permute-start(bf16[2,64,512]{2,1,0:T(8,128)(2,1)S(1)} %get-tuple-element.35), channel_id=1, source_target_pairs={{0,2},{1,3},{2,0},{3,1},{4,6},{5,7},{6,4},{7,5},{8,10},{9,11},{10,... | collective-permute-start | bytes 393224 | tf_op jit(solution)/shard_map/ppermute | solution.py:329
  16.8 7.0 %collective-permute-start.7 = (bf16[2,64,512]{2,1,0:T(8,128)(2,1)S(1)}, bf16[2,64,512]{2,1,0:T(8,128)(2,1)S(1)}, u32[]{:S(2)}, u32[]{:S(2)}) collective-permute-start(bf16[2,64,512]{2,1,0:T(8,128)(2,1)S(1)} %get-tuple-element.36), channel_id=1, source_target_pairs={{0,6},{1,7},{2,4},{3,5},{4,2},{5,3},{6,0},{7,1},{8,14},{9,15},{10,... | collective-permute-start | bytes 393224 | tf_op jit(solution)/shard_map/ppermute | solution.py:329
  17.8 5.9 %collective-permute-start.8 = (bf16[2,64,512]{2,1,0:T(8,128)(2,1)S(1)}, bf16[2,64,512]{2,1,0:T(8,128)(2,1)S(1)}, u32[]{:S(2)}, u32[]{:S(2)}) collective-permute-start(bf16[2,64,512]{2,1,0:T(8,128)(2,1)S(1)} %get-tuple-element.37), channel_id=1, source_target_pairs={{0,4},{1,5},{2,6},{3,7},{4,0},{5,1},{6,2},{7,3},{8,12},{9,13},{10,... | collective-permute-start | bytes 393224 | tf_op jit(solution)/shard_map/ppermute | solution.py:329
  18.7 1.2 %collective-permute-start.2 = (s32[1,4]{1,0:T(1,128)S(1)}, s32[1,4]{1,0:T(1,128)S(1)}, u32[]{:S(2)}, u32[]{:S(2)}) collective-permute-start(s32[1,4]{1,0:T(1,128)S(1)} %copy-done.3), channel_id=1, source_target_pairs={{0,1},{1,0},{2,3},{3,2},{4,5},{5,4},{6,7},{7,6},{8,9},{9,8},{10,11... | collective-permute-start | bytes 56 | tf_op jit(solution)/shard_map/ppermute | solution.py:332

commit v15 on v13

--- a/solution.py
+++ b/solution.py
@@ -46,29 +46,32 @@
     )(chol_tiles)
 
 
-def pick_kernel(list_ref, theta_ref, *out_refs):
+def pick_kernel(list_ref, early_ref, late_ref, *out_refs, part):
     listed = list_ref.shape[0]
     width = out_refs[0].shape[2] // listed
     me = lax.axis_index("chol")
+    early = lax.rem(me // (CORES * part), 2) == 1
     for offset, out_ref in enumerate(out_refs):
         device = me ^ (offset * CORES)
         for b, group in enumerate((device, device ^ 1)):
             for m in range(listed):
                 start = pl.multiple_of(list_ref[m, group] * width, width)
-                out_ref[b, :, m * width:(m + 1) * width] = theta_ref[0, :, pl.ds(start, width)]
-
-
-def pick_tiles(listing, theta, depth, count):
-    piece = jax.ShapeDtypeStruct((CORES, theta.shape[1], depth), theta.dtype)
+                out_ref[b, :, m * width:(m + 1) * width] = jnp.where(
+                    early, early_ref[0, :, pl.ds(start, width)], late_ref[0, :, pl.ds(start, width)]
+                )
+
+
+def pick_tiles(listing, early, late, depth, count, part):
+    piece = jax.ShapeDtypeStruct((CORES, early.shape[1], depth), early.dtype)
     return pl.pallas_call(
-        pick_kernel,
-        in_specs=[SMEM, VMEM],
+        functools.partial(pick_kernel, part=part),
+        in_specs=[SMEM, VMEM, VMEM],
         out_specs=[VMEM] * count,
         out_shape=[piece] * count,
         compiler_params=PARAMS,
         cost_estimate=SMALL,
         name="pick_tiles",
-    )(listing, theta)
+    )(listing, early, late)
 
 
 def fold_rows(blocks, sub):
@@ -324,11 +327,19 @@
     def to_core(x):
         return lax.ppermute(x, "chol", [(i, i ^ 1) for i in range(groups)])
 
-    far = to_chip(theta, half)
-    near = [theta] + [to_chip(theta, offset) for offset in range(1, half)]
+    part = half // 2
+
+    def across(x, early):
+        pairs = [(i, i ^ (half * CORES)) for i in range(groups) if bool((i // CORES) & part) == early]
+        return lax.ppermute(x, "chol", pairs)
+
+    first, second = across(theta, True), across(theta, False)
+    near = [theta] + [to_chip(theta, offset) for offset in range(1, half - 1)]
     own, own_turned = prepare_block(chol_tiles)
-    near[2], far, near[1], own = lax.optimization_barrier((near[2], far, near[1], own))
-    pieces = pick_tiles(listing, far, own.shape[1], half)
+    near[2], own, late_theta = lax.optimization_barrier((near[2], own, theta))
+    near.append(to_chip(late_theta, half - 1))
+    first, near[1], second = lax.optimization_barrier((first, near[1], second))
+    pieces = pick_tiles(listing, first, second, own.shape[1], half, part)
     beyond = [pieces[0]] + [to_chip(pieces[offset], offset) for offset in range(1, half)]
     other_chol, late_screen, near[-1] = lax.optimization_barrier((to_core(chol_tiles), screen, near[-1]))
     other, other_turned = prepare_block(other_chol)

time: 39.7 us -> 41.9 us (1.055)
  starting transfers between devices: 11.3 us -> 13.9 us
  blocking collectives: 11.4 us -> 9.54 us
  waiting for transfers between devices: 5.63 us -> 6.83 us
    ppermute x0 -> x2, starting transfers between devices: none -> 5.14 us  [across(): return lax.ppermute(x, 'chol', pairs)]
    ppermute x0 -> x2, waiting for transfers between devices: none -> 4.68 us  [across(): return lax.ppermute(x, 'chol', pairs)]
    ppermute x7 -> x6, waiting for transfers between devices: 5.23 us -> 1.04 us  [to_chip(): lax.ppermute(x, 'chol', [(i, i ^ offset * CORES) for i in range(groups)])]
    ppermute x7 -> x6, starting transfers between devices: 10.7 us -> 8.18 us  [to_chip(): lax.ppermute(x, 'chol', [(i, i ^ offset * CORES) for i in range(groups)])]
    all_to_all x1, blocking collectives: 11.4 us -> 9.54 us  [body(): lax.all_to_all(rows, 'chol', split_axis=0, concat_axis=0, tiled=True, axi...]
    ppermute x2, waiting for transfers between devices: 0.39 us -> 1.11 us  [to_core(): return lax.ppermute(x, 'chol', [(i, i ^ 1) for i in range(groups)])]
  transfers between devices with their start and end apart: 9 -> 10, of which waited for: 4 -> 3; matrix products, arithmetic and copies ran while one was open for 0% -> 0% of each run, Pallas kernels for 13% -> 12%
where the time goes in v15:
time: 41.9 us; the launch traced here: 41.7 us
  starting transfers between devices  13.9 us (33%)
  blocking collectives  9.54 us (23%)
  Pallas kernels  8.88 us (21%)
  waiting for transfers between devices  6.83 us (16%)
  local copies, waits for them, and re-layouts  1.77 us (4%)
  between operations  0.72 us (2%)
    all_to_all x1, blocking collectives, body(): lax.all_to_all(rows, 'chol', split_axis=0, concat_axis=0, tiled=True, axi...  9.54 us
    ppermute x6, starting transfers between devices, to_chip(): lax.ppermute(x, 'chol', [(i, i ^ offset * CORES) for i in range(groups)])  8.18 us
    pallas_call x2, Pallas kernels, chip_terms(): pl.pallas_call(functools.partial(terms_kernel, first=first, count=count,...  5.33 us
    ppermute x2, starting transfers between devices, across(): return lax.ppermute(x, 'chol', pairs)  5.14 us
    ppermute x2, waiting for transfers between devices, across(): return lax.ppermute(x, 'chol', pairs)  4.68 us
    unnamed x8, local copies, waits for them, and re-layouts  1.77 us
    pallas_call x2, Pallas kernels, prepare_block(): pl.pallas_call(prepare_kernel, in_specs=[VMEM], out_specs=[VMEM, VMEM], o...  1.43 us
    pallas_call x1, Pallas kernels, finish(): pl.pallas_call(functools.partial(finish_kernel, used=used, scale=scale),...  1.37 us
  transfers between devices with their start and end apart: 10, of which 3 were waited for; matrix products, arithmetic and copies ran while one was open for 0% of the time, Pallas kernels for 12%

profile of v15, /device:TPU:0, one launch (start us, length us, event | category | flops | bytes accessed | tf_op | source)
XLA Modules:
  0.0 41.7 jit_solution(3644801014530184134)
XLA Ops:
  0.6 0.5 %collective-permute-start = (bf16[1,4,32,64,128]{4,3,2,1,0:T(8,128)(2,1)}, bf16[1,4,32,64,128]{4,3,2,1,0:T(8,128)(2,1)S(1)}, u32[]{:S(2)}, u32[]{:S(2)}) collective-permute-start(bf16[1,4,32,64,128]{4,3,2,1,0:T(8,128)(2,1)} %chol_ref.1), channel_id=1, source_target_pairs={{0,1},{1,0},{2,3},{3,2},{4,5},{5,4},{6,7},{7,6},{8,9},{9,8},{10,11... | collective-permute-start | bytes 6291464 | tf_op jit(solution)/shard_map/ppermute | solution.py:328
  1.1 2.6 %collective-permute-start.1 = (bf16[1,64,1280]{2,1,0:T(8,128)(2,1)}, bf16[1,64,1280]{2,1,0:T(8,128)(2,1)S(1)}, u32[]{:S(2)}, u32[]{:S(2)}) collective-permute-start(bf16[1,64,1280]{2,1,0:T(8,128)(2,1)} %refs_7_.1), channel_id=1, source_target_pairs={{0,4},{1,5},{2,6},{3,7},{4,0},{5,1},{6,2},{7,3},{8,12},{9,13},{10,... | collective-permute-start | bytes 491528 | tf_op jit(solution)/shard_map/ppermute | solution.py:325
  3.8 0.7 %collective-permute-start.4 = (bf16[1,64,1280]{2,1,0:T(8,128)(2,1)}, bf16[1,64,1280]{2,1,0:T(8,128)(2,1)S(1)}, u32[]{:S(2)}, u32[]{:S(2)}) collective-permute-start(bf16[1,64,1280]{2,1,0:T(8,128)(2,1)} %refs_7_.1), channel_id=1, source_target_pairs={{4,12},{5,13},{6,14},{7,15},{12,4},{13,5},{14,6},{15,7},{20,28},{2... | collective-permute-start | bytes 491528 | tf_op jit(solution)/shard_map/ppermute | solution.py:334
  4.5 1.6 %collective-permute-start.5 = (bf16[1,64,1280]{2,1,0:T(8,128)(2,1)}, bf16[1,64,1280]{2,1,0:T(8,128)(2,1)S(1)}, u32[]{:S(2)}, u32[]{:S(2)}) collective-permute-start(bf16[1,64,1280]{2,1,0:T(8,128)(2,1)} %refs_7_.1), channel_id=1, source_target_pairs={{0,2},{1,3},{2,0},{3,1},{4,6},{5,7},{6,4},{7,5},{8,10},{9,11},{10,... | collective-permute-start | bytes 491528 | tf_op jit(solution)/shard_map/ppermute | solution.py:325
  6.0 4.5 %collective-permute-start.6 = (bf16[1,64,1280]{2,1,0:T(8,128)(2,1)}, bf16[1,64,1280]{2,1,0:T(8,128)(2,1)S(1)}, u32[]{:S(2)}, u32[]{:S(2)}) collective-permute-start(bf16[1,64,1280]{2,1,0:T(8,128)(2,1)} %refs_7_.1), channel_id=1, source_target_pairs={{0,8},{1,9},{2,10},{3,11},{8,0},{9,1},{10,2},{11,3},{16,24},{17,25... | collective-permute-start | bytes 491528 | tf_op jit(solution)/shard_map/ppermute | solution.py:334
  10.5 0.0 copy-start
  10.6 1.6 %copy-done = bf16[1,4,32,64,128]{4,3,2,1,0:T(8,128)(2,1)S(1)} copy-done((bf16[1,4,32,64,128]{4,3,2,1,0:T(8,128)(2,1)S(1)}, bf16[1,4,32,64,128]{4,3,2,1,0:T(8,128)(2,1)}, u32[]{:S(2)}) %copy-start) | copy-done | bytes 2097176
  12.1 0.7 %prepare_block.2 = (bf16[2048,512]{1,0:T(8,128)(2,1)S(1)}, bf16[512,2048]{1,0:T(8,128)(2,1)S(1)}) custom-call(bf16[1,4,32,64,128]{4,3,2,1,0:T(8,128)(2,1)S(1)} %copy-done), custom_call_target="tpu_custom_call" | custom-call | tf_op jit(solution)/shard_map/prepare_block/pallas_call | solution.py:35
  12.9 0.0 collective-permute-done.1.refs_9_
  12.9 0.2 copy-done.1
  13.1 0.4 collective-permute-start.2
  13.4 0.0 collective-permute-done.4.early_ref
  13.4 0.0 collective-permute-done.5.refs_8_
  13.5 4.7 %collective-permute-done.6.late_ref = bf16[1,64,1280]{2,1,0:T(8,128)(2,1)S(1)} collective-permute-done((bf16[1,64,1280]{2,1,0:T(8,128)(2,1)}, bf16[1,64,1280]{2,1,0:T(8,128)(2,1)S(1)}, u32[]{:S(2)}, u32[]{:S(2)}) %collective-permute-start.6) | collective-permute-done | bytes 163872 | tf_op jit(solution)/shard_map/ppermute | solution.py:334
  18.1 0.0 copy-done.2
  18.1 0.8 %pick_tiles.1 = (bf16[2,64,512]{2,1,0:T(8,128)(2,1)S(1)}, bf16[2,64,512]{2,1,0:T(8,128)(2,1)S(1)}, bf16[2,64,512]{2,1,0:T(8,128)(2,1)S(1)}, bf16[2,64,512]{2,1,0:T(8,128)(2,1)S(1)}) custom-call(s32[4,16]{1,0:T(4,128)S(1)} %bitcast.2, bf16[1,64,1280]{2,1,0:T(8,128)(2,1)S(1)} %collective-permute-done.4.early_ref, ...), custom_call_target="tpu_custom_call" | custom-call | tf_op jit(solution)/shard_map/pick_tiles/pallas_call | solution.py:66
  18.9 1.1 %collective-permute-start.7 = (bf16[2,64,512]{2,1,0:T(8,128)(2,1)S(1)}, bf16[2,64,512]{2,1,0:T(8,128)(2,1)S(1)}, u32[]{:S(2)}, u32[]{:S(2)}) collective-permute-start(bf16[2,64,512]{2,1,0:T(8,128)(2,1)S(1)} %get-tuple-element.39), channel_id=1, source_target_pairs={{0,2},{1,3},{2,0},{3,1},{4,6},{5,7},{6,4},{7,5},{8,10},{9,11},{10,... | collective-permute-start | bytes 393224 | tf_op jit(solution)/shard_map/ppermute | solution.py:325
  20.0 0.0 collective-permute-start.8
  20.0 2.5 %collective-permute-start.9 = (bf16[2,64,512]{2,1,0:T(8,128)(2,1)S(1)}, bf16[2,64,512]{2,1,0:T(8,128)(2,1)S(1)}, u32[]{:S(2)}, u32[]{:S(2)}) collective-permute-start(bf16[2,64,512]{2,1,0:T(8,128)(2,1)S(1)} %get-tuple-element.41), channel_id=1, source_target_pairs={{0,6},{1,7},{2,4},{3,5},{4,2},{5,3},{6,0},{7,1},{8,14},{9,15},{10,... | collective-permute-start | bytes 393224 | tf_op jit(solution)/shard_map/ppermute | solution.py:325
  22.5 0.0 collective-permute-done.2.refs_10_
  22.5 0.0 collective-permute-done.chol_ref
  22.5 0.7 %prepare_block.3 = (bf16[2048,512]{1,0:T(8,128)(2,1)S(1)}, bf16[512,2048]{1,0:T(8,128)(2,1)S(1)}) custom-call(bf16[1,4,32,64,128]{4,3,2,1,0:T(8,128)(2,1)S(1)} %collective-permute-done.chol_ref), custom_call_target="tpu_custom_call" | custom-call | tf_op jit(solution)/shard_map/prepare_block/pallas_call | solution.py:35
  23.2 0.0 copy-done.3
  23.2 0.1 collective-permute-start.3
  23.3 1.1 %collective-permute-done.3.refs_2_ = s32[1,4]{1,0:T(1,128)S(1)} collective-permute-done((s32[1,4]{1,0:T(1,128)S(1)}, s32[1,4]{1,0:T(1,128)S(1)}, u32[]{:S(2)}, u32[]{:S(2)}) %collective-permute-start.3) | collective-permute-done | bytes 48 | tf_op jit(solution)/shard_map/ppermute | solution.py:328
  24.4 2.9 %chip_terms.2 = (f32[8,1,128]{2,1,0:T(1,128)S(1)}, f32[2,512]{1,0:T(2,128)S(1)}) custom-call(s32[4,16]{1,0:T(4,128)S(1)} %bitcast.3, s32[1,4]{1,0:T(1,128)S(1)} %copy-done.3, s32[1,4]{1,0:T(1,128)S(1)} %collective-permute-done.3.refs_2_, bf16[2048,512]{1,0:T(8,128)(2,1)S(1)} %get-tuple-element.26.refs_3_.refs_2_, ...), custom_call_target="tpu_custom_call" | custom-call | tf_op jit(solution)/shard_map/chip_terms/pallas_call | solution.py:253
  27.3 0.0 collective-permute-done.7.refs_7_
  27.3 0.0 collective-permute-done.8.refs_8_
  27.3 1.0 %collective-permute-done.9.refs_9_ = bf16[2,64,512]{2,1,0:T(8,128)(2,1)S(1)} collective-permute-done((bf16[2,64,512]{2,1,0:T(8,128)(2,1)S(1)}, bf16[2,64,512]{2,1,0:T(8,128)(2,1)S(1)}, u32[]{:S(2)}, u32[]{:S(2)}) %collective-permute-start.9) | collective-permute-done | bytes 131104 | tf_op jit(solution)/shard_map/ppermute | solution.py:325
  28.3 2.4 %chip_terms.3 = f32[8,1,128]{2,1,0:T(1,128)S(1)} custom-call(f32[2,512]{1,0:T(2,128)S(1)} %get-tuple-element.34.refs_0_, f32[8,1,128]{2,1,0:T(1,128)S(1)} %get-tuple-element.35.refs_1_, bf16[2048,512]{1,0:T(8,128)(2,1)S(1)} %get-tuple-element.26.refs_3_.refs_2_, bf16[512,2048]{1,0:T(8,128)(2,1)S(1)} %get-tuple-element.27.refs_4_.refs_3_, ...), custom_call_target="tpu_custom_call" | custom-call | tf_op jit(solution)/shard_map/chip_terms/pallas_call | solution.py:253
  30.8 9.5 %all_to_all.5.rows_ref = f32[8,1,128]{2,1,0:T(1,128)} all-to-all(f32[8,1,128]{2,1,0:T(1,128)S(1)} %chip_terms.3), channel_id=1, replica_groups={{0,2,4,6,8,10,12,14},{1,3,5,7,9,11,13,15},{16,18,20,22,24,26,28,30},{17..., dimensions={0} | all-to-all | bytes 8192 | tf_op jit(solution)/shard_map/all_to_all | solution.py:352
  40.3 1.4 %finish.1 = (f32[1,512]{1,0:T(1,128)}, f32[1,1]{1,0:T(1,128)}) custom-call(f32[8,1,128]{2,1,0:T(1,128)} %all_to_all.5.rows_ref), custom_call_target="tpu_custom_call" | custom-call | tf_op jit(solution)/shard_map/finish/pallas_call | solution.py:303
  (3 shorter events, 0.0 us)
Async XLA Ops:
  0.6 21.8 %collective-permute-start = (bf16[1,4,32,64,128]{4,3,2,1,0:T(8,128)(2,1)}, bf16[1,4,32,64,128]{4,3,2,1,0:T(8,128)(2,1)S(1)}, u32[]{:S(2)}, u32[]{:S(2)}) collective-permute-start(bf16[1,4,32,64,128]{4,3,2,1,0:T(8,128)(2,1)} %chol_ref.1), channel_id=1, source_target_pairs={{0,1},{1,0},{2,3},{3,2},{4,5},{5,4},{6,7},{7,6},{8,9},{9,8},{10,11... | collective-permute-start | bytes 6291464 | tf_op jit(solution)/shard_map/ppermute | solution.py:328
  1.1 11.7 %collective-permute-start.1 = (bf16[1,64,1280]{2,1,0:T(8,128)(2,1)}, bf16[1,64,1280]{2,1,0:T(8,128)(2,1)S(1)}, u32[]{:S(2)}, u32[]{:S(2)}) collective-permute-start(bf16[1,64,1280]{2,1,0:T(8,128)(2,1)} %refs_7_.1), channel_id=1, source_target_pairs={{0,4},{1,5},{2,6},{3,7},{4,0},{5,1},{6,2},{7,3},{8,12},{9,13},{10,... | collective-permute-start | bytes 491528 | tf_op jit(solution)/shard_map/ppermute | solution.py:325
  3.8 9.6 %collective-permute-start.4 = (bf16[1,64,1280]{2,1,0:T(8,128)(2,1)}, bf16[1,64,1280]{2,1,0:T(8,128)(2,1)S(1)}, u32[]{:S(2)}, u32[]{:S(2)}) collective-permute-start(bf16[1,64,1280]{2,1,0:T(8,128)(2,1)} %refs_7_.1), channel_id=1, source_target_pairs={{4,12},{5,13},{6,14},{7,15},{12,4},{13,5},{14,6},{15,7},{20,28},{2... | collective-permute-start | bytes 491528 | tf_op jit(solution)/shard_map/ppermute | solution.py:334
  4.5 9.0 %collective-permute-start.5 = (bf16[1,64,1280]{2,1,0:T(8,128)(2,1)}, bf16[1,64,1280]{2,1,0:T(8,128)(2,1)S(1)}, u32[]{:S(2)}, u32[]{:S(2)}) collective-permute-start(bf16[1,64,1280]{2,1,0:T(8,128)(2,1)} %refs_7_.1), channel_id=1, source_target_pairs={{0,2},{1,3},{2,0},{3,1},{4,6},{5,7},{6,4},{7,5},{8,10},{9,11},{10,... | collective-permute-start | bytes 491528 | tf_op jit(solution)/shard_map/ppermute | solution.py:325
  6.0 12.1 %collective-permute-start.6 = (bf16[1,64,1280]{2,1,0:T(8,128)(2,1)}, bf16[1,64,1280]{2,1,0:T(8,128)(2,1)S(1)}, u32[]{:S(2)}, u32[]{:S(2)}) collective-permute-start(bf16[1,64,1280]{2,1,0:T(8,128)(2,1)} %refs_7_.1), channel_id=1, source_target_pairs={{0,8},{1,9},{2,10},{3,11},{8,0},{9,1},{10,2},{11,3},{16,24},{17,25... | collective-permute-start | bytes 491528 | tf_op jit(solution)/shard_map/ppermute | solution.py:334
  10.5 1.6 %copy-start = (bf16[1,4,32,64,128]{4,3,2,1,0:T(8,128)(2,1)S(1)}, bf16[1,4,32,64,128]{4,3,2,1,0:T(8,128)(2,1)}, u32[]{:S(2)}) copy-start(bf16[1,4,32,64,128]{4,3,2,1,0:T(8,128)(2,1)} %chol_ref.1) | copy-start | bytes 6291460
  12.1 0.9 %copy-start.1 = (bf16[1,64,1280]{2,1,0:T(8,128)(2,1)S(1)}, bf16[1,64,1280]{2,1,0:T(8,128)(2,1)}, u32[]{:S(2)}) copy-start(bf16[1,64,1280]{2,1,0:T(8,128)(2,1)} %refs_7_.1) | copy-start | bytes 491524
  12.1 6.0 %copy-start.2 = (s32[16,4]{0,1:T(4,128)S(1)}, s32[16,4]{0,1:T(4,128)}, u32[]{:S(2)}) copy-start(s32[16,4]{0,1:T(4,128)} %param.7) | copy-start | bytes 772
  12.1 11.0 %copy-start.3 = (s32[1,4]{1,0:T(1,128)S(1)}, s32[1,4]{1,0:T(1,128)}, u32[]{:S(2)}) copy-start(s32[1,4]{1,0:T(1,128)} %refs_1_.1) | copy-start | bytes 52
  13.1 9.4 %collective-permute-start.2 = (bf16[1,64,1280]{2,1,0:T(8,128)(2,1)S(1)}, bf16[1,64,1280]{2,1,0:T(8,128)(2,1)S(1)}, u32[]{:S(2)}, u32[]{:S(2)}) collective-permute-start(bf16[1,64,1280]{2,1,0:T(8,128)(2,1)S(1)} %copy-done.1), channel_id=1, source_target_pairs={{0,6},{1,7},{2,4},{3,5},{4,2},{5,3},{6,0},{7,1},{8,14},{9,15},{10,... | collective-permute-start | bytes 491528 | tf_op jit(solution)/shard_map/ppermute | solution.py:325
  18.9 8.4 %collective-permute-start.7 = (bf16[2,64,512]{2,1,0:T(8,128)(2,1)S(1)}, bf16[2,64,512]{2,1,0:T(8,128)(2,1)S(1)}, u32[]{:S(2)}, u32[]{:S(2)}) collective-permute-start(bf16[2,64,512]{2,1,0:T(8,128)(2,1)S(1)} %get-tuple-element.39), channel_id=1, source_target_pairs={{0,2},{1,3},{2,0},{3,1},{4,6},{5,7},{6,4},{7,5},{8,10},{9,11},{10,... | collective-permute-start | bytes 393224 | tf_op jit(solution)/shard_map/ppermute | solution.py:325
  20.0 7.3 %collective-permute-start.8 = (bf16[2,64,512]{2,1,0:T(8,128)(2,1)S(1)}, bf16[2,64,512]{2,1,0:T(8,128)(2,1)S(1)}, u32[]{:S(2)}, u32[]{:S(2)}) collective-permute-start(bf16[2,64,512]{2,1,0:T(8,128)(2,1)S(1)} %get-tuple-element.40), channel_id=1, source_target_pairs={{0,4},{1,5},{2,6},{3,7},{4,0},{5,1},{6,2},{7,3},{8,12},{9,13},{10,... | collective-permute-start | bytes 393224 | tf_op jit(solution)/shard_map/ppermute | solution.py:325
  20.0 8.3 %collective-permute-start.9 = (bf16[2,64,512]{2,1,0:T(8,128)(2,1)S(1)}, bf16[2,64,512]{2,1,0:T(8,128)(2,1)S(1)}, u32[]{:S(2)}, u32[]{:S(2)}) collective-permute-start(bf16[2,64,512]{2,1,0:T(8,128)(2,1)S(1)} %get-tuple-element.41), channel_id=1, source_target_pairs={{0,6},{1,7},{2,4},{3,5},{4,2},{5,3},{6,0},{7,1},{8,14},{9,15},{10,... | collective-permute-start | bytes 393224 | tf_op jit(solution)/shard_map/ppermute | solution.py:325
  23.2 1.2 %collective-permute-start.3 = (s32[1,4]{1,0:T(1,128)S(1)}, s32[1,4]{1,0:T(1,128)S(1)}, u32[]{:S(2)}, u32[]{:S(2)}) collective-permute-start(s32[1,4]{1,0:T(1,128)S(1)} %copy-done.3), channel_id=1, source_target_pairs={{0,1},{1,0},{2,3},{3,2},{4,5},{5,4},{6,7},{7,6},{8,9},{9,8},{10,11... | collective-permute-start | bytes 56 | tf_op jit(solution)/shard_map/ppermute | solution.py:328

commit v16 on v13

--- a/solution.py
+++ b/solution.py
@@ -146,11 +146,11 @@
     ]
 
 
-def terms_kernel(*refs, first, count, picked, chunks, vectors, batch):
-    if picked:
+def terms_kernel(*refs, first, count, screened, chunks, vectors, batch):
+    if screened:
+        screen_refs, refs = refs[:2], refs[2:]
+    else:
         mask_ref, carried_ref, refs = refs[0], refs[1], refs[2:]
-    else:
-        list_ref, screen_refs, refs = refs[0], refs[1:3], refs[3:]
     block_refs, theta_refs, rest = refs[:4], refs[4:4 + count], refs[4 + count:]
     out_ref, picked_ref, rows_ref = rest[0], rest[-2], rest[-1]
     occupied = block_refs[0].shape[0] // vectors
@@ -162,30 +162,20 @@
     core = lax.rem(me, CORES)
     chip = me // CORES
 
-    if picked:
-        masks = [mask_ref[b:b + 1, :] for b in range(CORES)]
-        out_ref[...] = carried_ref[...]
-    else:
-        listed = list_ref.shape[0]
-        width = depth // listed
-        masks = mask_kernel_rows(screen_refs, listed, width)
+    if screened:
+        listed = screen_refs[0].shape[1]
+        masks = mask_kernel_rows(screen_refs, listed, depth // listed)
         mask_ref = rest[1]
         for b in range(CORES):
             mask_ref[b:b + 1, :] = masks[b]
         out_ref[...] = jnp.zeros(out_ref.shape, out_ref.dtype)
-    for b, group in enumerate((me, me ^ 1)):
+    else:
+        masks = [mask_ref[b:b + 1, :] for b in range(CORES)]
+        out_ref[...] = carried_ref[...]
+    for b in range(CORES):
         mask = masks[b].astype(picked_ref.dtype)
-        if picked:
-            for i, ref in enumerate(theta_refs):
-                picked_ref[b, i * occupied:(i + 1) * occupied, :] = ref[b] * mask
-        else:
-            for m in range(listed):
-                start = pl.multiple_of(list_ref[m, group] * width, width)
-                tile_mask = mask[:, m * width:(m + 1) * width]
-                for i, ref in enumerate(theta_refs):
-                    picked_ref[b, i * occupied:(i + 1) * occupied, m * width:(m + 1) * width] = (
-                        ref[0, :, pl.ds(start, width)] * tile_mask
-                    )
+        for i, ref in enumerate(theta_refs):
+            picked_ref[b, i * occupied:(i + 1) * occupied, :] = ref[b] * mask
 
     def one_batch(index):
         start = index * occupied
@@ -238,20 +228,20 @@
             one_batch(step * batch)
 
 
-def chip_terms(scalars, so_far, blocks, thetas, first, chunks, vectors, chips, out_width):
+def chip_terms(screens, so_far, blocks, thetas, first, chunks, vectors, chips, out_width):
     count = len(thetas)
     batch = min(count, BATCH)
     rows, depth = blocks[0].shape
     occupied = rows // vectors
     vector_operands = [*so_far, *blocks, *thetas]
     out_shape = [jax.ShapeDtypeStruct((chips, 1, out_width), jnp.float32)]
-    if scalars:
+    if screens:
         out_shape.append(jax.ShapeDtypeStruct((CORES, depth), jnp.float32))
     return pl.pallas_call(
         functools.partial(
-            terms_kernel, first=first, count=count, picked=not scalars, chunks=chunks, vectors=vectors, batch=batch
+            terms_kernel, first=first, count=count, screened=bool(screens), chunks=chunks, vectors=vectors, batch=batch
         ),
-        in_specs=[SMEM] * len(scalars) + [VMEM] * len(vector_operands),
+        in_specs=[SMEM] * len(screens) + [VMEM] * len(vector_operands),
         out_specs=[VMEM] * len(out_shape),
         out_shape=out_shape,
         scratch_shapes=[
@@ -261,7 +251,7 @@
         compiler_params=PARAMS,
         cost_estimate=SMALL,
         name="chip_terms",
-    )(*scalars, *vector_operands)
+    )(*screens, *vector_operands)
 
 
 def energy_terms(rows, used):
@@ -316,6 +306,7 @@
     vectors = chol_tiles.shape[2]
     used = CORES * vectors
     out_width = LANES * ((used + 8 + LANES - 1) // LANES)
+    depth = chol_tiles.shape[1] * chol_tiles.shape[4]
     listing = tile_list.T
 
     def to_chip(x, offset):
@@ -325,17 +316,21 @@
         return lax.ppermute(x, "chol", [(i, i ^ 1) for i in range(groups)])
 
     far = to_chip(theta, half)
-    near = [theta] + [to_chip(theta, offset) for offset in range(1, half)]
+
+    def spread(walker):
+        pieces = pick_tiles(listing, walker, depth, half)
+        return [pieces[0]] + [to_chip(pieces[offset], offset) for offset in range(1, half)]
+
+    near = spread(theta)
     own, own_turned = prepare_block(chol_tiles)
-    near[2], far, near[1], own = lax.optimization_barrier((near[2], far, near[1], own))
-    pieces = pick_tiles(listing, far, own.shape[1], half)
-    beyond = [pieces[0]] + [to_chip(pieces[offset], offset) for offset in range(1, half)]
+    far, near[1], near[2], own = lax.optimization_barrier((far, near[1], near[2], own))
+    beyond = spread(far)
     other_chol, late_screen, near[-1] = lax.optimization_barrier((to_core(chol_tiles), screen, near[-1]))
     other, other_turned = prepare_block(other_chol)
     blocks = [own, own_turned, other, other_turned]
 
-    scalars = [listing, screen, to_core(late_screen)]
-    rows, masks = chip_terms(scalars, [], blocks, near, 0, NEAR, vectors, chips, out_width)
+    screens = [screen, to_core(late_screen)]
+    rows, masks = chip_terms(screens, [], blocks, near, 0, NEAR, vectors, chips, out_width)
     rows, = chip_terms([], [masks, rows], blocks, beyond, half, BEYOND, vectors, chips, out_width)
     same_core = [list(range(core, groups, CORES)) for core in range(CORES)]
     back = lax.all_to_all(rows, "chol", split_axis=0, concat_axis=0, tiled=True, axis_index_groups=same_core)

time: 39.7 us -> 40 us (level)
  blocking collectives: 11.4 us -> 9.66 us
  local copies, waits for them, and re-layouts: 1.6 us -> 3.23 us
  Pallas kernels: 8.84 us -> 9.34 us
    all_to_all x1, blocking collectives: 11.4 us -> 9.66 us  [body(): lax.all_to_all(rows, 'chol', split_axis=0, concat_axis=0, tiled=True, axi...]
    unnamed x8 -> x10, local copies, waits for them, and re-layouts: 1.6 us -> 3.23 us
    pallas_call x1 -> x2, Pallas kernels: 0.72 us -> 1.43 us  [pick_tiles(): pl.pallas_call(pick_kernel, in_specs=[SMEM, VMEM], out_specs=[VMEM] * cou...]
  transfers between devices with their start and end apart: 9 -> 9, of which waited for: 4 -> 3; matrix products, arithmetic and copies ran while one was open for 0% -> 0% of each run, Pallas kernels for 13% -> 14%
where the time goes in v16:
time: 40 us; the launch traced here: 39.7 us
  starting transfers between devices  11.4 us (28%)
  blocking collectives  9.66 us (24%)
  Pallas kernels  9.34 us (23%)
  waiting for transfers between devices  5.43 us (14%)
  local copies, waits for them, and re-layouts  3.23 us (8%)
  between operations  0.71 us (2%)
    ppermute x7, starting transfers between devices, to_chip(): lax.ppermute(x, 'chol', [(i, i ^ offset * CORES) for i in range(groups)])  10.8 us
    all_to_all x1, blocking collectives, body(): lax.all_to_all(rows, 'chol', split_axis=0, concat_axis=0, tiled=True, axi...  9.66 us
    pallas_call x2, Pallas kernels, chip_terms(): pl.pallas_call(functools.partial(terms_kernel, first=first, count=count,...  5.11 us
    ppermute x7, waiting for transfers between devices, to_chip(): lax.ppermute(x, 'chol', [(i, i ^ offset * CORES) for i in range(groups)])  5.04 us
    unnamed x10, local copies, waits for them, and re-layouts  3.23 us
    pallas_call x2, Pallas kernels, pick_tiles(): pl.pallas_call(pick_kernel, in_specs=[SMEM, VMEM], out_specs=[VMEM] * cou...  1.43 us
    pallas_call x2, Pallas kernels, prepare_block(): pl.pallas_call(prepare_kernel, in_specs=[VMEM], out_specs=[VMEM, VMEM], o...  1.43 us
    pallas_call x1, Pallas kernels, finish(): pl.pallas_call(functools.partial(finish_kernel, used=used, scale=scale),...  1.37 us
  transfers between devices with their start and end apart: 9, of which 3 were waited for; matrix products, arithmetic and copies ran while one was open for 0% of the time, Pallas kernels for 14%

profile of v16, /device:TPU:0, one launch (start us, length us, event | category | flops | bytes accessed | tf_op | source)
XLA Modules:
  0.0 39.7 jit_solution(10451575238561276463)
XLA Ops:
  0.6 0.0 copy-start.4
  0.6 0.5 %collective-permute-start = (bf16[1,4,32,64,128]{4,3,2,1,0:T(8,128)(2,1)}, bf16[1,4,32,64,128]{4,3,2,1,0:T(8,128)(2,1)S(1)}, u32[]{:S(2)}, u32[]{:S(2)}) collective-permute-start(bf16[1,4,32,64,128]{4,3,2,1,0:T(8,128)(2,1)} %chol_ref.1), channel_id=1, source_target_pairs={{0,1},{1,0},{2,3},{3,2},{4,5},{5,4},{6,7},{7,6},{8,9},{9,8},{10,11... | collective-permute-start | bytes 6291464 | tf_op jit(solution)/shard_map/ppermute | solution.py:316
  1.2 3.7 %collective-permute-start.3 = (bf16[1,64,1280]{2,1,0:T(8,128)(2,1)}, bf16[1,64,1280]{2,1,0:T(8,128)(2,1)S(1)}, u32[]{:S(2)}, u32[]{:S(2)}) collective-permute-start(bf16[1,64,1280]{2,1,0:T(8,128)(2,1)} %theta_ref.1), channel_id=1, source_target_pairs={{0,8},{1,9},{2,10},{3,11},{4,12},{5,13},{6,14},{7,15},{8,0},{9,1},... | collective-permute-start | bytes 491528 | tf_op jit(solution)/shard_map/ppermute | solution.py:313
  4.8 0.9 %copy-done.1 = bf16[1,64,1280]{2,1,0:T(8,128)(2,1)S(1)} copy-done((bf16[1,64,1280]{2,1,0:T(8,128)(2,1)S(1)}, bf16[1,64,1280]{2,1,0:T(8,128)(2,1)}, u32[]{:S(2)}) %copy-start.1) | copy-done | bytes 163864
  5.8 0.7 %copy-done.2 = s32[16,4]{0,1:T(4,128)S(1)} copy-done((s32[16,4]{0,1:T(4,128)S(1)}, s32[16,4]{0,1:T(4,128)}, u32[]{:S(2)}) %copy-start.2) | copy-done | bytes 280
  6.5 0.7 %pick_tiles.2 = (bf16[2,64,512]{2,1,0:T(8,128)(2,1)S(1)}, bf16[2,64,512]{2,1,0:T(8,128)(2,1)S(1)}, bf16[2,64,512]{2,1,0:T(8,128)(2,1)S(1)}, bf16[2,64,512]{2,1,0:T(8,128)(2,1)S(1)}) custom-call(s32[4,16]{1,0:T(4,128)S(1)} %bitcast.2, bf16[1,64,1280]{2,1,0:T(8,128)(2,1)S(1)} %copy-done.1), custom_call_target="tpu_custom_call" | custom-call | tf_op jit(solution)/shard_map/pick_tiles/pallas_call | solution.py:63
  7.2 1.6 %collective-permute-start.4 = (bf16[2,64,512]{2,1,0:T(8,128)(2,1)S(1)}, bf16[2,64,512]{2,1,0:T(8,128)(2,1)S(1)}, u32[]{:S(2)}, u32[]{:S(2)}) collective-permute-start(bf16[2,64,512]{2,1,0:T(8,128)(2,1)S(1)} %get-tuple-element.27), channel_id=1, source_target_pairs={{0,2},{1,3},{2,0},{3,1},{4,6},{5,7},{6,4},{7,5},{8,10},{9,11},{10,... | collective-permute-start | bytes 393224 | tf_op jit(solution)/shard_map/ppermute | solution.py:313
  8.8 1.6 %collective-permute-start.5 = (bf16[2,64,512]{2,1,0:T(8,128)(2,1)S(1)}, bf16[2,64,512]{2,1,0:T(8,128)(2,1)S(1)}, u32[]{:S(2)}, u32[]{:S(2)}) collective-permute-start(bf16[2,64,512]{2,1,0:T(8,128)(2,1)S(1)} %get-tuple-element.28), channel_id=1, source_target_pairs={{0,4},{1,5},{2,6},{3,7},{4,0},{5,1},{6,2},{7,3},{8,12},{9,13},{10,... | collective-permute-start | bytes 393224 | tf_op jit(solution)/shard_map/ppermute | solution.py:313
  10.3 0.4 collective-permute-start.1
  10.7 1.6 %copy-done = bf16[1,4,32,64,128]{4,3,2,1,0:T(8,128)(2,1)S(1)} copy-done((bf16[1,4,32,64,128]{4,3,2,1,0:T(8,128)(2,1)S(1)}, bf16[1,4,32,64,128]{4,3,2,1,0:T(8,128)(2,1)}, u32[]{:S(2)}) %copy-start) | copy-done | bytes 2097176
  12.3 0.7 %prepare_block.2 = (bf16[2048,512]{1,0:T(8,128)(2,1)S(1)}, bf16[512,2048]{1,0:T(8,128)(2,1)S(1)}) custom-call(bf16[1,4,32,64,128]{4,3,2,1,0:T(8,128)(2,1)S(1)} %copy-done), custom_call_target="tpu_custom_call" | custom-call | tf_op jit(solution)/shard_map/prepare_block/pallas_call | solution.py:35
  13.0 0.0 collective-permute-done.4.refs_7_
  13.1 3.2 %collective-permute-done.5.refs_8_ = bf16[2,64,512]{2,1,0:T(8,128)(2,1)S(1)} collective-permute-done((bf16[2,64,512]{2,1,0:T(8,128)(2,1)S(1)}, bf16[2,64,512]{2,1,0:T(8,128)(2,1)S(1)}, u32[]{:S(2)}, u32[]{:S(2)}) %collective-permute-start.5) | collective-permute-done | bytes 131104 | tf_op jit(solution)/shard_map/ppermute | solution.py:313
  16.2 0.0 collective-permute-done.3.theta_ref
  16.2 0.0 copy-done.3
  16.2 0.7 %pick_tiles.3 = (bf16[2,64,512]{2,1,0:T(8,128)(2,1)S(1)}, bf16[2,64,512]{2,1,0:T(8,128)(2,1)S(1)}, bf16[2,64,512]{2,1,0:T(8,128)(2,1)S(1)}, bf16[2,64,512]{2,1,0:T(8,128)(2,1)S(1)}) custom-call(s32[4,16]{1,0:T(4,128)S(1)} %bitcast.3, bf16[1,64,1280]{2,1,0:T(8,128)(2,1)S(1)} %collective-permute-done.3.theta_ref), custom_call_target="tpu_custom_call" | custom-call | tf_op jit(solution)/shard_map/pick_tiles/pallas_call | solution.py:63
  17.0 1.5 %collective-permute-start.6 = (bf16[2,64,512]{2,1,0:T(8,128)(2,1)S(1)}, bf16[2,64,512]{2,1,0:T(8,128)(2,1)S(1)}, u32[]{:S(2)}, u32[]{:S(2)}) collective-permute-start(bf16[2,64,512]{2,1,0:T(8,128)(2,1)S(1)} %get-tuple-element.43), channel_id=1, source_target_pairs={{0,2},{1,3},{2,0},{3,1},{4,6},{5,7},{6,4},{7,5},{8,10},{9,11},{10,... | collective-permute-start | bytes 393224 | tf_op jit(solution)/shard_map/ppermute | solution.py:313
  18.5 0.0 collective-permute-start.7
  18.5 2.0 %collective-permute-start.8 = (bf16[2,64,512]{2,1,0:T(8,128)(2,1)S(1)}, bf16[2,64,512]{2,1,0:T(8,128)(2,1)S(1)}, u32[]{:S(2)}, u32[]{:S(2)}) collective-permute-start(bf16[2,64,512]{2,1,0:T(8,128)(2,1)S(1)} %get-tuple-element.45), channel_id=1, source_target_pairs={{0,6},{1,7},{2,4},{3,5},{4,2},{5,3},{6,0},{7,1},{8,14},{9,15},{10,... | collective-permute-start | bytes 393224 | tf_op jit(solution)/shard_map/ppermute | solution.py:313
  20.5 0.0 collective-permute-done.1.refs_9_
  20.5 0.0 collective-permute-done.chol_ref
  20.5 0.0 copy-done.4
  20.5 0.1 collective-permute-start.2
  20.6 0.7 %prepare_block.3 = (bf16[2048,512]{1,0:T(8,128)(2,1)S(1)}, bf16[512,2048]{1,0:T(8,128)(2,1)S(1)}) custom-call(bf16[1,4,32,64,128]{4,3,2,1,0:T(8,128)(2,1)S(1)} %collective-permute-done.chol_ref), custom_call_target="tpu_custom_call" | custom-call | tf_op jit(solution)/shard_map/prepare_block/pallas_call | solution.py:35
  21.3 0.4 collective-permute-done.2.refs_1_
  21.7 2.8 %chip_terms.2 = (f32[8,1,128]{2,1,0:T(1,128)S(1)}, f32[2,512]{1,0:T(2,128)S(1)}) custom-call(s32[1,4]{1,0:T(1,128)S(1)} %copy-done.4, s32[1,4]{1,0:T(1,128)S(1)} %collective-permute-done.2.refs_1_, bf16[2048,512]{1,0:T(8,128)(2,1)S(1)} %get-tuple-element.30.refs_2_, bf16[512,2048]{1,0:T(8,128)(2,1)S(1)} %get-tuple-element.31.refs_3_, ...), custom_call_target="tpu_custom_call" | custom-call | tf_op jit(solution)/shard_map/chip_terms/pallas_call | solution.py:240
  24.5 0.0 collective-permute-done.6.refs_7_
  24.5 0.0 collective-permute-done.7.refs_8_
  24.5 1.8 %collective-permute-done.8.refs_9_ = bf16[2,64,512]{2,1,0:T(8,128)(2,1)S(1)} collective-permute-done((bf16[2,64,512]{2,1,0:T(8,128)(2,1)S(1)}, bf16[2,64,512]{2,1,0:T(8,128)(2,1)S(1)}, u32[]{:S(2)}, u32[]{:S(2)}) %collective-permute-start.8) | collective-permute-done | bytes 131104 | tf_op jit(solution)/shard_map/ppermute | solution.py:313
  26.4 2.4 %chip_terms.3 = f32[8,1,128]{2,1,0:T(1,128)S(1)} custom-call(f32[2,512]{1,0:T(2,128)S(1)} %get-tuple-element.39.refs_0_, f32[8,1,128]{2,1,0:T(1,128)S(1)} %get-tuple-element.40.refs_1_, bf16[2048,512]{1,0:T(8,128)(2,1)S(1)} %get-tuple-element.30.refs_2_, bf16[512,2048]{1,0:T(8,128)(2,1)S(1)} %get-tuple-element.31.refs_3_, ...), custom_call_target="tpu_custom_call" | custom-call | tf_op jit(solution)/shard_map/chip_terms/pallas_call | solution.py:240
  28.7 9.7 %all_to_all.5.rows_ref = f32[8,1,128]{2,1,0:T(1,128)} all-to-all(f32[8,1,128]{2,1,0:T(1,128)S(1)} %chip_terms.3), channel_id=1, replica_groups={{0,2,4,6,8,10,12,14},{1,3,5,7,9,11,13,15},{16,18,20,22,24,26,28,30},{17..., dimensions={0} | all-to-all | bytes 8192 | tf_op jit(solution)/shard_map/all_to_all | solution.py:336
  38.4 1.4 %finish.1 = (f32[1,512]{1,0:T(1,128)}, f32[1,1]{1,0:T(1,128)}) custom-call(f32[8,1,128]{2,1,0:T(1,128)} %all_to_all.5.rows_ref), custom_call_target="tpu_custom_call" | custom-call | tf_op jit(solution)/shard_map/finish/pallas_call | solution.py:290
  (4 shorter events, 0.0 us)
Async XLA Ops:
  0.6 19.9 %copy-start.4 = (s32[1,4]{1,0:T(1,128)S(1)}, s32[1,4]{1,0:T(1,128)}, u32[]{:S(2)}) copy-start(s32[1,4]{1,0:T(1,128)} %refs_0_.1) | copy-start | bytes 52
  0.6 19.9 %collective-permute-start = (bf16[1,4,32,64,128]{4,3,2,1,0:T(8,128)(2,1)}, bf16[1,4,32,64,128]{4,3,2,1,0:T(8,128)(2,1)S(1)}, u32[]{:S(2)}, u32[]{:S(2)}) collective-permute-start(bf16[1,4,32,64,128]{4,3,2,1,0:T(8,128)(2,1)} %chol_ref.1), channel_id=1, source_target_pairs={{0,1},{1,0},{2,3},{3,2},{4,5},{5,4},{6,7},{7,6},{8,9},{9,8},{10,11... | collective-permute-start | bytes 6291464 | tf_op jit(solution)/shard_map/ppermute | solution.py:316
  1.2 15.1 %collective-permute-start.3 = (bf16[1,64,1280]{2,1,0:T(8,128)(2,1)}, bf16[1,64,1280]{2,1,0:T(8,128)(2,1)S(1)}, u32[]{:S(2)}, u32[]{:S(2)}) collective-permute-start(bf16[1,64,1280]{2,1,0:T(8,128)(2,1)} %theta_ref.1), channel_id=1, source_target_pairs={{0,8},{1,9},{2,10},{3,11},{4,12},{5,13},{6,14},{7,15},{8,0},{9,1},... | collective-permute-start | bytes 491528 | tf_op jit(solution)/shard_map/ppermute | solution.py:313
  4.8 0.9 %copy-start.1 = (bf16[1,64,1280]{2,1,0:T(8,128)(2,1)S(1)}, bf16[1,64,1280]{2,1,0:T(8,128)(2,1)}, u32[]{:S(2)}) copy-start(bf16[1,64,1280]{2,1,0:T(8,128)(2,1)} %theta_ref.1) | copy-start | bytes 491524
  5.8 0.7 %copy-start.2 = (s32[16,4]{0,1:T(4,128)S(1)}, s32[16,4]{0,1:T(4,128)}, u32[]{:S(2)}) copy-start(s32[16,4]{0,1:T(4,128)} %param.7) | copy-start | bytes 772
  6.5 9.8 %copy-start.3 = (s32[16,4]{0,1:T(4,128)S(1)}, s32[16,4]{0,1:T(4,128)}, u32[]{:S(2)}) copy-start(s32[16,4]{0,1:T(4,128)} %param.7) | copy-start | bytes 772
  7.2 5.9 %collective-permute-start.4 = (bf16[2,64,512]{2,1,0:T(8,128)(2,1)S(1)}, bf16[2,64,512]{2,1,0:T(8,128)(2,1)S(1)}, u32[]{:S(2)}, u32[]{:S(2)}) collective-permute-start(bf16[2,64,512]{2,1,0:T(8,128)(2,1)S(1)} %get-tuple-element.27), channel_id=1, source_target_pairs={{0,2},{1,3},{2,0},{3,1},{4,6},{5,7},{6,4},{7,5},{8,10},{9,11},{10,... | collective-permute-start | bytes 393224 | tf_op jit(solution)/shard_map/ppermute | solution.py:313
  8.8 7.5 %collective-permute-start.5 = (bf16[2,64,512]{2,1,0:T(8,128)(2,1)S(1)}, bf16[2,64,512]{2,1,0:T(8,128)(2,1)S(1)}, u32[]{:S(2)}, u32[]{:S(2)}) collective-permute-start(bf16[2,64,512]{2,1,0:T(8,128)(2,1)S(1)} %get-tuple-element.28), channel_id=1, source_target_pairs={{0,4},{1,5},{2,6},{3,7},{4,0},{5,1},{6,2},{7,3},{8,12},{9,13},{10,... | collective-permute-start | bytes 393224 | tf_op jit(solution)/shard_map/ppermute | solution.py:313
  10.3 10.2 %collective-permute-start.1 = (bf16[2,64,512]{2,1,0:T(8,128)(2,1)S(1)}, bf16[2,64,512]{2,1,0:T(8,128)(2,1)S(1)}, u32[]{:S(2)}, u32[]{:S(2)}) collective-permute-start(bf16[2,64,512]{2,1,0:T(8,128)(2,1)S(1)} %get-tuple-element.25), channel_id=1, source_target_pairs={{0,6},{1,7},{2,4},{3,5},{4,2},{5,3},{6,0},{7,1},{8,14},{9,15},{10,... | collective-permute-start | bytes 393224 | tf_op jit(solution)/shard_map/ppermute | solution.py:313
  10.7 1.6 %copy-start = (bf16[1,4,32,64,128]{4,3,2,1,0:T(8,128)(2,1)S(1)}, bf16[1,4,32,64,128]{4,3,2,1,0:T(8,128)(2,1)}, u32[]{:S(2)}) copy-start(bf16[1,4,32,64,128]{4,3,2,1,0:T(8,128)(2,1)} %chol_ref.1) | copy-start | bytes 6291460
  17.0 7.5 %collective-permute-start.6 = (bf16[2,64,512]{2,1,0:T(8,128)(2,1)S(1)}, bf16[2,64,512]{2,1,0:T(8,128)(2,1)S(1)}, u32[]{:S(2)}, u32[]{:S(2)}) collective-permute-start(bf16[2,64,512]{2,1,0:T(8,128)(2,1)S(1)} %get-tuple-element.43), channel_id=1, source_target_pairs={{0,2},{1,3},{2,0},{3,1},{4,6},{5,7},{6,4},{7,5},{8,10},{9,11},{10,... | collective-permute-start | bytes 393224 | tf_op jit(solution)/shard_map/ppermute | solution.py:313
  18.5 6.0 %collective-permute-start.7 = (bf16[2,64,512]{2,1,0:T(8,128)(2,1)S(1)}, bf16[2,64,512]{2,1,0:T(8,128)(2,1)S(1)}, u32[]{:S(2)}, u32[]{:S(2)}) collective-permute-start(bf16[2,64,512]{2,1,0:T(8,128)(2,1)S(1)} %get-tuple-element.44), channel_id=1, source_target_pairs={{0,4},{1,5},{2,6},{3,7},{4,0},{5,1},{6,2},{7,3},{8,12},{9,13},{10,... | collective-permute-start | bytes 393224 | tf_op jit(solution)/shard_map/ppermute | solution.py:313
  18.5 7.9 %collective-permute-start.8 = (bf16[2,64,512]{2,1,0:T(8,128)(2,1)S(1)}, bf16[2,64,512]{2,1,0:T(8,128)(2,1)S(1)}, u32[]{:S(2)}, u32[]{:S(2)}) collective-permute-start(bf16[2,64,512]{2,1,0:T(8,128)(2,1)S(1)} %get-tuple-element.45), channel_id=1, source_target_pairs={{0,6},{1,7},{2,4},{3,5},{4,2},{5,3},{6,0},{7,1},{8,14},{9,15},{10,... | collective-permute-start | bytes 393224 | tf_op jit(solution)/shard_map/ppermute | solution.py:313
  20.5 1.2 %collective-permute-start.2 = (s32[1,4]{1,0:T(1,128)S(1)}, s32[1,4]{1,0:T(1,128)S(1)}, u32[]{:S(2)}, u32[]{:S(2)}) collective-permute-start(s32[1,4]{1,0:T(1,128)S(1)} %copy-done.4), channel_id=1, source_target_pairs={{0,1},{1,0},{2,3},{3,2},{4,5},{5,4},{6,7},{7,6},{8,9},{9,8},{10,11... | collective-permute-start | bytes 56 | tf_op jit(solution)/shard_map/ppermute | solution.py:316

commit v17 on v16

--- a/solution.py
+++ b/solution.py
@@ -323,9 +323,10 @@
 
     near = spread(theta)
     own, own_turned = prepare_block(chol_tiles)
-    far, near[1], near[2], own = lax.optimization_barrier((far, near[1], near[2], own))
+    other_chol = to_core(chol_tiles)
+    far, near[1], other_chol, own = lax.optimization_barrier((far, near[1], other_chol, own))
     beyond = spread(far)
-    other_chol, late_screen, near[-1] = lax.optimization_barrier((to_core(chol_tiles), screen, near[-1]))
+    other_chol, late_screen, near[-1] = lax.optimization_barrier((other_chol, screen, near[-1]))
     other, other_turned = prepare_block(other_chol)
     blocks = [own, own_turned, other, other_turned]
 

time: 40 us -> 39.6 us (0.990)
  waiting for transfers between devices: 5.43 us -> 2.85 us
  starting transfers between devices: 11.4 us -> 13.2 us
  blocking collectives: 9.66 us -> 10.1 us
    ppermute x7, waiting for transfers between devices: 5.04 us -> 1.75 us  [to_chip(): lax.ppermute(x, 'chol', [(i, i ^ offset * CORES) for i in range(groups)])]
    ppermute x7, starting transfers between devices: 10.8 us -> 12.6 us  [to_chip(): lax.ppermute(x, 'chol', [(i, i ^ offset * CORES) for i in range(groups)])]
    ppermute x2, waiting for transfers between devices: 0.39 us -> 1.1 us  [to_core(): return lax.ppermute(x, 'chol', [(i, i ^ 1) for i in range(groups)])]
    all_to_all x1, blocking collectives: 9.66 us -> 10.1 us  [body(): lax.all_to_all(rows, 'chol', split_axis=0, concat_axis=0, tiled=True, axi...]
where the time goes in v17:
time: 39.6 us; the launch traced here: 39.4 us
  starting transfers between devices  13.2 us (33%)
  blocking collectives  10.1 us (26%)
  Pallas kernels  9.35 us (24%)
  local copies, waits for them, and re-layouts  3.23 us (8%)
  waiting for transfers between devices  2.85 us (7%)
  between operations  0.72 us (2%)
    ppermute x7, starting transfers between devices, to_chip(): lax.ppermute(x, 'chol', [(i, i ^ offset * CORES) for i in range(groups)])  12.6 us
    all_to_all x1, blocking collectives, body(): lax.all_to_all(rows, 'chol', split_axis=0, concat_axis=0, tiled=True, axi...  10.1 us
    pallas_call x2, Pallas kernels, chip_terms(): pl.pallas_call(functools.partial(terms_kernel, first=first, count=count,...  5.12 us
    unnamed x10, local copies, waits for them, and re-layouts  3.23 us
    ppermute x7, waiting for transfers between devices, to_chip(): lax.ppermute(x, 'chol', [(i, i ^ offset * CORES) for i in range(groups)])  1.75 us
    pallas_call x2, Pallas kernels, pick_tiles(): pl.pallas_call(pick_kernel, in_specs=[SMEM, VMEM], out_specs=[VMEM] * cou...  1.43 us
    pallas_call x2, Pallas kernels, prepare_block(): pl.pallas_call(prepare_kernel, in_specs=[VMEM], out_specs=[VMEM, VMEM], o...  1.43 us
    pallas_call x1, Pallas kernels, finish(): pl.pallas_call(functools.partial(finish_kernel, used=used, scale=scale),...  1.37 us
  transfers between devices with their start and end apart: 9, of which 3 were waited for; matrix products, arithmetic and copies ran while one was open for 0% of the time, Pallas kernels for 14%

profile of v17, /device:TPU:0, one launch (start us, length us, event | category | flops | bytes accessed | tf_op | source)
XLA Modules:
  0.0 39.4 jit_solution(7865600256269508566)
XLA Ops:
  0.6 0.5 %collective-permute-start.2 = (bf16[1,4,32,64,128]{4,3,2,1,0:T(8,128)(2,1)}, bf16[1,4,32,64,128]{4,3,2,1,0:T(8,128)(2,1)S(1)}, u32[]{:S(2)}, u32[]{:S(2)}) collective-permute-start(bf16[1,4,32,64,128]{4,3,2,1,0:T(8,128)(2,1)} %chol_ref.1), channel_id=1, source_target_pairs={{0,1},{1,0},{2,3},{3,2},{4,5},{5,4},{6,7},{7,6},{8,9},{9,8},{10,11... | collective-permute-start | bytes 6291464 | tf_op jit(solution)/shard_map/ppermute | solution.py:316
  1.1 3.7 %collective-permute-start = (bf16[1,64,1280]{2,1,0:T(8,128)(2,1)}, bf16[1,64,1280]{2,1,0:T(8,128)(2,1)S(1)}, u32[]{:S(2)}, u32[]{:S(2)}) collective-permute-start(bf16[1,64,1280]{2,1,0:T(8,128)(2,1)} %theta_ref.1), channel_id=1, source_target_pairs={{0,8},{1,9},{2,10},{3,11},{4,12},{5,13},{6,14},{7,15},{8,0},{9,1},... | collective-permute-start | bytes 491528 | tf_op jit(solution)/shard_map/ppermute | solution.py:313
  4.8 0.0 copy-start.1
  4.8 0.9 %copy-done.1 = bf16[1,64,1280]{2,1,0:T(8,128)(2,1)S(1)} copy-done((bf16[1,64,1280]{2,1,0:T(8,128)(2,1)S(1)}, bf16[1,64,1280]{2,1,0:T(8,128)(2,1)}, u32[]{:S(2)}) %copy-start.1) | copy-done | bytes 163864
  5.8 0.7 %copy-done.2 = s32[16,4]{0,1:T(4,128)S(1)} copy-done((s32[16,4]{0,1:T(4,128)S(1)}, s32[16,4]{0,1:T(4,128)}, u32[]{:S(2)}) %copy-start.2) | copy-done | bytes 280
  6.4 0.7 %pick_tiles.2 = (bf16[2,64,512]{2,1,0:T(8,128)(2,1)S(1)}, bf16[2,64,512]{2,1,0:T(8,128)(2,1)S(1)}, bf16[2,64,512]{2,1,0:T(8,128)(2,1)S(1)}, bf16[2,64,512]{2,1,0:T(8,128)(2,1)S(1)}) custom-call(s32[4,16]{1,0:T(4,128)S(1)} %bitcast.2, bf16[1,64,1280]{2,1,0:T(8,128)(2,1)S(1)} %copy-done.1), custom_call_target="tpu_custom_call" | custom-call | tf_op jit(solution)/shard_map/pick_tiles/pallas_call | solution.py:63
  7.2 1.6 %collective-permute-start.1 = (bf16[2,64,512]{2,1,0:T(8,128)(2,1)S(1)}, bf16[2,64,512]{2,1,0:T(8,128)(2,1)S(1)}, u32[]{:S(2)}, u32[]{:S(2)}) collective-permute-start(bf16[2,64,512]{2,1,0:T(8,128)(2,1)S(1)} %get-tuple-element.25), channel_id=1, source_target_pairs={{0,2},{1,3},{2,0},{3,1},{4,6},{5,7},{6,4},{7,5},{8,10},{9,11},{10,... | collective-permute-start | bytes 393224 | tf_op jit(solution)/shard_map/ppermute | solution.py:313
  8.8 1.5 %collective-permute-start.3 = (bf16[2,64,512]{2,1,0:T(8,128)(2,1)S(1)}, bf16[2,64,512]{2,1,0:T(8,128)(2,1)S(1)}, u32[]{:S(2)}, u32[]{:S(2)}) collective-permute-start(bf16[2,64,512]{2,1,0:T(8,128)(2,1)S(1)} %get-tuple-element.28), channel_id=1, source_target_pairs={{0,6},{1,7},{2,4},{3,5},{4,2},{5,3},{6,0},{7,1},{8,14},{9,15},{10,... | collective-permute-start | bytes 393224 | tf_op jit(solution)/shard_map/ppermute | solution.py:313
  10.3 0.4 %collective-permute-start.5 = (bf16[2,64,512]{2,1,0:T(8,128)(2,1)S(1)}, bf16[2,64,512]{2,1,0:T(8,128)(2,1)S(1)}, u32[]{:S(2)}, u32[]{:S(2)}) collective-permute-start(bf16[2,64,512]{2,1,0:T(8,128)(2,1)S(1)} %get-tuple-element.37), channel_id=1, source_target_pairs={{0,4},{1,5},{2,6},{3,7},{4,0},{5,1},{6,2},{7,3},{8,12},{9,13},{10,... | collective-permute-start | bytes 393224 | tf_op jit(solution)/shard_map/ppermute | solution.py:313
  10.7 1.6 %copy-done = bf16[1,4,32,64,128]{4,3,2,1,0:T(8,128)(2,1)S(1)} copy-done((bf16[1,4,32,64,128]{4,3,2,1,0:T(8,128)(2,1)S(1)}, bf16[1,4,32,64,128]{4,3,2,1,0:T(8,128)(2,1)}, u32[]{:S(2)}) %copy-start) | copy-done | bytes 2097176
  12.3 0.7 %prepare_block.2 = (bf16[2048,512]{1,0:T(8,128)(2,1)S(1)}, bf16[512,2048]{1,0:T(8,128)(2,1)S(1)}) custom-call(bf16[1,4,32,64,128]{4,3,2,1,0:T(8,128)(2,1)S(1)} %copy-done), custom_call_target="tpu_custom_call" | custom-call | tf_op jit(solution)/shard_map/prepare_block/pallas_call | solution.py:35
  13.0 0.0 collective-permute-done.1.refs_7_
  13.0 0.4 collective-permute-done.theta_ref
  13.4 0.0 collective-permute-done.2.chol_ref
  13.4 0.0 copy-done.3
  13.4 0.7 %pick_tiles.3 = (bf16[2,64,512]{2,1,0:T(8,128)(2,1)S(1)}, bf16[2,64,512]{2,1,0:T(8,128)(2,1)S(1)}, bf16[2,64,512]{2,1,0:T(8,128)(2,1)S(1)}, bf16[2,64,512]{2,1,0:T(8,128)(2,1)S(1)}) custom-call(s32[4,16]{1,0:T(4,128)S(1)} %bitcast.3, bf16[1,64,1280]{2,1,0:T(8,128)(2,1)S(1)} %collective-permute-done.theta_ref), custom_call_target="tpu_custom_call" | custom-call | tf_op jit(solution)/shard_map/pick_tiles/pallas_call | solution.py:63
  14.2 1.7 %collective-permute-start.6 = (bf16[2,64,512]{2,1,0:T(8,128)(2,1)S(1)}, bf16[2,64,512]{2,1,0:T(8,128)(2,1)S(1)}, u32[]{:S(2)}, u32[]{:S(2)}) collective-permute-start(bf16[2,64,512]{2,1,0:T(8,128)(2,1)S(1)} %get-tuple-element.43), channel_id=1, source_target_pairs={{0,2},{1,3},{2,0},{3,1},{4,6},{5,7},{6,4},{7,5},{8,10},{9,11},{10,... | collective-permute-start | bytes 393224 | tf_op jit(solution)/shard_map/ppermute | solution.py:313
  15.8 3.7 %collective-permute-start.7 = (bf16[2,64,512]{2,1,0:T(8,128)(2,1)S(1)}, bf16[2,64,512]{2,1,0:T(8,128)(2,1)S(1)}, u32[]{:S(2)}, u32[]{:S(2)}) collective-permute-start(bf16[2,64,512]{2,1,0:T(8,128)(2,1)S(1)} %get-tuple-element.44), channel_id=1, source_target_pairs={{0,4},{1,5},{2,6},{3,7},{4,0},{5,1},{6,2},{7,3},{8,12},{9,13},{10,... | collective-permute-start | bytes 393224 | tf_op jit(solution)/shard_map/ppermute | solution.py:313
  19.5 0.0 collective-permute-start.8
  19.5 0.0 collective-permute-done.3.refs_9_
  19.5 0.7 %prepare_block.3 = (bf16[2048,512]{1,0:T(8,128)(2,1)S(1)}, bf16[512,2048]{1,0:T(8,128)(2,1)S(1)}) custom-call(bf16[1,4,32,64,128]{4,3,2,1,0:T(8,128)(2,1)S(1)} %collective-permute-done.2.chol_ref), custom_call_target="tpu_custom_call" | custom-call | tf_op jit(solution)/shard_map/prepare_block/pallas_call | solution.py:35
  20.2 0.0 copy-done.4
  20.2 0.1 collective-permute-start.4
  20.3 0.0 collective-permute-done.5.refs_8_
  20.3 1.1 %collective-permute-done.4.refs_1_ = s32[1,4]{1,0:T(1,128)S(1)} collective-permute-done((s32[1,4]{1,0:T(1,128)S(1)}, s32[1,4]{1,0:T(1,128)S(1)}, u32[]{:S(2)}, u32[]{:S(2)}) %collective-permute-start.4) | collective-permute-done | bytes 48 | tf_op jit(solution)/shard_map/ppermute | solution.py:316
  21.4 2.8 %chip_terms.2 = (f32[8,1,128]{2,1,0:T(1,128)S(1)}, f32[2,512]{1,0:T(2,128)S(1)}) custom-call(s32[1,4]{1,0:T(1,128)S(1)} %copy-done.4, s32[1,4]{1,0:T(1,128)S(1)} %collective-permute-done.4.refs_1_, bf16[2048,512]{1,0:T(8,128)(2,1)S(1)} %get-tuple-element.30.refs_2_, bf16[512,2048]{1,0:T(8,128)(2,1)S(1)} %get-tuple-element.31.refs_3_, ...), custom_call_target="tpu_custom_call" | custom-call | tf_op jit(solution)/shard_map/chip_terms/pallas_call | solution.py:240
  24.2 0.0 collective-permute-done.6.refs_7_
  24.2 0.0 collective-permute-done.7.refs_8_
  24.2 1.3 %collective-permute-done.8.refs_9_ = bf16[2,64,512]{2,1,0:T(8,128)(2,1)S(1)} collective-permute-done((bf16[2,64,512]{2,1,0:T(8,128)(2,1)S(1)}, bf16[2,64,512]{2,1,0:T(8,128)(2,1)S(1)}, u32[]{:S(2)}, u32[]{:S(2)}) %collective-permute-start.8) | collective-permute-done | bytes 131104 | tf_op jit(solution)/shard_map/ppermute | solution.py:313
  25.6 2.4 %chip_terms.3 = f32[8,1,128]{2,1,0:T(1,128)S(1)} custom-call(f32[2,512]{1,0:T(2,128)S(1)} %get-tuple-element.39.refs_0_, f32[8,1,128]{2,1,0:T(1,128)S(1)} %get-tuple-element.40.refs_1_, bf16[2048,512]{1,0:T(8,128)(2,1)S(1)} %get-tuple-element.30.refs_2_, bf16[512,2048]{1,0:T(8,128)(2,1)S(1)} %get-tuple-element.31.refs_3_, ...), custom_call_target="tpu_custom_call" | custom-call | tf_op jit(solution)/shard_map/chip_terms/pallas_call | solution.py:240
  27.9 10.1 %all_to_all.5.rows_ref = f32[8,1,128]{2,1,0:T(1,128)} all-to-all(f32[8,1,128]{2,1,0:T(1,128)S(1)} %chip_terms.3), channel_id=1, replica_groups={{0,2,4,6,8,10,12,14},{1,3,5,7,9,11,13,15},{16,18,20,22,24,26,28,30},{17..., dimensions={0} | all-to-all | bytes 8192 | tf_op jit(solution)/shard_map/all_to_all | solution.py:337
  38.0 1.4 %finish.1 = (f32[1,512]{1,0:T(1,128)}, f32[1,1]{1,0:T(1,128)}) custom-call(f32[8,1,128]{2,1,0:T(1,128)} %all_to_all.5.rows_ref), custom_call_target="tpu_custom_call" | custom-call | tf_op jit(solution)/shard_map/finish/pallas_call | solution.py:290
  (4 shorter events, 0.0 us)
Async XLA Ops:
  0.6 12.8 %collective-permute-start.2 = (bf16[1,4,32,64,128]{4,3,2,1,0:T(8,128)(2,1)}, bf16[1,4,32,64,128]{4,3,2,1,0:T(8,128)(2,1)S(1)}, u32[]{:S(2)}, u32[]{:S(2)}) collective-permute-start(bf16[1,4,32,64,128]{4,3,2,1,0:T(8,128)(2,1)} %chol_ref.1), channel_id=1, source_target_pairs={{0,1},{1,0},{2,3},{3,2},{4,5},{5,4},{6,7},{7,6},{8,9},{9,8},{10,11... | collective-permute-start | bytes 6291464 | tf_op jit(solution)/shard_map/ppermute | solution.py:316
  1.1 12.3 %collective-permute-start = (bf16[1,64,1280]{2,1,0:T(8,128)(2,1)}, bf16[1,64,1280]{2,1,0:T(8,128)(2,1)S(1)}, u32[]{:S(2)}, u32[]{:S(2)}) collective-permute-start(bf16[1,64,1280]{2,1,0:T(8,128)(2,1)} %theta_ref.1), channel_id=1, source_target_pairs={{0,8},{1,9},{2,10},{3,11},{4,12},{5,13},{6,14},{7,15},{8,0},{9,1},... | collective-permute-start | bytes 491528 | tf_op jit(solution)/shard_map/ppermute | solution.py:313
  4.8 0.9 %copy-start.1 = (bf16[1,64,1280]{2,1,0:T(8,128)(2,1)S(1)}, bf16[1,64,1280]{2,1,0:T(8,128)(2,1)}, u32[]{:S(2)}) copy-start(bf16[1,64,1280]{2,1,0:T(8,128)(2,1)} %theta_ref.1) | copy-start | bytes 491524
  5.8 0.7 %copy-start.2 = (s32[16,4]{0,1:T(4,128)S(1)}, s32[16,4]{0,1:T(4,128)}, u32[]{:S(2)}) copy-start(s32[16,4]{0,1:T(4,128)} %param.7) | copy-start | bytes 772
  6.4 7.0 %copy-start.3 = (s32[16,4]{0,1:T(4,128)S(1)}, s32[16,4]{0,1:T(4,128)}, u32[]{:S(2)}) copy-start(s32[16,4]{0,1:T(4,128)} %param.7) | copy-start | bytes 772
  7.2 5.9 %collective-permute-start.1 = (bf16[2,64,512]{2,1,0:T(8,128)(2,1)S(1)}, bf16[2,64,512]{2,1,0:T(8,128)(2,1)S(1)}, u32[]{:S(2)}, u32[]{:S(2)}) collective-permute-start(bf16[2,64,512]{2,1,0:T(8,128)(2,1)S(1)} %get-tuple-element.25), channel_id=1, source_target_pairs={{0,2},{1,3},{2,0},{3,1},{4,6},{5,7},{6,4},{7,5},{8,10},{9,11},{10,... | collective-permute-start | bytes 393224 | tf_op jit(solution)/shard_map/ppermute | solution.py:313
  8.8 10.8 %collective-permute-start.3 = (bf16[2,64,512]{2,1,0:T(8,128)(2,1)S(1)}, bf16[2,64,512]{2,1,0:T(8,128)(2,1)S(1)}, u32[]{:S(2)}, u32[]{:S(2)}) collective-permute-start(bf16[2,64,512]{2,1,0:T(8,128)(2,1)S(1)} %get-tuple-element.28), channel_id=1, source_target_pairs={{0,6},{1,7},{2,4},{3,5},{4,2},{5,3},{6,0},{7,1},{8,14},{9,15},{10,... | collective-permute-start | bytes 393224 | tf_op jit(solution)/shard_map/ppermute | solution.py:313
  10.3 10.1 %collective-permute-start.5 = (bf16[2,64,512]{2,1,0:T(8,128)(2,1)S(1)}, bf16[2,64,512]{2,1,0:T(8,128)(2,1)S(1)}, u32[]{:S(2)}, u32[]{:S(2)}) collective-permute-start(bf16[2,64,512]{2,1,0:T(8,128)(2,1)S(1)} %get-tuple-element.37), channel_id=1, source_target_pairs={{0,4},{1,5},{2,6},{3,7},{4,0},{5,1},{6,2},{7,3},{8,12},{9,13},{10,... | collective-permute-start | bytes 393224 | tf_op jit(solution)/shard_map/ppermute | solution.py:313
  10.7 1.6 %copy-start = (bf16[1,4,32,64,128]{4,3,2,1,0:T(8,128)(2,1)S(1)}, bf16[1,4,32,64,128]{4,3,2,1,0:T(8,128)(2,1)}, u32[]{:S(2)}) copy-start(bf16[1,4,32,64,128]{4,3,2,1,0:T(8,128)(2,1)} %chol_ref.1) | copy-start | bytes 6291460
  12.3 7.9 %copy-start.4 = (s32[1,4]{1,0:T(1,128)S(1)}, s32[1,4]{1,0:T(1,128)}, u32[]{:S(2)}) copy-start(s32[1,4]{1,0:T(1,128)} %refs_0_.1) | copy-start | bytes 52
  14.2 10.1 %collective-permute-start.6 = (bf16[2,64,512]{2,1,0:T(8,128)(2,1)S(1)}, bf16[2,64,512]{2,1,0:T(8,128)(2,1)S(1)}, u32[]{:S(2)}, u32[]{:S(2)}) collective-permute-start(bf16[2,64,512]{2,1,0:T(8,128)(2,1)S(1)} %get-tuple-element.43), channel_id=1, source_target_pairs={{0,2},{1,3},{2,0},{3,1},{4,6},{5,7},{6,4},{7,5},{8,10},{9,11},{10,... | collective-permute-start | bytes 393224 | tf_op jit(solution)/shard_map/ppermute | solution.py:313
  15.8 8.4 %collective-permute-start.7 = (bf16[2,64,512]{2,1,0:T(8,128)(2,1)S(1)}, bf16[2,64,512]{2,1,0:T(8,128)(2,1)S(1)}, u32[]{:S(2)}, u32[]{:S(2)}) collective-permute-start(bf16[2,64,512]{2,1,0:T(8,128)(2,1)S(1)} %get-tuple-element.44), channel_id=1, source_target_pairs={{0,4},{1,5},{2,6},{3,7},{4,0},{5,1},{6,2},{7,3},{8,12},{9,13},{10,... | collective-permute-start | bytes 393224 | tf_op jit(solution)/shard_map/ppermute | solution.py:313
  19.5 6.1 %collective-permute-start.8 = (bf16[2,64,512]{2,1,0:T(8,128)(2,1)S(1)}, bf16[2,64,512]{2,1,0:T(8,128)(2,1)S(1)}, u32[]{:S(2)}, u32[]{:S(2)}) collective-permute-start(bf16[2,64,512]{2,1,0:T(8,128)(2,1)S(1)} %get-tuple-element.45), channel_id=1, source_target_pairs={{0,6},{1,7},{2,4},{3,5},{4,2},{5,3},{6,0},{7,1},{8,14},{9,15},{10,... | collective-permute-start | bytes 393224 | tf_op jit(solution)/shard_map/ppermute | solution.py:313
  20.2 1.2 %collective-permute-start.4 = (s32[1,4]{1,0:T(1,128)S(1)}, s32[1,4]{1,0:T(1,128)S(1)}, u32[]{:S(2)}, u32[]{:S(2)}) collective-permute-start(s32[1,4]{1,0:T(1,128)S(1)} %copy-done.4), channel_id=1, source_target_pairs={{0,1},{1,0},{2,3},{3,2},{4,5},{5,4},{6,7},{7,6},{8,9},{9,8},{10,11... | collective-permute-start | bytes 56 | tf_op jit(solution)/shard_map/ppermute | solution.py:316

commit v18 on v17

--- a/solution.py
+++ b/solution.py
@@ -332,7 +332,8 @@
 
     screens = [screen, to_core(late_screen)]
     rows, masks = chip_terms(screens, [], blocks, near, 0, NEAR, vectors, chips, out_width)
-    rows, = chip_terms([], [masks, rows], blocks, beyond, half, BEYOND, vectors, chips, out_width)
+    rows, = chip_terms([], [masks, rows], blocks, beyond[:half // 2], half, BEYOND, vectors, chips, out_width)
+    rows, = chip_terms([], [masks, rows], blocks, beyond[half // 2:], half + half // 2, BEYOND, vectors, chips, out_width)
     same_core = [list(range(core, groups, CORES)) for core in range(CORES)]
     back = lax.all_to_all(rows, "chol", split_axis=0, concat_axis=0, tiled=True, axis_index_groups=same_core)
     return finish(back, used, 1.0 / (2.0 * occupied * occupied))

time: 39.6 us -> 40.2 us (1.015)
  Pallas kernels: 9.35 us -> 10.9 us
  waiting for transfers between devices: 2.85 us -> 1.51 us
    pallas_call x2 -> x3, Pallas kernels: 5.12 us -> 6.67 us  [chip_terms(): pl.pallas_call(functools.partial(terms_kernel, first=first, count=count,...]
    ppermute x7, waiting for transfers between devices: 1.75 us -> 0.41 us  [to_chip(): lax.ppermute(x, 'chol', [(i, i ^ offset * CORES) for i in range(groups)])]
  transfers between devices with their start and end apart: 9 -> 9, of which waited for: 3 -> 2; matrix products, arithmetic and copies ran while one was open for 0% -> 0% of each run, Pallas kernels for 14% -> 19%
where the time goes in v18:
time: 40.2 us; the launch traced here: 39.9 us
  starting transfers between devices  13.2 us (33%)
  Pallas kernels  10.9 us (27%)
  blocking collectives  10.4 us (26%)
  local copies, waits for them, and re-layouts  3.23 us (8%)
  waiting for transfers between devices  1.51 us (4%)
  between operations  0.71 us (2%)
    ppermute x7, starting transfers between devices, to_chip(): lax.ppermute(x, 'chol', [(i, i ^ offset * CORES) for i in range(groups)])  12.6 us
    all_to_all x1, blocking collectives, body(): lax.all_to_all(rows, 'chol', split_axis=0, concat_axis=0, tiled=True, axi...  10.4 us
    pallas_call x3, Pallas kernels, chip_terms(): pl.pallas_call(functools.partial(terms_kernel, first=first, count=count,...  6.67 us
    unnamed x10, local copies, waits for them, and re-layouts  3.23 us
    pallas_call x2, Pallas kernels, pick_tiles(): pl.pallas_call(pick_kernel, in_specs=[SMEM, VMEM], out_specs=[VMEM] * cou...  1.43 us
    pallas_call x2, Pallas kernels, prepare_block(): pl.pallas_call(prepare_kernel, in_specs=[VMEM], out_specs=[VMEM, VMEM], o...  1.43 us
    pallas_call x1, Pallas kernels, finish(): pl.pallas_call(functools.partial(finish_kernel, used=used, scale=scale),...  1.37 us
    ppermute x2, waiting for transfers between devices, to_core(): return lax.ppermute(x, 'chol', [(i, i ^ 1) for i in range(groups)])  1.1 us
  transfers between devices with their start and end apart: 9, of which 2 were waited for; matrix products, arithmetic and copies ran while one was open for 0% of the time, Pallas kernels for 19%

profile of v18, /device:TPU:0, one launch (start us, length us, event | category | flops | bytes accessed | tf_op | source)
XLA Modules:
  0.0 39.9 jit_solution(5765329779941653683)
XLA Ops:
  0.6 0.5 %collective-permute-start.2 = (bf16[1,4,32,64,128]{4,3,2,1,0:T(8,128)(2,1)}, bf16[1,4,32,64,128]{4,3,2,1,0:T(8,128)(2,1)S(1)}, u32[]{:S(2)}, u32[]{:S(2)}) collective-permute-start(bf16[1,4,32,64,128]{4,3,2,1,0:T(8,128)(2,1)} %chol_ref.1), channel_id=1, source_target_pairs={{0,1},{1,0},{2,3},{3,2},{4,5},{5,4},{6,7},{7,6},{8,9},{9,8},{10,11... | collective-permute-start | bytes 6291464 | tf_op jit(solution)/shard_map/ppermute | solution.py:316
  1.1 3.7 %collective-permute-start = (bf16[1,64,1280]{2,1,0:T(8,128)(2,1)}, bf16[1,64,1280]{2,1,0:T(8,128)(2,1)S(1)}, u32[]{:S(2)}, u32[]{:S(2)}) collective-permute-start(bf16[1,64,1280]{2,1,0:T(8,128)(2,1)} %theta_ref.1), channel_id=1, source_target_pairs={{0,8},{1,9},{2,10},{3,11},{4,12},{5,13},{6,14},{7,15},{8,0},{9,1},... | collective-permute-start | bytes 491528 | tf_op jit(solution)/shard_map/ppermute | solution.py:313
  4.8 0.9 %copy-done.1 = bf16[1,64,1280]{2,1,0:T(8,128)(2,1)S(1)} copy-done((bf16[1,64,1280]{2,1,0:T(8,128)(2,1)S(1)}, bf16[1,64,1280]{2,1,0:T(8,128)(2,1)}, u32[]{:S(2)}) %copy-start.1) | copy-done | bytes 163864
  5.8 0.7 %copy-done.2 = s32[16,4]{0,1:T(4,128)S(1)} copy-done((s32[16,4]{0,1:T(4,128)S(1)}, s32[16,4]{0,1:T(4,128)}, u32[]{:S(2)}) %copy-start.2) | copy-done | bytes 280
  6.4 0.7 %pick_tiles.2 = (bf16[2,64,512]{2,1,0:T(8,128)(2,1)S(1)}, bf16[2,64,512]{2,1,0:T(8,128)(2,1)S(1)}, bf16[2,64,512]{2,1,0:T(8,128)(2,1)S(1)}, bf16[2,64,512]{2,1,0:T(8,128)(2,1)S(1)}) custom-call(s32[4,16]{1,0:T(4,128)S(1)} %bitcast.2, bf16[1,64,1280]{2,1,0:T(8,128)(2,1)S(1)} %copy-done.1), custom_call_target="tpu_custom_call" | custom-call | tf_op jit(solution)/shard_map/pick_tiles/pallas_call | solution.py:63
  7.2 1.6 %collective-permute-start.1 = (bf16[2,64,512]{2,1,0:T(8,128)(2,1)S(1)}, bf16[2,64,512]{2,1,0:T(8,128)(2,1)S(1)}, u32[]{:S(2)}, u32[]{:S(2)}) collective-permute-start(bf16[2,64,512]{2,1,0:T(8,128)(2,1)S(1)} %get-tuple-element.25), channel_id=1, source_target_pairs={{0,2},{1,3},{2,0},{3,1},{4,6},{5,7},{6,4},{7,5},{8,10},{9,11},{10,... | collective-permute-start | bytes 393224 | tf_op jit(solution)/shard_map/ppermute | solution.py:313
  8.8 1.5 %collective-permute-start.3 = (bf16[2,64,512]{2,1,0:T(8,128)(2,1)S(1)}, bf16[2,64,512]{2,1,0:T(8,128)(2,1)S(1)}, u32[]{:S(2)}, u32[]{:S(2)}) collective-permute-start(bf16[2,64,512]{2,1,0:T(8,128)(2,1)S(1)} %get-tuple-element.28), channel_id=1, source_target_pairs={{0,6},{1,7},{2,4},{3,5},{4,2},{5,3},{6,0},{7,1},{8,14},{9,15},{10,... | collective-permute-start | bytes 393224 | tf_op jit(solution)/shard_map/ppermute | solution.py:313
  10.3 0.4 %collective-permute-start.5 = (bf16[2,64,512]{2,1,0:T(8,128)(2,1)S(1)}, bf16[2,64,512]{2,1,0:T(8,128)(2,1)S(1)}, u32[]{:S(2)}, u32[]{:S(2)}) collective-permute-start(bf16[2,64,512]{2,1,0:T(8,128)(2,1)S(1)} %get-tuple-element.37), channel_id=1, source_target_pairs={{0,4},{1,5},{2,6},{3,7},{4,0},{5,1},{6,2},{7,3},{8,12},{9,13},{10,... | collective-permute-start | bytes 393224 | tf_op jit(solution)/shard_map/ppermute | solution.py:313
  10.7 1.6 %copy-done = bf16[1,4,32,64,128]{4,3,2,1,0:T(8,128)(2,1)S(1)} copy-done((bf16[1,4,32,64,128]{4,3,2,1,0:T(8,128)(2,1)S(1)}, bf16[1,4,32,64,128]{4,3,2,1,0:T(8,128)(2,1)}, u32[]{:S(2)}) %copy-start) | copy-done | bytes 2097176
  12.3 0.7 %prepare_block.2 = (bf16[2048,512]{1,0:T(8,128)(2,1)S(1)}, bf16[512,2048]{1,0:T(8,128)(2,1)S(1)}) custom-call(bf16[1,4,32,64,128]{4,3,2,1,0:T(8,128)(2,1)S(1)} %copy-done), custom_call_target="tpu_custom_call" | custom-call | tf_op jit(solution)/shard_map/prepare_block/pallas_call | solution.py:35
  13.0 0.0 collective-permute-done.1.refs_7_
  13.0 0.4 collective-permute-done.theta_ref
  13.4 0.0 collective-permute-done.2.chol_ref
  13.4 0.0 copy-done.3
  13.4 0.7 %pick_tiles.3 = (bf16[2,64,512]{2,1,0:T(8,128)(2,1)S(1)}, bf16[2,64,512]{2,1,0:T(8,128)(2,1)S(1)}, bf16[2,64,512]{2,1,0:T(8,128)(2,1)S(1)}, bf16[2,64,512]{2,1,0:T(8,128)(2,1)S(1)}) custom-call(s32[4,16]{1,0:T(4,128)S(1)} %bitcast.3, bf16[1,64,1280]{2,1,0:T(8,128)(2,1)S(1)} %collective-permute-done.theta_ref), custom_call_target="tpu_custom_call" | custom-call | tf_op jit(solution)/shard_map/pick_tiles/pallas_call | solution.py:63
  14.2 1.7 %collective-permute-start.6 = (bf16[2,64,512]{2,1,0:T(8,128)(2,1)S(1)}, bf16[2,64,512]{2,1,0:T(8,128)(2,1)S(1)}, u32[]{:S(2)}, u32[]{:S(2)}) collective-permute-start(bf16[2,64,512]{2,1,0:T(8,128)(2,1)S(1)} %get-tuple-element.43), channel_id=1, source_target_pairs={{0,2},{1,3},{2,0},{3,1},{4,6},{5,7},{6,4},{7,5},{8,10},{9,11},{10,... | collective-permute-start | bytes 393224 | tf_op jit(solution)/shard_map/ppermute | solution.py:313
  15.8 3.7 %collective-permute-start.7 = (bf16[2,64,512]{2,1,0:T(8,128)(2,1)S(1)}, bf16[2,64,512]{2,1,0:T(8,128)(2,1)S(1)}, u32[]{:S(2)}, u32[]{:S(2)}) collective-permute-start(bf16[2,64,512]{2,1,0:T(8,128)(2,1)S(1)} %get-tuple-element.44), channel_id=1, source_target_pairs={{0,4},{1,5},{2,6},{3,7},{4,0},{5,1},{6,2},{7,3},{8,12},{9,13},{10,... | collective-permute-start | bytes 393224 | tf_op jit(solution)/shard_map/ppermute | solution.py:313
  19.5 0.0 collective-permute-start.8
  19.5 0.0 collective-permute-done.3.refs_9_
  19.5 0.7 %prepare_block.3 = (bf16[2048,512]{1,0:T(8,128)(2,1)S(1)}, bf16[512,2048]{1,0:T(8,128)(2,1)S(1)}) custom-call(bf16[1,4,32,64,128]{4,3,2,1,0:T(8,128)(2,1)S(1)} %collective-permute-done.2.chol_ref), custom_call_target="tpu_custom_call" | custom-call | tf_op jit(solution)/shard_map/prepare_block/pallas_call | solution.py:35
  20.2 0.0 copy-done.4
  20.2 0.1 collective-permute-start.4
  20.3 0.0 collective-permute-done.5.refs_8_
  20.3 1.1 %collective-permute-done.4.refs_1_ = s32[1,4]{1,0:T(1,128)S(1)} collective-permute-done((s32[1,4]{1,0:T(1,128)S(1)}, s32[1,4]{1,0:T(1,128)S(1)}, u32[]{:S(2)}, u32[]{:S(2)}) %collective-permute-start.4) | collective-permute-done | bytes 48 | tf_op jit(solution)/shard_map/ppermute | solution.py:316
  21.4 2.8 %chip_terms.3 = (f32[8,1,128]{2,1,0:T(1,128)S(1)}, f32[2,512]{1,0:T(2,128)S(1)}) custom-call(s32[1,4]{1,0:T(1,128)S(1)} %copy-done.4, s32[1,4]{1,0:T(1,128)S(1)} %collective-permute-done.4.refs_1_, bf16[2048,512]{1,0:T(8,128)(2,1)S(1)} %get-tuple-element.30.refs_2_, bf16[512,2048]{1,0:T(8,128)(2,1)S(1)} %get-tuple-element.31.refs_3_, ...), custom_call_target="tpu_custom_call" | custom-call | tf_op jit(solution)/shard_map/chip_terms/pallas_call | solution.py:240
  24.2 0.0 collective-permute-done.6.refs_7_
  24.2 1.9 %chip_terms.4.refs_1_ = f32[8,1,128]{2,1,0:T(1,128)S(1)} custom-call(f32[2,512]{1,0:T(2,128)S(1)} %get-tuple-element.39.refs_0_, f32[8,1,128]{2,1,0:T(1,128)S(1)} %get-tuple-element.40.refs_1_, bf16[2048,512]{1,0:T(8,128)(2,1)S(1)} %get-tuple-element.30.refs_2_, bf16[512,2048]{1,0:T(8,128)(2,1)S(1)} %get-tuple-element.31.refs_3_, ...), custom_call_target="tpu_custom_call" | custom-call | tf_op jit(solution)/shard_map/chip_terms/pallas_call | solution.py:240
  26.2 0.0 collective-permute-done.7.refs_6_
  26.2 0.0 collective-permute-done.8.refs_7_
  26.2 2.0 %chip_terms.5 = f32[8,1,128]{2,1,0:T(1,128)S(1)} custom-call(f32[2,512]{1,0:T(2,128)S(1)} %get-tuple-element.39.refs_0_, f32[8,1,128]{2,1,0:T(1,128)S(1)} %chip_terms.4.refs_1_, bf16[2048,512]{1,0:T(8,128)(2,1)S(1)} %get-tuple-element.30.refs_2_, bf16[512,2048]{1,0:T(8,128)(2,1)S(1)} %get-tuple-element.31.refs_3_, ...), custom_call_target="tpu_custom_call" | custom-call | tf_op jit(solution)/shard_map/chip_terms/pallas_call | solution.py:240
  28.1 10.4 %all_to_all.5.rows_ref = f32[8,1,128]{2,1,0:T(1,128)} all-to-all(f32[8,1,128]{2,1,0:T(1,128)S(1)} %chip_terms.5), channel_id=1, replica_groups={{0,2,4,6,8,10,12,14},{1,3,5,7,9,11,13,15},{16,18,20,22,24,26,28,30},{17..., dimensions={0} | all-to-all | bytes 8192 | tf_op jit(solution)/shard_map/all_to_all | solution.py:338
  38.6 1.4 %finish.1 = (f32[1,512]{1,0:T(1,128)}, f32[1,1]{1,0:T(1,128)}) custom-call(f32[8,1,128]{2,1,0:T(1,128)} %all_to_all.5.rows_ref), custom_call_target="tpu_custom_call" | custom-call | tf_op jit(solution)/shard_map/finish/pallas_call | solution.py:290
  (5 shorter events, 0.0 us)
Async XLA Ops:
  0.6 12.8 %collective-permute-start.2 = (bf16[1,4,32,64,128]{4,3,2,1,0:T(8,128)(2,1)}, bf16[1,4,32,64,128]{4,3,2,1,0:T(8,128)(2,1)S(1)}, u32[]{:S(2)}, u32[]{:S(2)}) collective-permute-start(bf16[1,4,32,64,128]{4,3,2,1,0:T(8,128)(2,1)} %chol_ref.1), channel_id=1, source_target_pairs={{0,1},{1,0},{2,3},{3,2},{4,5},{5,4},{6,7},{7,6},{8,9},{9,8},{10,11... | collective-permute-start | bytes 6291464 | tf_op jit(solution)/shard_map/ppermute | solution.py:316
  1.1 12.3 %collective-permute-start = (bf16[1,64,1280]{2,1,0:T(8,128)(2,1)}, bf16[1,64,1280]{2,1,0:T(8,128)(2,1)S(1)}, u32[]{:S(2)}, u32[]{:S(2)}) collective-permute-start(bf16[1,64,1280]{2,1,0:T(8,128)(2,1)} %theta_ref.1), channel_id=1, source_target_pairs={{0,8},{1,9},{2,10},{3,11},{4,12},{5,13},{6,14},{7,15},{8,0},{9,1},... | collective-permute-start | bytes 491528 | tf_op jit(solution)/shard_map/ppermute | solution.py:313
  4.8 0.9 %copy-start.1 = (bf16[1,64,1280]{2,1,0:T(8,128)(2,1)S(1)}, bf16[1,64,1280]{2,1,0:T(8,128)(2,1)}, u32[]{:S(2)}) copy-start(bf16[1,64,1280]{2,1,0:T(8,128)(2,1)} %theta_ref.1) | copy-start | bytes 491524
  5.8 0.7 %copy-start.2 = (s32[16,4]{0,1:T(4,128)S(1)}, s32[16,4]{0,1:T(4,128)}, u32[]{:S(2)}) copy-start(s32[16,4]{0,1:T(4,128)} %param.7) | copy-start | bytes 772
  6.4 7.0 %copy-start.3 = (s32[16,4]{0,1:T(4,128)S(1)}, s32[16,4]{0,1:T(4,128)}, u32[]{:S(2)}) copy-start(s32[16,4]{0,1:T(4,128)} %param.7) | copy-start | bytes 772
  7.2 5.9 %collective-permute-start.1 = (bf16[2,64,512]{2,1,0:T(8,128)(2,1)S(1)}, bf16[2,64,512]{2,1,0:T(8,128)(2,1)S(1)}, u32[]{:S(2)}, u32[]{:S(2)}) collective-permute-start(bf16[2,64,512]{2,1,0:T(8,128)(2,1)S(1)} %get-tuple-element.25), channel_id=1, source_target_pairs={{0,2},{1,3},{2,0},{3,1},{4,6},{5,7},{6,4},{7,5},{8,10},{9,11},{10,... | collective-permute-start | bytes 393224 | tf_op jit(solution)/shard_map/ppermute | solution.py:313
  8.8 10.8 %collective-permute-start.3 = (bf16[2,64,512]{2,1,0:T(8,128)(2,1)S(1)}, bf16[2,64,512]{2,1,0:T(8,128)(2,1)S(1)}, u32[]{:S(2)}, u32[]{:S(2)}) collective-permute-start(bf16[2,64,512]{2,1,0:T(8,128)(2,1)S(1)} %get-tuple-element.28), channel_id=1, source_target_pairs={{0,6},{1,7},{2,4},{3,5},{4,2},{5,3},{6,0},{7,1},{8,14},{9,15},{10,... | collective-permute-start | bytes 393224 | tf_op jit(solution)/shard_map/ppermute | solution.py:313
  10.3 10.1 %collective-permute-start.5 = (bf16[2,64,512]{2,1,0:T(8,128)(2,1)S(1)}, bf16[2,64,512]{2,1,0:T(8,128)(2,1)S(1)}, u32[]{:S(2)}, u32[]{:S(2)}) collective-permute-start(bf16[2,64,512]{2,1,0:T(8,128)(2,1)S(1)} %get-tuple-element.37), channel_id=1, source_target_pairs={{0,4},{1,5},{2,6},{3,7},{4,0},{5,1},{6,2},{7,3},{8,12},{9,13},{10,... | collective-permute-start | bytes 393224 | tf_op jit(solution)/shard_map/ppermute | solution.py:313
  10.7 1.6 %copy-start = (bf16[1,4,32,64,128]{4,3,2,1,0:T(8,128)(2,1)S(1)}, bf16[1,4,32,64,128]{4,3,2,1,0:T(8,128)(2,1)}, u32[]{:S(2)}) copy-start(bf16[1,4,32,64,128]{4,3,2,1,0:T(8,128)(2,1)} %chol_ref.1) | copy-start | bytes 6291460
  12.3 7.9 %copy-start.4 = (s32[1,4]{1,0:T(1,128)S(1)}, s32[1,4]{1,0:T(1,128)}, u32[]{:S(2)}) copy-start(s32[1,4]{1,0:T(1,128)} %refs_0_.1) | copy-start | bytes 52
  14.2 10.1 %collective-permute-start.6 = (bf16[2,64,512]{2,1,0:T(8,128)(2,1)S(1)}, bf16[2,64,512]{2,1,0:T(8,128)(2,1)S(1)}, u32[]{:S(2)}, u32[]{:S(2)}) collective-permute-start(bf16[2,64,512]{2,1,0:T(8,128)(2,1)S(1)} %get-tuple-element.43), channel_id=1, source_target_pairs={{0,2},{1,3},{2,0},{3,1},{4,6},{5,7},{6,4},{7,5},{8,10},{9,11},{10,... | collective-permute-start | bytes 393224 | tf_op jit(solution)/shard_map/ppermute | solution.py:313
  15.8 10.4 %collective-permute-start.7 = (bf16[2,64,512]{2,1,0:T(8,128)(2,1)S(1)}, bf16[2,64,512]{2,1,0:T(8,128)(2,1)S(1)}, u32[]{:S(2)}, u32[]{:S(2)}) collective-permute-start(bf16[2,64,512]{2,1,0:T(8,128)(2,1)S(1)} %get-tuple-element.44), channel_id=1, source_target_pairs={{0,4},{1,5},{2,6},{3,7},{4,0},{5,1},{6,2},{7,3},{8,12},{9,13},{10,... | collective-permute-start | bytes 393224 | tf_op jit(solution)/shard_map/ppermute | solution.py:313
  19.5 6.7 %collective-permute-start.8 = (bf16[2,64,512]{2,1,0:T(8,128)(2,1)S(1)}, bf16[2,64,512]{2,1,0:T(8,128)(2,1)S(1)}, u32[]{:S(2)}, u32[]{:S(2)}) collective-permute-start(bf16[2,64,512]{2,1,0:T(8,128)(2,1)S(1)} %get-tuple-element.45), channel_id=1, source_target_pairs={{0,6},{1,7},{2,4},{3,5},{4,2},{5,3},{6,0},{7,1},{8,14},{9,15},{10,... | collective-permute-start | bytes 393224 | tf_op jit(solution)/shard_map/ppermute | solution.py:313
  20.2 1.2 %collective-permute-start.4 = (s32[1,4]{1,0:T(1,128)S(1)}, s32[1,4]{1,0:T(1,128)S(1)}, u32[]{:S(2)}, u32[]{:S(2)}) collective-permute-start(s32[1,4]{1,0:T(1,128)S(1)} %copy-done.4), channel_id=1, source_target_pairs={{0,1},{1,0},{2,3},{3,2},{4,5},{5,4},{6,7},{7,6},{8,9},{9,8},{10,11... | collective-permute-start | bytes 56 | tf_op jit(solution)/shard_map/ppermute | solution.py:316

commit v19 on v17

--- a/solution.py
+++ b/solution.py
@@ -137,6 +137,10 @@
             store_rows(k0 + k8, t, fold_rows(diagonals, sub8))
 
 
+def send_order(place, count):
+    return jnp.where(place <= 1, place, jnp.where(place == 2, count - 1, place - 1))
+
+
 def mask_kernel_rows(screen_refs, listed, width):
     return [
         jnp.concatenate(
@@ -217,7 +221,10 @@
             lax.dot_general(segment, part, NT, preferred_element_type=jnp.float32) for part in parts
         )
         for i in range(batch):
-            owner = chip ^ (first + index + i)
+            place = jnp.int32(index + i)
+            if not screened:
+                place = send_order(place, count)
+            owner = chip ^ (first + place)
             out_ref[pl.ds(owner, 1), 0, :used + 8] = sums[i:i + 1]
 
     if count == batch:
@@ -317,15 +324,18 @@
 
     far = to_chip(theta, half)
 
-    def spread(walker):
-        pieces = pick_tiles(listing, walker, depth, half)
+    def spread(walker, late=False):
+        pieces = list(pick_tiles(listing, walker, depth, half))
+        if late:
+            pieces[-2], near[1] = lax.optimization_barrier((pieces[-2], near[1]))
         return [pieces[0]] + [to_chip(pieces[offset], offset) for offset in range(1, half)]
 
     near = spread(theta)
     own, own_turned = prepare_block(chol_tiles)
     other_chol = to_core(chol_tiles)
-    far, near[1], other_chol, own = lax.optimization_barrier((far, near[1], other_chol, own))
-    beyond = spread(far)
+    far, other_chol, own = lax.optimization_barrier((far, other_chol, own))
+    beyond = spread(far, True)
+    beyond = beyond[:2] + beyond[-1:] + beyond[2:-1]
     other_chol, late_screen, near[-1] = lax.optimization_barrier((other_chol, screen, near[-1]))
     other, other_turned = prepare_block(other_chol)
     blocks = [own, own_turned, other, other_turned]

time: 39.6 us -> 39.7 us (level)
  blocking collectives: 10.1 us -> 11.1 us
  starting transfers between devices: 13.2 us -> 12.3 us
    all_to_all x1, blocking collectives: 10.1 us -> 11.1 us  [body(): lax.all_to_all(rows, 'chol', split_axis=0, concat_axis=0, tiled=True, axi...]
    ppermute x7, starting transfers between devices: 12.6 us -> 11.8 us  [to_chip(): lax.ppermute(x, 'chol', [(i, i ^ offset * CORES) for i in range(groups)])]
    ppermute x2, waiting for transfers between devices: 1.1 us -> 0.39 us  [to_core(): return lax.ppermute(x, 'chol', [(i, i ^ 1) for i in range(groups)])]
    ppermute x7, waiting for transfers between devices: 1.75 us -> 2.39 us  [to_chip(): lax.ppermute(x, 'chol', [(i, i ^ offset * CORES) for i in range(groups)])]
  transfers between devices with their start and end apart: 9 -> 9, of which waited for: 3 -> 4; matrix products, arithmetic and copies ran while one was open for 0% -> 0% of each run, Pallas kernels for 14% -> 14%
where the time goes in v19:
time: 39.7 us; the launch traced here: 39.4 us
  starting transfers between devices  12.3 us (31%)
  blocking collectives  11.1 us (28%)
  Pallas kernels  9.35 us (24%)
  local copies, waits for them, and re-layouts  3.23 us (8%)
  waiting for transfers between devices  2.78 us (7%)
  between operations  0.7 us (2%)
    ppermute x7, starting transfers between devices, to_chip(): lax.ppermute(x, 'chol', [(i, i ^ offset * CORES) for i in range(groups)])  11.8 us
    all_to_all x1, blocking collectives, body(): lax.all_to_all(rows, 'chol', split_axis=0, concat_axis=0, tiled=True, axi...  11.1 us
    pallas_call x2, Pallas kernels, chip_terms(): pl.pallas_call(functools.partial(terms_kernel, first=first, count=count,...  5.12 us
    unnamed x10, local copies, waits for them, and re-layouts  3.23 us
    ppermute x7, waiting for transfers between devices, to_chip(): lax.ppermute(x, 'chol', [(i, i ^ offset * CORES) for i in range(groups)])  2.39 us
    pallas_call x2, Pallas kernels, pick_tiles(): pl.pallas_call(pick_kernel, in_specs=[SMEM, VMEM], out_specs=[VMEM] * cou...  1.43 us
    pallas_call x2, Pallas kernels, prepare_block(): pl.pallas_call(prepare_kernel, in_specs=[VMEM], out_specs=[VMEM, VMEM], o...  1.43 us
    pallas_call x1, Pallas kernels, finish(): pl.pallas_call(functools.partial(finish_kernel, used=used, scale=scale),...  1.37 us
  transfers between devices with their start and end apart: 9, of which 4 were waited for; matrix products, arithmetic and copies ran while one was open for 0% of the time, Pallas kernels for 14%

profile of v19, /device:TPU:0, one launch (start us, length us, event | category | flops | bytes accessed | tf_op | source)
XLA Modules:
  0.0 39.4 jit_solution(918430917691020911)
XLA Ops:
  0.6 0.0 copy-start.4
  0.6 0.5 %collective-permute-start.1 = (bf16[1,4,32,64,128]{4,3,2,1,0:T(8,128)(2,1)}, bf16[1,4,32,64,128]{4,3,2,1,0:T(8,128)(2,1)S(1)}, u32[]{:S(2)}, u32[]{:S(2)}) collective-permute-start(bf16[1,4,32,64,128]{4,3,2,1,0:T(8,128)(2,1)} %chol_ref.1), channel_id=1, source_target_pairs={{0,1},{1,0},{2,3},{3,2},{4,5},{5,4},{6,7},{7,6},{8,9},{9,8},{10,11... | collective-permute-start | bytes 6291464 | tf_op jit(solution)/shard_map/ppermute | solution.py:323
  1.2 3.7 %collective-permute-start = (bf16[1,64,1280]{2,1,0:T(8,128)(2,1)}, bf16[1,64,1280]{2,1,0:T(8,128)(2,1)S(1)}, u32[]{:S(2)}, u32[]{:S(2)}) collective-permute-start(bf16[1,64,1280]{2,1,0:T(8,128)(2,1)} %theta_ref.1), channel_id=1, source_target_pairs={{0,8},{1,9},{2,10},{3,11},{4,12},{5,13},{6,14},{7,15},{8,0},{9,1},... | collective-permute-start | bytes 491528 | tf_op jit(solution)/shard_map/ppermute | solution.py:320
  4.8 0.9 %copy-done.1 = bf16[1,64,1280]{2,1,0:T(8,128)(2,1)S(1)} copy-done((bf16[1,64,1280]{2,1,0:T(8,128)(2,1)S(1)}, bf16[1,64,1280]{2,1,0:T(8,128)(2,1)}, u32[]{:S(2)}) %copy-start.1) | copy-done | bytes 163864
  5.8 0.7 %copy-done.2 = s32[16,4]{0,1:T(4,128)S(1)} copy-done((s32[16,4]{0,1:T(4,128)S(1)}, s32[16,4]{0,1:T(4,128)}, u32[]{:S(2)}) %copy-start.2) | copy-done | bytes 280
  6.5 0.7 %pick_tiles.2 = (bf16[2,64,512]{2,1,0:T(8,128)(2,1)S(1)}, bf16[2,64,512]{2,1,0:T(8,128)(2,1)S(1)}, bf16[2,64,512]{2,1,0:T(8,128)(2,1)S(1)}, bf16[2,64,512]{2,1,0:T(8,128)(2,1)S(1)}) custom-call(s32[4,16]{1,0:T(4,128)S(1)} %bitcast.2, bf16[1,64,1280]{2,1,0:T(8,128)(2,1)S(1)} %copy-done.1), custom_call_target="tpu_custom_call" | custom-call | tf_op jit(solution)/shard_map/pick_tiles/pallas_call | solution.py:63
  7.2 1.6 %collective-permute-start.4 = (bf16[2,64,512]{2,1,0:T(8,128)(2,1)S(1)}, bf16[2,64,512]{2,1,0:T(8,128)(2,1)S(1)}, u32[]{:S(2)}, u32[]{:S(2)}) collective-permute-start(bf16[2,64,512]{2,1,0:T(8,128)(2,1)S(1)} %get-tuple-element.38), channel_id=1, source_target_pairs={{0,2},{1,3},{2,0},{3,1},{4,6},{5,7},{6,4},{7,5},{8,10},{9,11},{10,... | collective-permute-start | bytes 393224 | tf_op jit(solution)/shard_map/ppermute | solution.py:320
  8.8 1.5 %collective-permute-start.2 = (bf16[2,64,512]{2,1,0:T(8,128)(2,1)S(1)}, bf16[2,64,512]{2,1,0:T(8,128)(2,1)S(1)}, u32[]{:S(2)}, u32[]{:S(2)}) collective-permute-start(bf16[2,64,512]{2,1,0:T(8,128)(2,1)S(1)} %get-tuple-element.28), channel_id=1, source_target_pairs={{0,6},{1,7},{2,4},{3,5},{4,2},{5,3},{6,0},{7,1},{8,14},{9,15},{10,... | collective-permute-start | bytes 393224 | tf_op jit(solution)/shard_map/ppermute | solution.py:320
  10.3 0.4 %collective-permute-start.5 = (bf16[2,64,512]{2,1,0:T(8,128)(2,1)S(1)}, bf16[2,64,512]{2,1,0:T(8,128)(2,1)S(1)}, u32[]{:S(2)}, u32[]{:S(2)}) collective-permute-start(bf16[2,64,512]{2,1,0:T(8,128)(2,1)S(1)} %get-tuple-element.40), channel_id=1, source_target_pairs={{0,4},{1,5},{2,6},{3,7},{4,0},{5,1},{6,2},{7,3},{8,12},{9,13},{10,... | collective-permute-start | bytes 393224 | tf_op jit(solution)/shard_map/ppermute | solution.py:320
  10.7 1.6 %copy-done = bf16[1,4,32,64,128]{4,3,2,1,0:T(8,128)(2,1)S(1)} copy-done((bf16[1,4,32,64,128]{4,3,2,1,0:T(8,128)(2,1)S(1)}, bf16[1,4,32,64,128]{4,3,2,1,0:T(8,128)(2,1)}, u32[]{:S(2)}) %copy-start) | copy-done | bytes 2097176
  12.3 0.7 %prepare_block.2 = (bf16[2048,512]{1,0:T(8,128)(2,1)S(1)}, bf16[512,2048]{1,0:T(8,128)(2,1)S(1)}) custom-call(bf16[1,4,32,64,128]{4,3,2,1,0:T(8,128)(2,1)S(1)} %copy-done), custom_call_target="tpu_custom_call" | custom-call | tf_op jit(solution)/shard_map/prepare_block/pallas_call | solution.py:35
  13.0 0.4 collective-permute-done.theta_ref
  13.4 0.0 collective-permute-done.1.chol_ref
  13.4 0.0 copy-done.3
  13.4 0.7 %pick_tiles.3 = (bf16[2,64,512]{2,1,0:T(8,128)(2,1)S(1)}, bf16[2,64,512]{2,1,0:T(8,128)(2,1)S(1)}, bf16[2,64,512]{2,1,0:T(8,128)(2,1)S(1)}, bf16[2,64,512]{2,1,0:T(8,128)(2,1)S(1)}) custom-call(s32[4,16]{1,0:T(4,128)S(1)} %bitcast.3, bf16[1,64,1280]{2,1,0:T(8,128)(2,1)S(1)} %collective-permute-done.theta_ref), custom_call_target="tpu_custom_call" | custom-call | tf_op jit(solution)/shard_map/pick_tiles/pallas_call | solution.py:63
  14.2 0.0 collective-permute-done.4.refs_7_
  14.2 1.7 %collective-permute-start.6 = (bf16[2,64,512]{2,1,0:T(8,128)(2,1)S(1)}, bf16[2,64,512]{2,1,0:T(8,128)(2,1)S(1)}, u32[]{:S(2)}, u32[]{:S(2)}) collective-permute-start(bf16[2,64,512]{2,1,0:T(8,128)(2,1)S(1)} %get-tuple-element.45), channel_id=1, source_target_pairs={{0,2},{1,3},{2,0},{3,1},{4,6},{5,7},{6,4},{7,5},{8,10},{9,11},{10,... | collective-permute-start | bytes 393224 | tf_op jit(solution)/shard_map/ppermute | solution.py:320
  15.8 2.4 %collective-permute-start.7 = (bf16[2,64,512]{2,1,0:T(8,128)(2,1)S(1)}, bf16[2,64,512]{2,1,0:T(8,128)(2,1)S(1)}, u32[]{:S(2)}, u32[]{:S(2)}) collective-permute-start(bf16[2,64,512]{2,1,0:T(8,128)(2,1)S(1)} %get-tuple-element.46), channel_id=1, source_target_pairs={{0,6},{1,7},{2,4},{3,5},{4,2},{5,3},{6,0},{7,1},{8,14},{9,15},{10,... | collective-permute-start | bytes 393224 | tf_op jit(solution)/shard_map/ppermute | solution.py:320
  18.2 0.5 %collective-permute-start.8 = (bf16[2,64,512]{2,1,0:T(8,128)(2,1)S(1)}, bf16[2,64,512]{2,1,0:T(8,128)(2,1)S(1)}, u32[]{:S(2)}, u32[]{:S(2)}) collective-permute-start(bf16[2,64,512]{2,1,0:T(8,128)(2,1)S(1)} %get-tuple-element.47), channel_id=1, source_target_pairs={{0,4},{1,5},{2,6},{3,7},{4,0},{5,1},{6,2},{7,3},{8,12},{9,13},{10,... | collective-permute-start | bytes 393224 | tf_op jit(solution)/shard_map/ppermute | solution.py:320
  18.7 0.0 collective-permute-done.2.refs_9_
  18.7 0.0 copy-done.4
  18.7 0.0 collective-permute-start.3
  18.7 0.7 %prepare_block.3 = (bf16[2048,512]{1,0:T(8,128)(2,1)S(1)}, bf16[512,2048]{1,0:T(8,128)(2,1)S(1)}) custom-call(bf16[1,4,32,64,128]{4,3,2,1,0:T(8,128)(2,1)S(1)} %collective-permute-done.1.chol_ref), custom_call_target="tpu_custom_call" | custom-call | tf_op jit(solution)/shard_map/prepare_block/pallas_call | solution.py:35
  19.5 0.0 collective-permute-done.5.refs_8_
  19.5 0.4 collective-permute-done.3.refs_1_
  19.9 2.8 %chip_terms.2 = (f32[8,1,128]{2,1,0:T(1,128)S(1)}, f32[2,512]{1,0:T(2,128)S(1)}) custom-call(s32[1,4]{1,0:T(1,128)S(1)} %copy-done.4, s32[1,4]{1,0:T(1,128)S(1)} %collective-permute-done.3.refs_1_, bf16[2048,512]{1,0:T(8,128)(2,1)S(1)} %get-tuple-element.30.refs_2_, bf16[512,2048]{1,0:T(8,128)(2,1)S(1)} %get-tuple-element.31.refs_3_, ...), custom_call_target="tpu_custom_call" | custom-call | tf_op jit(solution)/shard_map/chip_terms/pallas_call | solution.py:247
  22.6 0.0 collective-permute-done.6.refs_7_
  22.6 0.5 %collective-permute-done.7.refs_8_ = bf16[2,64,512]{2,1,0:T(8,128)(2,1)S(1)} collective-permute-done((bf16[2,64,512]{2,1,0:T(8,128)(2,1)S(1)}, bf16[2,64,512]{2,1,0:T(8,128)(2,1)S(1)}, u32[]{:S(2)}, u32[]{:S(2)}) %collective-permute-start.7) | collective-permute-done | bytes 131104 | tf_op jit(solution)/shard_map/ppermute | solution.py:320
  23.2 1.5 %collective-permute-done.8.refs_9_ = bf16[2,64,512]{2,1,0:T(8,128)(2,1)S(1)} collective-permute-done((bf16[2,64,512]{2,1,0:T(8,128)(2,1)S(1)}, bf16[2,64,512]{2,1,0:T(8,128)(2,1)S(1)}, u32[]{:S(2)}, u32[]{:S(2)}) %collective-permute-start.8) | collective-permute-done | bytes 131104 | tf_op jit(solution)/shard_map/ppermute | solution.py:320
  24.6 2.4 %chip_terms.3 = f32[8,1,128]{2,1,0:T(1,128)S(1)} custom-call(f32[2,512]{1,0:T(2,128)S(1)} %get-tuple-element.42.refs_0_, f32[8,1,128]{2,1,0:T(1,128)S(1)} %get-tuple-element.43.refs_1_, bf16[2048,512]{1,0:T(8,128)(2,1)S(1)} %get-tuple-element.30.refs_2_, bf16[512,2048]{1,0:T(8,128)(2,1)S(1)} %get-tuple-element.31.refs_3_, ...), custom_call_target="tpu_custom_call" | custom-call | tf_op jit(solution)/shard_map/chip_terms/pallas_call | solution.py:247
  27.0 11.1 %all_to_all.5.rows_ref = f32[8,1,128]{2,1,0:T(1,128)} all-to-all(f32[8,1,128]{2,1,0:T(1,128)S(1)} %chip_terms.3), channel_id=1, replica_groups={{0,2,4,6,8,10,12,14},{1,3,5,7,9,11,13,15},{16,18,20,22,24,26,28,30},{17..., dimensions={0} | all-to-all | bytes 8192 | tf_op jit(solution)/shard_map/all_to_all | solution.py:347
  38.1 1.4 %finish.1 = (f32[1,512]{1,0:T(1,128)}, f32[1,1]{1,0:T(1,128)}) custom-call(f32[8,1,128]{2,1,0:T(1,128)} %all_to_all.5.rows_ref), custom_call_target="tpu_custom_call" | custom-call | tf_op jit(solution)/shard_map/finish/pallas_call | solution.py:297
  (4 shorter events, 0.0 us)
Async XLA Ops:
  0.6 18.1 %copy-start.4 = (s32[1,4]{1,0:T(1,128)S(1)}, s32[1,4]{1,0:T(1,128)}, u32[]{:S(2)}) copy-start(s32[1,4]{1,0:T(1,128)} %refs_0_.1) | copy-start | bytes 52
  0.6 12.8 %collective-permute-start.1 = (bf16[1,4,32,64,128]{4,3,2,1,0:T(8,128)(2,1)}, bf16[1,4,32,64,128]{4,3,2,1,0:T(8,128)(2,1)S(1)}, u32[]{:S(2)}, u32[]{:S(2)}) collective-permute-start(bf16[1,4,32,64,128]{4,3,2,1,0:T(8,128)(2,1)} %chol_ref.1), channel_id=1, source_target_pairs={{0,1},{1,0},{2,3},{3,2},{4,5},{5,4},{6,7},{7,6},{8,9},{9,8},{10,11... | collective-permute-start | bytes 6291464 | tf_op jit(solution)/shard_map/ppermute | solution.py:323
  1.2 12.3 %collective-permute-start = (bf16[1,64,1280]{2,1,0:T(8,128)(2,1)}, bf16[1,64,1280]{2,1,0:T(8,128)(2,1)S(1)}, u32[]{:S(2)}, u32[]{:S(2)}) collective-permute-start(bf16[1,64,1280]{2,1,0:T(8,128)(2,1)} %theta_ref.1), channel_id=1, source_target_pairs={{0,8},{1,9},{2,10},{3,11},{4,12},{5,13},{6,14},{7,15},{8,0},{9,1},... | collective-permute-start | bytes 491528 | tf_op jit(solution)/shard_map/ppermute | solution.py:320
  4.8 0.9 %copy-start.1 = (bf16[1,64,1280]{2,1,0:T(8,128)(2,1)S(1)}, bf16[1,64,1280]{2,1,0:T(8,128)(2,1)}, u32[]{:S(2)}) copy-start(bf16[1,64,1280]{2,1,0:T(8,128)(2,1)} %theta_ref.1) | copy-start | bytes 491524
  5.8 0.7 %copy-start.2 = (s32[16,4]{0,1:T(4,128)S(1)}, s32[16,4]{0,1:T(4,128)}, u32[]{:S(2)}) copy-start(s32[16,4]{0,1:T(4,128)} %param.7) | copy-start | bytes 772
  6.5 7.0 %copy-start.3 = (s32[16,4]{0,1:T(4,128)S(1)}, s32[16,4]{0,1:T(4,128)}, u32[]{:S(2)}) copy-start(s32[16,4]{0,1:T(4,128)} %param.7) | copy-start | bytes 772
  7.2 7.0 %collective-permute-start.4 = (bf16[2,64,512]{2,1,0:T(8,128)(2,1)S(1)}, bf16[2,64,512]{2,1,0:T(8,128)(2,1)S(1)}, u32[]{:S(2)}, u32[]{:S(2)}) collective-permute-start(bf16[2,64,512]{2,1,0:T(8,128)(2,1)S(1)} %get-tuple-element.38), channel_id=1, source_target_pairs={{0,2},{1,3},{2,0},{3,1},{4,6},{5,7},{6,4},{7,5},{8,10},{9,11},{10,... | collective-permute-start | bytes 393224 | tf_op jit(solution)/shard_map/ppermute | solution.py:320
  8.8 10.0 %collective-permute-start.2 = (bf16[2,64,512]{2,1,0:T(8,128)(2,1)S(1)}, bf16[2,64,512]{2,1,0:T(8,128)(2,1)S(1)}, u32[]{:S(2)}, u32[]{:S(2)}) collective-permute-start(bf16[2,64,512]{2,1,0:T(8,128)(2,1)S(1)} %get-tuple-element.28), channel_id=1, source_target_pairs={{0,6},{1,7},{2,4},{3,5},{4,2},{5,3},{6,0},{7,1},{8,14},{9,15},{10,... | collective-permute-start | bytes 393224 | tf_op jit(solution)/shard_map/ppermute | solution.py:320
  10.3 9.2 %collective-permute-start.5 = (bf16[2,64,512]{2,1,0:T(8,128)(2,1)S(1)}, bf16[2,64,512]{2,1,0:T(8,128)(2,1)S(1)}, u32[]{:S(2)}, u32[]{:S(2)}) collective-permute-start(bf16[2,64,512]{2,1,0:T(8,128)(2,1)S(1)} %get-tuple-element.40), channel_id=1, source_target_pairs={{0,4},{1,5},{2,6},{3,7},{4,0},{5,1},{6,2},{7,3},{8,12},{9,13},{10,... | collective-permute-start | bytes 393224 | tf_op jit(solution)/shard_map/ppermute | solution.py:320
  10.7 1.6 %copy-start = (bf16[1,4,32,64,128]{4,3,2,1,0:T(8,128)(2,1)S(1)}, bf16[1,4,32,64,128]{4,3,2,1,0:T(8,128)(2,1)}, u32[]{:S(2)}) copy-start(bf16[1,4,32,64,128]{4,3,2,1,0:T(8,128)(2,1)} %chol_ref.1) | copy-start | bytes 6291460
  14.2 8.5 %collective-permute-start.6 = (bf16[2,64,512]{2,1,0:T(8,128)(2,1)S(1)}, bf16[2,64,512]{2,1,0:T(8,128)(2,1)S(1)}, u32[]{:S(2)}, u32[]{:S(2)}) collective-permute-start(bf16[2,64,512]{2,1,0:T(8,128)(2,1)S(1)} %get-tuple-element.45), channel_id=1, source_target_pairs={{0,2},{1,3},{2,0},{3,1},{4,6},{5,7},{6,4},{7,5},{8,10},{9,11},{10,... | collective-permute-start | bytes 393224 | tf_op jit(solution)/shard_map/ppermute | solution.py:320
  15.8 7.3 %collective-permute-start.7 = (bf16[2,64,512]{2,1,0:T(8,128)(2,1)S(1)}, bf16[2,64,512]{2,1,0:T(8,128)(2,1)S(1)}, u32[]{:S(2)}, u32[]{:S(2)}) collective-permute-start(bf16[2,64,512]{2,1,0:T(8,128)(2,1)S(1)} %get-tuple-element.46), channel_id=1, source_target_pairs={{0,6},{1,7},{2,4},{3,5},{4,2},{5,3},{6,0},{7,1},{8,14},{9,15},{10,... | collective-permute-start | bytes 393224 | tf_op jit(solution)/shard_map/ppermute | solution.py:320
  18.2 6.4 %collective-permute-start.8 = (bf16[2,64,512]{2,1,0:T(8,128)(2,1)S(1)}, bf16[2,64,512]{2,1,0:T(8,128)(2,1)S(1)}, u32[]{:S(2)}, u32[]{:S(2)}) collective-permute-start(bf16[2,64,512]{2,1,0:T(8,128)(2,1)S(1)} %get-tuple-element.47), channel_id=1, source_target_pairs={{0,4},{1,5},{2,6},{3,7},{4,0},{5,1},{6,2},{7,3},{8,12},{9,13},{10,... | collective-permute-start | bytes 393224 | tf_op jit(solution)/shard_map/ppermute | solution.py:320
  18.7 1.1 %collective-permute-start.3 = (s32[1,4]{1,0:T(1,128)S(1)}, s32[1,4]{1,0:T(1,128)S(1)}, u32[]{:S(2)}, u32[]{:S(2)}) collective-permute-start(s32[1,4]{1,0:T(1,128)S(1)} %copy-done.4), channel_id=1, source_target_pairs={{0,1},{1,0},{2,3},{3,2},{4,5},{5,4},{6,7},{7,6},{8,9},{9,8},{10,11... | collective-permute-start | bytes 56 | tf_op jit(solution)/shard_map/ppermute | solution.py:323

commit v20 on v17

--- a/solution.py
+++ b/solution.py
@@ -279,7 +279,7 @@
         total = total + energy_terms(rows_ref[d], used)
     energy_buf[...] = jnp.sum(total, axis=1, keepdims=True) * scale
     energy_copy = pltpu.make_async_copy(energy_buf, energy_ref, sems.at[1])
-    energy_copy.start()
+    energy_copy.start(priority=1)
     bias_copy.wait()
     energy_copy.wait()
 

time: 39.6 us -> 39.6 us (level)
  no operation moved by 1% of the time
where the time goes in v20:
time: 39.6 us; the launch traced here: 39.4 us
  starting transfers between devices  13.2 us (33%)
  blocking collectives  10.1 us (26%)
  Pallas kernels  9.35 us (24%)
  local copies, waits for them, and re-layouts  3.23 us (8%)
  waiting for transfers between devices  2.85 us (7%)
  between operations  0.72 us (2%)
    ppermute x7, starting transfers between devices, to_chip(): lax.ppermute(x, 'chol', [(i, i ^ offset * CORES) for i in range(groups)])  12.6 us
    all_to_all x1, blocking collectives, body(): lax.all_to_all(rows, 'chol', split_axis=0, concat_axis=0, tiled=True, axi...  10.1 us
    pallas_call x2, Pallas kernels, chip_terms(): pl.pallas_call(functools.partial(terms_kernel, first=first, count=count,...  5.12 us
    unnamed x10, local copies, waits for them, and re-layouts  3.23 us
    ppermute x7, waiting for transfers between devices, to_chip(): lax.ppermute(x, 'chol', [(i, i ^ offset * CORES) for i in range(groups)])  1.75 us
    pallas_call x2, Pallas kernels, pick_tiles(): pl.pallas_call(pick_kernel, in_specs=[SMEM, VMEM], out_specs=[VMEM] * cou...  1.43 us
    pallas_call x2, Pallas kernels, prepare_block(): pl.pallas_call(prepare_kernel, in_specs=[VMEM], out_specs=[VMEM, VMEM], o...  1.43 us
    pallas_call x1, Pallas kernels, finish(): pl.pallas_call(functools.partial(finish_kernel, used=used, scale=scale),...  1.37 us
  transfers between devices with their start and end apart: 9, of which 3 were waited for; matrix products, arithmetic and copies ran while one was open for 0% of the time, Pallas kernels for 14%

profile of v20, /device:TPU:0, one launch (start us, length us, event | category | flops | bytes accessed | tf_op | source)
XLA Modules:
  0.0 39.4 jit_solution(7566503849305075603)
XLA Ops:
  0.6 0.5 %collective-permute-start.2 = (bf16[1,4,32,64,128]{4,3,2,1,0:T(8,128)(2,1)}, bf16[1,4,32,64,128]{4,3,2,1,0:T(8,128)(2,1)S(1)}, u32[]{:S(2)}, u32[]{:S(2)}) collective-permute-start(bf16[1,4,32,64,128]{4,3,2,1,0:T(8,128)(2,1)} %chol_ref.1), channel_id=1, source_target_pairs={{0,1},{1,0},{2,3},{3,2},{4,5},{5,4},{6,7},{7,6},{8,9},{9,8},{10,11... | collective-permute-start | bytes 6291464 | tf_op jit(solution)/shard_map/ppermute | solution.py:316
  1.1 3.7 %collective-permute-start = (bf16[1,64,1280]{2,1,0:T(8,128)(2,1)}, bf16[1,64,1280]{2,1,0:T(8,128)(2,1)S(1)}, u32[]{:S(2)}, u32[]{:S(2)}) collective-permute-start(bf16[1,64,1280]{2,1,0:T(8,128)(2,1)} %theta_ref.1), channel_id=1, source_target_pairs={{0,8},{1,9},{2,10},{3,11},{4,12},{5,13},{6,14},{7,15},{8,0},{9,1},... | collective-permute-start | bytes 491528 | tf_op jit(solution)/shard_map/ppermute | solution.py:313
  4.8 0.0 copy-start.1
  4.8 0.9 %copy-done.1 = bf16[1,64,1280]{2,1,0:T(8,128)(2,1)S(1)} copy-done((bf16[1,64,1280]{2,1,0:T(8,128)(2,1)S(1)}, bf16[1,64,1280]{2,1,0:T(8,128)(2,1)}, u32[]{:S(2)}) %copy-start.1) | copy-done | bytes 163864
  5.8 0.7 %copy-done.2 = s32[16,4]{0,1:T(4,128)S(1)} copy-done((s32[16,4]{0,1:T(4,128)S(1)}, s32[16,4]{0,1:T(4,128)}, u32[]{:S(2)}) %copy-start.2) | copy-done | bytes 280
  6.4 0.7 %pick_tiles.2 = (bf16[2,64,512]{2,1,0:T(8,128)(2,1)S(1)}, bf16[2,64,512]{2,1,0:T(8,128)(2,1)S(1)}, bf16[2,64,512]{2,1,0:T(8,128)(2,1)S(1)}, bf16[2,64,512]{2,1,0:T(8,128)(2,1)S(1)}) custom-call(s32[4,16]{1,0:T(4,128)S(1)} %bitcast.2, bf16[1,64,1280]{2,1,0:T(8,128)(2,1)S(1)} %copy-done.1), custom_call_target="tpu_custom_call" | custom-call | tf_op jit(solution)/shard_map/pick_tiles/pallas_call | solution.py:63
  7.2 1.6 %collective-permute-start.1 = (bf16[2,64,512]{2,1,0:T(8,128)(2,1)S(1)}, bf16[2,64,512]{2,1,0:T(8,128)(2,1)S(1)}, u32[]{:S(2)}, u32[]{:S(2)}) collective-permute-start(bf16[2,64,512]{2,1,0:T(8,128)(2,1)S(1)} %get-tuple-element.25), channel_id=1, source_target_pairs={{0,2},{1,3},{2,0},{3,1},{4,6},{5,7},{6,4},{7,5},{8,10},{9,11},{10,... | collective-permute-start | bytes 393224 | tf_op jit(solution)/shard_map/ppermute | solution.py:313
  8.8 1.5 %collective-permute-start.3 = (bf16[2,64,512]{2,1,0:T(8,128)(2,1)S(1)}, bf16[2,64,512]{2,1,0:T(8,128)(2,1)S(1)}, u32[]{:S(2)}, u32[]{:S(2)}) collective-permute-start(bf16[2,64,512]{2,1,0:T(8,128)(2,1)S(1)} %get-tuple-element.28), channel_id=1, source_target_pairs={{0,6},{1,7},{2,4},{3,5},{4,2},{5,3},{6,0},{7,1},{8,14},{9,15},{10,... | collective-permute-start | bytes 393224 | tf_op jit(solution)/shard_map/ppermute | solution.py:313
  10.3 0.4 %collective-permute-start.5 = (bf16[2,64,512]{2,1,0:T(8,128)(2,1)S(1)}, bf16[2,64,512]{2,1,0:T(8,128)(2,1)S(1)}, u32[]{:S(2)}, u32[]{:S(2)}) collective-permute-start(bf16[2,64,512]{2,1,0:T(8,128)(2,1)S(1)} %get-tuple-element.37), channel_id=1, source_target_pairs={{0,4},{1,5},{2,6},{3,7},{4,0},{5,1},{6,2},{7,3},{8,12},{9,13},{10,... | collective-permute-start | bytes 393224 | tf_op jit(solution)/shard_map/ppermute | solution.py:313
  10.7 1.6 %copy-done = bf16[1,4,32,64,128]{4,3,2,1,0:T(8,128)(2,1)S(1)} copy-done((bf16[1,4,32,64,128]{4,3,2,1,0:T(8,128)(2,1)S(1)}, bf16[1,4,32,64,128]{4,3,2,1,0:T(8,128)(2,1)}, u32[]{:S(2)}) %copy-start) | copy-done | bytes 2097176
  12.3 0.7 %prepare_block.2 = (bf16[2048,512]{1,0:T(8,128)(2,1)S(1)}, bf16[512,2048]{1,0:T(8,128)(2,1)S(1)}) custom-call(bf16[1,4,32,64,128]{4,3,2,1,0:T(8,128)(2,1)S(1)} %copy-done), custom_call_target="tpu_custom_call" | custom-call | tf_op jit(solution)/shard_map/prepare_block/pallas_call | solution.py:35
  13.0 0.0 collective-permute-done.1.refs_7_
  13.0 0.4 collective-permute-done.theta_ref
  13.4 0.0 collective-permute-done.2.chol_ref
  13.4 0.0 copy-done.3
  13.4 0.7 %pick_tiles.3 = (bf16[2,64,512]{2,1,0:T(8,128)(2,1)S(1)}, bf16[2,64,512]{2,1,0:T(8,128)(2,1)S(1)}, bf16[2,64,512]{2,1,0:T(8,128)(2,1)S(1)}, bf16[2,64,512]{2,1,0:T(8,128)(2,1)S(1)}) custom-call(s32[4,16]{1,0:T(4,128)S(1)} %bitcast.3, bf16[1,64,1280]{2,1,0:T(8,128)(2,1)S(1)} %collective-permute-done.theta_ref), custom_call_target="tpu_custom_call" | custom-call | tf_op jit(solution)/shard_map/pick_tiles/pallas_call | solution.py:63
  14.2 1.7 %collective-permute-start.6 = (bf16[2,64,512]{2,1,0:T(8,128)(2,1)S(1)}, bf16[2,64,512]{2,1,0:T(8,128)(2,1)S(1)}, u32[]{:S(2)}, u32[]{:S(2)}) collective-permute-start(bf16[2,64,512]{2,1,0:T(8,128)(2,1)S(1)} %get-tuple-element.43), channel_id=1, source_target_pairs={{0,2},{1,3},{2,0},{3,1},{4,6},{5,7},{6,4},{7,5},{8,10},{9,11},{10,... | collective-permute-start | bytes 393224 | tf_op jit(solution)/shard_map/ppermute | solution.py:313
  15.8 3.7 %collective-permute-start.7 = (bf16[2,64,512]{2,1,0:T(8,128)(2,1)S(1)}, bf16[2,64,512]{2,1,0:T(8,128)(2,1)S(1)}, u32[]{:S(2)}, u32[]{:S(2)}) collective-permute-start(bf16[2,64,512]{2,1,0:T(8,128)(2,1)S(1)} %get-tuple-element.44), channel_id=1, source_target_pairs={{0,4},{1,5},{2,6},{3,7},{4,0},{5,1},{6,2},{7,3},{8,12},{9,13},{10,... | collective-permute-start | bytes 393224 | tf_op jit(solution)/shard_map/ppermute | solution.py:313
  19.5 0.0 collective-permute-start.8
  19.5 0.0 collective-permute-done.3.refs_9_
  19.5 0.7 %prepare_block.3 = (bf16[2048,512]{1,0:T(8,128)(2,1)S(1)}, bf16[512,2048]{1,0:T(8,128)(2,1)S(1)}) custom-call(bf16[1,4,32,64,128]{4,3,2,1,0:T(8,128)(2,1)S(1)} %collective-permute-done.2.chol_ref), custom_call_target="tpu_custom_call" | custom-call | tf_op jit(solution)/shard_map/prepare_block/pallas_call | solution.py:35
  20.2 0.0 copy-done.4
  20.2 0.1 collective-permute-start.4
  20.3 0.0 collective-permute-done.5.refs_8_
  20.3 1.1 %collective-permute-done.4.refs_1_ = s32[1,4]{1,0:T(1,128)S(1)} collective-permute-done((s32[1,4]{1,0:T(1,128)S(1)}, s32[1,4]{1,0:T(1,128)S(1)}, u32[]{:S(2)}, u32[]{:S(2)}) %collective-permute-start.4) | collective-permute-done | bytes 48 | tf_op jit(solution)/shard_map/ppermute | solution.py:316
  21.4 2.8 %chip_terms.2 = (f32[8,1,128]{2,1,0:T(1,128)S(1)}, f32[2,512]{1,0:T(2,128)S(1)}) custom-call(s32[1,4]{1,0:T(1,128)S(1)} %copy-done.4, s32[1,4]{1,0:T(1,128)S(1)} %collective-permute-done.4.refs_1_, bf16[2048,512]{1,0:T(8,128)(2,1)S(1)} %get-tuple-element.30.refs_2_, bf16[512,2048]{1,0:T(8,128)(2,1)S(1)} %get-tuple-element.31.refs_3_, ...), custom_call_target="tpu_custom_call" | custom-call | tf_op jit(solution)/shard_map/chip_terms/pallas_call | solution.py:240
  24.2 0.0 collective-permute-done.6.refs_7_
  24.2 0.0 collective-permute-done.7.refs_8_
  24.2 1.3 %collective-permute-done.8.refs_9_ = bf16[2,64,512]{2,1,0:T(8,128)(2,1)S(1)} collective-permute-done((bf16[2,64,512]{2,1,0:T(8,128)(2,1)S(1)}, bf16[2,64,512]{2,1,0:T(8,128)(2,1)S(1)}, u32[]{:S(2)}, u32[]{:S(2)}) %collective-permute-start.8) | collective-permute-done | bytes 131104 | tf_op jit(solution)/shard_map/ppermute | solution.py:313
  25.6 2.4 %chip_terms.3 = f32[8,1,128]{2,1,0:T(1,128)S(1)} custom-call(f32[2,512]{1,0:T(2,128)S(1)} %get-tuple-element.39.refs_0_, f32[8,1,128]{2,1,0:T(1,128)S(1)} %get-tuple-element.40.refs_1_, bf16[2048,512]{1,0:T(8,128)(2,1)S(1)} %get-tuple-element.30.refs_2_, bf16[512,2048]{1,0:T(8,128)(2,1)S(1)} %get-tuple-element.31.refs_3_, ...), custom_call_target="tpu_custom_call" | custom-call | tf_op jit(solution)/shard_map/chip_terms/pallas_call | solution.py:240
  27.9 10.1 %all_to_all.5.rows_ref = f32[8,1,128]{2,1,0:T(1,128)} all-to-all(f32[8,1,128]{2,1,0:T(1,128)S(1)} %chip_terms.3), channel_id=1, replica_groups={{0,2,4,6,8,10,12,14},{1,3,5,7,9,11,13,15},{16,18,20,22,24,26,28,30},{17..., dimensions={0} | all-to-all | bytes 8192 | tf_op jit(solution)/shard_map/all_to_all | solution.py:337
  38.0 1.4 %finish.1 = (f32[1,512]{1,0:T(1,128)}, f32[1,1]{1,0:T(1,128)}) custom-call(f32[8,1,128]{2,1,0:T(1,128)} %all_to_all.5.rows_ref), custom_call_target="tpu_custom_call" | custom-call | tf_op jit(solution)/shard_map/finish/pallas_call | solution.py:290
  (4 shorter events, 0.0 us)
Async XLA Ops:
  0.6 12.8 %collective-permute-start.2 = (bf16[1,4,32,64,128]{4,3,2,1,0:T(8,128)(2,1)}, bf16[1,4,32,64,128]{4,3,2,1,0:T(8,128)(2,1)S(1)}, u32[]{:S(2)}, u32[]{:S(2)}) collective-permute-start(bf16[1,4,32,64,128]{4,3,2,1,0:T(8,128)(2,1)} %chol_ref.1), channel_id=1, source_target_pairs={{0,1},{1,0},{2,3},{3,2},{4,5},{5,4},{6,7},{7,6},{8,9},{9,8},{10,11... | collective-permute-start | bytes 6291464 | tf_op jit(solution)/shard_map/ppermute | solution.py:316
  1.1 12.3 %collective-permute-start = (bf16[1,64,1280]{2,1,0:T(8,128)(2,1)}, bf16[1,64,1280]{2,1,0:T(8,128)(2,1)S(1)}, u32[]{:S(2)}, u32[]{:S(2)}) collective-permute-start(bf16[1,64,1280]{2,1,0:T(8,128)(2,1)} %theta_ref.1), channel_id=1, source_target_pairs={{0,8},{1,9},{2,10},{3,11},{4,12},{5,13},{6,14},{7,15},{8,0},{9,1},... | collective-permute-start | bytes 491528 | tf_op jit(solution)/shard_map/ppermute | solution.py:313
  4.8 0.9 %copy-start.1 = (bf16[1,64,1280]{2,1,0:T(8,128)(2,1)S(1)}, bf16[1,64,1280]{2,1,0:T(8,128)(2,1)}, u32[]{:S(2)}) copy-start(bf16[1,64,1280]{2,1,0:T(8,128)(2,1)} %theta_ref.1) | copy-start | bytes 491524
  5.8 0.7 %copy-start.2 = (s32[16,4]{0,1:T(4,128)S(1)}, s32[16,4]{0,1:T(4,128)}, u32[]{:S(2)}) copy-start(s32[16,4]{0,1:T(4,128)} %param.7) | copy-start | bytes 772
  6.4 7.0 %copy-start.3 = (s32[16,4]{0,1:T(4,128)S(1)}, s32[16,4]{0,1:T(4,128)}, u32[]{:S(2)}) copy-start(s32[16,4]{0,1:T(4,128)} %param.7) | copy-start | bytes 772
  7.2 5.9 %collective-permute-start.1 = (bf16[2,64,512]{2,1,0:T(8,128)(2,1)S(1)}, bf16[2,64,512]{2,1,0:T(8,128)(2,1)S(1)}, u32[]{:S(2)}, u32[]{:S(2)}) collective-permute-start(bf16[2,64,512]{2,1,0:T(8,128)(2,1)S(1)} %get-tuple-element.25), channel_id=1, source_target_pairs={{0,2},{1,3},{2,0},{3,1},{4,6},{5,7},{6,4},{7,5},{8,10},{9,11},{10,... | collective-permute-start | bytes 393224 | tf_op jit(solution)/shard_map/ppermute | solution.py:313
  8.8 10.8 %collective-permute-start.3 = (bf16[2,64,512]{2,1,0:T(8,128)(2,1)S(1)}, bf16[2,64,512]{2,1,0:T(8,128)(2,1)S(1)}, u32[]{:S(2)}, u32[]{:S(2)}) collective-permute-start(bf16[2,64,512]{2,1,0:T(8,128)(2,1)S(1)} %get-tuple-element.28), channel_id=1, source_target_pairs={{0,6},{1,7},{2,4},{3,5},{4,2},{5,3},{6,0},{7,1},{8,14},{9,15},{10,... | collective-permute-start | bytes 393224 | tf_op jit(solution)/shard_map/ppermute | solution.py:313
  10.3 10.1 %collective-permute-start.5 = (bf16[2,64,512]{2,1,0:T(8,128)(2,1)S(1)}, bf16[2,64,512]{2,1,0:T(8,128)(2,1)S(1)}, u32[]{:S(2)}, u32[]{:S(2)}) collective-permute-start(bf16[2,64,512]{2,1,0:T(8,128)(2,1)S(1)} %get-tuple-element.37), channel_id=1, source_target_pairs={{0,4},{1,5},{2,6},{3,7},{4,0},{5,1},{6,2},{7,3},{8,12},{9,13},{10,... | collective-permute-start | bytes 393224 | tf_op jit(solution)/shard_map/ppermute | solution.py:313
  10.7 1.6 %copy-start = (bf16[1,4,32,64,128]{4,3,2,1,0:T(8,128)(2,1)S(1)}, bf16[1,4,32,64,128]{4,3,2,1,0:T(8,128)(2,1)}, u32[]{:S(2)}) copy-start(bf16[1,4,32,64,128]{4,3,2,1,0:T(8,128)(2,1)} %chol_ref.1) | copy-start | bytes 6291460
  12.3 7.9 %copy-start.4 = (s32[1,4]{1,0:T(1,128)S(1)}, s32[1,4]{1,0:T(1,128)}, u32[]{:S(2)}) copy-start(s32[1,4]{1,0:T(1,128)} %refs_0_.1) | copy-start | bytes 52
  14.2 10.1 %collective-permute-start.6 = (bf16[2,64,512]{2,1,0:T(8,128)(2,1)S(1)}, bf16[2,64,512]{2,1,0:T(8,128)(2,1)S(1)}, u32[]{:S(2)}, u32[]{:S(2)}) collective-permute-start(bf16[2,64,512]{2,1,0:T(8,128)(2,1)S(1)} %get-tuple-element.43), channel_id=1, source_target_pairs={{0,2},{1,3},{2,0},{3,1},{4,6},{5,7},{6,4},{7,5},{8,10},{9,11},{10,... | collective-permute-start | bytes 393224 | tf_op jit(solution)/shard_map/ppermute | solution.py:313
  15.8 8.4 %collective-permute-start.7 = (bf16[2,64,512]{2,1,0:T(8,128)(2,1)S(1)}, bf16[2,64,512]{2,1,0:T(8,128)(2,1)S(1)}, u32[]{:S(2)}, u32[]{:S(2)}) collective-permute-start(bf16[2,64,512]{2,1,0:T(8,128)(2,1)S(1)} %get-tuple-element.44), channel_id=1, source_target_pairs={{0,4},{1,5},{2,6},{3,7},{4,0},{5,1},{6,2},{7,3},{8,12},{9,13},{10,... | collective-permute-start | bytes 393224 | tf_op jit(solution)/shard_map/ppermute | solution.py:313
  19.5 6.1 %collective-permute-start.8 = (bf16[2,64,512]{2,1,0:T(8,128)(2,1)S(1)}, bf16[2,64,512]{2,1,0:T(8,128)(2,1)S(1)}, u32[]{:S(2)}, u32[]{:S(2)}) collective-permute-start(bf16[2,64,512]{2,1,0:T(8,128)(2,1)S(1)} %get-tuple-element.45), channel_id=1, source_target_pairs={{0,6},{1,7},{2,4},{3,5},{4,2},{5,3},{6,0},{7,1},{8,14},{9,15},{10,... | collective-permute-start | bytes 393224 | tf_op jit(solution)/shard_map/ppermute | solution.py:313
  20.2 1.2 %collective-permute-start.4 = (s32[1,4]{1,0:T(1,128)S(1)}, s32[1,4]{1,0:T(1,128)S(1)}, u32[]{:S(2)}, u32[]{:S(2)}) collective-permute-start(s32[1,4]{1,0:T(1,128)S(1)} %copy-done.4), channel_id=1, source_target_pairs={{0,1},{1,0},{2,3},{3,2},{4,5},{5,4},{6,7},{7,6},{8,9},{9,8},{10,11... | collective-permute-start | bytes 56 | tf_op jit(solution)/shard_map/ppermute | solution.py:316

commit v21 on v17

--- a/solution.py
+++ b/solution.py
@@ -91,9 +91,9 @@
     return pairs[0]
 
 
-def chunk_products(block_ref, turned_ref, theta, occupied, k0, size, by_matmul):
+def chunk_products(block_ref, turned_ref, theta, theta_turned, occupied, k0, size, by_matmul):
     span = slice(k0 * occupied, (k0 + size) * occupied)
-    inner_mat = lax.dot_general(block_ref[span, :], theta, NT, preferred_element_type=jnp.float32)
+    inner_mat = lax.dot_general(block_ref[span, :], theta_turned, NN, preferred_element_type=jnp.float32)
     if not by_matmul:
         return inner_mat, None
     turned = slice(k0 * occupied, (k0 + by_matmul) * occupied)
@@ -184,14 +184,15 @@
         tasks = []
         for b in range(CORES):
             theta, k0 = picked_ref[b, rows, :], 0
+            walkers = (theta, theta.T)
             while k0 < vectors:
                 for size, by_matmul in chunks:
-                    tasks.append((b, theta, k0, size, by_matmul))
+                    tasks.append((b, walkers, k0, size, by_matmul))
                     k0 += size
 
         def products(task):
-            b, theta, k0, size, by_matmul = task
-            return chunk_products(block_refs[2 * b], block_refs[2 * b + 1], theta, occupied, k0, size, by_matmul)
+            b, walkers, k0, size, by_matmul = task
+            return chunk_products(block_refs[2 * b], block_refs[2 * b + 1], *walkers, occupied, k0, size, by_matmul)
 
         ahead = products(tasks[0])
         for i, (b, _, k0, size, by_matmul) in enumerate(tasks):

time: 39.6 us -> 39.6 us (level)
  no operation moved by 1% of the time
where the time goes in v21:
time: 39.6 us; the launch traced here: 39.4 us
  starting transfers between devices  13.2 us (33%)
  blocking collectives  10.1 us (26%)
  Pallas kernels  9.35 us (24%)
  local copies, waits for them, and re-layouts  3.23 us (8%)
  waiting for transfers between devices  2.85 us (7%)
  between operations  0.72 us (2%)
    ppermute x7, starting transfers between devices, to_chip(): lax.ppermute(x, 'chol', [(i, i ^ offset * CORES) for i in range(groups)])  12.6 us
    all_to_all x1, blocking collectives, body(): lax.all_to_all(rows, 'chol', split_axis=0, concat_axis=0, tiled=True, axi...  10.1 us
    pallas_call x2, Pallas kernels, chip_terms(): pl.pallas_call(functools.partial(terms_kernel, first=first, count=count,...  5.12 us
    unnamed x10, local copies, waits for them, and re-layouts  3.23 us
    ppermute x7, waiting for transfers between devices, to_chip(): lax.ppermute(x, 'chol', [(i, i ^ offset * CORES) for i in range(groups)])  1.75 us
    pallas_call x2, Pallas kernels, pick_tiles(): pl.pallas_call(pick_kernel, in_specs=[SMEM, VMEM], out_specs=[VMEM] * cou...  1.43 us
    pallas_call x2, Pallas kernels, prepare_block(): pl.pallas_call(prepare_kernel, in_specs=[VMEM], out_specs=[VMEM, VMEM], o...  1.43 us
    pallas_call x1, Pallas kernels, finish(): pl.pallas_call(functools.partial(finish_kernel, used=used, scale=scale),...  1.37 us
  transfers between devices with their start and end apart: 9, of which 3 were waited for; matrix products, arithmetic and copies ran while one was open for 0% of the time, Pallas kernels for 14%

profile of v21, /device:TPU:0, one launch (start us, length us, event | category | flops | bytes accessed | tf_op | source)
XLA Modules:
  0.0 39.4 jit_solution(7865600256269508566)
XLA Ops:
  0.6 0.5 %collective-permute-start.2 = (bf16[1,4,32,64,128]{4,3,2,1,0:T(8,128)(2,1)}, bf16[1,4,32,64,128]{4,3,2,1,0:T(8,128)(2,1)S(1)}, u32[]{:S(2)}, u32[]{:S(2)}) collective-permute-start(bf16[1,4,32,64,128]{4,3,2,1,0:T(8,128)(2,1)} %chol_ref.1), channel_id=1, source_target_pairs={{0,1},{1,0},{2,3},{3,2},{4,5},{5,4},{6,7},{7,6},{8,9},{9,8},{10,11... | collective-permute-start | bytes 6291464 | tf_op jit(solution)/shard_map/ppermute | solution.py:317
  1.1 3.7 %collective-permute-start = (bf16[1,64,1280]{2,1,0:T(8,128)(2,1)}, bf16[1,64,1280]{2,1,0:T(8,128)(2,1)S(1)}, u32[]{:S(2)}, u32[]{:S(2)}) collective-permute-start(bf16[1,64,1280]{2,1,0:T(8,128)(2,1)} %theta_ref.1), channel_id=1, source_target_pairs={{0,8},{1,9},{2,10},{3,11},{4,12},{5,13},{6,14},{7,15},{8,0},{9,1},... | collective-permute-start | bytes 491528 | tf_op jit(solution)/shard_map/ppermute | solution.py:314
  4.8 0.0 copy-start.1
  4.8 0.9 %copy-done.1 = bf16[1,64,1280]{2,1,0:T(8,128)(2,1)S(1)} copy-done((bf16[1,64,1280]{2,1,0:T(8,128)(2,1)S(1)}, bf16[1,64,1280]{2,1,0:T(8,128)(2,1)}, u32[]{:S(2)}) %copy-start.1) | copy-done | bytes 163864
  5.8 0.7 %copy-done.2 = s32[16,4]{0,1:T(4,128)S(1)} copy-done((s32[16,4]{0,1:T(4,128)S(1)}, s32[16,4]{0,1:T(4,128)}, u32[]{:S(2)}) %copy-start.2) | copy-done | bytes 280
  6.4 0.7 %pick_tiles.2 = (bf16[2,64,512]{2,1,0:T(8,128)(2,1)S(1)}, bf16[2,64,512]{2,1,0:T(8,128)(2,1)S(1)}, bf16[2,64,512]{2,1,0:T(8,128)(2,1)S(1)}, bf16[2,64,512]{2,1,0:T(8,128)(2,1)S(1)}) custom-call(s32[4,16]{1,0:T(4,128)S(1)} %bitcast.2, bf16[1,64,1280]{2,1,0:T(8,128)(2,1)S(1)} %copy-done.1), custom_call_target="tpu_custom_call" | custom-call | tf_op jit(solution)/shard_map/pick_tiles/pallas_call | solution.py:63
  7.2 1.6 %collective-permute-start.1 = (bf16[2,64,512]{2,1,0:T(8,128)(2,1)S(1)}, bf16[2,64,512]{2,1,0:T(8,128)(2,1)S(1)}, u32[]{:S(2)}, u32[]{:S(2)}) collective-permute-start(bf16[2,64,512]{2,1,0:T(8,128)(2,1)S(1)} %get-tuple-element.25), channel_id=1, source_target_pairs={{0,2},{1,3},{2,0},{3,1},{4,6},{5,7},{6,4},{7,5},{8,10},{9,11},{10,... | collective-permute-start | bytes 393224 | tf_op jit(solution)/shard_map/ppermute | solution.py:314
  8.8 1.5 %collective-permute-start.3 = (bf16[2,64,512]{2,1,0:T(8,128)(2,1)S(1)}, bf16[2,64,512]{2,1,0:T(8,128)(2,1)S(1)}, u32[]{:S(2)}, u32[]{:S(2)}) collective-permute-start(bf16[2,64,512]{2,1,0:T(8,128)(2,1)S(1)} %get-tuple-element.28), channel_id=1, source_target_pairs={{0,6},{1,7},{2,4},{3,5},{4,2},{5,3},{6,0},{7,1},{8,14},{9,15},{10,... | collective-permute-start | bytes 393224 | tf_op jit(solution)/shard_map/ppermute | solution.py:314
  10.3 0.4 %collective-permute-start.5 = (bf16[2,64,512]{2,1,0:T(8,128)(2,1)S(1)}, bf16[2,64,512]{2,1,0:T(8,128)(2,1)S(1)}, u32[]{:S(2)}, u32[]{:S(2)}) collective-permute-start(bf16[2,64,512]{2,1,0:T(8,128)(2,1)S(1)} %get-tuple-element.37), channel_id=1, source_target_pairs={{0,4},{1,5},{2,6},{3,7},{4,0},{5,1},{6,2},{7,3},{8,12},{9,13},{10,... | collective-permute-start | bytes 393224 | tf_op jit(solution)/shard_map/ppermute | solution.py:314
  10.7 1.6 %copy-done = bf16[1,4,32,64,128]{4,3,2,1,0:T(8,128)(2,1)S(1)} copy-done((bf16[1,4,32,64,128]{4,3,2,1,0:T(8,128)(2,1)S(1)}, bf16[1,4,32,64,128]{4,3,2,1,0:T(8,128)(2,1)}, u32[]{:S(2)}) %copy-start) | copy-done | bytes 2097176
  12.3 0.7 %prepare_block.2 = (bf16[2048,512]{1,0:T(8,128)(2,1)S(1)}, bf16[512,2048]{1,0:T(8,128)(2,1)S(1)}) custom-call(bf16[1,4,32,64,128]{4,3,2,1,0:T(8,128)(2,1)S(1)} %copy-done), custom_call_target="tpu_custom_call" | custom-call | tf_op jit(solution)/shard_map/prepare_block/pallas_call | solution.py:35
  13.0 0.0 collective-permute-done.1.refs_7_
  13.0 0.4 collective-permute-done.theta_ref
  13.4 0.0 collective-permute-done.2.chol_ref
  13.4 0.0 copy-done.3
  13.4 0.7 %pick_tiles.3 = (bf16[2,64,512]{2,1,0:T(8,128)(2,1)S(1)}, bf16[2,64,512]{2,1,0:T(8,128)(2,1)S(1)}, bf16[2,64,512]{2,1,0:T(8,128)(2,1)S(1)}, bf16[2,64,512]{2,1,0:T(8,128)(2,1)S(1)}) custom-call(s32[4,16]{1,0:T(4,128)S(1)} %bitcast.3, bf16[1,64,1280]{2,1,0:T(8,128)(2,1)S(1)} %collective-permute-done.theta_ref), custom_call_target="tpu_custom_call" | custom-call | tf_op jit(solution)/shard_map/pick_tiles/pallas_call | solution.py:63
  14.2 1.7 %collective-permute-start.6 = (bf16[2,64,512]{2,1,0:T(8,128)(2,1)S(1)}, bf16[2,64,512]{2,1,0:T(8,128)(2,1)S(1)}, u32[]{:S(2)}, u32[]{:S(2)}) collective-permute-start(bf16[2,64,512]{2,1,0:T(8,128)(2,1)S(1)} %get-tuple-element.43), channel_id=1, source_target_pairs={{0,2},{1,3},{2,0},{3,1},{4,6},{5,7},{6,4},{7,5},{8,10},{9,11},{10,... | collective-permute-start | bytes 393224 | tf_op jit(solution)/shard_map/ppermute | solution.py:314
  15.8 3.7 %collective-permute-start.7 = (bf16[2,64,512]{2,1,0:T(8,128)(2,1)S(1)}, bf16[2,64,512]{2,1,0:T(8,128)(2,1)S(1)}, u32[]{:S(2)}, u32[]{:S(2)}) collective-permute-start(bf16[2,64,512]{2,1,0:T(8,128)(2,1)S(1)} %get-tuple-element.44), channel_id=1, source_target_pairs={{0,4},{1,5},{2,6},{3,7},{4,0},{5,1},{6,2},{7,3},{8,12},{9,13},{10,... | collective-permute-start | bytes 393224 | tf_op jit(solution)/shard_map/ppermute | solution.py:314
  19.5 0.0 collective-permute-start.8
  19.5 0.0 collective-permute-done.3.refs_9_
  19.5 0.7 %prepare_block.3 = (bf16[2048,512]{1,0:T(8,128)(2,1)S(1)}, bf16[512,2048]{1,0:T(8,128)(2,1)S(1)}) custom-call(bf16[1,4,32,64,128]{4,3,2,1,0:T(8,128)(2,1)S(1)} %collective-permute-done.2.chol_ref), custom_call_target="tpu_custom_call" | custom-call | tf_op jit(solution)/shard_map/prepare_block/pallas_call | solution.py:35
  20.2 0.0 copy-done.4
  20.2 0.1 collective-permute-start.4
  20.3 0.0 collective-permute-done.5.refs_8_
  20.3 1.1 %collective-permute-done.4.refs_1_ = s32[1,4]{1,0:T(1,128)S(1)} collective-permute-done((s32[1,4]{1,0:T(1,128)S(1)}, s32[1,4]{1,0:T(1,128)S(1)}, u32[]{:S(2)}, u32[]{:S(2)}) %collective-permute-start.4) | collective-permute-done | bytes 48 | tf_op jit(solution)/shard_map/ppermute | solution.py:317
  21.4 2.8 %chip_terms.2 = (f32[8,1,128]{2,1,0:T(1,128)S(1)}, f32[2,512]{1,0:T(2,128)S(1)}) custom-call(s32[1,4]{1,0:T(1,128)S(1)} %copy-done.4, s32[1,4]{1,0:T(1,128)S(1)} %collective-permute-done.4.refs_1_, bf16[2048,512]{1,0:T(8,128)(2,1)S(1)} %get-tuple-element.30.refs_2_, bf16[512,2048]{1,0:T(8,128)(2,1)S(1)} %get-tuple-element.31.refs_3_, ...), custom_call_target="tpu_custom_call" | custom-call | tf_op jit(solution)/shard_map/chip_terms/pallas_call | solution.py:241
  24.2 0.0 collective-permute-done.6.refs_7_
  24.2 0.0 collective-permute-done.7.refs_8_
  24.2 1.3 %collective-permute-done.8.refs_9_ = bf16[2,64,512]{2,1,0:T(8,128)(2,1)S(1)} collective-permute-done((bf16[2,64,512]{2,1,0:T(8,128)(2,1)S(1)}, bf16[2,64,512]{2,1,0:T(8,128)(2,1)S(1)}, u32[]{:S(2)}, u32[]{:S(2)}) %collective-permute-start.8) | collective-permute-done | bytes 131104 | tf_op jit(solution)/shard_map/ppermute | solution.py:314
  25.6 2.4 %chip_terms.3 = f32[8,1,128]{2,1,0:T(1,128)S(1)} custom-call(f32[2,512]{1,0:T(2,128)S(1)} %get-tuple-element.39.refs_0_, f32[8,1,128]{2,1,0:T(1,128)S(1)} %get-tuple-element.40.refs_1_, bf16[2048,512]{1,0:T(8,128)(2,1)S(1)} %get-tuple-element.30.refs_2_, bf16[512,2048]{1,0:T(8,128)(2,1)S(1)} %get-tuple-element.31.refs_3_, ...), custom_call_target="tpu_custom_call" | custom-call | tf_op jit(solution)/shard_map/chip_terms/pallas_call | solution.py:241
  27.9 10.1 %all_to_all.5.rows_ref = f32[8,1,128]{2,1,0:T(1,128)} all-to-all(f32[8,1,128]{2,1,0:T(1,128)S(1)} %chip_terms.3), channel_id=1, replica_groups={{0,2,4,6,8,10,12,14},{1,3,5,7,9,11,13,15},{16,18,20,22,24,26,28,30},{17..., dimensions={0} | all-to-all | bytes 8192 | tf_op jit(solution)/shard_map/all_to_all | solution.py:338
  38.0 1.4 %finish.1 = (f32[1,512]{1,0:T(1,128)}, f32[1,1]{1,0:T(1,128)}) custom-call(f32[8,1,128]{2,1,0:T(1,128)} %all_to_all.5.rows_ref), custom_call_target="tpu_custom_call" | custom-call | tf_op jit(solution)/shard_map/finish/pallas_call | solution.py:291
  (4 shorter events, 0.0 us)
Async XLA Ops:
  0.6 12.8 %collective-permute-start.2 = (bf16[1,4,32,64,128]{4,3,2,1,0:T(8,128)(2,1)}, bf16[1,4,32,64,128]{4,3,2,1,0:T(8,128)(2,1)S(1)}, u32[]{:S(2)}, u32[]{:S(2)}) collective-permute-start(bf16[1,4,32,64,128]{4,3,2,1,0:T(8,128)(2,1)} %chol_ref.1), channel_id=1, source_target_pairs={{0,1},{1,0},{2,3},{3,2},{4,5},{5,4},{6,7},{7,6},{8,9},{9,8},{10,11... | collective-permute-start | bytes 6291464 | tf_op jit(solution)/shard_map/ppermute | solution.py:317
  1.1 12.3 %collective-permute-start = (bf16[1,64,1280]{2,1,0:T(8,128)(2,1)}, bf16[1,64,1280]{2,1,0:T(8,128)(2,1)S(1)}, u32[]{:S(2)}, u32[]{:S(2)}) collective-permute-start(bf16[1,64,1280]{2,1,0:T(8,128)(2,1)} %theta_ref.1), channel_id=1, source_target_pairs={{0,8},{1,9},{2,10},{3,11},{4,12},{5,13},{6,14},{7,15},{8,0},{9,1},... | collective-permute-start | bytes 491528 | tf_op jit(solution)/shard_map/ppermute | solution.py:314
  4.8 0.9 %copy-start.1 = (bf16[1,64,1280]{2,1,0:T(8,128)(2,1)S(1)}, bf16[1,64,1280]{2,1,0:T(8,128)(2,1)}, u32[]{:S(2)}) copy-start(bf16[1,64,1280]{2,1,0:T(8,128)(2,1)} %theta_ref.1) | copy-start | bytes 491524
  5.8 0.7 %copy-start.2 = (s32[16,4]{0,1:T(4,128)S(1)}, s32[16,4]{0,1:T(4,128)}, u32[]{:S(2)}) copy-start(s32[16,4]{0,1:T(4,128)} %param.7) | copy-start | bytes 772
  6.4 7.0 %copy-start.3 = (s32[16,4]{0,1:T(4,128)S(1)}, s32[16,4]{0,1:T(4,128)}, u32[]{:S(2)}) copy-start(s32[16,4]{0,1:T(4,128)} %param.7) | copy-start | bytes 772
  7.2 5.9 %collective-permute-start.1 = (bf16[2,64,512]{2,1,0:T(8,128)(2,1)S(1)}, bf16[2,64,512]{2,1,0:T(8,128)(2,1)S(1)}, u32[]{:S(2)}, u32[]{:S(2)}) collective-permute-start(bf16[2,64,512]{2,1,0:T(8,128)(2,1)S(1)} %get-tuple-element.25), channel_id=1, source_target_pairs={{0,2},{1,3},{2,0},{3,1},{4,6},{5,7},{6,4},{7,5},{8,10},{9,11},{10,... | collective-permute-start | bytes 393224 | tf_op jit(solution)/shard_map/ppermute | solution.py:314
  8.8 10.8 %collective-permute-start.3 = (bf16[2,64,512]{2,1,0:T(8,128)(2,1)S(1)}, bf16[2,64,512]{2,1,0:T(8,128)(2,1)S(1)}, u32[]{:S(2)}, u32[]{:S(2)}) collective-permute-start(bf16[2,64,512]{2,1,0:T(8,128)(2,1)S(1)} %get-tuple-element.28), channel_id=1, source_target_pairs={{0,6},{1,7},{2,4},{3,5},{4,2},{5,3},{6,0},{7,1},{8,14},{9,15},{10,... | collective-permute-start | bytes 393224 | tf_op jit(solution)/shard_map/ppermute | solution.py:314
  10.3 10.1 %collective-permute-start.5 = (bf16[2,64,512]{2,1,0:T(8,128)(2,1)S(1)}, bf16[2,64,512]{2,1,0:T(8,128)(2,1)S(1)}, u32[]{:S(2)}, u32[]{:S(2)}) collective-permute-start(bf16[2,64,512]{2,1,0:T(8,128)(2,1)S(1)} %get-tuple-element.37), channel_id=1, source_target_pairs={{0,4},{1,5},{2,6},{3,7},{4,0},{5,1},{6,2},{7,3},{8,12},{9,13},{10,... | collective-permute-start | bytes 393224 | tf_op jit(solution)/shard_map/ppermute | solution.py:314
  10.7 1.6 %copy-start = (bf16[1,4,32,64,128]{4,3,2,1,0:T(8,128)(2,1)S(1)}, bf16[1,4,32,64,128]{4,3,2,1,0:T(8,128)(2,1)}, u32[]{:S(2)}) copy-start(bf16[1,4,32,64,128]{4,3,2,1,0:T(8,128)(2,1)} %chol_ref.1) | copy-start | bytes 6291460
  12.3 7.9 %copy-start.4 = (s32[1,4]{1,0:T(1,128)S(1)}, s32[1,4]{1,0:T(1,128)}, u32[]{:S(2)}) copy-start(s32[1,4]{1,0:T(1,128)} %refs_0_.1) | copy-start | bytes 52
  14.2 10.1 %collective-permute-start.6 = (bf16[2,64,512]{2,1,0:T(8,128)(2,1)S(1)}, bf16[2,64,512]{2,1,0:T(8,128)(2,1)S(1)}, u32[]{:S(2)}, u32[]{:S(2)}) collective-permute-start(bf16[2,64,512]{2,1,0:T(8,128)(2,1)S(1)} %get-tuple-element.43), channel_id=1, source_target_pairs={{0,2},{1,3},{2,0},{3,1},{4,6},{5,7},{6,4},{7,5},{8,10},{9,11},{10,... | collective-permute-start | bytes 393224 | tf_op jit(solution)/shard_map/ppermute | solution.py:314
  15.8 8.4 %collective-permute-start.7 = (bf16[2,64,512]{2,1,0:T(8,128)(2,1)S(1)}, bf16[2,64,512]{2,1,0:T(8,128)(2,1)S(1)}, u32[]{:S(2)}, u32[]{:S(2)}) collective-permute-start(bf16[2,64,512]{2,1,0:T(8,128)(2,1)S(1)} %get-tuple-element.44), channel_id=1, source_target_pairs={{0,4},{1,5},{2,6},{3,7},{4,0},{5,1},{6,2},{7,3},{8,12},{9,13},{10,... | collective-permute-start | bytes 393224 | tf_op jit(solution)/shard_map/ppermute | solution.py:314
  19.5 6.1 %collective-permute-start.8 = (bf16[2,64,512]{2,1,0:T(8,128)(2,1)S(1)}, bf16[2,64,512]{2,1,0:T(8,128)(2,1)S(1)}, u32[]{:S(2)}, u32[]{:S(2)}) collective-permute-start(bf16[2,64,512]{2,1,0:T(8,128)(2,1)S(1)} %get-tuple-element.45), channel_id=1, source_target_pairs={{0,6},{1,7},{2,4},{3,5},{4,2},{5,3},{6,0},{7,1},{8,14},{9,15},{10,... | collective-permute-start | bytes 393224 | tf_op jit(solution)/shard_map/ppermute | solution.py:314
  20.2 1.2 %collective-permute-start.4 = (s32[1,4]{1,0:T(1,128)S(1)}, s32[1,4]{1,0:T(1,128)S(1)}, u32[]{:S(2)}, u32[]{:S(2)}) collective-permute-start(s32[1,4]{1,0:T(1,128)S(1)} %copy-done.4), channel_id=1, source_target_pairs={{0,1},{1,0},{2,3},{3,2},{4,5},{5,4},{6,7},{7,6},{8,9},{9,8},{10,11... | collective-permute-start | bytes 56 | tf_op jit(solution)/shard_map/ppermute | solution.py:317

commit v22 on v21

--- a/solution.py
+++ b/solution.py
@@ -218,7 +218,7 @@
             lax.dot_general(segment, part, NT, preferred_element_type=jnp.float32) for part in parts
         )
         for i in range(batch):
-            owner = chip ^ (first + index + i)
+            owner = chip ^ (first + index + i) ^ (out_ref.shape[0] // 2)
             out_ref[pl.ds(owner, 1), 0, :used + 8] = sums[i:i + 1]
 
     if count == batch:
@@ -262,17 +262,18 @@
 
 def finish_kernel(rows_ref, bias_ref, energy_ref, bias_buf, energy_buf, sems, *, used, scale):
     chips, _, width = rows_ref.shape
+    half = chips // 2
     fit = LANES // used if width == LANES else 0
     lane = lax.broadcasted_iota(jnp.int32, (1, width), 1)
     if fit and chips % fit == 0:
         for d in range(0, chips, fit):
-            packed = rows_ref[d]
+            packed = rows_ref[d ^ half]
             for i in range(1, fit):
-                packed = jnp.where(lane < i * used, packed, pltpu.roll(rows_ref[d + i], i * used, 1))
+                packed = jnp.where(lane < i * used, packed, pltpu.roll(rows_ref[(d + i) ^ half], i * used, 1))
             bias_buf[:, d * used:(d + fit) * used] = packed
     else:
         for d in range(chips):
-            bias_buf[:, d * used:(d + 1) * used] = rows_ref[d, :, :used]
+            bias_buf[:, d * used:(d + 1) * used] = rows_ref[d ^ half, :, :used]
     bias_copy = pltpu.make_async_copy(bias_buf, bias_ref, sems.at[0])
     bias_copy.start()
     total = energy_terms(rows_ref[0], used)
@@ -334,7 +335,7 @@
     screens = [screen, to_core(late_screen)]
     rows, masks = chip_terms(screens, [], blocks, near, 0, NEAR, vectors, chips, out_width)
     rows, = chip_terms([], [masks, rows], blocks, beyond, half, BEYOND, vectors, chips, out_width)
-    same_core = [list(range(core, groups, CORES)) for core in range(CORES)]
+    same_core = [[(rank ^ half) * CORES + core for rank in range(chips)] for core in range(CORES)]
     back = lax.all_to_all(rows, "chol", split_axis=0, concat_axis=0, tiled=True, axis_index_groups=same_core)
     return finish(back, used, 1.0 / (2.0 * occupied * occupied))
 

time: 39.6 us -> 38.1 us (0.962)
  blocking collectives: 10.1 us -> 8.51 us
    all_to_all x1, blocking collectives: 10.1 us -> 8.51 us  [body(): lax.all_to_all(rows, 'chol', split_axis=0, concat_axis=0, tiled=True, axi...]
  transfers between devices with their start and end apart: 9 -> 9, of which waited for: 3 -> 3; matrix products, arithmetic and copies ran while one was open for 0% -> 0% of each run, Pallas kernels for 14% -> 15%
where the time goes in v22:
time: 38.1 us; the launch traced here: 37.8 us
  starting transfers between devices  13.2 us (35%)
  Pallas kernels  9.35 us (25%)
  blocking collectives  8.51 us (22%)
  local copies, waits for them, and re-layouts  3.23 us (8%)
  waiting for transfers between devices  2.85 us (7%)
  between operations  0.72 us (2%)
    ppermute x7, starting transfers between devices, to_chip(): lax.ppermute(x, 'chol', [(i, i ^ offset * CORES) for i in range(groups)])  12.6 us
    all_to_all x1, blocking collectives, body(): lax.all_to_all(rows, 'chol', split_axis=0, concat_axis=0, tiled=True, axi...  8.51 us
    pallas_call x2, Pallas kernels, chip_terms(): pl.pallas_call(functools.partial(terms_kernel, first=first, count=count,...  5.12 us
    unnamed x10, local copies, waits for them, and re-layouts  3.23 us
    ppermute x7, waiting for transfers between devices, to_chip(): lax.ppermute(x, 'chol', [(i, i ^ offset * CORES) for i in range(groups)])  1.75 us
    pallas_call x2, Pallas kernels, pick_tiles(): pl.pallas_call(pick_kernel, in_specs=[SMEM, VMEM], out_specs=[VMEM] * cou...  1.43 us
    pallas_call x2, Pallas kernels, prepare_block(): pl.pallas_call(prepare_kernel, in_specs=[VMEM], out_specs=[VMEM, VMEM], o...  1.43 us
    pallas_call x1, Pallas kernels, finish(): pl.pallas_call(functools.partial(finish_kernel, used=used, scale=scale),...  1.37 us
  transfers between devices with their start and end apart: 9, of which 3 were waited for; matrix products, arithmetic and copies ran while one was open for 0% of the time, Pallas kernels for 15%

profile of v22, /device:TPU:0, one launch (start us, length us, event | category | flops | bytes accessed | tf_op | source)
XLA Modules:
  0.0 37.8 jit_solution(16165385604997574186)
XLA Ops:
  0.6 0.5 %collective-permute-start.2 = (bf16[1,4,32,64,128]{4,3,2,1,0:T(8,128)(2,1)}, bf16[1,4,32,64,128]{4,3,2,1,0:T(8,128)(2,1)S(1)}, u32[]{:S(2)}, u32[]{:S(2)}) collective-permute-start(bf16[1,4,32,64,128]{4,3,2,1,0:T(8,128)(2,1)} %chol_ref.1), channel_id=1, source_target_pairs={{0,1},{1,0},{2,3},{3,2},{4,5},{5,4},{6,7},{7,6},{8,9},{9,8},{10,11... | collective-permute-start | bytes 6291464 | tf_op jit(solution)/shard_map/ppermute | solution.py:318
  1.1 3.7 %collective-permute-start = (bf16[1,64,1280]{2,1,0:T(8,128)(2,1)}, bf16[1,64,1280]{2,1,0:T(8,128)(2,1)S(1)}, u32[]{:S(2)}, u32[]{:S(2)}) collective-permute-start(bf16[1,64,1280]{2,1,0:T(8,128)(2,1)} %theta_ref.1), channel_id=1, source_target_pairs={{0,8},{1,9},{2,10},{3,11},{4,12},{5,13},{6,14},{7,15},{8,0},{9,1},... | collective-permute-start | bytes 491528 | tf_op jit(solution)/shard_map/ppermute | solution.py:315
  4.8 0.0 copy-start.1
  4.8 0.9 %copy-done.1 = bf16[1,64,1280]{2,1,0:T(8,128)(2,1)S(1)} copy-done((bf16[1,64,1280]{2,1,0:T(8,128)(2,1)S(1)}, bf16[1,64,1280]{2,1,0:T(8,128)(2,1)}, u32[]{:S(2)}) %copy-start.1) | copy-done | bytes 163864
  5.8 0.7 %copy-done.2 = s32[16,4]{0,1:T(4,128)S(1)} copy-done((s32[16,4]{0,1:T(4,128)S(1)}, s32[16,4]{0,1:T(4,128)}, u32[]{:S(2)}) %copy-start.2) | copy-done | bytes 280
  6.4 0.7 %pick_tiles.2 = (bf16[2,64,512]{2,1,0:T(8,128)(2,1)S(1)}, bf16[2,64,512]{2,1,0:T(8,128)(2,1)S(1)}, bf16[2,64,512]{2,1,0:T(8,128)(2,1)S(1)}, bf16[2,64,512]{2,1,0:T(8,128)(2,1)S(1)}) custom-call(s32[4,16]{1,0:T(4,128)S(1)} %bitcast.2, bf16[1,64,1280]{2,1,0:T(8,128)(2,1)S(1)} %copy-done.1), custom_call_target="tpu_custom_call" | custom-call | tf_op jit(solution)/shard_map/pick_tiles/pallas_call | solution.py:63
  7.2 1.6 %collective-permute-start.1 = (bf16[2,64,512]{2,1,0:T(8,128)(2,1)S(1)}, bf16[2,64,512]{2,1,0:T(8,128)(2,1)S(1)}, u32[]{:S(2)}, u32[]{:S(2)}) collective-permute-start(bf16[2,64,512]{2,1,0:T(8,128)(2,1)S(1)} %get-tuple-element.25), channel_id=1, source_target_pairs={{0,2},{1,3},{2,0},{3,1},{4,6},{5,7},{6,4},{7,5},{8,10},{9,11},{10,... | collective-permute-start | bytes 393224 | tf_op jit(solution)/shard_map/ppermute | solution.py:315
  8.8 1.5 %collective-permute-start.3 = (bf16[2,64,512]{2,1,0:T(8,128)(2,1)S(1)}, bf16[2,64,512]{2,1,0:T(8,128)(2,1)S(1)}, u32[]{:S(2)}, u32[]{:S(2)}) collective-permute-start(bf16[2,64,512]{2,1,0:T(8,128)(2,1)S(1)} %get-tuple-element.28), channel_id=1, source_target_pairs={{0,6},{1,7},{2,4},{3,5},{4,2},{5,3},{6,0},{7,1},{8,14},{9,15},{10,... | collective-permute-start | bytes 393224 | tf_op jit(solution)/shard_map/ppermute | solution.py:315
  10.3 0.4 %collective-permute-start.5 = (bf16[2,64,512]{2,1,0:T(8,128)(2,1)S(1)}, bf16[2,64,512]{2,1,0:T(8,128)(2,1)S(1)}, u32[]{:S(2)}, u32[]{:S(2)}) collective-permute-start(bf16[2,64,512]{2,1,0:T(8,128)(2,1)S(1)} %get-tuple-element.37), channel_id=1, source_target_pairs={{0,4},{1,5},{2,6},{3,7},{4,0},{5,1},{6,2},{7,3},{8,12},{9,13},{10,... | collective-permute-start | bytes 393224 | tf_op jit(solution)/shard_map/ppermute | solution.py:315
  10.7 1.6 %copy-done = bf16[1,4,32,64,128]{4,3,2,1,0:T(8,128)(2,1)S(1)} copy-done((bf16[1,4,32,64,128]{4,3,2,1,0:T(8,128)(2,1)S(1)}, bf16[1,4,32,64,128]{4,3,2,1,0:T(8,128)(2,1)}, u32[]{:S(2)}) %copy-start) | copy-done | bytes 2097176
  12.3 0.7 %prepare_block.2 = (bf16[2048,512]{1,0:T(8,128)(2,1)S(1)}, bf16[512,2048]{1,0:T(8,128)(2,1)S(1)}) custom-call(bf16[1,4,32,64,128]{4,3,2,1,0:T(8,128)(2,1)S(1)} %copy-done), custom_call_target="tpu_custom_call" | custom-call | tf_op jit(solution)/shard_map/prepare_block/pallas_call | solution.py:35
  13.0 0.0 collective-permute-done.1.refs_7_
  13.0 0.4 collective-permute-done.theta_ref
  13.4 0.0 collective-permute-done.2.chol_ref
  13.4 0.0 copy-done.3
  13.4 0.7 %pick_tiles.3 = (bf16[2,64,512]{2,1,0:T(8,128)(2,1)S(1)}, bf16[2,64,512]{2,1,0:T(8,128)(2,1)S(1)}, bf16[2,64,512]{2,1,0:T(8,128)(2,1)S(1)}, bf16[2,64,512]{2,1,0:T(8,128)(2,1)S(1)}) custom-call(s32[4,16]{1,0:T(4,128)S(1)} %bitcast.3, bf16[1,64,1280]{2,1,0:T(8,128)(2,1)S(1)} %collective-permute-done.theta_ref), custom_call_target="tpu_custom_call" | custom-call | tf_op jit(solution)/shard_map/pick_tiles/pallas_call | solution.py:63
  14.2 1.7 %collective-permute-start.6 = (bf16[2,64,512]{2,1,0:T(8,128)(2,1)S(1)}, bf16[2,64,512]{2,1,0:T(8,128)(2,1)S(1)}, u32[]{:S(2)}, u32[]{:S(2)}) collective-permute-start(bf16[2,64,512]{2,1,0:T(8,128)(2,1)S(1)} %get-tuple-element.43), channel_id=1, source_target_pairs={{0,2},{1,3},{2,0},{3,1},{4,6},{5,7},{6,4},{7,5},{8,10},{9,11},{10,... | collective-permute-start | bytes 393224 | tf_op jit(solution)/shard_map/ppermute | solution.py:315
  15.8 3.7 %collective-permute-start.7 = (bf16[2,64,512]{2,1,0:T(8,128)(2,1)S(1)}, bf16[2,64,512]{2,1,0:T(8,128)(2,1)S(1)}, u32[]{:S(2)}, u32[]{:S(2)}) collective-permute-start(bf16[2,64,512]{2,1,0:T(8,128)(2,1)S(1)} %get-tuple-element.44), channel_id=1, source_target_pairs={{0,4},{1,5},{2,6},{3,7},{4,0},{5,1},{6,2},{7,3},{8,12},{9,13},{10,... | collective-permute-start | bytes 393224 | tf_op jit(solution)/shard_map/ppermute | solution.py:315
  19.5 0.0 collective-permute-start.8
  19.5 0.0 collective-permute-done.3.refs_9_
  19.5 0.7 %prepare_block.3 = (bf16[2048,512]{1,0:T(8,128)(2,1)S(1)}, bf16[512,2048]{1,0:T(8,128)(2,1)S(1)}) custom-call(bf16[1,4,32,64,128]{4,3,2,1,0:T(8,128)(2,1)S(1)} %collective-permute-done.2.chol_ref), custom_call_target="tpu_custom_call" | custom-call | tf_op jit(solution)/shard_map/prepare_block/pallas_call | solution.py:35
  20.2 0.0 copy-done.4
  20.2 0.1 collective-permute-start.4
  20.3 0.0 collective-permute-done.5.refs_8_
  20.3 1.1 %collective-permute-done.4.refs_1_ = s32[1,4]{1,0:T(1,128)S(1)} collective-permute-done((s32[1,4]{1,0:T(1,128)S(1)}, s32[1,4]{1,0:T(1,128)S(1)}, u32[]{:S(2)}, u32[]{:S(2)}) %collective-permute-start.4) | collective-permute-done | bytes 48 | tf_op jit(solution)/shard_map/ppermute | solution.py:318
  21.4 2.8 %chip_terms.2 = (f32[8,1,128]{2,1,0:T(1,128)S(1)}, f32[2,512]{1,0:T(2,128)S(1)}) custom-call(s32[1,4]{1,0:T(1,128)S(1)} %copy-done.4, s32[1,4]{1,0:T(1,128)S(1)} %collective-permute-done.4.refs_1_, bf16[2048,512]{1,0:T(8,128)(2,1)S(1)} %get-tuple-element.30.refs_2_, bf16[512,2048]{1,0:T(8,128)(2,1)S(1)} %get-tuple-element.31.refs_3_, ...), custom_call_target="tpu_custom_call" | custom-call | tf_op jit(solution)/shard_map/chip_terms/pallas_call | solution.py:241
  24.2 0.0 collective-permute-done.6.refs_7_
  24.2 0.0 collective-permute-done.7.refs_8_
  24.2 1.3 %collective-permute-done.8.refs_9_ = bf16[2,64,512]{2,1,0:T(8,128)(2,1)S(1)} collective-permute-done((bf16[2,64,512]{2,1,0:T(8,128)(2,1)S(1)}, bf16[2,64,512]{2,1,0:T(8,128)(2,1)S(1)}, u32[]{:S(2)}, u32[]{:S(2)}) %collective-permute-start.8) | collective-permute-done | bytes 131104 | tf_op jit(solution)/shard_map/ppermute | solution.py:315
  25.6 2.4 %chip_terms.3 = f32[8,1,128]{2,1,0:T(1,128)S(1)} custom-call(f32[2,512]{1,0:T(2,128)S(1)} %get-tuple-element.39.refs_0_, f32[8,1,128]{2,1,0:T(1,128)S(1)} %get-tuple-element.40.refs_1_, bf16[2048,512]{1,0:T(8,128)(2,1)S(1)} %get-tuple-element.30.refs_2_, bf16[512,2048]{1,0:T(8,128)(2,1)S(1)} %get-tuple-element.31.refs_3_, ...), custom_call_target="tpu_custom_call" | custom-call | tf_op jit(solution)/shard_map/chip_terms/pallas_call | solution.py:241
  27.9 8.5 %all_to_all.5.rows_ref = f32[8,1,128]{2,1,0:T(1,128)} all-to-all(f32[8,1,128]{2,1,0:T(1,128)S(1)} %chip_terms.3), channel_id=1, replica_groups={{8,10,12,14,0,2,4,6},{9,11,13,15,1,3,5,7},{24,26,28,30,16,18,20,22},{25..., dimensions={0} | all-to-all | bytes 8192 | tf_op jit(solution)/shard_map/all_to_all | solution.py:339
  36.5 1.4 %finish.1 = (f32[1,512]{1,0:T(1,128)}, f32[1,1]{1,0:T(1,128)}) custom-call(f32[8,1,128]{2,1,0:T(1,128)} %all_to_all.5.rows_ref), custom_call_target="tpu_custom_call" | custom-call | tf_op jit(solution)/shard_map/finish/pallas_call | solution.py:292
  (4 shorter events, 0.0 us)
Async XLA Ops:
  0.6 12.8 %collective-permute-start.2 = (bf16[1,4,32,64,128]{4,3,2,1,0:T(8,128)(2,1)}, bf16[1,4,32,64,128]{4,3,2,1,0:T(8,128)(2,1)S(1)}, u32[]{:S(2)}, u32[]{:S(2)}) collective-permute-start(bf16[1,4,32,64,128]{4,3,2,1,0:T(8,128)(2,1)} %chol_ref.1), channel_id=1, source_target_pairs={{0,1},{1,0},{2,3},{3,2},{4,5},{5,4},{6,7},{7,6},{8,9},{9,8},{10,11... | collective-permute-start | bytes 6291464 | tf_op jit(solution)/shard_map/ppermute | solution.py:318
  1.1 12.3 %collective-permute-start = (bf16[1,64,1280]{2,1,0:T(8,128)(2,1)}, bf16[1,64,1280]{2,1,0:T(8,128)(2,1)S(1)}, u32[]{:S(2)}, u32[]{:S(2)}) collective-permute-start(bf16[1,64,1280]{2,1,0:T(8,128)(2,1)} %theta_ref.1), channel_id=1, source_target_pairs={{0,8},{1,9},{2,10},{3,11},{4,12},{5,13},{6,14},{7,15},{8,0},{9,1},... | collective-permute-start | bytes 491528 | tf_op jit(solution)/shard_map/ppermute | solution.py:315
  4.8 0.9 %copy-start.1 = (bf16[1,64,1280]{2,1,0:T(8,128)(2,1)S(1)}, bf16[1,64,1280]{2,1,0:T(8,128)(2,1)}, u32[]{:S(2)}) copy-start(bf16[1,64,1280]{2,1,0:T(8,128)(2,1)} %theta_ref.1) | copy-start | bytes 491524
  5.8 0.7 %copy-start.2 = (s32[16,4]{0,1:T(4,128)S(1)}, s32[16,4]{0,1:T(4,128)}, u32[]{:S(2)}) copy-start(s32[16,4]{0,1:T(4,128)} %param.7) | copy-start | bytes 772
  6.4 7.0 %copy-start.3 = (s32[16,4]{0,1:T(4,128)S(1)}, s32[16,4]{0,1:T(4,128)}, u32[]{:S(2)}) copy-start(s32[16,4]{0,1:T(4,128)} %param.7) | copy-start | bytes 772
  7.2 5.9 %collective-permute-start.1 = (bf16[2,64,512]{2,1,0:T(8,128)(2,1)S(1)}, bf16[2,64,512]{2,1,0:T(8,128)(2,1)S(1)}, u32[]{:S(2)}, u32[]{:S(2)}) collective-permute-start(bf16[2,64,512]{2,1,0:T(8,128)(2,1)S(1)} %get-tuple-element.25), channel_id=1, source_target_pairs={{0,2},{1,3},{2,0},{3,1},{4,6},{5,7},{6,4},{7,5},{8,10},{9,11},{10,... | collective-permute-start | bytes 393224 | tf_op jit(solution)/shard_map/ppermute | solution.py:315
  8.8 10.8 %collective-permute-start.3 = (bf16[2,64,512]{2,1,0:T(8,128)(2,1)S(1)}, bf16[2,64,512]{2,1,0:T(8,128)(2,1)S(1)}, u32[]{:S(2)}, u32[]{:S(2)}) collective-permute-start(bf16[2,64,512]{2,1,0:T(8,128)(2,1)S(1)} %get-tuple-element.28), channel_id=1, source_target_pairs={{0,6},{1,7},{2,4},{3,5},{4,2},{5,3},{6,0},{7,1},{8,14},{9,15},{10,... | collective-permute-start | bytes 393224 | tf_op jit(solution)/shard_map/ppermute | solution.py:315
  10.3 10.1 %collective-permute-start.5 = (bf16[2,64,512]{2,1,0:T(8,128)(2,1)S(1)}, bf16[2,64,512]{2,1,0:T(8,128)(2,1)S(1)}, u32[]{:S(2)}, u32[]{:S(2)}) collective-permute-start(bf16[2,64,512]{2,1,0:T(8,128)(2,1)S(1)} %get-tuple-element.37), channel_id=1, source_target_pairs={{0,4},{1,5},{2,6},{3,7},{4,0},{5,1},{6,2},{7,3},{8,12},{9,13},{10,... | collective-permute-start | bytes 393224 | tf_op jit(solution)/shard_map/ppermute | solution.py:315
  10.7 1.6 %copy-start = (bf16[1,4,32,64,128]{4,3,2,1,0:T(8,128)(2,1)S(1)}, bf16[1,4,32,64,128]{4,3,2,1,0:T(8,128)(2,1)}, u32[]{:S(2)}) copy-start(bf16[1,4,32,64,128]{4,3,2,1,0:T(8,128)(2,1)} %chol_ref.1) | copy-start | bytes 6291460
  12.3 7.9 %copy-start.4 = (s32[1,4]{1,0:T(1,128)S(1)}, s32[1,4]{1,0:T(1,128)}, u32[]{:S(2)}) copy-start(s32[1,4]{1,0:T(1,128)} %refs_0_.1) | copy-start | bytes 52
  14.2 10.1 %collective-permute-start.6 = (bf16[2,64,512]{2,1,0:T(8,128)(2,1)S(1)}, bf16[2,64,512]{2,1,0:T(8,128)(2,1)S(1)}, u32[]{:S(2)}, u32[]{:S(2)}) collective-permute-start(bf16[2,64,512]{2,1,0:T(8,128)(2,1)S(1)} %get-tuple-element.43), channel_id=1, source_target_pairs={{0,2},{1,3},{2,0},{3,1},{4,6},{5,7},{6,4},{7,5},{8,10},{9,11},{10,... | collective-permute-start | bytes 393224 | tf_op jit(solution)/shard_map/ppermute | solution.py:315
  15.8 8.4 %collective-permute-start.7 = (bf16[2,64,512]{2,1,0:T(8,128)(2,1)S(1)}, bf16[2,64,512]{2,1,0:T(8,128)(2,1)S(1)}, u32[]{:S(2)}, u32[]{:S(2)}) collective-permute-start(bf16[2,64,512]{2,1,0:T(8,128)(2,1)S(1)} %get-tuple-element.44), channel_id=1, source_target_pairs={{0,4},{1,5},{2,6},{3,7},{4,0},{5,1},{6,2},{7,3},{8,12},{9,13},{10,... | collective-permute-start | bytes 393224 | tf_op jit(solution)/shard_map/ppermute | solution.py:315
  19.5 6.1 %collective-permute-start.8 = (bf16[2,64,512]{2,1,0:T(8,128)(2,1)S(1)}, bf16[2,64,512]{2,1,0:T(8,128)(2,1)S(1)}, u32[]{:S(2)}, u32[]{:S(2)}) collective-permute-start(bf16[2,64,512]{2,1,0:T(8,128)(2,1)S(1)} %get-tuple-element.45), channel_id=1, source_target_pairs={{0,6},{1,7},{2,4},{3,5},{4,2},{5,3},{6,0},{7,1},{8,14},{9,15},{10,... | collective-permute-start | bytes 393224 | tf_op jit(solution)/shard_map/ppermute | solution.py:315
  20.2 1.2 %collective-permute-start.4 = (s32[1,4]{1,0:T(1,128)S(1)}, s32[1,4]{1,0:T(1,128)S(1)}, u32[]{:S(2)}, u32[]{:S(2)}) collective-permute-start(s32[1,4]{1,0:T(1,128)S(1)} %copy-done.4), channel_id=1, source_target_pairs={{0,1},{1,0},{2,3},{3,2},{4,5},{5,4},{6,7},{7,6},{8,9},{9,8},{10,11... | collective-permute-start | bytes 56 | tf_op jit(solution)/shard_map/ppermute | solution.py:318

commit v23 on v22

--- a/solution.py
+++ b/solution.py
@@ -137,6 +137,10 @@
             store_rows(k0 + k8, t, fold_rows(diagonals, sub8))
 
 
+def send_order(place, count):
+    return jnp.where(place == 0, 0, jnp.where(place == count - 1, 1, place + 1))
+
+
 def mask_kernel_rows(screen_refs, listed, width):
     return [
         jnp.concatenate(
@@ -218,7 +222,10 @@
             lax.dot_general(segment, part, NT, preferred_element_type=jnp.float32) for part in parts
         )
         for i in range(batch):
-            owner = chip ^ (first + index + i) ^ (out_ref.shape[0] // 2)
+            place = jnp.int32(index + i)
+            if not screened:
+                place = send_order(place, count)
+            owner = chip ^ (first + place) ^ (out_ref.shape[0] // 2)
             out_ref[pl.ds(owner, 1), 0, :used + 8] = sums[i:i + 1]
 
     if count == batch:
@@ -319,15 +326,18 @@
 
     far = to_chip(theta, half)
 
-    def spread(walker):
-        pieces = pick_tiles(listing, walker, depth, half)
+    def spread(walker, late=False):
+        pieces = list(pick_tiles(listing, walker, depth, half))
+        if late:
+            pieces[1], near[1] = lax.optimization_barrier((pieces[1], near[1]))
         return [pieces[0]] + [to_chip(pieces[offset], offset) for offset in range(1, half)]
 
     near = spread(theta)
     own, own_turned = prepare_block(chol_tiles)
     other_chol = to_core(chol_tiles)
-    far, near[1], other_chol, own = lax.optimization_barrier((far, near[1], other_chol, own))
-    beyond = spread(far)
+    far, other_chol, own = lax.optimization_barrier((far, other_chol, own))
+    beyond = spread(far, True)
+    beyond = beyond[:1] + beyond[2:] + beyond[1:2]
     other_chol, late_screen, near[-1] = lax.optimization_barrier((other_chol, screen, near[-1]))
     other, other_turned = prepare_block(other_chol)
     blocks = [own, own_turned, other, other_turned]

time: 38.1 us -> 38.3 us (level)
  waiting for transfers between devices: 2.85 us -> 4.1 us
  starting transfers between devices: 13.2 us -> 12.3 us
    ppermute x7, waiting for transfers between devices: 1.75 us -> 3.71 us  [to_chip(): lax.ppermute(x, 'chol', [(i, i ^ offset * CORES) for i in range(groups)])]
    ppermute x7, starting transfers between devices: 12.6 us -> 11.8 us  [to_chip(): lax.ppermute(x, 'chol', [(i, i ^ offset * CORES) for i in range(groups)])]
    ppermute x2, waiting for transfers between devices: 1.1 us -> 0.39 us  [to_core(): return lax.ppermute(x, 'chol', [(i, i ^ 1) for i in range(groups)])]
  transfers between devices with their start and end apart: 9 -> 9, of which waited for: 3 -> 4; matrix products, arithmetic and copies ran while one was open for 0% -> 0% of each run, Pallas kernels for 15% -> 15%
where the time goes in v23:
time: 38.3 us; the launch traced here: 38.1 us
  starting transfers between devices  12.3 us (32%)
  Pallas kernels  9.35 us (24%)
  blocking collectives  8.42 us (22%)
  waiting for transfers between devices  4.1 us (11%)
  local copies, waits for them, and re-layouts  3.23 us (8%)
  between operations  0.7 us (2%)
    ppermute x7, starting transfers between devices, to_chip(): lax.ppermute(x, 'chol', [(i, i ^ offset * CORES) for i in range(groups)])  11.8 us
    all_to_all x1, blocking collectives, body(): lax.all_to_all(rows, 'chol', split_axis=0, concat_axis=0, tiled=True, axi...  8.42 us
    pallas_call x2, Pallas kernels, chip_terms(): pl.pallas_call(functools.partial(terms_kernel, first=first, count=count,...  5.12 us
    ppermute x7, waiting for transfers between devices, to_chip(): lax.ppermute(x, 'chol', [(i, i ^ offset * CORES) for i in range(groups)])  3.71 us
    unnamed x10, local copies, waits for them, and re-layouts  3.23 us
    pallas_call x2, Pallas kernels, pick_tiles(): pl.pallas_call(pick_kernel, in_specs=[SMEM, VMEM], out_specs=[VMEM] * cou...  1.43 us
    pallas_call x2, Pallas kernels, prepare_block(): pl.pallas_call(prepare_kernel, in_specs=[VMEM], out_specs=[VMEM, VMEM], o...  1.43 us
    pallas_call x1, Pallas kernels, finish(): pl.pallas_call(functools.partial(finish_kernel, used=used, scale=scale),...  1.37 us
  transfers between devices with their start and end apart: 9, of which 4 were waited for; matrix products, arithmetic and copies ran while one was open for 0% of the time, Pallas kernels for 15%

profile of v23, /device:TPU:0, one launch (start us, length us, event | category | flops | bytes accessed | tf_op | source)
XLA Modules:
  0.0 38.1 jit_solution(3051204645777514019)
XLA Ops:
  0.6 0.0 copy-start.4
  0.6 0.5 %collective-permute-start.1 = (bf16[1,4,32,64,128]{4,3,2,1,0:T(8,128)(2,1)}, bf16[1,4,32,64,128]{4,3,2,1,0:T(8,128)(2,1)S(1)}, u32[]{:S(2)}, u32[]{:S(2)}) collective-permute-start(bf16[1,4,32,64,128]{4,3,2,1,0:T(8,128)(2,1)} %chol_ref.1), channel_id=1, source_target_pairs={{0,1},{1,0},{2,3},{3,2},{4,5},{5,4},{6,7},{7,6},{8,9},{9,8},{10,11... | collective-permute-start | bytes 6291464 | tf_op jit(solution)/shard_map/ppermute | solution.py:325
  1.2 3.7 %collective-permute-start = (bf16[1,64,1280]{2,1,0:T(8,128)(2,1)}, bf16[1,64,1280]{2,1,0:T(8,128)(2,1)S(1)}, u32[]{:S(2)}, u32[]{:S(2)}) collective-permute-start(bf16[1,64,1280]{2,1,0:T(8,128)(2,1)} %theta_ref.1), channel_id=1, source_target_pairs={{0,8},{1,9},{2,10},{3,11},{4,12},{5,13},{6,14},{7,15},{8,0},{9,1},... | collective-permute-start | bytes 491528 | tf_op jit(solution)/shard_map/ppermute | solution.py:322
  4.8 0.9 %copy-done.1 = bf16[1,64,1280]{2,1,0:T(8,128)(2,1)S(1)} copy-done((bf16[1,64,1280]{2,1,0:T(8,128)(2,1)S(1)}, bf16[1,64,1280]{2,1,0:T(8,128)(2,1)}, u32[]{:S(2)}) %copy-start.1) | copy-done | bytes 163864
  5.8 0.7 %copy-done.2 = s32[16,4]{0,1:T(4,128)S(1)} copy-done((s32[16,4]{0,1:T(4,128)S(1)}, s32[16,4]{0,1:T(4,128)}, u32[]{:S(2)}) %copy-start.2) | copy-done | bytes 280
  6.5 0.7 %pick_tiles.2 = (bf16[2,64,512]{2,1,0:T(8,128)(2,1)S(1)}, bf16[2,64,512]{2,1,0:T(8,128)(2,1)S(1)}, bf16[2,64,512]{2,1,0:T(8,128)(2,1)S(1)}, bf16[2,64,512]{2,1,0:T(8,128)(2,1)S(1)}) custom-call(s32[4,16]{1,0:T(4,128)S(1)} %bitcast.2, bf16[1,64,1280]{2,1,0:T(8,128)(2,1)S(1)} %copy-done.1), custom_call_target="tpu_custom_call" | custom-call | tf_op jit(solution)/shard_map/pick_tiles/pallas_call | solution.py:63
  7.2 1.6 %collective-permute-start.4 = (bf16[2,64,512]{2,1,0:T(8,128)(2,1)S(1)}, bf16[2,64,512]{2,1,0:T(8,128)(2,1)S(1)}, u32[]{:S(2)}, u32[]{:S(2)}) collective-permute-start(bf16[2,64,512]{2,1,0:T(8,128)(2,1)S(1)} %get-tuple-element.38), channel_id=1, source_target_pairs={{0,2},{1,3},{2,0},{3,1},{4,6},{5,7},{6,4},{7,5},{8,10},{9,11},{10,... | collective-permute-start | bytes 393224 | tf_op jit(solution)/shard_map/ppermute | solution.py:322
  8.8 1.5 %collective-permute-start.2 = (bf16[2,64,512]{2,1,0:T(8,128)(2,1)S(1)}, bf16[2,64,512]{2,1,0:T(8,128)(2,1)S(1)}, u32[]{:S(2)}, u32[]{:S(2)}) collective-permute-start(bf16[2,64,512]{2,1,0:T(8,128)(2,1)S(1)} %get-tuple-element.28), channel_id=1, source_target_pairs={{0,6},{1,7},{2,4},{3,5},{4,2},{5,3},{6,0},{7,1},{8,14},{9,15},{10,... | collective-permute-start | bytes 393224 | tf_op jit(solution)/shard_map/ppermute | solution.py:322
  10.3 0.4 %collective-permute-start.5 = (bf16[2,64,512]{2,1,0:T(8,128)(2,1)S(1)}, bf16[2,64,512]{2,1,0:T(8,128)(2,1)S(1)}, u32[]{:S(2)}, u32[]{:S(2)}) collective-permute-start(bf16[2,64,512]{2,1,0:T(8,128)(2,1)S(1)} %get-tuple-element.40), channel_id=1, source_target_pairs={{0,4},{1,5},{2,6},{3,7},{4,0},{5,1},{6,2},{7,3},{8,12},{9,13},{10,... | collective-permute-start | bytes 393224 | tf_op jit(solution)/shard_map/ppermute | solution.py:322
  10.7 1.6 %copy-done = bf16[1,4,32,64,128]{4,3,2,1,0:T(8,128)(2,1)S(1)} copy-done((bf16[1,4,32,64,128]{4,3,2,1,0:T(8,128)(2,1)S(1)}, bf16[1,4,32,64,128]{4,3,2,1,0:T(8,128)(2,1)}, u32[]{:S(2)}) %copy-start) | copy-done | bytes 2097176
  12.3 0.7 %prepare_block.2 = (bf16[2048,512]{1,0:T(8,128)(2,1)S(1)}, bf16[512,2048]{1,0:T(8,128)(2,1)S(1)}) custom-call(bf16[1,4,32,64,128]{4,3,2,1,0:T(8,128)(2,1)S(1)} %copy-done), custom_call_target="tpu_custom_call" | custom-call | tf_op jit(solution)/shard_map/prepare_block/pallas_call | solution.py:35
  13.0 0.4 %collective-permute-done.theta_ref = bf16[1,64,1280]{2,1,0:T(8,128)(2,1)S(1)} collective-permute-done((bf16[1,64,1280]{2,1,0:T(8,128)(2,1)}, bf16[1,64,1280]{2,1,0:T(8,128)(2,1)S(1)}, u32[]{:S(2)}, u32[]{:S(2)}) %collective-permute-start) | collective-permute-done | bytes 163872 | tf_op jit(solution)/shard_map/ppermute | solution.py:322
  13.4 0.0 collective-permute-done.1.chol_ref
  13.4 0.0 copy-done.3
  13.4 0.7 %pick_tiles.3 = (bf16[2,64,512]{2,1,0:T(8,128)(2,1)S(1)}, bf16[2,64,512]{2,1,0:T(8,128)(2,1)S(1)}, bf16[2,64,512]{2,1,0:T(8,128)(2,1)S(1)}, bf16[2,64,512]{2,1,0:T(8,128)(2,1)S(1)}) custom-call(s32[4,16]{1,0:T(4,128)S(1)} %bitcast.3, bf16[1,64,1280]{2,1,0:T(8,128)(2,1)S(1)} %collective-permute-done.theta_ref), custom_call_target="tpu_custom_call" | custom-call | tf_op jit(solution)/shard_map/pick_tiles/pallas_call | solution.py:63
  14.2 0.0 collective-permute-done.4.refs_7_
  14.2 2.6 %collective-permute-start.6 = (bf16[2,64,512]{2,1,0:T(8,128)(2,1)S(1)}, bf16[2,64,512]{2,1,0:T(8,128)(2,1)S(1)}, u32[]{:S(2)}, u32[]{:S(2)}) collective-permute-start(bf16[2,64,512]{2,1,0:T(8,128)(2,1)S(1)} %get-tuple-element.45), channel_id=1, source_target_pairs={{0,4},{1,5},{2,6},{3,7},{4,0},{5,1},{6,2},{7,3},{8,12},{9,13},{10,... | collective-permute-start | bytes 393224 | tf_op jit(solution)/shard_map/ppermute | solution.py:322
  16.8 1.4 %collective-permute-start.7 = (bf16[2,64,512]{2,1,0:T(8,128)(2,1)S(1)}, bf16[2,64,512]{2,1,0:T(8,128)(2,1)S(1)}, u32[]{:S(2)}, u32[]{:S(2)}) collective-permute-start(bf16[2,64,512]{2,1,0:T(8,128)(2,1)S(1)} %get-tuple-element.46), channel_id=1, source_target_pairs={{0,6},{1,7},{2,4},{3,5},{4,2},{5,3},{6,0},{7,1},{8,14},{9,15},{10,... | collective-permute-start | bytes 393224 | tf_op jit(solution)/shard_map/ppermute | solution.py:322
  18.2 0.6 %collective-permute-start.8 = (bf16[2,64,512]{2,1,0:T(8,128)(2,1)S(1)}, bf16[2,64,512]{2,1,0:T(8,128)(2,1)S(1)}, u32[]{:S(2)}, u32[]{:S(2)}) collective-permute-start(bf16[2,64,512]{2,1,0:T(8,128)(2,1)S(1)} %get-tuple-element.47), channel_id=1, source_target_pairs={{0,2},{1,3},{2,0},{3,1},{4,6},{5,7},{6,4},{7,5},{8,10},{9,11},{10,... | collective-permute-start | bytes 393224 | tf_op jit(solution)/shard_map/ppermute | solution.py:322
  18.7 0.0 collective-permute-done.2.refs_9_
  18.7 0.0 copy-done.4
  18.7 0.0 collective-permute-start.3
  18.7 0.7 %prepare_block.3 = (bf16[2048,512]{1,0:T(8,128)(2,1)S(1)}, bf16[512,2048]{1,0:T(8,128)(2,1)S(1)}) custom-call(bf16[1,4,32,64,128]{4,3,2,1,0:T(8,128)(2,1)S(1)} %collective-permute-done.1.chol_ref), custom_call_target="tpu_custom_call" | custom-call | tf_op jit(solution)/shard_map/prepare_block/pallas_call | solution.py:35
  19.5 0.0 collective-permute-done.5.refs_8_
  19.5 0.4 %collective-permute-done.3.refs_1_ = s32[1,4]{1,0:T(1,128)S(1)} collective-permute-done((s32[1,4]{1,0:T(1,128)S(1)}, s32[1,4]{1,0:T(1,128)S(1)}, u32[]{:S(2)}, u32[]{:S(2)}) %collective-permute-start.3) | collective-permute-done | bytes 48 | tf_op jit(solution)/shard_map/ppermute | solution.py:325
  19.9 2.8 %chip_terms.2 = (f32[8,1,128]{2,1,0:T(1,128)S(1)}, f32[2,512]{1,0:T(2,128)S(1)}) custom-call(s32[1,4]{1,0:T(1,128)S(1)} %copy-done.4, s32[1,4]{1,0:T(1,128)S(1)} %collective-permute-done.3.refs_1_, bf16[2048,512]{1,0:T(8,128)(2,1)S(1)} %get-tuple-element.30.refs_2_, bf16[512,2048]{1,0:T(8,128)(2,1)S(1)} %get-tuple-element.31.refs_3_, ...), custom_call_target="tpu_custom_call" | custom-call | tf_op jit(solution)/shard_map/chip_terms/pallas_call | solution.py:248
  22.6 0.0 collective-permute-done.6.refs_7_
  22.6 3.1 %collective-permute-done.7.refs_8_ = bf16[2,64,512]{2,1,0:T(8,128)(2,1)S(1)} collective-permute-done((bf16[2,64,512]{2,1,0:T(8,128)(2,1)S(1)}, bf16[2,64,512]{2,1,0:T(8,128)(2,1)S(1)}, u32[]{:S(2)}, u32[]{:S(2)}) %collective-permute-start.7) | collective-permute-done | bytes 131104 | tf_op jit(solution)/shard_map/ppermute | solution.py:322
  25.7 0.2 collective-permute-done.8.refs_9_
  25.9 2.4 %chip_terms.3 = f32[8,1,128]{2,1,0:T(1,128)S(1)} custom-call(f32[2,512]{1,0:T(2,128)S(1)} %get-tuple-element.42.refs_0_, f32[8,1,128]{2,1,0:T(1,128)S(1)} %get-tuple-element.43.refs_1_, bf16[2048,512]{1,0:T(8,128)(2,1)S(1)} %get-tuple-element.30.refs_2_, bf16[512,2048]{1,0:T(8,128)(2,1)S(1)} %get-tuple-element.31.refs_3_, ...), custom_call_target="tpu_custom_call" | custom-call | tf_op jit(solution)/shard_map/chip_terms/pallas_call | solution.py:248
  28.3 8.4 %all_to_all.5.rows_ref = f32[8,1,128]{2,1,0:T(1,128)} all-to-all(f32[8,1,128]{2,1,0:T(1,128)S(1)} %chip_terms.3), channel_id=1, replica_groups={{8,10,12,14,0,2,4,6},{9,11,13,15,1,3,5,7},{24,26,28,30,16,18,20,22},{25..., dimensions={0} | all-to-all | bytes 8192 | tf_op jit(solution)/shard_map/all_to_all | solution.py:349
  36.7 1.4 %finish.1 = (f32[1,512]{1,0:T(1,128)}, f32[1,1]{1,0:T(1,128)}) custom-call(f32[8,1,128]{2,1,0:T(1,128)} %all_to_all.5.rows_ref), custom_call_target="tpu_custom_call" | custom-call | tf_op jit(solution)/shard_map/finish/pallas_call | solution.py:299
  (4 shorter events, 0.0 us)
Async XLA Ops:
  0.6 18.1 %copy-start.4 = (s32[1,4]{1,0:T(1,128)S(1)}, s32[1,4]{1,0:T(1,128)}, u32[]{:S(2)}) copy-start(s32[1,4]{1,0:T(1,128)} %refs_0_.1) | copy-start | bytes 52
  0.6 12.8 %collective-permute-start.1 = (bf16[1,4,32,64,128]{4,3,2,1,0:T(8,128)(2,1)}, bf16[1,4,32,64,128]{4,3,2,1,0:T(8,128)(2,1)S(1)}, u32[]{:S(2)}, u32[]{:S(2)}) collective-permute-start(bf16[1,4,32,64,128]{4,3,2,1,0:T(8,128)(2,1)} %chol_ref.1), channel_id=1, source_target_pairs={{0,1},{1,0},{2,3},{3,2},{4,5},{5,4},{6,7},{7,6},{8,9},{9,8},{10,11... | collective-permute-start | bytes 6291464 | tf_op jit(solution)/shard_map/ppermute | solution.py:325
  1.2 12.3 %collective-permute-start = (bf16[1,64,1280]{2,1,0:T(8,128)(2,1)}, bf16[1,64,1280]{2,1,0:T(8,128)(2,1)S(1)}, u32[]{:S(2)}, u32[]{:S(2)}) collective-permute-start(bf16[1,64,1280]{2,1,0:T(8,128)(2,1)} %theta_ref.1), channel_id=1, source_target_pairs={{0,8},{1,9},{2,10},{3,11},{4,12},{5,13},{6,14},{7,15},{8,0},{9,1},... | collective-permute-start | bytes 491528 | tf_op jit(solution)/shard_map/ppermute | solution.py:322
  4.8 0.9 %copy-start.1 = (bf16[1,64,1280]{2,1,0:T(8,128)(2,1)S(1)}, bf16[1,64,1280]{2,1,0:T(8,128)(2,1)}, u32[]{:S(2)}) copy-start(bf16[1,64,1280]{2,1,0:T(8,128)(2,1)} %theta_ref.1) | copy-start | bytes 491524
  5.8 0.7 %copy-start.2 = (s32[16,4]{0,1:T(4,128)S(1)}, s32[16,4]{0,1:T(4,128)}, u32[]{:S(2)}) copy-start(s32[16,4]{0,1:T(4,128)} %param.7) | copy-start | bytes 772
  6.5 7.0 %copy-start.3 = (s32[16,4]{0,1:T(4,128)S(1)}, s32[16,4]{0,1:T(4,128)}, u32[]{:S(2)}) copy-start(s32[16,4]{0,1:T(4,128)} %param.7) | copy-start | bytes 772
  7.2 7.0 %collective-permute-start.4 = (bf16[2,64,512]{2,1,0:T(8,128)(2,1)S(1)}, bf16[2,64,512]{2,1,0:T(8,128)(2,1)S(1)}, u32[]{:S(2)}, u32[]{:S(2)}) collective-permute-start(bf16[2,64,512]{2,1,0:T(8,128)(2,1)S(1)} %get-tuple-element.38), channel_id=1, source_target_pairs={{0,2},{1,3},{2,0},{3,1},{4,6},{5,7},{6,4},{7,5},{8,10},{9,11},{10,... | collective-permute-start | bytes 393224 | tf_op jit(solution)/shard_map/ppermute | solution.py:322
  8.8 10.0 %collective-permute-start.2 = (bf16[2,64,512]{2,1,0:T(8,128)(2,1)S(1)}, bf16[2,64,512]{2,1,0:T(8,128)(2,1)S(1)}, u32[]{:S(2)}, u32[]{:S(2)}) collective-permute-start(bf16[2,64,512]{2,1,0:T(8,128)(2,1)S(1)} %get-tuple-element.28), channel_id=1, source_target_pairs={{0,6},{1,7},{2,4},{3,5},{4,2},{5,3},{6,0},{7,1},{8,14},{9,15},{10,... | collective-permute-start | bytes 393224 | tf_op jit(solution)/shard_map/ppermute | solution.py:322
  10.3 9.2 %collective-permute-start.5 = (bf16[2,64,512]{2,1,0:T(8,128)(2,1)S(1)}, bf16[2,64,512]{2,1,0:T(8,128)(2,1)S(1)}, u32[]{:S(2)}, u32[]{:S(2)}) collective-permute-start(bf16[2,64,512]{2,1,0:T(8,128)(2,1)S(1)} %get-tuple-element.40), channel_id=1, source_target_pairs={{0,4},{1,5},{2,6},{3,7},{4,0},{5,1},{6,2},{7,3},{8,12},{9,13},{10,... | collective-permute-start | bytes 393224 | tf_op jit(solution)/shard_map/ppermute | solution.py:322
  10.7 1.6 %copy-start = (bf16[1,4,32,64,128]{4,3,2,1,0:T(8,128)(2,1)S(1)}, bf16[1,4,32,64,128]{4,3,2,1,0:T(8,128)(2,1)}, u32[]{:S(2)}) copy-start(bf16[1,4,32,64,128]{4,3,2,1,0:T(8,128)(2,1)} %chol_ref.1) | copy-start | bytes 6291460
  14.2 8.5 %collective-permute-start.6 = (bf16[2,64,512]{2,1,0:T(8,128)(2,1)S(1)}, bf16[2,64,512]{2,1,0:T(8,128)(2,1)S(1)}, u32[]{:S(2)}, u32[]{:S(2)}) collective-permute-start(bf16[2,64,512]{2,1,0:T(8,128)(2,1)S(1)} %get-tuple-element.45), channel_id=1, source_target_pairs={{0,4},{1,5},{2,6},{3,7},{4,0},{5,1},{6,2},{7,3},{8,12},{9,13},{10,... | collective-permute-start | bytes 393224 | tf_op jit(solution)/shard_map/ppermute | solution.py:322
  16.8 8.9 %collective-permute-start.7 = (bf16[2,64,512]{2,1,0:T(8,128)(2,1)S(1)}, bf16[2,64,512]{2,1,0:T(8,128)(2,1)S(1)}, u32[]{:S(2)}, u32[]{:S(2)}) collective-permute-start(bf16[2,64,512]{2,1,0:T(8,128)(2,1)S(1)} %get-tuple-element.46), channel_id=1, source_target_pairs={{0,6},{1,7},{2,4},{3,5},{4,2},{5,3},{6,0},{7,1},{8,14},{9,15},{10,... | collective-permute-start | bytes 393224 | tf_op jit(solution)/shard_map/ppermute | solution.py:322
  18.2 7.8 %collective-permute-start.8 = (bf16[2,64,512]{2,1,0:T(8,128)(2,1)S(1)}, bf16[2,64,512]{2,1,0:T(8,128)(2,1)S(1)}, u32[]{:S(2)}, u32[]{:S(2)}) collective-permute-start(bf16[2,64,512]{2,1,0:T(8,128)(2,1)S(1)} %get-tuple-element.47), channel_id=1, source_target_pairs={{0,2},{1,3},{2,0},{3,1},{4,6},{5,7},{6,4},{7,5},{8,10},{9,11},{10,... | collective-permute-start | bytes 393224 | tf_op jit(solution)/shard_map/ppermute | solution.py:322
  18.7 1.1 %collective-permute-start.3 = (s32[1,4]{1,0:T(1,128)S(1)}, s32[1,4]{1,0:T(1,128)S(1)}, u32[]{:S(2)}, u32[]{:S(2)}) collective-permute-start(s32[1,4]{1,0:T(1,128)S(1)} %copy-done.4), channel_id=1, source_target_pairs={{0,1},{1,0},{2,3},{3,2},{4,5},{5,4},{6,7},{7,6},{8,9},{9,8},{10,11... | collective-permute-start | bytes 56 | tf_op jit(solution)/shard_map/ppermute | solution.py:325

commit v24 on v21

--- a/solution.py
+++ b/solution.py
@@ -218,7 +218,7 @@
             lax.dot_general(segment, part, NT, preferred_element_type=jnp.float32) for part in parts
         )
         for i in range(batch):
-            owner = chip ^ (first + index + i)
+            owner = chip ^ (first + index + i) ^ (out_ref.shape[0] // 2 + 1)
             out_ref[pl.ds(owner, 1), 0, :used + 8] = sums[i:i + 1]
 
     if count == batch:
@@ -262,17 +262,18 @@
 
 def finish_kernel(rows_ref, bias_ref, energy_ref, bias_buf, energy_buf, sems, *, used, scale):
     chips, _, width = rows_ref.shape
+    turn = chips // 2 + 1
     fit = LANES // used if width == LANES else 0
     lane = lax.broadcasted_iota(jnp.int32, (1, width), 1)
     if fit and chips % fit == 0:
         for d in range(0, chips, fit):
-            packed = rows_ref[d]
+            packed = rows_ref[d ^ turn]
             for i in range(1, fit):
-                packed = jnp.where(lane < i * used, packed, pltpu.roll(rows_ref[d + i], i * used, 1))
+                packed = jnp.where(lane < i * used, packed, pltpu.roll(rows_ref[(d + i) ^ turn], i * used, 1))
             bias_buf[:, d * used:(d + fit) * used] = packed
     else:
         for d in range(chips):
-            bias_buf[:, d * used:(d + 1) * used] = rows_ref[d, :, :used]
+            bias_buf[:, d * used:(d + 1) * used] = rows_ref[d ^ turn, :, :used]
     bias_copy = pltpu.make_async_copy(bias_buf, bias_ref, sems.at[0])
     bias_copy.start()
     total = energy_terms(rows_ref[0], used)
@@ -334,7 +335,7 @@
     screens = [screen, to_core(late_screen)]
     rows, masks = chip_terms(screens, [], blocks, near, 0, NEAR, vectors, chips, out_width)
     rows, = chip_terms([], [masks, rows], blocks, beyond, half, BEYOND, vectors, chips, out_width)
-    same_core = [list(range(core, groups, CORES)) for core in range(CORES)]
+    same_core = [[(rank ^ (half + 1)) * CORES + core for rank in range(chips)] for core in range(CORES)]
     back = lax.all_to_all(rows, "chol", split_axis=0, concat_axis=0, tiled=True, axis_index_groups=same_core)
     return finish(back, used, 1.0 / (2.0 * occupied * occupied))
 

time: 39.6 us -> 38 us (0.960)
  blocking collectives: 10.1 us -> 8.39 us
    all_to_all x1, blocking collectives: 10.1 us -> 8.39 us  [body(): lax.all_to_all(rows, 'chol', split_axis=0, concat_axis=0, tiled=True, axi...]
  transfers between devices with their start and end apart: 9 -> 9, of which waited for: 3 -> 3; matrix products, arithmetic and copies ran while one was open for 0% -> 0% of each run, Pallas kernels for 14% -> 15%
where the time goes in v24:
time: 38 us; the launch traced here: 37.7 us
  starting transfers between devices  13.2 us (35%)
  Pallas kernels  9.35 us (25%)
  blocking collectives  8.39 us (22%)
  local copies, waits for them, and re-layouts  3.23 us (8%)
  waiting for transfers between devices  2.85 us (8%)
  between operations  0.72 us (2%)
    ppermute x7, starting transfers between devices, to_chip(): lax.ppermute(x, 'chol', [(i, i ^ offset * CORES) for i in range(groups)])  12.6 us
    all_to_all x1, blocking collectives, body(): lax.all_to_all(rows, 'chol', split_axis=0, concat_axis=0, tiled=True, axi...  8.39 us
    pallas_call x2, Pallas kernels, chip_terms(): pl.pallas_call(functools.partial(terms_kernel, first=first, count=count,...  5.12 us
    unnamed x10, local copies, waits for them, and re-layouts  3.23 us
    ppermute x7, waiting for transfers between devices, to_chip(): lax.ppermute(x, 'chol', [(i, i ^ offset * CORES) for i in range(groups)])  1.75 us
    pallas_call x2, Pallas kernels, pick_tiles(): pl.pallas_call(pick_kernel, in_specs=[SMEM, VMEM], out_specs=[VMEM] * cou...  1.43 us
    pallas_call x2, Pallas kernels, prepare_block(): pl.pallas_call(prepare_kernel, in_specs=[VMEM], out_specs=[VMEM, VMEM], o...  1.43 us
    pallas_call x1, Pallas kernels, finish(): pl.pallas_call(functools.partial(finish_kernel, used=used, scale=scale),...  1.37 us
  transfers between devices with their start and end apart: 9, of which 3 were waited for; matrix products, arithmetic and copies ran while one was open for 0% of the time, Pallas kernels for 15%

profile of v24, /device:TPU:0, one launch (start us, length us, event | category | flops | bytes accessed | tf_op | source)
XLA Modules:
  0.0 37.7 jit_solution(5982641017061675438)
XLA Ops:
  0.6 0.5 %collective-permute-start.2 = (bf16[1,4,32,64,128]{4,3,2,1,0:T(8,128)(2,1)}, bf16[1,4,32,64,128]{4,3,2,1,0:T(8,128)(2,1)S(1)}, u32[]{:S(2)}, u32[]{:S(2)}) collective-permute-start(bf16[1,4,32,64,128]{4,3,2,1,0:T(8,128)(2,1)} %chol_ref.1), channel_id=1, source_target_pairs={{0,1},{1,0},{2,3},{3,2},{4,5},{5,4},{6,7},{7,6},{8,9},{9,8},{10,11... | collective-permute-start | bytes 6291464 | tf_op jit(solution)/shard_map/ppermute | solution.py:318
  1.1 3.7 %collective-permute-start = (bf16[1,64,1280]{2,1,0:T(8,128)(2,1)}, bf16[1,64,1280]{2,1,0:T(8,128)(2,1)S(1)}, u32[]{:S(2)}, u32[]{:S(2)}) collective-permute-start(bf16[1,64,1280]{2,1,0:T(8,128)(2,1)} %theta_ref.1), channel_id=1, source_target_pairs={{0,8},{1,9},{2,10},{3,11},{4,12},{5,13},{6,14},{7,15},{8,0},{9,1},... | collective-permute-start | bytes 491528 | tf_op jit(solution)/shard_map/ppermute | solution.py:315
  4.8 0.9 %copy-done.1 = bf16[1,64,1280]{2,1,0:T(8,128)(2,1)S(1)} copy-done((bf16[1,64,1280]{2,1,0:T(8,128)(2,1)S(1)}, bf16[1,64,1280]{2,1,0:T(8,128)(2,1)}, u32[]{:S(2)}) %copy-start.1) | copy-done | bytes 163864
  5.8 0.7 %copy-done.2 = s32[16,4]{0,1:T(4,128)S(1)} copy-done((s32[16,4]{0,1:T(4,128)S(1)}, s32[16,4]{0,1:T(4,128)}, u32[]{:S(2)}) %copy-start.2) | copy-done | bytes 280
  6.4 0.0 copy-start.3
  6.4 0.7 %pick_tiles.2 = (bf16[2,64,512]{2,1,0:T(8,128)(2,1)S(1)}, bf16[2,64,512]{2,1,0:T(8,128)(2,1)S(1)}, bf16[2,64,512]{2,1,0:T(8,128)(2,1)S(1)}, bf16[2,64,512]{2,1,0:T(8,128)(2,1)S(1)}) custom-call(s32[4,16]{1,0:T(4,128)S(1)} %bitcast.2, bf16[1,64,1280]{2,1,0:T(8,128)(2,1)S(1)} %copy-done.1), custom_call_target="tpu_custom_call" | custom-call | tf_op jit(solution)/shard_map/pick_tiles/pallas_call | solution.py:63
  7.2 1.6 %collective-permute-start.1 = (bf16[2,64,512]{2,1,0:T(8,128)(2,1)S(1)}, bf16[2,64,512]{2,1,0:T(8,128)(2,1)S(1)}, u32[]{:S(2)}, u32[]{:S(2)}) collective-permute-start(bf16[2,64,512]{2,1,0:T(8,128)(2,1)S(1)} %get-tuple-element.25), channel_id=1, source_target_pairs={{0,2},{1,3},{2,0},{3,1},{4,6},{5,7},{6,4},{7,5},{8,10},{9,11},{10,... | collective-permute-start | bytes 393224 | tf_op jit(solution)/shard_map/ppermute | solution.py:315
  8.8 1.5 %collective-permute-start.3 = (bf16[2,64,512]{2,1,0:T(8,128)(2,1)S(1)}, bf16[2,64,512]{2,1,0:T(8,128)(2,1)S(1)}, u32[]{:S(2)}, u32[]{:S(2)}) collective-permute-start(bf16[2,64,512]{2,1,0:T(8,128)(2,1)S(1)} %get-tuple-element.28), channel_id=1, source_target_pairs={{0,6},{1,7},{2,4},{3,5},{4,2},{5,3},{6,0},{7,1},{8,14},{9,15},{10,... | collective-permute-start | bytes 393224 | tf_op jit(solution)/shard_map/ppermute | solution.py:315
  10.3 0.4 %collective-permute-start.5 = (bf16[2,64,512]{2,1,0:T(8,128)(2,1)S(1)}, bf16[2,64,512]{2,1,0:T(8,128)(2,1)S(1)}, u32[]{:S(2)}, u32[]{:S(2)}) collective-permute-start(bf16[2,64,512]{2,1,0:T(8,128)(2,1)S(1)} %get-tuple-element.37), channel_id=1, source_target_pairs={{0,4},{1,5},{2,6},{3,7},{4,0},{5,1},{6,2},{7,3},{8,12},{9,13},{10,... | collective-permute-start | bytes 393224 | tf_op jit(solution)/shard_map/ppermute | solution.py:315
  10.7 1.6 %copy-done = bf16[1,4,32,64,128]{4,3,2,1,0:T(8,128)(2,1)S(1)} copy-done((bf16[1,4,32,64,128]{4,3,2,1,0:T(8,128)(2,1)S(1)}, bf16[1,4,32,64,128]{4,3,2,1,0:T(8,128)(2,1)}, u32[]{:S(2)}) %copy-start) | copy-done | bytes 2097176
  12.3 0.7 %prepare_block.2 = (bf16[2048,512]{1,0:T(8,128)(2,1)S(1)}, bf16[512,2048]{1,0:T(8,128)(2,1)S(1)}) custom-call(bf16[1,4,32,64,128]{4,3,2,1,0:T(8,128)(2,1)S(1)} %copy-done), custom_call_target="tpu_custom_call" | custom-call | tf_op jit(solution)/shard_map/prepare_block/pallas_call | solution.py:35
  13.0 0.0 collective-permute-done.1.refs_7_
  13.0 0.4 collective-permute-done.theta_ref
  13.4 0.0 collective-permute-done.2.chol_ref
  13.4 0.0 copy-done.3
  13.4 0.7 %pick_tiles.3 = (bf16[2,64,512]{2,1,0:T(8,128)(2,1)S(1)}, bf16[2,64,512]{2,1,0:T(8,128)(2,1)S(1)}, bf16[2,64,512]{2,1,0:T(8,128)(2,1)S(1)}, bf16[2,64,512]{2,1,0:T(8,128)(2,1)S(1)}) custom-call(s32[4,16]{1,0:T(4,128)S(1)} %bitcast.3, bf16[1,64,1280]{2,1,0:T(8,128)(2,1)S(1)} %collective-permute-done.theta_ref), custom_call_target="tpu_custom_call" | custom-call | tf_op jit(solution)/shard_map/pick_tiles/pallas_call | solution.py:63
  14.2 1.7 %collective-permute-start.6 = (bf16[2,64,512]{2,1,0:T(8,128)(2,1)S(1)}, bf16[2,64,512]{2,1,0:T(8,128)(2,1)S(1)}, u32[]{:S(2)}, u32[]{:S(2)}) collective-permute-start(bf16[2,64,512]{2,1,0:T(8,128)(2,1)S(1)} %get-tuple-element.43), channel_id=1, source_target_pairs={{0,2},{1,3},{2,0},{3,1},{4,6},{5,7},{6,4},{7,5},{8,10},{9,11},{10,... | collective-permute-start | bytes 393224 | tf_op jit(solution)/shard_map/ppermute | solution.py:315
  15.8 3.7 %collective-permute-start.7 = (bf16[2,64,512]{2,1,0:T(8,128)(2,1)S(1)}, bf16[2,64,512]{2,1,0:T(8,128)(2,1)S(1)}, u32[]{:S(2)}, u32[]{:S(2)}) collective-permute-start(bf16[2,64,512]{2,1,0:T(8,128)(2,1)S(1)} %get-tuple-element.44), channel_id=1, source_target_pairs={{0,4},{1,5},{2,6},{3,7},{4,0},{5,1},{6,2},{7,3},{8,12},{9,13},{10,... | collective-permute-start | bytes 393224 | tf_op jit(solution)/shard_map/ppermute | solution.py:315
  19.5 0.0 collective-permute-start.8
  19.5 0.0 collective-permute-done.3.refs_9_
  19.5 0.7 %prepare_block.3 = (bf16[2048,512]{1,0:T(8,128)(2,1)S(1)}, bf16[512,2048]{1,0:T(8,128)(2,1)S(1)}) custom-call(bf16[1,4,32,64,128]{4,3,2,1,0:T(8,128)(2,1)S(1)} %collective-permute-done.2.chol_ref), custom_call_target="tpu_custom_call" | custom-call | tf_op jit(solution)/shard_map/prepare_block/pallas_call | solution.py:35
  20.2 0.0 copy-done.4
  20.2 0.1 collective-permute-start.4
  20.3 0.0 collective-permute-done.5.refs_8_
  20.3 1.1 %collective-permute-done.4.refs_1_ = s32[1,4]{1,0:T(1,128)S(1)} collective-permute-done((s32[1,4]{1,0:T(1,128)S(1)}, s32[1,4]{1,0:T(1,128)S(1)}, u32[]{:S(2)}, u32[]{:S(2)}) %collective-permute-start.4) | collective-permute-done | bytes 48 | tf_op jit(solution)/shard_map/ppermute | solution.py:318
  21.4 2.8 %chip_terms.2 = (f32[8,1,128]{2,1,0:T(1,128)S(1)}, f32[2,512]{1,0:T(2,128)S(1)}) custom-call(s32[1,4]{1,0:T(1,128)S(1)} %copy-done.4, s32[1,4]{1,0:T(1,128)S(1)} %collective-permute-done.4.refs_1_, bf16[2048,512]{1,0:T(8,128)(2,1)S(1)} %get-tuple-element.30.refs_2_, bf16[512,2048]{1,0:T(8,128)(2,1)S(1)} %get-tuple-element.31.refs_3_, ...), custom_call_target="tpu_custom_call" | custom-call | tf_op jit(solution)/shard_map/chip_terms/pallas_call | solution.py:241
  24.2 0.0 collective-permute-done.6.refs_7_
  24.2 0.0 collective-permute-done.7.refs_8_
  24.2 1.3 %collective-permute-done.8.refs_9_ = bf16[2,64,512]{2,1,0:T(8,128)(2,1)S(1)} collective-permute-done((bf16[2,64,512]{2,1,0:T(8,128)(2,1)S(1)}, bf16[2,64,512]{2,1,0:T(8,128)(2,1)S(1)}, u32[]{:S(2)}, u32[]{:S(2)}) %collective-permute-start.8) | collective-permute-done | bytes 131104 | tf_op jit(solution)/shard_map/ppermute | solution.py:315
  25.6 2.4 %chip_terms.3 = f32[8,1,128]{2,1,0:T(1,128)S(1)} custom-call(f32[2,512]{1,0:T(2,128)S(1)} %get-tuple-element.39.refs_0_, f32[8,1,128]{2,1,0:T(1,128)S(1)} %get-tuple-element.40.refs_1_, bf16[2048,512]{1,0:T(8,128)(2,1)S(1)} %get-tuple-element.30.refs_2_, bf16[512,2048]{1,0:T(8,128)(2,1)S(1)} %get-tuple-element.31.refs_3_, ...), custom_call_target="tpu_custom_call" | custom-call | tf_op jit(solution)/shard_map/chip_terms/pallas_call | solution.py:241
  27.9 8.4 %all_to_all.5.rows_ref = f32[8,1,128]{2,1,0:T(1,128)} all-to-all(f32[8,1,128]{2,1,0:T(1,128)S(1)} %chip_terms.3), channel_id=1, replica_groups={{10,8,14,12,2,0,6,4},{11,9,15,13,3,1,7,5},{26,24,30,28,18,16,22,20},{27..., dimensions={0} | all-to-all | bytes 8192 | tf_op jit(solution)/shard_map/all_to_all | solution.py:339
  36.3 1.4 %finish.1 = (f32[1,512]{1,0:T(1,128)}, f32[1,1]{1,0:T(1,128)}) custom-call(f32[8,1,128]{2,1,0:T(1,128)} %all_to_all.5.rows_ref), custom_call_target="tpu_custom_call" | custom-call | tf_op jit(solution)/shard_map/finish/pallas_call | solution.py:292
  (4 shorter events, 0.0 us)
Async XLA Ops:
  0.6 12.8 %collective-permute-start.2 = (bf16[1,4,32,64,128]{4,3,2,1,0:T(8,128)(2,1)}, bf16[1,4,32,64,128]{4,3,2,1,0:T(8,128)(2,1)S(1)}, u32[]{:S(2)}, u32[]{:S(2)}) collective-permute-start(bf16[1,4,32,64,128]{4,3,2,1,0:T(8,128)(2,1)} %chol_ref.1), channel_id=1, source_target_pairs={{0,1},{1,0},{2,3},{3,2},{4,5},{5,4},{6,7},{7,6},{8,9},{9,8},{10,11... | collective-permute-start | bytes 6291464 | tf_op jit(solution)/shard_map/ppermute | solution.py:318
  1.1 12.3 %collective-permute-start = (bf16[1,64,1280]{2,1,0:T(8,128)(2,1)}, bf16[1,64,1280]{2,1,0:T(8,128)(2,1)S(1)}, u32[]{:S(2)}, u32[]{:S(2)}) collective-permute-start(bf16[1,64,1280]{2,1,0:T(8,128)(2,1)} %theta_ref.1), channel_id=1, source_target_pairs={{0,8},{1,9},{2,10},{3,11},{4,12},{5,13},{6,14},{7,15},{8,0},{9,1},... | collective-permute-start | bytes 491528 | tf_op jit(solution)/shard_map/ppermute | solution.py:315
  4.8 0.9 %copy-start.1 = (bf16[1,64,1280]{2,1,0:T(8,128)(2,1)S(1)}, bf16[1,64,1280]{2,1,0:T(8,128)(2,1)}, u32[]{:S(2)}) copy-start(bf16[1,64,1280]{2,1,0:T(8,128)(2,1)} %theta_ref.1) | copy-start | bytes 491524
  5.8 0.7 %copy-start.2 = (s32[16,4]{0,1:T(4,128)S(1)}, s32[16,4]{0,1:T(4,128)}, u32[]{:S(2)}) copy-start(s32[16,4]{0,1:T(4,128)} %param.7) | copy-start | bytes 772
  6.4 7.0 %copy-start.3 = (s32[16,4]{0,1:T(4,128)S(1)}, s32[16,4]{0,1:T(4,128)}, u32[]{:S(2)}) copy-start(s32[16,4]{0,1:T(4,128)} %param.7) | copy-start | bytes 772
  7.2 5.9 %collective-permute-start.1 = (bf16[2,64,512]{2,1,0:T(8,128)(2,1)S(1)}, bf16[2,64,512]{2,1,0:T(8,128)(2,1)S(1)}, u32[]{:S(2)}, u32[]{:S(2)}) collective-permute-start(bf16[2,64,512]{2,1,0:T(8,128)(2,1)S(1)} %get-tuple-element.25), channel_id=1, source_target_pairs={{0,2},{1,3},{2,0},{3,1},{4,6},{5,7},{6,4},{7,5},{8,10},{9,11},{10,... | collective-permute-start | bytes 393224 | tf_op jit(solution)/shard_map/ppermute | solution.py:315
  8.8 10.8 %collective-permute-start.3 = (bf16[2,64,512]{2,1,0:T(8,128)(2,1)S(1)}, bf16[2,64,512]{2,1,0:T(8,128)(2,1)S(1)}, u32[]{:S(2)}, u32[]{:S(2)}) collective-permute-start(bf16[2,64,512]{2,1,0:T(8,128)(2,1)S(1)} %get-tuple-element.28), channel_id=1, source_target_pairs={{0,6},{1,7},{2,4},{3,5},{4,2},{5,3},{6,0},{7,1},{8,14},{9,15},{10,... | collective-permute-start | bytes 393224 | tf_op jit(solution)/shard_map/ppermute | solution.py:315
  10.3 10.1 %collective-permute-start.5 = (bf16[2,64,512]{2,1,0:T(8,128)(2,1)S(1)}, bf16[2,64,512]{2,1,0:T(8,128)(2,1)S(1)}, u32[]{:S(2)}, u32[]{:S(2)}) collective-permute-start(bf16[2,64,512]{2,1,0:T(8,128)(2,1)S(1)} %get-tuple-element.37), channel_id=1, source_target_pairs={{0,4},{1,5},{2,6},{3,7},{4,0},{5,1},{6,2},{7,3},{8,12},{9,13},{10,... | collective-permute-start | bytes 393224 | tf_op jit(solution)/shard_map/ppermute | solution.py:315
  10.7 1.6 %copy-start = (bf16[1,4,32,64,128]{4,3,2,1,0:T(8,128)(2,1)S(1)}, bf16[1,4,32,64,128]{4,3,2,1,0:T(8,128)(2,1)}, u32[]{:S(2)}) copy-start(bf16[1,4,32,64,128]{4,3,2,1,0:T(8,128)(2,1)} %chol_ref.1) | copy-start | bytes 6291460
  12.3 7.9 %copy-start.4 = (s32[1,4]{1,0:T(1,128)S(1)}, s32[1,4]{1,0:T(1,128)}, u32[]{:S(2)}) copy-start(s32[1,4]{1,0:T(1,128)} %refs_0_.1) | copy-start | bytes 52
  14.2 10.1 %collective-permute-start.6 = (bf16[2,64,512]{2,1,0:T(8,128)(2,1)S(1)}, bf16[2,64,512]{2,1,0:T(8,128)(2,1)S(1)}, u32[]{:S(2)}, u32[]{:S(2)}) collective-permute-start(bf16[2,64,512]{2,1,0:T(8,128)(2,1)S(1)} %get-tuple-element.43), channel_id=1, source_target_pairs={{0,2},{1,3},{2,0},{3,1},{4,6},{5,7},{6,4},{7,5},{8,10},{9,11},{10,... | collective-permute-start | bytes 393224 | tf_op jit(solution)/shard_map/ppermute | solution.py:315
  15.8 8.4 %collective-permute-start.7 = (bf16[2,64,512]{2,1,0:T(8,128)(2,1)S(1)}, bf16[2,64,512]{2,1,0:T(8,128)(2,1)S(1)}, u32[]{:S(2)}, u32[]{:S(2)}) collective-permute-start(bf16[2,64,512]{2,1,0:T(8,128)(2,1)S(1)} %get-tuple-element.44), channel_id=1, source_target_pairs={{0,4},{1,5},{2,6},{3,7},{4,0},{5,1},{6,2},{7,3},{8,12},{9,13},{10,... | collective-permute-start | bytes 393224 | tf_op jit(solution)/shard_map/ppermute | solution.py:315
  19.5 6.1 %collective-permute-start.8 = (bf16[2,64,512]{2,1,0:T(8,128)(2,1)S(1)}, bf16[2,64,512]{2,1,0:T(8,128)(2,1)S(1)}, u32[]{:S(2)}, u32[]{:S(2)}) collective-permute-start(bf16[2,64,512]{2,1,0:T(8,128)(2,1)S(1)} %get-tuple-element.45), channel_id=1, source_target_pairs={{0,6},{1,7},{2,4},{3,5},{4,2},{5,3},{6,0},{7,1},{8,14},{9,15},{10,... | collective-permute-start | bytes 393224 | tf_op jit(solution)/shard_map/ppermute | solution.py:315
  20.2 1.2 %collective-permute-start.4 = (s32[1,4]{1,0:T(1,128)S(1)}, s32[1,4]{1,0:T(1,128)S(1)}, u32[]{:S(2)}, u32[]{:S(2)}) collective-permute-start(s32[1,4]{1,0:T(1,128)S(1)} %copy-done.4), channel_id=1, source_target_pairs={{0,1},{1,0},{2,3},{3,2},{4,5},{5,4},{6,7},{7,6},{8,9},{9,8},{10,11... | collective-permute-start | bytes 56 | tf_op jit(solution)/shard_map/ppermute | solution.py:318

commit v25 on v24

--- a/solution.py
+++ b/solution.py
@@ -218,7 +218,7 @@
             lax.dot_general(segment, part, NT, preferred_element_type=jnp.float32) for part in parts
         )
         for i in range(batch):
-            owner = chip ^ (first + index + i) ^ (out_ref.shape[0] // 2 + 1)
+            owner = chip ^ (first + index + i) ^ (out_ref.shape[0] // 4 + 1)
             out_ref[pl.ds(owner, 1), 0, :used + 8] = sums[i:i + 1]
 
     if count == batch:
@@ -262,7 +262,7 @@
 
 def finish_kernel(rows_ref, bias_ref, energy_ref, bias_buf, energy_buf, sems, *, used, scale):
     chips, _, width = rows_ref.shape
-    turn = chips // 2 + 1
+    turn = chips // 4 + 1
     fit = LANES // used if width == LANES else 0
     lane = lax.broadcasted_iota(jnp.int32, (1, width), 1)
     if fit and chips % fit == 0:
@@ -335,7 +335,7 @@
     screens = [screen, to_core(late_screen)]
     rows, masks = chip_terms(screens, [], blocks, near, 0, NEAR, vectors, chips, out_width)
     rows, = chip_terms([], [masks, rows], blocks, beyond, half, BEYOND, vectors, chips, out_width)
-    same_core = [[(rank ^ (half + 1)) * CORES + core for rank in range(chips)] for core in range(CORES)]
+    same_core = [[(rank ^ (half // 2 + 1)) * CORES + core for rank in range(chips)] for core in range(CORES)]
     back = lax.all_to_all(rows, "chol", split_axis=0, concat_axis=0, tiled=True, axis_index_groups=same_core)
     return finish(back, used, 1.0 / (2.0 * occupied * occupied))
 

time: 38 us -> 38.9 us (1.024)
  blocking collectives: 8.39 us -> 9.29 us
    all_to_all x1, blocking collectives: 8.39 us -> 9.29 us  [body(): lax.all_to_all(rows, 'chol', split_axis=0, concat_axis=0, tiled=True, axi...]
where the time goes in v25:
time: 38.9 us; the launch traced here: 38.6 us
  starting transfers between devices  13.2 us (34%)
  Pallas kernels  9.35 us (24%)
  blocking collectives  9.29 us (24%)
  local copies, waits for them, and re-layouts  3.23 us (8%)
  waiting for transfers between devices  2.85 us (7%)
  between operations  0.72 us (2%)
    ppermute x7, starting transfers between devices, to_chip(): lax.ppermute(x, 'chol', [(i, i ^ offset * CORES) for i in range(groups)])  12.6 us
    all_to_all x1, blocking collectives, body(): lax.all_to_all(rows, 'chol', split_axis=0, concat_axis=0, tiled=True, axi...  9.29 us
    pallas_call x2, Pallas kernels, chip_terms(): pl.pallas_call(functools.partial(terms_kernel, first=first, count=count,...  5.12 us
    unnamed x10, local copies, waits for them, and re-layouts  3.23 us
    ppermute x7, waiting for transfers between devices, to_chip(): lax.ppermute(x, 'chol', [(i, i ^ offset * CORES) for i in range(groups)])  1.75 us
    pallas_call x2, Pallas kernels, pick_tiles(): pl.pallas_call(pick_kernel, in_specs=[SMEM, VMEM], out_specs=[VMEM] * cou...  1.43 us
    pallas_call x2, Pallas kernels, prepare_block(): pl.pallas_call(prepare_kernel, in_specs=[VMEM], out_specs=[VMEM, VMEM], o...  1.43 us
    pallas_call x1, Pallas kernels, finish(): pl.pallas_call(functools.partial(finish_kernel, used=used, scale=scale),...  1.37 us
  transfers between devices with their start and end apart: 9, of which 3 were waited for; matrix products, arithmetic and copies ran while one was open for 0% of the time, Pallas kernels for 15%

profile of v25, /device:TPU:0, one launch (start us, length us, event | category | flops | bytes accessed | tf_op | source)
XLA Modules:
  0.0 38.6 jit_solution(6275454821650988866)
XLA Ops:
  0.6 0.5 %collective-permute-start.2 = (bf16[1,4,32,64,128]{4,3,2,1,0:T(8,128)(2,1)}, bf16[1,4,32,64,128]{4,3,2,1,0:T(8,128)(2,1)S(1)}, u32[]{:S(2)}, u32[]{:S(2)}) collective-permute-start(bf16[1,4,32,64,128]{4,3,2,1,0:T(8,128)(2,1)} %chol_ref.1), channel_id=1, source_target_pairs={{0,1},{1,0},{2,3},{3,2},{4,5},{5,4},{6,7},{7,6},{8,9},{9,8},{10,11... | collective-permute-start | bytes 6291464 | tf_op jit(solution)/shard_map/ppermute | solution.py:318
  1.1 3.7 %collective-permute-start = (bf16[1,64,1280]{2,1,0:T(8,128)(2,1)}, bf16[1,64,1280]{2,1,0:T(8,128)(2,1)S(1)}, u32[]{:S(2)}, u32[]{:S(2)}) collective-permute-start(bf16[1,64,1280]{2,1,0:T(8,128)(2,1)} %theta_ref.1), channel_id=1, source_target_pairs={{0,8},{1,9},{2,10},{3,11},{4,12},{5,13},{6,14},{7,15},{8,0},{9,1},... | collective-permute-start | bytes 491528 | tf_op jit(solution)/shard_map/ppermute | solution.py:315
  4.8 0.0 copy-start.1
  4.8 0.9 %copy-done.1 = bf16[1,64,1280]{2,1,0:T(8,128)(2,1)S(1)} copy-done((bf16[1,64,1280]{2,1,0:T(8,128)(2,1)S(1)}, bf16[1,64,1280]{2,1,0:T(8,128)(2,1)}, u32[]{:S(2)}) %copy-start.1) | copy-done | bytes 163864
  5.8 0.7 %copy-done.2 = s32[16,4]{0,1:T(4,128)S(1)} copy-done((s32[16,4]{0,1:T(4,128)S(1)}, s32[16,4]{0,1:T(4,128)}, u32[]{:S(2)}) %copy-start.2) | copy-done | bytes 280
  6.4 0.7 %pick_tiles.2 = (bf16[2,64,512]{2,1,0:T(8,128)(2,1)S(1)}, bf16[2,64,512]{2,1,0:T(8,128)(2,1)S(1)}, bf16[2,64,512]{2,1,0:T(8,128)(2,1)S(1)}, bf16[2,64,512]{2,1,0:T(8,128)(2,1)S(1)}) custom-call(s32[4,16]{1,0:T(4,128)S(1)} %bitcast.2, bf16[1,64,1280]{2,1,0:T(8,128)(2,1)S(1)} %copy-done.1), custom_call_target="tpu_custom_call" | custom-call | tf_op jit(solution)/shard_map/pick_tiles/pallas_call | solution.py:63
  7.2 1.6 %collective-permute-start.1 = (bf16[2,64,512]{2,1,0:T(8,128)(2,1)S(1)}, bf16[2,64,512]{2,1,0:T(8,128)(2,1)S(1)}, u32[]{:S(2)}, u32[]{:S(2)}) collective-permute-start(bf16[2,64,512]{2,1,0:T(8,128)(2,1)S(1)} %get-tuple-element.25), channel_id=1, source_target_pairs={{0,2},{1,3},{2,0},{3,1},{4,6},{5,7},{6,4},{7,5},{8,10},{9,11},{10,... | collective-permute-start | bytes 393224 | tf_op jit(solution)/shard_map/ppermute | solution.py:315
  8.8 1.5 %collective-permute-start.3 = (bf16[2,64,512]{2,1,0:T(8,128)(2,1)S(1)}, bf16[2,64,512]{2,1,0:T(8,128)(2,1)S(1)}, u32[]{:S(2)}, u32[]{:S(2)}) collective-permute-start(bf16[2,64,512]{2,1,0:T(8,128)(2,1)S(1)} %get-tuple-element.28), channel_id=1, source_target_pairs={{0,6},{1,7},{2,4},{3,5},{4,2},{5,3},{6,0},{7,1},{8,14},{9,15},{10,... | collective-permute-start | bytes 393224 | tf_op jit(solution)/shard_map/ppermute | solution.py:315
  10.3 0.4 %collective-permute-start.5 = (bf16[2,64,512]{2,1,0:T(8,128)(2,1)S(1)}, bf16[2,64,512]{2,1,0:T(8,128)(2,1)S(1)}, u32[]{:S(2)}, u32[]{:S(2)}) collective-permute-start(bf16[2,64,512]{2,1,0:T(8,128)(2,1)S(1)} %get-tuple-element.37), channel_id=1, source_target_pairs={{0,4},{1,5},{2,6},{3,7},{4,0},{5,1},{6,2},{7,3},{8,12},{9,13},{10,... | collective-permute-start | bytes 393224 | tf_op jit(solution)/shard_map/ppermute | solution.py:315
  10.7 1.6 %copy-done = bf16[1,4,32,64,128]{4,3,2,1,0:T(8,128)(2,1)S(1)} copy-done((bf16[1,4,32,64,128]{4,3,2,1,0:T(8,128)(2,1)S(1)}, bf16[1,4,32,64,128]{4,3,2,1,0:T(8,128)(2,1)}, u32[]{:S(2)}) %copy-start) | copy-done | bytes 2097176
  12.3 0.7 %prepare_block.2 = (bf16[2048,512]{1,0:T(8,128)(2,1)S(1)}, bf16[512,2048]{1,0:T(8,128)(2,1)S(1)}) custom-call(bf16[1,4,32,64,128]{4,3,2,1,0:T(8,128)(2,1)S(1)} %copy-done), custom_call_target="tpu_custom_call" | custom-call | tf_op jit(solution)/shard_map/prepare_block/pallas_call | solution.py:35
  13.0 0.0 collective-permute-done.1.refs_7_
  13.0 0.4 collective-permute-done.theta_ref
  13.4 0.0 collective-permute-done.2.chol_ref
  13.4 0.0 copy-done.3
  13.4 0.7 %pick_tiles.3 = (bf16[2,64,512]{2,1,0:T(8,128)(2,1)S(1)}, bf16[2,64,512]{2,1,0:T(8,128)(2,1)S(1)}, bf16[2,64,512]{2,1,0:T(8,128)(2,1)S(1)}, bf16[2,64,512]{2,1,0:T(8,128)(2,1)S(1)}) custom-call(s32[4,16]{1,0:T(4,128)S(1)} %bitcast.3, bf16[1,64,1280]{2,1,0:T(8,128)(2,1)S(1)} %collective-permute-done.theta_ref), custom_call_target="tpu_custom_call" | custom-call | tf_op jit(solution)/shard_map/pick_tiles/pallas_call | solution.py:63
  14.2 1.7 %collective-permute-start.6 = (bf16[2,64,512]{2,1,0:T(8,128)(2,1)S(1)}, bf16[2,64,512]{2,1,0:T(8,128)(2,1)S(1)}, u32[]{:S(2)}, u32[]{:S(2)}) collective-permute-start(bf16[2,64,512]{2,1,0:T(8,128)(2,1)S(1)} %get-tuple-element.43), channel_id=1, source_target_pairs={{0,2},{1,3},{2,0},{3,1},{4,6},{5,7},{6,4},{7,5},{8,10},{9,11},{10,... | collective-permute-start | bytes 393224 | tf_op jit(solution)/shard_map/ppermute | solution.py:315
  15.8 3.7 %collective-permute-start.7 = (bf16[2,64,512]{2,1,0:T(8,128)(2,1)S(1)}, bf16[2,64,512]{2,1,0:T(8,128)(2,1)S(1)}, u32[]{:S(2)}, u32[]{:S(2)}) collective-permute-start(bf16[2,64,512]{2,1,0:T(8,128)(2,1)S(1)} %get-tuple-element.44), channel_id=1, source_target_pairs={{0,4},{1,5},{2,6},{3,7},{4,0},{5,1},{6,2},{7,3},{8,12},{9,13},{10,... | collective-permute-start | bytes 393224 | tf_op jit(solution)/shard_map/ppermute | solution.py:315
  19.5 0.0 collective-permute-start.8
  19.5 0.0 collective-permute-done.3.refs_9_
  19.5 0.7 %prepare_block.3 = (bf16[2048,512]{1,0:T(8,128)(2,1)S(1)}, bf16[512,2048]{1,0:T(8,128)(2,1)S(1)}) custom-call(bf16[1,4,32,64,128]{4,3,2,1,0:T(8,128)(2,1)S(1)} %collective-permute-done.2.chol_ref), custom_call_target="tpu_custom_call" | custom-call | tf_op jit(solution)/shard_map/prepare_block/pallas_call | solution.py:35
  20.2 0.0 copy-done.4
  20.2 0.1 collective-permute-start.4
  20.3 0.0 collective-permute-done.5.refs_8_
  20.3 1.1 %collective-permute-done.4.refs_1_ = s32[1,4]{1,0:T(1,128)S(1)} collective-permute-done((s32[1,4]{1,0:T(1,128)S(1)}, s32[1,4]{1,0:T(1,128)S(1)}, u32[]{:S(2)}, u32[]{:S(2)}) %collective-permute-start.4) | collective-permute-done | bytes 48 | tf_op jit(solution)/shard_map/ppermute | solution.py:318
  21.4 2.8 %chip_terms.2 = (f32[8,1,128]{2,1,0:T(1,128)S(1)}, f32[2,512]{1,0:T(2,128)S(1)}) custom-call(s32[1,4]{1,0:T(1,128)S(1)} %copy-done.4, s32[1,4]{1,0:T(1,128)S(1)} %collective-permute-done.4.refs_1_, bf16[2048,512]{1,0:T(8,128)(2,1)S(1)} %get-tuple-element.30.refs_2_, bf16[512,2048]{1,0:T(8,128)(2,1)S(1)} %get-tuple-element.31.refs_3_, ...), custom_call_target="tpu_custom_call" | custom-call | tf_op jit(solution)/shard_map/chip_terms/pallas_call | solution.py:241
  24.2 0.0 collective-permute-done.6.refs_7_
  24.2 0.0 collective-permute-done.7.refs_8_
  24.2 1.3 %collective-permute-done.8.refs_9_ = bf16[2,64,512]{2,1,0:T(8,128)(2,1)S(1)} collective-permute-done((bf16[2,64,512]{2,1,0:T(8,128)(2,1)S(1)}, bf16[2,64,512]{2,1,0:T(8,128)(2,1)S(1)}, u32[]{:S(2)}, u32[]{:S(2)}) %collective-permute-start.8) | collective-permute-done | bytes 131104 | tf_op jit(solution)/shard_map/ppermute | solution.py:315
  25.6 2.4 %chip_terms.3 = f32[8,1,128]{2,1,0:T(1,128)S(1)} custom-call(f32[2,512]{1,0:T(2,128)S(1)} %get-tuple-element.39.refs_0_, f32[8,1,128]{2,1,0:T(1,128)S(1)} %get-tuple-element.40.refs_1_, bf16[2048,512]{1,0:T(8,128)(2,1)S(1)} %get-tuple-element.30.refs_2_, bf16[512,2048]{1,0:T(8,128)(2,1)S(1)} %get-tuple-element.31.refs_3_, ...), custom_call_target="tpu_custom_call" | custom-call | tf_op jit(solution)/shard_map/chip_terms/pallas_call | solution.py:241
  27.9 9.3 %all_to_all.5.rows_ref = f32[8,1,128]{2,1,0:T(1,128)} all-to-all(f32[8,1,128]{2,1,0:T(1,128)S(1)} %chip_terms.3), channel_id=1, replica_groups={{6,4,2,0,14,12,10,8},{7,5,3,1,15,13,11,9},{22,20,18,16,30,28,26,24},{23..., dimensions={0} | all-to-all | bytes 8192 | tf_op jit(solution)/shard_map/all_to_all | solution.py:339
  37.2 1.4 %finish.1 = (f32[1,512]{1,0:T(1,128)}, f32[1,1]{1,0:T(1,128)}) custom-call(f32[8,1,128]{2,1,0:T(1,128)} %all_to_all.5.rows_ref), custom_call_target="tpu_custom_call" | custom-call | tf_op jit(solution)/shard_map/finish/pallas_call | solution.py:292
  (4 shorter events, 0.0 us)
Async XLA Ops:
  0.6 12.8 %collective-permute-start.2 = (bf16[1,4,32,64,128]{4,3,2,1,0:T(8,128)(2,1)}, bf16[1,4,32,64,128]{4,3,2,1,0:T(8,128)(2,1)S(1)}, u32[]{:S(2)}, u32[]{:S(2)}) collective-permute-start(bf16[1,4,32,64,128]{4,3,2,1,0:T(8,128)(2,1)} %chol_ref.1), channel_id=1, source_target_pairs={{0,1},{1,0},{2,3},{3,2},{4,5},{5,4},{6,7},{7,6},{8,9},{9,8},{10,11... | collective-permute-start | bytes 6291464 | tf_op jit(solution)/shard_map/ppermute | solution.py:318
  1.1 12.3 %collective-permute-start = (bf16[1,64,1280]{2,1,0:T(8,128)(2,1)}, bf16[1,64,1280]{2,1,0:T(8,128)(2,1)S(1)}, u32[]{:S(2)}, u32[]{:S(2)}) collective-permute-start(bf16[1,64,1280]{2,1,0:T(8,128)(2,1)} %theta_ref.1), channel_id=1, source_target_pairs={{0,8},{1,9},{2,10},{3,11},{4,12},{5,13},{6,14},{7,15},{8,0},{9,1},... | collective-permute-start | bytes 491528 | tf_op jit(solution)/shard_map/ppermute | solution.py:315
  4.8 0.9 %copy-start.1 = (bf16[1,64,1280]{2,1,0:T(8,128)(2,1)S(1)}, bf16[1,64,1280]{2,1,0:T(8,128)(2,1)}, u32[]{:S(2)}) copy-start(bf16[1,64,1280]{2,1,0:T(8,128)(2,1)} %theta_ref.1) | copy-start | bytes 491524
  5.8 0.7 %copy-start.2 = (s32[16,4]{0,1:T(4,128)S(1)}, s32[16,4]{0,1:T(4,128)}, u32[]{:S(2)}) copy-start(s32[16,4]{0,1:T(4,128)} %param.7) | copy-start | bytes 772
  6.4 7.0 %copy-start.3 = (s32[16,4]{0,1:T(4,128)S(1)}, s32[16,4]{0,1:T(4,128)}, u32[]{:S(2)}) copy-start(s32[16,4]{0,1:T(4,128)} %param.7) | copy-start | bytes 772
  7.2 5.9 %collective-permute-start.1 = (bf16[2,64,512]{2,1,0:T(8,128)(2,1)S(1)}, bf16[2,64,512]{2,1,0:T(8,128)(2,1)S(1)}, u32[]{:S(2)}, u32[]{:S(2)}) collective-permute-start(bf16[2,64,512]{2,1,0:T(8,128)(2,1)S(1)} %get-tuple-element.25), channel_id=1, source_target_pairs={{0,2},{1,3},{2,0},{3,1},{4,6},{5,7},{6,4},{7,5},{8,10},{9,11},{10,... | collective-permute-start | bytes 393224 | tf_op jit(solution)/shard_map/ppermute | solution.py:315
  8.8 10.8 %collective-permute-start.3 = (bf16[2,64,512]{2,1,0:T(8,128)(2,1)S(1)}, bf16[2,64,512]{2,1,0:T(8,128)(2,1)S(1)}, u32[]{:S(2)}, u32[]{:S(2)}) collective-permute-start(bf16[2,64,512]{2,1,0:T(8,128)(2,1)S(1)} %get-tuple-element.28), channel_id=1, source_target_pairs={{0,6},{1,7},{2,4},{3,5},{4,2},{5,3},{6,0},{7,1},{8,14},{9,15},{10,... | collective-permute-start | bytes 393224 | tf_op jit(solution)/shard_map/ppermute | solution.py:315
  10.3 10.1 %collective-permute-start.5 = (bf16[2,64,512]{2,1,0:T(8,128)(2,1)S(1)}, bf16[2,64,512]{2,1,0:T(8,128)(2,1)S(1)}, u32[]{:S(2)}, u32[]{:S(2)}) collective-permute-start(bf16[2,64,512]{2,1,0:T(8,128)(2,1)S(1)} %get-tuple-element.37), channel_id=1, source_target_pairs={{0,4},{1,5},{2,6},{3,7},{4,0},{5,1},{6,2},{7,3},{8,12},{9,13},{10,... | collective-permute-start | bytes 393224 | tf_op jit(solution)/shard_map/ppermute | solution.py:315
  10.7 1.6 %copy-start = (bf16[1,4,32,64,128]{4,3,2,1,0:T(8,128)(2,1)S(1)}, bf16[1,4,32,64,128]{4,3,2,1,0:T(8,128)(2,1)}, u32[]{:S(2)}) copy-start(bf16[1,4,32,64,128]{4,3,2,1,0:T(8,128)(2,1)} %chol_ref.1) | copy-start | bytes 6291460
  12.3 7.9 %copy-start.4 = (s32[1,4]{1,0:T(1,128)S(1)}, s32[1,4]{1,0:T(1,128)}, u32[]{:S(2)}) copy-start(s32[1,4]{1,0:T(1,128)} %refs_0_.1) | copy-start | bytes 52
  14.2 10.1 %collective-permute-start.6 = (bf16[2,64,512]{2,1,0:T(8,128)(2,1)S(1)}, bf16[2,64,512]{2,1,0:T(8,128)(2,1)S(1)}, u32[]{:S(2)}, u32[]{:S(2)}) collective-permute-start(bf16[2,64,512]{2,1,0:T(8,128)(2,1)S(1)} %get-tuple-element.43), channel_id=1, source_target_pairs={{0,2},{1,3},{2,0},{3,1},{4,6},{5,7},{6,4},{7,5},{8,10},{9,11},{10,... | collective-permute-start | bytes 393224 | tf_op jit(solution)/shard_map/ppermute | solution.py:315
  15.8 8.4 %collective-permute-start.7 = (bf16[2,64,512]{2,1,0:T(8,128)(2,1)S(1)}, bf16[2,64,512]{2,1,0:T(8,128)(2,1)S(1)}, u32[]{:S(2)}, u32[]{:S(2)}) collective-permute-start(bf16[2,64,512]{2,1,0:T(8,128)(2,1)S(1)} %get-tuple-element.44), channel_id=1, source_target_pairs={{0,4},{1,5},{2,6},{3,7},{4,0},{5,1},{6,2},{7,3},{8,12},{9,13},{10,... | collective-permute-start | bytes 393224 | tf_op jit(solution)/shard_map/ppermute | solution.py:315
  19.5 6.1 %collective-permute-start.8 = (bf16[2,64,512]{2,1,0:T(8,128)(2,1)S(1)}, bf16[2,64,512]{2,1,0:T(8,128)(2,1)S(1)}, u32[]{:S(2)}, u32[]{:S(2)}) collective-permute-start(bf16[2,64,512]{2,1,0:T(8,128)(2,1)S(1)} %get-tuple-element.45), channel_id=1, source_target_pairs={{0,6},{1,7},{2,4},{3,5},{4,2},{5,3},{6,0},{7,1},{8,14},{9,15},{10,... | collective-permute-start | bytes 393224 | tf_op jit(solution)/shard_map/ppermute | solution.py:315
  20.2 1.2 %collective-permute-start.4 = (s32[1,4]{1,0:T(1,128)S(1)}, s32[1,4]{1,0:T(1,128)S(1)}, u32[]{:S(2)}, u32[]{:S(2)}) collective-permute-start(s32[1,4]{1,0:T(1,128)S(1)} %copy-done.4), channel_id=1, source_target_pairs={{0,1},{1,0},{2,3},{3,2},{4,5},{5,4},{6,7},{7,6},{8,9},{9,8},{10,11... | collective-permute-start | bytes 56 | tf_op jit(solution)/shard_map/ppermute | solution.py:318

commit v26 on v25

--- a/solution.py
+++ b/solution.py
@@ -218,7 +218,7 @@
             lax.dot_general(segment, part, NT, preferred_element_type=jnp.float32) for part in parts
         )
         for i in range(batch):
-            owner = chip ^ (first + index + i) ^ (out_ref.shape[0] // 4 + 1)
+            owner = chip ^ (first + index + i) ^ (out_ref.shape[0] * 3 // 4 + 1)
             out_ref[pl.ds(owner, 1), 0, :used + 8] = sums[i:i + 1]
 
     if count == batch:
@@ -262,7 +262,7 @@
 
 def finish_kernel(rows_ref, bias_ref, energy_ref, bias_buf, energy_buf, sems, *, used, scale):
     chips, _, width = rows_ref.shape
-    turn = chips // 4 + 1
+    turn = chips * 3 // 4 + 1
     fit = LANES // used if width == LANES else 0
     lane = lax.broadcasted_iota(jnp.int32, (1, width), 1)
     if fit and chips % fit == 0:
@@ -335,7 +335,7 @@
     screens = [screen, to_core(late_screen)]
     rows, masks = chip_terms(screens, [], blocks, near, 0, NEAR, vectors, chips, out_width)
     rows, = chip_terms([], [masks, rows], blocks, beyond, half, BEYOND, vectors, chips, out_width)
-    same_core = [[(rank ^ (half // 2 + 1)) * CORES + core for rank in range(chips)] for core in range(CORES)]
+    same_core = [[(rank ^ (half * 3 // 2 + 1)) * CORES + core for rank in range(chips)] for core in range(CORES)]
     back = lax.all_to_all(rows, "chol", split_axis=0, concat_axis=0, tiled=True, axis_index_groups=same_core)
     return finish(back, used, 1.0 / (2.0 * occupied * occupied))
 

time: 38.9 us -> 37.8 us (0.972)
  blocking collectives: 9.29 us -> 8.22 us
    all_to_all x1, blocking collectives: 9.29 us -> 8.22 us  [body(): lax.all_to_all(rows, 'chol', split_axis=0, concat_axis=0, tiled=True, axi...]
where the time goes in v26:
time: 37.8 us; the launch traced here: 37.5 us
  starting transfers between devices  13.2 us (35%)
  Pallas kernels  9.35 us (25%)
  blocking collectives  8.22 us (22%)
  local copies, waits for them, and re-layouts  3.23 us (9%)
  waiting for transfers between devices  2.85 us (8%)
  between operations  0.72 us (2%)
    ppermute x7, starting transfers between devices, to_chip(): lax.ppermute(x, 'chol', [(i, i ^ offset * CORES) for i in range(groups)])  12.6 us
    all_to_all x1, blocking collectives, body(): lax.all_to_all(rows, 'chol', split_axis=0, concat_axis=0, tiled=True, axi...  8.22 us
    pallas_call x2, Pallas kernels, chip_terms(): pl.pallas_call(functools.partial(terms_kernel, first=first, count=count,...  5.12 us
    unnamed x10, local copies, waits for them, and re-layouts  3.23 us
    ppermute x7, waiting for transfers between devices, to_chip(): lax.ppermute(x, 'chol', [(i, i ^ offset * CORES) for i in range(groups)])  1.75 us
    pallas_call x2, Pallas kernels, pick_tiles(): pl.pallas_call(pick_kernel, in_specs=[SMEM, VMEM], out_specs=[VMEM] * cou...  1.43 us
    pallas_call x2, Pallas kernels, prepare_block(): pl.pallas_call(prepare_kernel, in_specs=[VMEM], out_specs=[VMEM, VMEM], o...  1.43 us
    pallas_call x1, Pallas kernels, finish(): pl.pallas_call(functools.partial(finish_kernel, used=used, scale=scale),...  1.37 us
  transfers between devices with their start and end apart: 9, of which 3 were waited for; matrix products, arithmetic and copies ran while one was open for 0% of the time, Pallas kernels for 15%

profile of v26, /device:TPU:0, one launch (start us, length us, event | category | flops | bytes accessed | tf_op | source)
XLA Modules:
  0.0 37.5 jit_solution(18010761192032889773)
XLA Ops:
  0.6 0.5 %collective-permute-start.2 = (bf16[1,4,32,64,128]{4,3,2,1,0:T(8,128)(2,1)}, bf16[1,4,32,64,128]{4,3,2,1,0:T(8,128)(2,1)S(1)}, u32[]{:S(2)}, u32[]{:S(2)}) collective-permute-start(bf16[1,4,32,64,128]{4,3,2,1,0:T(8,128)(2,1)} %chol_ref.1), channel_id=1, source_target_pairs={{0,1},{1,0},{2,3},{3,2},{4,5},{5,4},{6,7},{7,6},{8,9},{9,8},{10,11... | collective-permute-start | bytes 6291464 | tf_op jit(solution)/shard_map/ppermute | solution.py:318
  1.1 3.7 %collective-permute-start = (bf16[1,64,1280]{2,1,0:T(8,128)(2,1)}, bf16[1,64,1280]{2,1,0:T(8,128)(2,1)S(1)}, u32[]{:S(2)}, u32[]{:S(2)}) collective-permute-start(bf16[1,64,1280]{2,1,0:T(8,128)(2,1)} %theta_ref.1), channel_id=1, source_target_pairs={{0,8},{1,9},{2,10},{3,11},{4,12},{5,13},{6,14},{7,15},{8,0},{9,1},... | collective-permute-start | bytes 491528 | tf_op jit(solution)/shard_map/ppermute | solution.py:315
  4.8 0.0 copy-start.1
  4.8 0.9 %copy-done.1 = bf16[1,64,1280]{2,1,0:T(8,128)(2,1)S(1)} copy-done((bf16[1,64,1280]{2,1,0:T(8,128)(2,1)S(1)}, bf16[1,64,1280]{2,1,0:T(8,128)(2,1)}, u32[]{:S(2)}) %copy-start.1) | copy-done | bytes 163864
  5.8 0.7 %copy-done.2 = s32[16,4]{0,1:T(4,128)S(1)} copy-done((s32[16,4]{0,1:T(4,128)S(1)}, s32[16,4]{0,1:T(4,128)}, u32[]{:S(2)}) %copy-start.2) | copy-done | bytes 280
  6.4 0.7 %pick_tiles.2 = (bf16[2,64,512]{2,1,0:T(8,128)(2,1)S(1)}, bf16[2,64,512]{2,1,0:T(8,128)(2,1)S(1)}, bf16[2,64,512]{2,1,0:T(8,128)(2,1)S(1)}, bf16[2,64,512]{2,1,0:T(8,128)(2,1)S(1)}) custom-call(s32[4,16]{1,0:T(4,128)S(1)} %bitcast.2, bf16[1,64,1280]{2,1,0:T(8,128)(2,1)S(1)} %copy-done.1), custom_call_target="tpu_custom_call" | custom-call | tf_op jit(solution)/shard_map/pick_tiles/pallas_call | solution.py:63
  7.2 1.6 %collective-permute-start.1 = (bf16[2,64,512]{2,1,0:T(8,128)(2,1)S(1)}, bf16[2,64,512]{2,1,0:T(8,128)(2,1)S(1)}, u32[]{:S(2)}, u32[]{:S(2)}) collective-permute-start(bf16[2,64,512]{2,1,0:T(8,128)(2,1)S(1)} %get-tuple-element.25), channel_id=1, source_target_pairs={{0,2},{1,3},{2,0},{3,1},{4,6},{5,7},{6,4},{7,5},{8,10},{9,11},{10,... | collective-permute-start | bytes 393224 | tf_op jit(solution)/shard_map/ppermute | solution.py:315
  8.8 1.5 %collective-permute-start.3 = (bf16[2,64,512]{2,1,0:T(8,128)(2,1)S(1)}, bf16[2,64,512]{2,1,0:T(8,128)(2,1)S(1)}, u32[]{:S(2)}, u32[]{:S(2)}) collective-permute-start(bf16[2,64,512]{2,1,0:T(8,128)(2,1)S(1)} %get-tuple-element.28), channel_id=1, source_target_pairs={{0,6},{1,7},{2,4},{3,5},{4,2},{5,3},{6,0},{7,1},{8,14},{9,15},{10,... | collective-permute-start | bytes 393224 | tf_op jit(solution)/shard_map/ppermute | solution.py:315
  10.3 0.4 %collective-permute-start.5 = (bf16[2,64,512]{2,1,0:T(8,128)(2,1)S(1)}, bf16[2,64,512]{2,1,0:T(8,128)(2,1)S(1)}, u32[]{:S(2)}, u32[]{:S(2)}) collective-permute-start(bf16[2,64,512]{2,1,0:T(8,128)(2,1)S(1)} %get-tuple-element.37), channel_id=1, source_target_pairs={{0,4},{1,5},{2,6},{3,7},{4,0},{5,1},{6,2},{7,3},{8,12},{9,13},{10,... | collective-permute-start | bytes 393224 | tf_op jit(solution)/shard_map/ppermute | solution.py:315
  10.7 1.6 %copy-done = bf16[1,4,32,64,128]{4,3,2,1,0:T(8,128)(2,1)S(1)} copy-done((bf16[1,4,32,64,128]{4,3,2,1,0:T(8,128)(2,1)S(1)}, bf16[1,4,32,64,128]{4,3,2,1,0:T(8,128)(2,1)}, u32[]{:S(2)}) %copy-start) | copy-done | bytes 2097176
  12.3 0.7 %prepare_block.2 = (bf16[2048,512]{1,0:T(8,128)(2,1)S(1)}, bf16[512,2048]{1,0:T(8,128)(2,1)S(1)}) custom-call(bf16[1,4,32,64,128]{4,3,2,1,0:T(8,128)(2,1)S(1)} %copy-done), custom_call_target="tpu_custom_call" | custom-call | tf_op jit(solution)/shard_map/prepare_block/pallas_call | solution.py:35
  13.0 0.0 collective-permute-done.1.refs_7_
  13.0 0.4 %collective-permute-done.theta_ref = bf16[1,64,1280]{2,1,0:T(8,128)(2,1)S(1)} collective-permute-done((bf16[1,64,1280]{2,1,0:T(8,128)(2,1)}, bf16[1,64,1280]{2,1,0:T(8,128)(2,1)S(1)}, u32[]{:S(2)}, u32[]{:S(2)}) %collective-permute-start) | collective-permute-done | bytes 163872 | tf_op jit(solution)/shard_map/ppermute | solution.py:315
  13.4 0.0 collective-permute-done.2.chol_ref
  13.4 0.0 copy-done.3
  13.4 0.7 %pick_tiles.3 = (bf16[2,64,512]{2,1,0:T(8,128)(2,1)S(1)}, bf16[2,64,512]{2,1,0:T(8,128)(2,1)S(1)}, bf16[2,64,512]{2,1,0:T(8,128)(2,1)S(1)}, bf16[2,64,512]{2,1,0:T(8,128)(2,1)S(1)}) custom-call(s32[4,16]{1,0:T(4,128)S(1)} %bitcast.3, bf16[1,64,1280]{2,1,0:T(8,128)(2,1)S(1)} %collective-permute-done.theta_ref), custom_call_target="tpu_custom_call" | custom-call | tf_op jit(solution)/shard_map/pick_tiles/pallas_call | solution.py:63
  14.2 1.7 %collective-permute-start.6 = (bf16[2,64,512]{2,1,0:T(8,128)(2,1)S(1)}, bf16[2,64,512]{2,1,0:T(8,128)(2,1)S(1)}, u32[]{:S(2)}, u32[]{:S(2)}) collective-permute-start(bf16[2,64,512]{2,1,0:T(8,128)(2,1)S(1)} %get-tuple-element.43), channel_id=1, source_target_pairs={{0,2},{1,3},{2,0},{3,1},{4,6},{5,7},{6,4},{7,5},{8,10},{9,11},{10,... | collective-permute-start | bytes 393224 | tf_op jit(solution)/shard_map/ppermute | solution.py:315
  15.8 3.7 %collective-permute-start.7 = (bf16[2,64,512]{2,1,0:T(8,128)(2,1)S(1)}, bf16[2,64,512]{2,1,0:T(8,128)(2,1)S(1)}, u32[]{:S(2)}, u32[]{:S(2)}) collective-permute-start(bf16[2,64,512]{2,1,0:T(8,128)(2,1)S(1)} %get-tuple-element.44), channel_id=1, source_target_pairs={{0,4},{1,5},{2,6},{3,7},{4,0},{5,1},{6,2},{7,3},{8,12},{9,13},{10,... | collective-permute-start | bytes 393224 | tf_op jit(solution)/shard_map/ppermute | solution.py:315
  19.5 0.0 collective-permute-start.8
  19.5 0.0 collective-permute-done.3.refs_9_
  19.5 0.7 %prepare_block.3 = (bf16[2048,512]{1,0:T(8,128)(2,1)S(1)}, bf16[512,2048]{1,0:T(8,128)(2,1)S(1)}) custom-call(bf16[1,4,32,64,128]{4,3,2,1,0:T(8,128)(2,1)S(1)} %collective-permute-done.2.chol_ref), custom_call_target="tpu_custom_call" | custom-call | tf_op jit(solution)/shard_map/prepare_block/pallas_call | solution.py:35
  20.2 0.0 copy-done.4
  20.2 0.1 collective-permute-start.4
  20.3 0.0 collective-permute-done.5.refs_8_
  20.3 1.1 %collective-permute-done.4.refs_1_ = s32[1,4]{1,0:T(1,128)S(1)} collective-permute-done((s32[1,4]{1,0:T(1,128)S(1)}, s32[1,4]{1,0:T(1,128)S(1)}, u32[]{:S(2)}, u32[]{:S(2)}) %collective-permute-start.4) | collective-permute-done | bytes 48 | tf_op jit(solution)/shard_map/ppermute | solution.py:318
  21.4 2.8 %chip_terms.2 = (f32[8,1,128]{2,1,0:T(1,128)S(1)}, f32[2,512]{1,0:T(2,128)S(1)}) custom-call(s32[1,4]{1,0:T(1,128)S(1)} %copy-done.4, s32[1,4]{1,0:T(1,128)S(1)} %collective-permute-done.4.refs_1_, bf16[2048,512]{1,0:T(8,128)(2,1)S(1)} %get-tuple-element.30.refs_2_, bf16[512,2048]{1,0:T(8,128)(2,1)S(1)} %get-tuple-element.31.refs_3_, ...), custom_call_target="tpu_custom_call" | custom-call | tf_op jit(solution)/shard_map/chip_terms/pallas_call | solution.py:241
  24.2 0.0 collective-permute-done.6.refs_7_
  24.2 0.0 collective-permute-done.7.refs_8_
  24.2 1.3 %collective-permute-done.8.refs_9_ = bf16[2,64,512]{2,1,0:T(8,128)(2,1)S(1)} collective-permute-done((bf16[2,64,512]{2,1,0:T(8,128)(2,1)S(1)}, bf16[2,64,512]{2,1,0:T(8,128)(2,1)S(1)}, u32[]{:S(2)}, u32[]{:S(2)}) %collective-permute-start.8) | collective-permute-done | bytes 131104 | tf_op jit(solution)/shard_map/ppermute | solution.py:315
  25.6 2.4 %chip_terms.3 = f32[8,1,128]{2,1,0:T(1,128)S(1)} custom-call(f32[2,512]{1,0:T(2,128)S(1)} %get-tuple-element.39.refs_0_, f32[8,1,128]{2,1,0:T(1,128)S(1)} %get-tuple-element.40.refs_1_, bf16[2048,512]{1,0:T(8,128)(2,1)S(1)} %get-tuple-element.30.refs_2_, bf16[512,2048]{1,0:T(8,128)(2,1)S(1)} %get-tuple-element.31.refs_3_, ...), custom_call_target="tpu_custom_call" | custom-call | tf_op jit(solution)/shard_map/chip_terms/pallas_call | solution.py:241
  27.9 8.2 %all_to_all.5.rows_ref = f32[8,1,128]{2,1,0:T(1,128)} all-to-all(f32[8,1,128]{2,1,0:T(1,128)S(1)} %chip_terms.3), channel_id=1, replica_groups={{14,12,10,8,6,4,2,0},{15,13,11,9,7,5,3,1},{30,28,26,24,22,20,18,16},{31..., dimensions={0} | all-to-all | bytes 8192 | tf_op jit(solution)/shard_map/all_to_all | solution.py:339
  36.2 1.4 %finish.1 = (f32[1,512]{1,0:T(1,128)}, f32[1,1]{1,0:T(1,128)}) custom-call(f32[8,1,128]{2,1,0:T(1,128)} %all_to_all.5.rows_ref), custom_call_target="tpu_custom_call" | custom-call | tf_op jit(solution)/shard_map/finish/pallas_call | solution.py:292
  (4 shorter events, 0.0 us)
Async XLA Ops:
  0.6 12.8 %collective-permute-start.2 = (bf16[1,4,32,64,128]{4,3,2,1,0:T(8,128)(2,1)}, bf16[1,4,32,64,128]{4,3,2,1,0:T(8,128)(2,1)S(1)}, u32[]{:S(2)}, u32[]{:S(2)}) collective-permute-start(bf16[1,4,32,64,128]{4,3,2,1,0:T(8,128)(2,1)} %chol_ref.1), channel_id=1, source_target_pairs={{0,1},{1,0},{2,3},{3,2},{4,5},{5,4},{6,7},{7,6},{8,9},{9,8},{10,11... | collective-permute-start | bytes 6291464 | tf_op jit(solution)/shard_map/ppermute | solution.py:318
  1.1 12.3 %collective-permute-start = (bf16[1,64,1280]{2,1,0:T(8,128)(2,1)}, bf16[1,64,1280]{2,1,0:T(8,128)(2,1)S(1)}, u32[]{:S(2)}, u32[]{:S(2)}) collective-permute-start(bf16[1,64,1280]{2,1,0:T(8,128)(2,1)} %theta_ref.1), channel_id=1, source_target_pairs={{0,8},{1,9},{2,10},{3,11},{4,12},{5,13},{6,14},{7,15},{8,0},{9,1},... | collective-permute-start | bytes 491528 | tf_op jit(solution)/shard_map/ppermute | solution.py:315
  4.8 0.9 %copy-start.1 = (bf16[1,64,1280]{2,1,0:T(8,128)(2,1)S(1)}, bf16[1,64,1280]{2,1,0:T(8,128)(2,1)}, u32[]{:S(2)}) copy-start(bf16[1,64,1280]{2,1,0:T(8,128)(2,1)} %theta_ref.1) | copy-start | bytes 491524
  5.8 0.7 %copy-start.2 = (s32[16,4]{0,1:T(4,128)S(1)}, s32[16,4]{0,1:T(4,128)}, u32[]{:S(2)}) copy-start(s32[16,4]{0,1:T(4,128)} %param.7) | copy-start | bytes 772
  6.4 7.0 %copy-start.3 = (s32[16,4]{0,1:T(4,128)S(1)}, s32[16,4]{0,1:T(4,128)}, u32[]{:S(2)}) copy-start(s32[16,4]{0,1:T(4,128)} %param.7) | copy-start | bytes 772
  7.2 5.9 %collective-permute-start.1 = (bf16[2,64,512]{2,1,0:T(8,128)(2,1)S(1)}, bf16[2,64,512]{2,1,0:T(8,128)(2,1)S(1)}, u32[]{:S(2)}, u32[]{:S(2)}) collective-permute-start(bf16[2,64,512]{2,1,0:T(8,128)(2,1)S(1)} %get-tuple-element.25), channel_id=1, source_target_pairs={{0,2},{1,3},{2,0},{3,1},{4,6},{5,7},{6,4},{7,5},{8,10},{9,11},{10,... | collective-permute-start | bytes 393224 | tf_op jit(solution)/shard_map/ppermute | solution.py:315
  8.8 10.8 %collective-permute-start.3 = (bf16[2,64,512]{2,1,0:T(8,128)(2,1)S(1)}, bf16[2,64,512]{2,1,0:T(8,128)(2,1)S(1)}, u32[]{:S(2)}, u32[]{:S(2)}) collective-permute-start(bf16[2,64,512]{2,1,0:T(8,128)(2,1)S(1)} %get-tuple-element.28), channel_id=1, source_target_pairs={{0,6},{1,7},{2,4},{3,5},{4,2},{5,3},{6,0},{7,1},{8,14},{9,15},{10,... | collective-permute-start | bytes 393224 | tf_op jit(solution)/shard_map/ppermute | solution.py:315
  10.3 10.1 %collective-permute-start.5 = (bf16[2,64,512]{2,1,0:T(8,128)(2,1)S(1)}, bf16[2,64,512]{2,1,0:T(8,128)(2,1)S(1)}, u32[]{:S(2)}, u32[]{:S(2)}) collective-permute-start(bf16[2,64,512]{2,1,0:T(8,128)(2,1)S(1)} %get-tuple-element.37), channel_id=1, source_target_pairs={{0,4},{1,5},{2,6},{3,7},{4,0},{5,1},{6,2},{7,3},{8,12},{9,13},{10,... | collective-permute-start | bytes 393224 | tf_op jit(solution)/shard_map/ppermute | solution.py:315
  10.7 1.6 %copy-start = (bf16[1,4,32,64,128]{4,3,2,1,0:T(8,128)(2,1)S(1)}, bf16[1,4,32,64,128]{4,3,2,1,0:T(8,128)(2,1)}, u32[]{:S(2)}) copy-start(bf16[1,4,32,64,128]{4,3,2,1,0:T(8,128)(2,1)} %chol_ref.1) | copy-start | bytes 6291460
  12.3 7.9 %copy-start.4 = (s32[1,4]{1,0:T(1,128)S(1)}, s32[1,4]{1,0:T(1,128)}, u32[]{:S(2)}) copy-start(s32[1,4]{1,0:T(1,128)} %refs_0_.1) | copy-start | bytes 52
  14.2 10.1 %collective-permute-start.6 = (bf16[2,64,512]{2,1,0:T(8,128)(2,1)S(1)}, bf16[2,64,512]{2,1,0:T(8,128)(2,1)S(1)}, u32[]{:S(2)}, u32[]{:S(2)}) collective-permute-start(bf16[2,64,512]{2,1,0:T(8,128)(2,1)S(1)} %get-tuple-element.43), channel_id=1, source_target_pairs={{0,2},{1,3},{2,0},{3,1},{4,6},{5,7},{6,4},{7,5},{8,10},{9,11},{10,... | collective-permute-start | bytes 393224 | tf_op jit(solution)/shard_map/ppermute | solution.py:315
  15.8 8.4 %collective-permute-start.7 = (bf16[2,64,512]{2,1,0:T(8,128)(2,1)S(1)}, bf16[2,64,512]{2,1,0:T(8,128)(2,1)S(1)}, u32[]{:S(2)}, u32[]{:S(2)}) collective-permute-start(bf16[2,64,512]{2,1,0:T(8,128)(2,1)S(1)} %get-tuple-element.44), channel_id=1, source_target_pairs={{0,4},{1,5},{2,6},{3,7},{4,0},{5,1},{6,2},{7,3},{8,12},{9,13},{10,... | collective-permute-start | bytes 393224 | tf_op jit(solution)/shard_map/ppermute | solution.py:315
  19.5 6.1 %collective-permute-start.8 = (bf16[2,64,512]{2,1,0:T(8,128)(2,1)S(1)}, bf16[2,64,512]{2,1,0:T(8,128)(2,1)S(1)}, u32[]{:S(2)}, u32[]{:S(2)}) collective-permute-start(bf16[2,64,512]{2,1,0:T(8,128)(2,1)S(1)} %get-tuple-element.45), channel_id=1, source_target_pairs={{0,6},{1,7},{2,4},{3,5},{4,2},{5,3},{6,0},{7,1},{8,14},{9,15},{10,... | collective-permute-start | bytes 393224 | tf_op jit(solution)/shard_map/ppermute | solution.py:315
  20.2 1.2 %collective-permute-start.4 = (s32[1,4]{1,0:T(1,128)S(1)}, s32[1,4]{1,0:T(1,128)S(1)}, u32[]{:S(2)}, u32[]{:S(2)}) collective-permute-start(s32[1,4]{1,0:T(1,128)S(1)} %copy-done.4), channel_id=1, source_target_pairs={{0,1},{1,0},{2,3},{3,2},{4,5},{5,4},{6,7},{7,6},{8,9},{9,8},{10,11... | collective-permute-start | bytes 56 | tf_op jit(solution)/shard_map/ppermute | solution.py:318
